TPU v7x, 32 devices: a whole 2x2x4 slice. The times are simulated.
32 devices in a mesh: dp: 2 (over y), fsdp: 8 (over z, core), seq: 2 (over x).
Axes of the slice: x: 2, y: 2, z: 4, core: 2. Of those that a mesh axis runs over, the one named last changes fastest.
Arguments:
- enc_ids: int32 [32, 512], P(('dp', 'fsdp'), 'seq'), may hold values from 0 to 32127
- span_mask: int32 [32, 512], P(('dp', 'fsdp'), 'seq'), may hold values 0 or 1
- segments: int32 [32, 512], P(('dp', 'fsdp'), 'seq'), may hold values from 0 to 3, never falling along the last dimension, each value on 1 to 384 neighbouring positions
- targets: int32 [32, 128], P(('dp', 'fsdp', 'seq')), may hold values from 0 to 32127
- loss_weights: int32 [32, 128], P(('dp', 'fsdp', 'seq')), may hold values from 0 to 1, as said below
- target_segments: int32 [32, 128], P(('dp', 'fsdp', 'seq')), may hold values from 0 to 3, as said below
- embedding: float32 [32128, 768], P('fsdp')
- emb_m: float32 [32128, 768], P('fsdp'), may hold values from -5.722046e-06 to 5.722046e-06
- emb_v: float32 [32128, 768], P('fsdp'), may hold values from 1.36141945e-14 to 5.4456778e-14
- gains: float32 [7, 768], replicated
- gain_m: float32 [7, 768], replicated, may hold values from -0.00012207031 to 0.00012207031
- gain_v: float32 [7, 768], replicated, may hold values from 5.4456778e-12 to 2.1782711e-11
- rel_bias: float32 [2, 32, 12], replicated, may hold values from -3 to 3
- rel_m: float32 [2, 32, 12], replicated, may hold values from -0.00012207031 to 0.00012207031
- rel_v: float32 [2, 32, 12], replicated, may hold values from 5.4456778e-12 to 2.1782711e-11
- enc_w: float32 [192, 36864], P('fsdp')
- enc_m: float32 [192, 36864], P('fsdp'), may hold values from -0.00010681152 to 0.00010681152
- enc_left: float32 [192, 36864], P('fsdp'), as said below
- enc_right: float32 [192, 36864], P('fsdp'), as said below
- enc_lroot: float32 [192, 36864], P('fsdp'), as said below
- enc_rroot: float32 [192, 36864], P('fsdp'), as said below
- dec_w: float32 [256, 36864], P('fsdp')
- dec_m: float32 [256, 36864], P('fsdp'), may hold values from -0.00010681152 to 0.00010681152
- dec_left: float32 [256, 36864], P('fsdp'), as said below
- dec_right: float32 [256, 36864], P('fsdp'), as said below
- dec_lroot: float32 [256, 36864], P('fsdp'), as said below
- dec_rroot: float32 [256, 36864], P('fsdp'), as said below
Outputs:
- loss_sum: float32 [], replicated
- loss_count: float32 [], replicated
- grad_norm: float32 [], replicated
- new_embedding: float32 [32128, 768], P('fsdp')
- new_emb_m: float32 [32128, 768], P('fsdp')
- new_emb_v: float32 [32128, 768], P('fsdp')
- new_gains: float32 [7, 768], replicated
- new_gain_m: float32 [7, 768], replicated
- new_gain_v: float32 [7, 768], replicated
- new_rel_bias: float32 [2, 32, 12], replicated
- new_rel_m: float32 [2, 32, 12], replicated
- new_rel_v: float32 [2, 32, 12], replicated
- new_enc_w: float32 [192, 36864], P('fsdp')
- new_enc_m: float32 [192, 36864], P('fsdp')
- new_enc_left: float32 [192, 36864], P('fsdp')
- new_enc_right: float32 [192, 36864], P('fsdp')
- new_dec_w: float32 [256, 36864], P('fsdp')
- new_dec_m: float32 [256, 36864], P('fsdp')
- new_dec_left: float32 [256, 36864], P('fsdp')
- new_dec_right: float32 [256, 36864], P('fsdp')
Inputs may be any that keep to these rules, and one draw needn't show every extreme that they name: `loss_weights`: 0 or 1; the share of ones differs between rows. `target_segments`: never falling along a row; every row holds each of the numbers 0 to 3. `enc_left`: each block, read as a 192 x 192 matrix, is symmetric. `enc_right`: each block, read as a 192 x 192 matrix, is symmetric. `enc_lroot`: each block, read as a 192 x 192 matrix, is symmetric. `enc_rroot`: each block, read as a 192 x 192 matrix, is symmetric. `dec_left`: each block, read as a 192 x 192 matrix, is symmetric. `dec_right`: each block, read as a 192 x 192 matrix, is symmetric. `dec_lroot`: each block, read as a 192 x 192 matrix, is symmetric. `dec_rroot`: each block, read as a 192 x 192 matrix, is symmetric.
All inputs are finite; a program needn't handle non-finite values. No bound on the sum of `span_mask` on one device may be relied on, other than what follows from the above.
Results may differ from a plain program's by a relative error of at most 0.00355.
Values may be sent and summed in bfloat16 or wider, within the bound.
No kernel may reach another device: no remote copies, remote signals or barrier semaphores. Data moves between devices by JAX's collectives and lax.ppermute only.
A program may use at most 512 MiB of HBM per device.

v0:
```python
import math

import jax
import jax.numpy as jnp
from jax import lax
from jax.sharding import PartitionSpec as P

D = 768
H = 12
DH = 64
FF = 3072
VOCAB = 32128
NBK = 32
REACH = 128
BLOCK = 192
STEP = 10


norm_eps = 1e-06
neg_fill = -1000000000.0
sentinel_offset = 29
beta_first = 0.9
beta_second = 0.999
adam_eps = 1e-08
adam_rate = 0.5
shampoo_rate = 0.01
stat_decay = 0.999
weight_decay = 0.01
clip_limit = 0.05
highest = lax.Precision.HIGHEST


def joined(value, axis, join):
    pieces = jax.tree.map(lambda part: lax.all_gather(part, axis), value)
    head = jax.tree.map(lambda part: part[0], pieces)
    tail = jax.tree.map(lambda part: part[1:], pieces)
    subtotal, _ = lax.scan(lambda subtotal, section: (join(subtotal, section), None), head, tail)
    return subtotal


def bucket_edges(buckets, exact, reach):
    edges = list(range(1, exact))
    spread = buckets - exact
    for place in range(spread):
        edges.append(int(math.ceil(exact * (reach / exact) ** (place / spread) - 1e-09)))
    return edges


def position_buckets(query_pos, key_pos, causal):
    offset = key_pos[None, :] - query_pos[:, None]
    if causal:
        distance = jnp.maximum(-offset, 0)
        result = jnp.zeros(offset.shape, jnp.int32)
        edges = bucket_edges(NBK, NBK // 2, REACH)
    else:
        distance = jnp.abs(offset)
        result = jnp.where(offset > 0, NBK // 2, 0).astype(jnp.int32)
        edges = bucket_edges(NBK // 2, NBK // 4, REACH)
    for edge in edges:
        result = result + (distance >= edge).astype(jnp.int32)
    return result


def bucket_onehot(buckets):
    return (buckets[None] == jnp.arange(NBK, dtype=jnp.int32)[:, None, None]).astype(jnp.float32)


def layer_shapes(decoder):
    if decoder:
        return [(D, 3 * D), (D, D), (D, D), (D, 2 * D), (D, D), (D, FF), (FF, D)]
    return [(D, 3 * D), (D, D), (D, FF), (FF, D)]


def as_blocks(flat):
    return flat.reshape(flat.shape[0], BLOCK, BLOCK)


def as_rows(blocks):
    return blocks.reshape(blocks.shape[0], BLOCK * BLOCK)


def unblock(blocks, shapes):
    matrix_list = []
    offset = 0
    for height, breadth in shapes:
        amount = height // BLOCK * (breadth // BLOCK)
        section = blocks[offset : offset + amount].reshape(
            height // BLOCK, breadth // BLOCK, BLOCK, BLOCK
        )
        matrix_list.append(section.transpose(0, 2, 1, 3).reshape(height, breadth))
        offset += amount
    return matrix_list


def rebuild_blocks(matrix_list):
    pieces = []
    for matrix in matrix_list:
        height, breadth = matrix.shape
        tiles = matrix.reshape(height // BLOCK, BLOCK, breadth // BLOCK, BLOCK).transpose(
            0, 2, 1, 3
        )
        pieces.append(tiles.reshape(-1, BLOCK * BLOCK))
    return jnp.concatenate(pieces, axis=0)


def heads(values):
    return values.reshape(values.shape[:-1] + (H, DH))


def merge_heads(values):
    return values.reshape(values.shape[:-2] + (D,))


def project(left, right):
    return jnp.matmul(left, right, preferred_element_type=jnp.float32)


def project_back(left, right):
    return jnp.einsum("btf,df->btd", left, right, preferred_element_type=jnp.float32)


def weight_grad(inputs, grads):
    return jnp.einsum("btd,btf->df", inputs, grads, preferred_element_type=jnp.float32)


def rms(values, gain):
    return values * lax.rsqrt(jnp.mean(values * values, axis=-1, keepdims=True) + norm_eps) * gain


def rms_back(values, gain, grad_out):
    inverse = lax.rsqrt(jnp.mean(values * values, axis=-1, keepdims=True) + norm_eps)
    normed = values * inverse
    grad_gain = jnp.sum(grad_out * normed, axis=(0, 1))
    grad_normed = grad_out * gain
    grad_values = inverse * (
        grad_normed - normed * jnp.mean(grad_normed * normed, axis=-1, keepdims=True)
    )
    return (grad_values, grad_gain)


def scores_of(query, keys, bias, mask):
    scores = jnp.einsum("bqhe,bkhe->bhqk", query, keys, preferred_element_type=jnp.float32)
    if bias is not None:
        scores = scores + bias[None]
    return jnp.where(mask[:, None], scores, neg_fill)


def attend(query, keys, values, bias, mask):
    scores = scores_of(query, keys, bias, mask)
    peak = jnp.max(scores, axis=-1, keepdims=True)
    raised = jnp.exp(scores - peak)
    normalizer = jnp.sum(raised, axis=-1, keepdims=True)
    probs = (raised / normalizer).astype(jnp.bfloat16)
    output = jnp.einsum("bhqk,bkhe->bqhe", probs, values, preferred_element_type=jnp.float32)
    return (merge_heads(output.astype(jnp.bfloat16)), peak + jnp.log(normalizer))


def attend_back(query, keys, values, bias, mask, lse, grad_out):
    probs = jnp.exp(scores_of(query, keys, bias, mask) - lse)
    grad_probs = jnp.einsum("bqhe,bkhe->bhqk", grad_out, values, preferred_element_type=jnp.float32)
    grad_values = jnp.einsum(
        "bhqk,bqhe->bkhe", probs.astype(jnp.bfloat16), grad_out, preferred_element_type=jnp.float32
    )
    grad_scores = (
        probs * (grad_probs - jnp.sum(probs * grad_probs, axis=-1, keepdims=True))
    ).astype(jnp.bfloat16)
    grad_query = jnp.einsum(
        "bhqk,bkhe->bqhe", grad_scores, keys, preferred_element_type=jnp.float32
    )
    grad_keys = jnp.einsum(
        "bhqk,bqhe->bkhe", grad_scores, query, preferred_element_type=jnp.float32
    )
    grad_bias = jnp.sum(grad_scores.astype(jnp.float32), axis=0)
    return (grad_query, grad_keys, grad_values, grad_bias)


def ff_forward(hidden, gain, w_in, w_down):
    normed = rms(hidden, gain).astype(jnp.bfloat16)
    inner = project(normed, w_in)
    active = jax.nn.gelu(inner).astype(jnp.bfloat16)
    return (hidden + project(active, w_down), (normed, inner, active))


def ff_back(hidden, gain, w_in, w_down, cache, grad_out):
    normed, inner, active = cache
    branch_grad = grad_out.astype(jnp.bfloat16)
    down_grad = weight_grad(active, branch_grad)
    grad_active = project_back(branch_grad, w_down)
    unused, gelu_back = jax.vjp(jax.nn.gelu, inner)
    grad_inner = gelu_back(grad_active)[0].astype(jnp.bfloat16)
    in_grad = weight_grad(normed, grad_inner)
    grad_part, grad_gain = rms_back(hidden, gain, project_back(grad_inner, w_in))
    return (grad_out + grad_part, grad_gain, in_grad, down_grad)


def table_rows(table, token_ids, vocab_first):
    local_ids = token_ids - vocab_first
    inside = (local_ids >= 0) & (local_ids < table.shape[0])
    picked = jnp.take(table, jnp.clip(local_ids, 0, table.shape[0] - 1), axis=0)
    return jnp.where(inside[..., None], picked.astype(jnp.float32), 0.0)


def table_grads(grads, token_ids, vocab_first, vocab_local):
    local_ids = token_ids.reshape(-1) - vocab_first
    inside = (local_ids >= 0) & (local_ids < vocab_local)
    slots = jnp.where(inside, local_ids, vocab_local)
    summed = jax.ops.segment_sum(
        grads.reshape(-1, D).astype(jnp.float32), slots, num_segments=vocab_local + 1
    )
    return summed[:vocab_local]


def combine_stats(first_part, second_part):
    peak = jnp.maximum(first_part[0], second_part[0])
    summed = first_part[1] * jnp.exp(first_part[0] - peak) + second_part[1] * jnp.exp(
        second_part[0] - peak
    )
    return (peak, summed, first_part[2] + second_part[2])


def fetch_blocks(master):
    return as_blocks(lax.all_gather(master.astype(jnp.bfloat16), "fsdp", axis=0, tiled=True))


def cross_send(payload):
    return lax.all_to_all(payload, "seq", split_axis=0, concat_axis=1, tiled=True)


def adam_update(weight, gradient, moment, second):
    moment = beta_first * moment + (1 - beta_first) * gradient
    second = beta_second * second + (1 - beta_second) * gradient * gradient
    corrected = moment / (1 - beta_first**STEP)
    scaled = second / (1 - beta_second**STEP)
    weight = weight - adam_rate * (
        corrected / (jnp.sqrt(scaled) + adam_eps) + weight_decay * weight
    )
    return (weight, moment, second)


def shampoo_update(weight, gradient, moment, left, right, left_root, right_root):
    weight, gradient, moment = (as_blocks(weight), as_blocks(gradient), as_blocks(moment))
    left, right, left_root, right_root = (
        as_blocks(left),
        as_blocks(right),
        as_blocks(left_root),
        as_blocks(right_root),
    )
    left = stat_decay * left + (1 - stat_decay) * jnp.einsum(
        "nij,nkj->nik", gradient, gradient, precision=highest
    )
    right = stat_decay * right + (1 - stat_decay) * jnp.einsum(
        "nji,njk->nik", gradient, gradient, precision=highest
    )
    moment = beta_first * moment + (1 - beta_first) * gradient
    shaped = jnp.einsum("nij,njk->nik", left_root, moment, precision=highest)
    direction = jnp.einsum("nij,njk->nik", shaped, right_root, precision=highest)
    weight = weight - shampoo_rate * (direction + weight_decay * weight)
    return (as_rows(weight), as_rows(moment), as_rows(left), as_rows(right))


def on_device(
    enc_ids,
    span_mask,
    segments,
    targets,
    loss_weights,
    target_segments,
    embedding,
    emb_m,
    emb_v,
    gains,
    gain_m,
    gain_v,
    rel_bias,
    rel_m,
    rel_v,
    enc_w,
    enc_m,
    enc_left,
    enc_right,
    enc_lroot,
    enc_rroot,
    dec_w,
    dec_m,
    dec_left,
    dec_right,
    dec_lroot,
    dec_rroot,
):
    fsdp_rank = lax.axis_index("fsdp")
    seq_rank = lax.axis_index("seq")
    seq_rows, half_len = enc_ids.shape
    dec_rows, dec_len = targets.shape
    enc_len = half_len * lax.axis_size("seq")
    enc_in = jnp.where(span_mask == 1, VOCAB - sentinel_offset, enc_ids)
    dec_in = jnp.concatenate([jnp.zeros((dec_rows, 1), jnp.int32), targets[:, :-1]], axis=1)
    all_enc, all_dec, all_targets, all_weights = (
        lax.all_gather(enc_in, "fsdp", axis=0, tiled=True),
        lax.all_gather(dec_in, "fsdp", axis=0, tiled=True),
        lax.all_gather(targets, "fsdp", axis=0, tiled=True),
        lax.all_gather(loss_weights, "fsdp", axis=0, tiled=True),
    )
    table = embedding.astype(jnp.bfloat16)
    vocab_local = table.shape[0]
    vocab_first = fsdp_rank * vocab_local
    hidden0, state0 = (
        lax.psum_scatter(
            table_rows(table, all_enc, vocab_first).astype(jnp.bfloat16),
            "fsdp",
            scatter_dimension=0,
            tiled=True,
        ).astype(jnp.float32),
        lax.psum_scatter(
            table_rows(table, all_dec, vocab_first).astype(jnp.bfloat16),
            "fsdp",
            scatter_dimension=0,
            tiled=True,
        ).astype(jnp.float32),
    )
    enc_mats = unblock(fetch_blocks(enc_w), layer_shapes(False))
    query_pos = seq_rank * half_len + jnp.arange(half_len, dtype=jnp.int32)
    enc_onehot = bucket_onehot(
        position_buckets(query_pos, jnp.arange(enc_len, dtype=jnp.int32), False)
    )
    enc_bias = jnp.einsum("nqk,nh->hqk", enc_onehot, rel_bias[0], precision=highest)
    normed0 = rms(hidden0, gains[0]).astype(jnp.bfloat16)
    enc_qkv = project(normed0, enc_mats[0]).astype(jnp.bfloat16)
    enc_query = heads(enc_qkv[..., :D])
    enc_keys, enc_values, key_segments = (
        lax.all_gather(heads(enc_qkv[..., D : 2 * D]), "seq", axis=1, tiled=True),
        lax.all_gather(heads(enc_qkv[..., 2 * D :]), "seq", axis=1, tiled=True),
        lax.all_gather(segments, "seq", axis=1, tiled=True),
    )
    enc_mask = segments[:, :, None] == key_segments[:, None, :]
    enc_attended, enc_lse = attend(enc_query, enc_keys, enc_values, enc_bias, enc_mask)
    hidden1 = hidden0 + project(enc_attended, enc_mats[1])
    hidden2, enc_cache = ff_forward(hidden1, gains[1], enc_mats[2], enc_mats[3])
    encoded = rms(hidden2, gains[2]).astype(jnp.bfloat16)
    dec_mats = unblock(fetch_blocks(dec_w), layer_shapes(True))
    pairs = cross_send(project(encoded, dec_mats[3]).astype(jnp.bfloat16))
    row_segments = lax.dynamic_slice_in_dim(key_segments, seq_rank * dec_rows, dec_rows, 0)
    cross_mask = target_segments[:, :, None] == row_segments[:, None, :]
    dec_pos = jnp.arange(dec_len, dtype=jnp.int32)
    dec_onehot = bucket_onehot(position_buckets(dec_pos, dec_pos, True))
    dec_bias = jnp.einsum("nqk,nh->hqk", dec_onehot, rel_bias[1], precision=highest)
    causal = (dec_pos[:, None] >= dec_pos[None, :])[None] & (
        target_segments[:, :, None] == target_segments[:, None, :]
    )
    normed3 = rms(state0, gains[3]).astype(jnp.bfloat16)
    self_qkv = project(normed3, dec_mats[0]).astype(jnp.bfloat16)
    self_query = heads(self_qkv[..., :D])
    self_keys = heads(self_qkv[..., D : 2 * D])
    self_values = heads(self_qkv[..., 2 * D :])
    self_attended, self_lse = attend(self_query, self_keys, self_values, dec_bias, causal)
    state1 = state0 + project(self_attended, dec_mats[1])
    normed4 = rms(state1, gains[4]).astype(jnp.bfloat16)
    cross_query = heads(project(normed4, dec_mats[2]).astype(jnp.bfloat16))
    cross_keys = heads(pairs[..., :D])
    cross_values = heads(pairs[..., D:])
    cross_attended, cross_lse = attend(cross_query, cross_keys, cross_values, None, cross_mask)
    state2 = state1 + project(cross_attended, dec_mats[4])
    state3, dec_cache = ff_forward(state2, gains[5], dec_mats[5], dec_mats[6])
    out_scale = D ** (-0.5)
    final = (rms(state3, gains[6]) * out_scale).astype(jnp.bfloat16)
    all_final = lax.all_gather(final.reshape(dec_rows * dec_len, D), "fsdp", axis=0, tiled=True)
    logits = jnp.einsum("nd,vd->nv", all_final, table, preferred_element_type=jnp.float32)
    local_ids = all_targets.reshape(-1) - vocab_first
    target_hot = local_ids[:, None] == jnp.arange(vocab_local, dtype=jnp.int32)[None, :]
    local_top = jnp.max(logits, axis=1)
    local_sum = jnp.sum(jnp.exp(logits - local_top[:, None]), axis=1)
    local_pick = jnp.sum(jnp.where(target_hot, logits, 0.0), axis=1)
    top_all, sum_all, pick_all = joined((local_top, local_sum, local_pick), "fsdp", combine_stats)
    lse = top_all + jnp.log(sum_all)
    token_weights = all_weights.reshape(-1).astype(jnp.float32)
    group_loss = jnp.sum(token_weights * (lse - pick_all))
    group_count = jnp.sum(token_weights)
    grad_logits = (
        token_weights[:, None] * (jnp.exp(logits - lse[:, None]) - target_hot.astype(jnp.float32))
    ).astype(jnp.bfloat16)
    emb_grad = jnp.einsum("nv,nd->vd", grad_logits, all_final, preferred_element_type=jnp.float32)
    grad_final = lax.psum_scatter(
        jnp.dot(grad_logits, table, preferred_element_type=jnp.float32),
        "fsdp",
        scatter_dimension=0,
        tiled=True,
    ).reshape(dec_rows, dec_len, D)
    grad_state3, gain_six = rms_back(state3, gains[6], grad_final * out_scale)
    dec_back = unblock(fetch_blocks(dec_w), layer_shapes(True))
    grad_state2, gain_five, dec_in_grad, dec_down_grad = ff_back(
        state2, gains[5], dec_back[5], dec_back[6], dec_cache, grad_state3
    )
    branch_grad = grad_state2.astype(jnp.bfloat16)
    cross_out_grad = weight_grad(cross_attended, branch_grad)
    grad_cross = project_back(branch_grad, dec_back[4]).astype(jnp.bfloat16)
    cq_grad, ck_grad, cv_grad, unused_bias = attend_back(
        cross_query, cross_keys, cross_values, None, cross_mask, cross_lse, heads(grad_cross)
    )
    grad_cq = merge_heads(cq_grad).astype(jnp.bfloat16)
    grad_pairs = jnp.concatenate([merge_heads(ck_grad), merge_heads(cv_grad)], axis=-1).astype(
        jnp.bfloat16
    )
    cross_query_grad = weight_grad(normed4, grad_cq)
    grad_state1_part, gain_four = rms_back(state1, gains[4], project_back(grad_cq, dec_back[2]))
    grad_state1 = grad_state2 + grad_state1_part
    returned = lax.all_to_all(grad_pairs, "seq", split_axis=1, concat_axis=0, tiled=True)
    cross_pair_grad = weight_grad(encoded, returned)
    grad_encoded = project_back(returned, dec_back[3])
    branch_grad = grad_state1.astype(jnp.bfloat16)
    self_out_grad = weight_grad(self_attended, branch_grad)
    grad_self = project_back(branch_grad, dec_back[1]).astype(jnp.bfloat16)
    sq_grad, sk_grad, sv_grad, dec_bias_grad = attend_back(
        self_query, self_keys, self_values, dec_bias, causal, self_lse, heads(grad_self)
    )
    grad_sqkv = jnp.concatenate(
        [merge_heads(sq_grad), merge_heads(sk_grad), merge_heads(sv_grad)], axis=-1
    ).astype(jnp.bfloat16)
    self_qkv_grad = weight_grad(normed3, grad_sqkv)
    grad_state0_part, gain_three = rms_back(state0, gains[3], project_back(grad_sqkv, dec_back[0]))
    grad_state0 = grad_state1 + grad_state0_part
    dec_rel_grad = jnp.einsum("nqk,hqk->nh", dec_onehot, dec_bias_grad, precision=highest)
    decoder_portion = rebuild_blocks(
        [
            self_qkv_grad,
            self_out_grad,
            cross_query_grad,
            cross_pair_grad,
            cross_out_grad,
            dec_in_grad,
            dec_down_grad,
        ]
    )
    enc_back = unblock(fetch_blocks(enc_w), layer_shapes(False))
    grad_hidden2, gain_two = rms_back(hidden2, gains[2], grad_encoded)
    grad_hidden1, gain_one, encoder_input_gradient, encoder_down_gradient = ff_back(
        hidden1, gains[1], enc_back[2], enc_back[3], enc_cache, grad_hidden2
    )
    branch_grad = grad_hidden1.astype(jnp.bfloat16)
    encoder_output_gradient = weight_grad(enc_attended, branch_grad)
    grad_attn = project_back(branch_grad, enc_back[1]).astype(jnp.bfloat16)
    eq_grad, ek_all, ev_all, enc_bias_grad = attend_back(
        enc_query, enc_keys, enc_values, enc_bias, enc_mask, enc_lse, heads(grad_attn)
    )
    ek_grad, ev_grad = (
        lax.psum_scatter(ek_all, "seq", scatter_dimension=1, tiled=True),
        lax.psum_scatter(ev_all, "seq", scatter_dimension=1, tiled=True),
    )
    grad_eqkv = jnp.concatenate(
        [merge_heads(eq_grad), merge_heads(ek_grad), merge_heads(ev_grad)], axis=-1
    ).astype(jnp.bfloat16)
    encoder_query_key_value_gradient = weight_grad(normed0, grad_eqkv)
    grad_hidden0_part, gain_zero = rms_back(hidden0, gains[0], project_back(grad_eqkv, enc_back[0]))
    grad_hidden0 = grad_hidden1 + grad_hidden0_part
    enc_rel_grad = jnp.einsum("nqk,hqk->nh", enc_onehot, enc_bias_grad, precision=highest)
    encoder_portion = rebuild_blocks(
        [
            encoder_query_key_value_gradient,
            encoder_output_gradient,
            encoder_input_gradient,
            encoder_down_gradient,
        ]
    )
    back_enc, back_dec = (
        lax.all_gather(grad_hidden0.astype(jnp.bfloat16), "fsdp", axis=0, tiled=True),
        lax.all_gather(grad_state0.astype(jnp.bfloat16), "fsdp", axis=0, tiled=True),
    )
    emb_grad = (
        emb_grad
        + table_grads(back_enc, all_enc, vocab_first, vocab_local)
        + table_grads(back_dec, all_dec, vocab_first, vocab_local)
    )
    gain_part = jnp.stack(
        [gain_zero, gain_one, gain_two, gain_three, gain_four, gain_five, gain_six]
    )
    rel_part = jnp.stack([enc_rel_grad, dec_rel_grad])
    enc_shard, dec_shard = (
        lax.psum_scatter(encoder_portion, "fsdp", scatter_dimension=0, tiled=True),
        lax.psum_scatter(decoder_portion, "fsdp", scatter_dimension=0, tiled=True),
    )
    enc_sum, dec_sum, emb_sum, gain_sum, rel_sum, loss_sum, count_sum = lax.psum(
        (enc_shard, dec_shard, emb_grad, gain_part, rel_part, group_loss, group_count),
        ("dp", "seq"),
    )
    loss_count = jnp.maximum(count_sum, 1.0)
    enc_grad = enc_sum / loss_count
    dec_grad = dec_sum / loss_count
    table_grad = emb_sum / loss_count
    local_squares = (
        jnp.sum(enc_grad * enc_grad)
        + jnp.sum(dec_grad * dec_grad)
        + jnp.sum(table_grad * table_grad)
    )
    squares_all, gain_total, rel_total = lax.psum((local_squares, gain_sum, rel_sum), "fsdp")
    gain_grad = gain_total / loss_count
    rel_grad = rel_total / loss_count
    grad_norm = jnp.sqrt(
        squares_all + jnp.sum(gain_grad * gain_grad) + jnp.sum(rel_grad * rel_grad)
    )
    factor = jnp.minimum(1.0, clip_limit / grad_norm)
    new_emb = adam_update(embedding, table_grad * factor, emb_m, emb_v)
    new_gain = adam_update(gains, gain_grad * factor, gain_m, gain_v)
    new_rel = adam_update(rel_bias, rel_grad * factor, rel_m, rel_v)
    new_enc = shampoo_update(
        enc_w, enc_grad * factor, enc_m, enc_left, enc_right, enc_lroot, enc_rroot
    )
    new_dec = shampoo_update(
        dec_w, dec_grad * factor, dec_m, dec_left, dec_right, dec_lroot, dec_rroot
    )
    return (
        loss_sum,
        loss_count,
        grad_norm,
        new_emb[0],
        new_emb[1],
        new_emb[2],
        new_gain[0],
        new_gain[1],
        new_gain[2],
        new_rel[0],
        new_rel[1],
        new_rel[2],
        new_enc[0],
        new_enc[1],
        new_enc[2],
        new_enc[3],
        new_dec[0],
        new_dec[1],
        new_dec[2],
        new_dec[3],
    )


def solution(mesh):
    in_specs = (
        P(("dp", "fsdp"), "seq"),
        P(("dp", "fsdp"), "seq"),
        P(("dp", "fsdp"), "seq"),
        P(("dp", "fsdp", "seq"), None),
        P(("dp", "fsdp", "seq"), None),
        P(("dp", "fsdp", "seq"), None),
        P("fsdp", None),
        P("fsdp", None),
        P("fsdp", None),
        P(),
        P(),
        P(),
        P(),
        P(),
        P(),
        P("fsdp", None),
        P("fsdp", None),
        P("fsdp", None),
        P("fsdp", None),
        P("fsdp", None),
        P("fsdp", None),
        P("fsdp", None),
        P("fsdp", None),
        P("fsdp", None),
        P("fsdp", None),
        P("fsdp", None),
        P("fsdp", None),
    )
    out_specs = (
        P(),
        P(),
        P(),
        P("fsdp", None),
        P("fsdp", None),
        P("fsdp", None),
        P(),
        P(),
        P(),
        P(),
        P(),
        P(),
        P("fsdp", None),
        P("fsdp", None),
        P("fsdp", None),
        P("fsdp", None),
        P("fsdp", None),
        P("fsdp", None),
        P("fsdp", None),
        P("fsdp", None),
    )
    return jax.shard_map(
        on_device, mesh=mesh, in_specs=in_specs, out_specs=out_specs, check_vma=False
    )
```

profile of v0, /device:TPU:0, one launch (start us, length us, event | category | flops | bytes accessed | tf_op | source)
XLA Modules:
  0.0 2646.2 jit_solution(17111926781580196772)
XLA Ops:
  7.9 14.4 all-gather.6
  30.7 22.6 gather_fusion.1
  84.3 45.4 %reduce-scatter.10.cloned.1.call-done = bf16[2,256,768]{2,1,0:T(8,128)(2,1)} async-done(((bf16[16,256,768]{2,1,0:T(8,128)(2,1)}), bf16[2,256,768]{2,1,0:T(8,128)(2,1)}) %reduce-scatter.10.cloned.1.call-update) | async-done | bytes 786448 | tf_op jit(solution)/shard_map/reduce_scatter | solution.py:307
  131.7 128.3 %all-gather.18.cloned.1.call-done = bf16[192,36864]{1,0:T(8,128)(2,1)} async-done(((bf16[24,36864]{1,0:T(8,128)(2,1)}), bf16[192,36864]{1,0:T(8,128)(2,1)}) %all-gather.18.cloned.1.call-update) | async-done | bytes 14155792 | tf_op jit(solution)/shard_map/all_gather | solution.py:222
  303.3 185.8 %copy.354 = pred[32,256,512]{2,0,1:T(32,128)(4,1)S(1)} copy(pred[32,256,512]{1,0,2:T(32,128)(4,1)S(1)} %iota_compare_fusion) | data formatting | bytes 8388608 | tf_op jit(solution)/shard_map/eq | solution.py:65
  836.7 14.0 all-gather.1
  855.7 14.0 all-gather.2
  870.3 14.0 all-gather.3
  901.5 14.1 fusion.223
  916.9 38.6 %reduce-scatter.12.cloned.1.call-done = f32[128,768]{1,0:T(8,128)} async-done(((f32[1024,768]{1,0:T(8,128)}), f32[128,768]{1,0:T(8,128)}) %reduce-scatter.12.cloned.1.call-update) | async-done | bytes 393232 | tf_op jit(solution)/shard_map/reduce_scatter | solution.py:381
  1019.9 16.3 all-to-all-done.1
  1125.4 32.5 %reduce-scatter.14.cloned.1.call-done = f32[2,256,12,64]{1,3,2,0:T(8,128)} async-done(((f32[2,512,12,64]{1,3,2,0:T(8,128)}), f32[2,256,12,64]{1,3,2,0:T(8,128)}) %reduce-scatter.14.cloned.1.call-update) | async-done | bytes 1572880 | tf_op jit(solution)/shard_map/reduce_scatter | solution.py:444
  1178.9 14.6 reshape.1245
  1225.1 13.8 reshape.1243
  1238.9 16.5 copy.383
  1292.0 12.9 copy.378
  1314.4 18.6 pad_maximum_fusion
  1454.0 13.1 scatter_custom_fusion.1
  1467.2 33.9 %scatter_custom_fusion = f32[4017,768]{1,0:T(8,128)} fusion(s32[4096]{0:T(1024)} %bitcast.630, bf16[4096,768]{1,0:T(8,128)(2,1)} %bitcast.563, f32[]{:T(128)} %constant.78.clone.1), kind=kCustom, calls=%fused_computation.15 | custom fusion | flops 6291456 | bytes 18632192 | tf_op jit(solution)/shard_map/scatter-add | solution.py:207
  1501.1 21.7 slice_add_fusion
  1522.7 87.7 %reduce-scatter.18.cloned.1.call-done = f32[24,36864]{1,0:T(8,128)} async-done(((f32[192,36864]{1,0:T(8,128)}), f32[24,36864]{1,0:T(8,128)}) %reduce-scatter.18.cloned.1.call-update) | async-done | bytes 3538960 | tf_op jit(solution)/shard_map/reduce_scatter | solution.py:476
  1610.5 365.6 %reduce-scatter.20.cloned.1.call-done = f32[32,36864]{1,0:T(8,128)} async-done(((f32[256,36864]{1,0:T(8,128)}), f32[32,36864]{1,0:T(8,128)}) %reduce-scatter.20.cloned.1.call-update) | async-done | bytes 4718608 | tf_op jit(solution)/shard_map/reduce_scatter | solution.py:477
  2074.9 19.4 all-reduce.1
  2094.9 256.7 %all-reduce.5.cloned.1.call-done = (f32[24,36864]{1,0:T(8,128)}, f32[32,36864]{1,0:T(8,128)}, f32[4016,768]{1,0:T(8,128)}) async-done(((f32[24,36864]{1,0:T(8,128)}, f32[32,36864]{1,0:T(8,128)}, f32[4016,768]{1,0:T(8,128)}), (f32[24,36864]{1,0:T(8,128)}, f32[32,36864]{1,0:T(8,128)}, f32[4016,768]{1,0:T(8,128)})) %all-reduce.5.cloned.1.call-update) | async-done | bytes 20594704 | tf_op jit(solution)/shard_map/psum | solution.py:479
  2369.6 30.1 %all-reduce = (f32[]{:T(128)}, f32[7,768]{1,0:T(8,128)}, f32[2,32,12]{1,2,0:T(8,128)S(1)}) all-reduce(f32[]{:T(128)S(6)} %add.788, f32[7,768]{1,0:T(8,128)} %get-tuple-element.204, f32[2,32,12]{1,2,0:T(8,128)} %get-tuple-element.205), channel_id=1, replica_groups=mesh['dp'=2,'fsdp'=8,'seq'=2] {'fsdp'}, use_global_device_ids=true, to_apply=%region_47.48 | all-reduce | flops 6145 | bytes 49160 | tf_op jit(solution)/shard_map/psum | solution.py:492
  2452.7 12.7 multiply_add_fusion.6
  2471.7 16.3 multiply_add_fusion.5
  2517.2 16.3 fusion.14
  2533.5 15.1 multiply_subtract_fusion.1
  2555.2 16.3 multiply_add_fusion.3
  2578.5 21.0 multiply_add_fusion.2
  2606.3 30.3 %multiply_subtract_fusion = (f32[4016,768]{1,0:T(8,128)}, f32[4016,768]{1,0:T(8,128)}, f32[4016,768]{1,0:T(8,128)}) fusion(f32[4016,768]{1,0:T(8,128)} %param.35, f32[]{:T(128)S(6)} %min.23, f32[4016,768]{1,0:T(8,128)} %get-tuple-element.208, f32[]{:T(128)} %max.28, f32[4016,768]{1,0:T(8,128)} %param.36, f32[4016,768]{1,0:T(8,128)} %param.37), kind=kLoop, calls=%fused_computation.28 | loop fusion | flops 52432896 | bytes 86360072 | tf_op jit(solution)/shard_map/sub | solution.py:234
  (710 shorter events, 1061.3 us)
Async XLA Ops:
  7.2 122.5 %reduce-scatter.10.cloned.1.call-start = ((), (), s32[]{:S(2)}) async-start(), calls=%async_computation.11 | async-start | bytes 7077888 | tf_op jit(solution)/shard_map/reduce_scatter | solution.py:307
  60.0 200.0 %all-gather.18.cloned.1.call-start = ((), (), s32[]{:S(2)}) async-start(), calls=%async_computation.12 | async-start | bytes 15925248 | tf_op jit(solution)/shard_map/all_gather | solution.py:222
  63.3 445.7 %reduce-scatter.8.cloned.1.call-start = ((), (), s32[]{:S(2)}) async-start(), calls=%async_computation.9 | async-start | bytes 1769472 | tf_op jit(solution)/shard_map/reduce_scatter | solution.py:313
  83.6 507.7 %all-gather.22.cloned.1.call-start = ((), (), s32[]{:S(2)}) async-start(), calls=%async_computation.14 | async-start | bytes 2359296 | tf_op jit(solution)/shard_map/all_gather | solution.py:330
  84.3 528.8 %copy-start.76 = (f32[768]{0:T(1024)}, f32[768]{0:T(1024)S(1)}, u32[]{:S(2)}) copy-start(f32[768]{0:T(1024)S(1)} %get-tuple-element.182) | copy-start | bytes 9220
  84.3 565.8 %copy-start.101 = (f32[768]{0:T(1024)}, f32[768]{0:T(1024)S(1)}, u32[]{:S(2)}) copy-start(f32[768]{0:T(1024)S(1)} %get-tuple-element.184) | copy-start | bytes 9220
  84.3 591.2 %copy-start.115 = (f32[768]{0:T(1024)}, f32[768]{0:T(1024)S(1)}, u32[]{:S(2)}) copy-start(f32[768]{0:T(1024)S(1)} %get-tuple-element.181) | copy-start | bytes 9220
  84.3 628.6 %copy-start.100 = (f32[768]{0:T(1024)}, f32[768]{0:T(1024)S(1)}, u32[]{:S(2)}) copy-start(f32[768]{0:T(1024)S(1)} %get-tuple-element.180) | copy-start | bytes 9220
  293.3 311.9 %all-gather.20.cloned.1.call-start = ((), (), s32[]{:S(2)}) async-start(), calls=%async_computation.13 | async-start | bytes 2359296 | tf_op jit(solution)/shard_map/all_gather | solution.py:331
  295.7 328.7 %all-gather.16.cloned.1.call-start = ((), (), s32[]{:S(2)}) async-start(), calls=%async_computation.10 | async-start | bytes 21233664 | tf_op jit(solution)/shard_map/all_gather | solution.py:222
  510.9 80.3 %copy-start.23 = (bf16[2,256,768]{1,2,0:T(8,128)(2,1)}, bf16[2,256,768]{1,2,0:T(8,128)(2,1)S(1)}, u32[]{:S(2)}) copy-start(bf16[2,256,768]{1,2,0:T(8,128)(2,1)S(1)} %copy.351) | copy-start | bytes 2359300
  518.5 93.6 %copy-start.73 = (bf16[768,768,1]{1,0,2:T(8,128)(2,1)}, bf16[768,768,1]{1,0,2:T(8,128)(2,1)S(1)}, u32[]{:S(2)}) copy-start(bf16[768,768,1]{1,0,2:T(8,128)(2,1)S(1)} %reshape.1359) | copy-start | bytes 3538948
  624.3 51.1 %copy-start.125 = (f32[2,256]{1,0:T(2,128)}, f32[2,256]{1,0:T(2,128)S(1)}, u32[]{:S(2)}) copy-start(f32[2,256]{1,0:T(2,128)S(1)} %add_rsqrt_fusion) | copy-start | bytes 6148
  680.3 107.3 %all-to-all-start = ((bf16[2,256,1536]{2,1,0:T(8,128)(2,1)}), bf16[2,256,1536]{2,1,0:T(8,128)(2,1)}, u32[]{:S(2)}, u32[]{:S(2)}) async-start(bf16[2,256,1536]{2,1,0:T(8,128)(2,1)} %convolution_convert_fusion.2), calls=%async_computation.2 | async-start | bytes 3145728 | tf_op jit(solution)/shard_map/all_to_all | solution.py:226
  684.9 142.4 %all-gather.28.cloned.1.call-start = ((), (), s32[]{:S(2)}) async-start(), calls=%async_computation.22 | async-start | bytes 1769472 | tf_op jit(solution)/shard_map/all_gather | solution.py:365
  803.4 152.2 %reduce-scatter.12.cloned.1.call-start = ((), (), s32[]{:S(2)}) async-start(), calls=%async_computation.15 | async-start | bytes 3538944 | tf_op jit(solution)/shard_map/reduce_scatter | solution.py:381
  812.7 87.6 %copy-start.133 = (f32[8,1,128]{2,1,0:T(1,128)}, f32[8,1,128]{2,1,0:T(1,128)S(1)}, u32[]{:S(2)}) copy-start(f32[8,1,128]{2,1,0:T(1,128)S(1)} %convert_element_type.743) | copy-start | bytes 12292
  1014.6 21.6 all-to-all-start.1
  1019.2 101.1 %reduce-scatter.16.cloned.1.call-start = ((), (), s32[]{:S(2)}) async-start(), calls=%async_computation.17 | async-start | bytes 4718592 | tf_op jit(solution)/shard_map/reduce_scatter | solution.py:445
  1068.3 89.6 %reduce-scatter.14.cloned.1.call-start = ((), (), s32[]{:S(2)}) async-start(), calls=%async_computation.16 | async-start | bytes 4718592 | tf_op jit(solution)/shard_map/reduce_scatter | solution.py:444
  1091.5 362.6 %all-gather.26.cloned.1.call-start = ((), (), s32[]{:S(2)}) async-start(), calls=%async_computation.21 | async-start | bytes 1769472 | tf_op jit(solution)/shard_map/all_gather | solution.py:464
  1111.7 355.5 %all-gather.24.cloned.1.call-start = ((), (), s32[]{:S(2)}) async-start(), calls=%async_computation.20 | async-start | bytes 7077888 | tf_op jit(solution)/shard_map/all_gather | solution.py:463
  1117.9 44.8 %copy-start.45 = (bf16[768,2304]{0,1:T(8,128)(2,1)S(1)}, bf16[768,2304]{0,1:T(8,128)(2,1)}, u32[]{:S(2)}) copy-start(bf16[768,2304]{0,1:T(8,128)(2,1)} %copy-done.44) | copy-start | bytes 10616836
  1117.9 44.8 %copy-start.127 = (f32[768]{0:T(1024)S(1)}, f32[768]{0:T(1024)}, u32[]{:S(2)}) copy-start(f32[768]{0:T(1024)} %get-tuple-element.183) | copy-start | bytes 9220
  1117.9 44.8 %copy-start.137 = (f32[2,256]{1,0:T(2,128)S(1)}, f32[2,256]{1,0:T(2,128)}, u32[]{:S(2)}) copy-start(f32[2,256]{1,0:T(2,128)} %add_rsqrt_fusion.2) | copy-start | bytes 6148
  1168.8 441.7 %reduce-scatter.18.cloned.1.call-start = ((), (), s32[]{:S(2)}) async-start(), calls=%async_computation.18 | async-start | bytes 31850496 | tf_op jit(solution)/shard_map/reduce_scatter | solution.py:476
  1333.1 642.9 %reduce-scatter.20.cloned.1.call-start = ((), (), s32[]{:S(2)}) async-start(), calls=%async_computation.19 | async-start | bytes 42467328 | tf_op jit(solution)/shard_map/reduce_scatter | solution.py:477
  1450.3 901.2 %all-reduce.5.cloned.1.call-start = ((), (), s32[]{:S(2)}) async-start(), calls=%async_computation.23 | async-start | bytes 41189376 | tf_op jit(solution)/shard_map/psum | solution.py:479
  1467.2 33.9 %copy-start.132 = (s32[1024]{0:T(1024)S(1)}, s32[1024]{0:T(1024)}, u32[]{:S(2)}) copy-start(s32[1024]{0:T(1024)} %copy-done.131) | copy-start | bytes 12292
  1467.2 33.9 %copy-start.134 = (f32[8,1,128]{2,1,0:T(1,128)S(1)}, f32[8,1,128]{2,1,0:T(1,128)}, u32[]{:S(2)}) copy-start(f32[8,1,128]{2,1,0:T(1,128)} %copy-done.133) | copy-start | bytes 12292
  1467.2 33.9 %copy-start.146 = (f32[1024]{0:T(1024)S(1)}, f32[1024]{0:T(1024)}, u32[]{:S(2)}) copy-start(f32[1024]{0:T(1024)} %copy-done.145) | copy-start | bytes 12292
  2359.2 47.0 %copy-start.13 = (f32[24,36864]{1,0:T(8,128)S(1)}, f32[24,36864]{1,0:T(8,128)}, u32[]{:S(2)}) copy-start(f32[24,36864]{1,0:T(8,128)} %get-tuple-element.206) | copy-start | bytes 10616836
  (157 other events, 1126.6 us)
Sparse Core Ops, SparseCore 0:
  60.1 69.5 reduce-scatter.9
  131.9 127.9 all-gather.17
  262.8 32.2 reduce-scatter.7
  296.5 25.3 all-gather.21
  323.2 27.1 all-gather.19
  352.5 168.2 all-gather.15
  803.5 23.8 all-gather.27
  915.7 39.7 reduce-scatter.11
  1068.4 43.3 reduce-scatter.15
  1114.6 43.3 reduce-scatter.13
  1159.6 25.0 all-gather.25
  1186.7 64.2 all-gather.23
  1333.2 277.1 reduce-scatter.17
  1612.7 363.2 reduce-scatter.19
  1980.8 370.6 all-reduce.4
where the time goes:
time: 2660 us; the launch traced here: 2650 us
  waiting for transfers between devices  976 us (37%)
  local copies, waits for them, and re-layouts  896 us (34%)
  matrix products  359 us (13%)
  other arithmetic  242 us (9%)
  blocking collectives  139 us (5%)
    reduce_scatter x1, waiting for transfers between devices, on_device(): lax.psum_scatter(decoder_portion, 'fsdp', scatter_dimension=0, tiled=True)  366 us
    psum x1, waiting for transfers between devices, on_device(): lax.psum((enc_shard, dec_shard, emb_grad, gain_part, rel_part, group_loss...  257 us
    eq x1, local copies, waits for them, and re-layouts, bucket_onehot(): buckets[None] == jnp.arange(NBK, dtype=jnp.int32)[:, None, None]  186 us
    reshape x22, local copies, waits for them, and re-layouts, unblock(): blocks[offset:offset + amount]  145 us
    all_gather x2, waiting for transfers between devices, fetch_blocks(): lax.all_gather(master.astype(jnp.bfloat16), 'fsdp', axis=0, tiled=True)  128 us
    reduce_scatter x1, waiting for transfers between devices, on_device(): lax.psum_scatter(encoder_portion, 'fsdp', scatter_dimension=0, tiled=True)  87.7 us
    reshape x11, local copies, waits for them, and re-layouts, rebuild_blocks(): pieces.append(tiles.reshape(-1, BLOCK * BLOCK))  85.5 us
    reshape x11, local copies, waits for them, and re-layouts, unblock(): matrix_list.append(section.transpose(0, 2, 1, 3).reshape(height, breadth))  74.7 us
  transfers between devices with their start and end apart: 17, of which 9 were waited for; matrix products, arithmetic and copies ran while one was open for 37% of the time, Pallas kernels for 0%

commit v1 on v0

v1 whole, which is shorter than its diff:
```python
import functools
import math

import jax
import jax.numpy as jnp
from jax import lax
from jax.experimental import pallas as pl
from jax.experimental.pallas import tpu as pltpu
from jax.sharding import PartitionSpec as P

D = 768
H = 12
DH = 64
FF = 3072
VOCAB = 32128
NBK = 32
REACH = 128
BLOCK = 192
STEP = 10
PAIR = 2 * BLOCK
TILE = 128
LANES = 128


norm_eps = 1e-06
neg_fill = -1000000000.0
sentinel_offset = 29
beta_first = 0.9
beta_second = 0.999
adam_eps = 1e-08
adam_rate = 0.5
shampoo_rate = 0.01
stat_decay = 0.999
weight_decay = 0.01
clip_limit = 0.05
highest = lax.Precision.HIGHEST


def bucket_edges(buckets, exact, reach):
    edges = list(range(1, exact))
    spread = buckets - exact
    for place in range(spread):
        edges.append(int(math.ceil(exact * (reach / exact) ** (place / spread) - 1e-09)))
    return edges


def offset_buckets(offset, causal):
    if causal:
        distance = jnp.maximum(-offset, 0)
        result = jnp.zeros(offset.shape, jnp.int32)
        edges = bucket_edges(NBK, NBK // 2, REACH)
    else:
        distance = jnp.abs(offset)
        result = jnp.where(offset > 0, NBK // 2, 0).astype(jnp.int32)
        edges = bucket_edges(NBK // 2, NBK // 4, REACH)
    for edge in edges:
        result = result + (distance >= edge).astype(jnp.int32)
    return result


def tile_reach(blocks):
    return min(blocks - 1, 2)


def tile_onehot(blocks, causal):
    reach = tile_reach(blocks)
    place = jnp.arange(TILE, dtype=jnp.int32)
    shift = jnp.arange(-reach, reach + 1, dtype=jnp.int32) * TILE
    offset = shift[:, None, None] + place[None, None, :] - place[None, :, None]
    buckets = offset_buckets(offset, causal).reshape(-1)
    return (jnp.arange(NBK, dtype=jnp.int32)[:, None] == buckets[None, :]).astype(jnp.float32)


def tile_bias(onehot, rel):
    flat = jnp.einsum("nh,np->hp", rel, onehot, precision=highest)
    return flat.reshape(H, -1, TILE, TILE)


def tile_bias_grad(onehot, grads):
    return jnp.einsum("np,hp->nh", onehot, grads.reshape(H, -1), precision=highest)


def head_lanes(half):
    lane = lax.broadcasted_iota(jnp.int32, (1, LANES), 1)
    return (lane // DH) == half


def block_scores(query, keys, bias_ref, half, row, row_segs, key_segs, causal):
    scores = lax.dot_general(query, keys, (((1,), (1,)), ((), ())), preferred_element_type=jnp.float32)
    width = keys.shape[0]
    if bias_ref is not None:
        reach = tile_reach(width // TILE)
        tiles = []
        for column in range(width // TILE):
            tiles.append(bias_ref[half, min(max(column - row, -reach), reach) + reach])
        scores = scores + (jnp.concatenate(tiles, axis=1) if len(tiles) > 1 else tiles[0])
    mask = row_segs == key_segs
    if causal:
        at_row = row * TILE + lax.broadcasted_iota(jnp.int32, scores.shape, 0)
        at_key = lax.broadcasted_iota(jnp.int32, scores.shape, 1)
        mask = mask & (at_row >= at_key)
    scores = jnp.where(mask, scores, neg_fill)
    raised = jnp.exp(scores - jnp.max(scores, axis=-1, keepdims=True))
    return raised * (1.0 / jnp.sum(raised, axis=-1, keepdims=True))


def attend_kernel(q_ref, k_ref, v_ref, *rest, biased, causal):
    bias_ref = rest[0] if biased else None
    sq_ref, sk_ref, o_ref = rest[-3:]
    keys = k_ref[0]
    values = v_ref[0]
    key_segs = sk_ref[0]
    for row in range(q_ref.shape[1] // TILE):
        part = pl.ds(row * TILE, TILE)
        query = q_ref[0, part, :]
        row_segs = sq_ref[0, part, :]
        result = None
        for half in range(2):
            lanes = head_lanes(half)
            probs = block_scores(
                jnp.where(lanes, query, 0), keys, bias_ref, half, row, row_segs, key_segs, causal
            )
            output = jnp.dot(
                probs.astype(jnp.bfloat16), values, preferred_element_type=jnp.float32
            )
            result = output if result is None else jnp.where(lanes, output, result)
        o_ref[0, part, :] = result.astype(jnp.bfloat16)


def attend_back_kernel(q_ref, k_ref, v_ref, g_ref, *rest, biased, causal):
    if biased:
        bias_ref, sq_ref, sk_ref, dq_ref, dk_ref, dv_ref, db_ref = rest
    else:
        sq_ref, sk_ref, dq_ref, dk_ref, dv_ref = rest
        bias_ref = db_ref = None
    keys = k_ref[0]
    values = v_ref[0]
    key_segs = sk_ref[0]
    width = keys.shape[0]
    if biased:

        @pl.when(pl.program_id(1) == 0)
        def _():
            db_ref[...] = jnp.zeros_like(db_ref)

    grad_keys = None
    grad_values = None
    for row in range(q_ref.shape[1] // TILE):
        part = pl.ds(row * TILE, TILE)
        query = q_ref[0, part, :]
        grad_out = g_ref[0, part, :]
        row_segs = sq_ref[0, part, :]
        grad_query = None
        for half in range(2):
            lanes = head_lanes(half)
            own_query = jnp.where(lanes, query, 0)
            own_grad = jnp.where(lanes, grad_out, 0)
            probs = block_scores(
                own_query, keys, bias_ref, half, row, row_segs, key_segs, causal
            )
            grad_probs = lax.dot_general(
                own_grad, values, (((1,), (1,)), ((), ())), preferred_element_type=jnp.float32
            )
            drop = jnp.sum(probs * grad_probs, axis=-1, keepdims=True)
            grad_scores = (probs * (grad_probs - drop)).astype(jnp.bfloat16)
            down = (((0,), (0,)), ((), ()))
            part_values = lax.dot_general(
                probs.astype(jnp.bfloat16), own_grad, down, preferred_element_type=jnp.float32
            )
            part_keys = lax.dot_general(
                grad_scores, own_query, down, preferred_element_type=jnp.float32
            )
            grad_values = part_values if grad_values is None else grad_values + part_values
            grad_keys = part_keys if grad_keys is None else grad_keys + part_keys
            own_grad_query = jnp.dot(grad_scores, keys, preferred_element_type=jnp.float32)
            grad_query = (
                own_grad_query if grad_query is None else jnp.where(lanes, own_grad_query, grad_query)
            )
            if biased:
                wide = grad_scores.astype(jnp.float32)
                reach = tile_reach(width // TILE)
                for column in range(width // TILE):
                    slot = min(max(column - row, -reach), reach) + reach
                    db_ref[half, slot] += wide[:, column * TILE : (column + 1) * TILE]
        dq_ref[0, part, :] = grad_query.astype(jnp.bfloat16)
    dk_ref[0] = grad_keys.astype(jnp.bfloat16)
    dv_ref[0] = grad_values.astype(jnp.bfloat16)


def attention_specs(query, keys, places, bias, row_segs, key_segs):
    q_at, k_at, v_at = places
    rows, nq = row_segs.shape
    nk = key_segs.shape[1]

    def panel(length, first):
        return pl.BlockSpec((1, length, LANES), lambda pair, row: (row, 0, first + pair))

    operands = [query, keys, keys]
    specs = [panel(nq, q_at), panel(nk, k_at), panel(nk, v_at)]
    tail = []
    tail_specs = []
    if bias is not None:
        tail.append(bias)
        tail_specs.append(
            pl.BlockSpec((2,) + bias.shape[1:], lambda pair, row: (pair, 0, 0, 0))
        )
    tail += [row_segs[:, :, None], key_segs[:, None, :]]
    tail_specs += [
        pl.BlockSpec((1, nq, 1), lambda pair, row: (row, 0, 0)),
        pl.BlockSpec((1, 1, nk), lambda pair, row: (row, 0, 0)),
    ]
    return operands, specs, tail, tail_specs, panel


def attention_cost(rows, nq, nk, products):
    return pl.CostEstimate(
        flops=2 * products * rows * H * nq * nk * LANES,
        bytes_accessed=2 * products * rows * (nq + nk) * D,
        transcendentals=rows * H * nq * nk,
    )


def attend(query, keys, places, bias, row_segs, key_segs, causal):
    rows, nq = row_segs.shape
    nk = key_segs.shape[1]
    operands, specs, tail, tail_specs, panel = attention_specs(
        query, keys, places, bias, row_segs, key_segs
    )
    return pl.pallas_call(
        functools.partial(attend_kernel, biased=bias is not None, causal=causal),
        out_shape=jax.ShapeDtypeStruct((rows, nq, D), jnp.bfloat16),
        grid=(H // 2, rows),
        in_specs=specs + tail_specs,
        out_specs=panel(nq, 0),
        cost_estimate=attention_cost(rows, nq, nk, 2),
        compiler_params=pltpu.CompilerParams(vmem_limit_bytes=32 << 20),
    )(*operands, *tail)


def attend_back(query, keys, places, bias, row_segs, key_segs, causal, grad_out):
    rows, nq = row_segs.shape
    nk = key_segs.shape[1]
    operands, specs, tail, tail_specs, panel = attention_specs(
        query, keys, places, bias, row_segs, key_segs
    )
    outs = [
        jax.ShapeDtypeStruct((rows, nq, D), jnp.bfloat16),
        jax.ShapeDtypeStruct((rows, nk, D), jnp.bfloat16),
        jax.ShapeDtypeStruct((rows, nk, D), jnp.bfloat16),
    ]
    out_specs = [panel(nq, 0), panel(nk, 0), panel(nk, 0)]
    if bias is not None:
        outs.append(jax.ShapeDtypeStruct(bias.shape, jnp.float32))
        out_specs.append(
            pl.BlockSpec((2,) + bias.shape[1:], lambda pair, row: (pair, 0, 0, 0))
        )
    return pl.pallas_call(
        functools.partial(attend_back_kernel, biased=bias is not None, causal=causal),
        out_shape=outs,
        grid=(H // 2, rows),
        in_specs=specs + [panel(nq, 0)] + tail_specs,
        out_specs=out_specs,
        cost_estimate=attention_cost(rows, nq, nk, 5),
        compiler_params=pltpu.CompilerParams(vmem_limit_bytes=32 << 20),
    )(*operands, grad_out, *tail)


def layer_shapes(decoder):
    if decoder:
        return [(D, 3 * D), (D, D), (D, D), (D, 2 * D), (D, D), (D, FF), (FF, D)]
    return [(D, 3 * D), (D, D), (D, FF), (FF, D)]


def as_blocks(flat):
    return flat.reshape(flat.shape[0], BLOCK, BLOCK)


def as_rows(blocks):
    return blocks.reshape(blocks.shape[0], BLOCK * BLOCK)


def as_pairs(blocks):
    amount = blocks.shape[0] // 2
    split = blocks.reshape(amount, 2, BLOCK, BLOCK)
    return jnp.concatenate([split[:, 0], split[:, 1]], axis=-1)


def from_pairs(pairs):
    amount = pairs.shape[0]
    split = jnp.stack([pairs[..., :BLOCK], pairs[..., BLOCK:]], axis=1)
    return split.reshape(2 * amount, BLOCK, BLOCK)


def matrices_of(pairs, shapes):
    matrix_list = []
    offset = 0
    for height, breadth in shapes:
        tall, wide = (height // BLOCK, breadth // PAIR)
        section = pairs[offset : offset + tall * wide].reshape(tall, wide, BLOCK, PAIR)
        matrix_list.append(section.transpose(0, 2, 1, 3).reshape(height, breadth))
        offset += tall * wide
    return matrix_list


def pairs_of(matrix):
    height, breadth = matrix.shape
    tiles = matrix.reshape(height // BLOCK, BLOCK, breadth // PAIR, PAIR)
    return tiles.transpose(0, 2, 1, 3).reshape(-1, BLOCK, PAIR)


def project(left, right):
    return jnp.matmul(left, right, preferred_element_type=jnp.float32)


def project_back(left, right):
    return jnp.einsum("btf,df->btd", left, right, preferred_element_type=jnp.float32)


def weight_grad(inputs, grads):
    return jnp.einsum("btd,btf->df", inputs, grads, preferred_element_type=jnp.float32)


def rms(values, gain):
    return values * lax.rsqrt(jnp.mean(values * values, axis=-1, keepdims=True) + norm_eps) * gain


def rms_back(values, gain, grad_out):
    inverse = lax.rsqrt(jnp.mean(values * values, axis=-1, keepdims=True) + norm_eps)
    normed = values * inverse
    grad_gain = jnp.sum(grad_out * normed, axis=(0, 1))
    grad_normed = grad_out * gain
    grad_values = inverse * (
        grad_normed - normed * jnp.mean(grad_normed * normed, axis=-1, keepdims=True)
    )
    return (grad_values, grad_gain)


def ff_forward(hidden, gain, w_in, w_down):
    normed = rms(hidden, gain).astype(jnp.bfloat16)
    inner = project(normed, w_in)
    active = jax.nn.gelu(inner).astype(jnp.bfloat16)
    return (hidden + project(active, w_down), (normed, inner, active))


def ff_back(hidden, gain, w_in, w_down, cache, grad_out):
    normed, inner, active = cache
    branch_grad = grad_out.astype(jnp.bfloat16)
    down_grad = weight_grad(active, branch_grad)
    grad_active = project_back(branch_grad, w_down)
    unused, gelu_back = jax.vjp(jax.nn.gelu, inner)
    grad_inner = gelu_back(grad_active)[0].astype(jnp.bfloat16)
    in_grad = weight_grad(normed, grad_inner)
    grad_part, grad_gain = rms_back(hidden, gain, project_back(grad_inner, w_in))
    return (grad_out + grad_part, grad_gain, in_grad, down_grad)


def table_rows(table, token_ids, vocab_first):
    local_ids = token_ids - vocab_first
    inside = (local_ids >= 0) & (local_ids < table.shape[0])
    picked = jnp.take(table, jnp.clip(local_ids, 0, table.shape[0] - 1), axis=0)
    return jnp.where(inside[..., None], picked, jnp.zeros((), table.dtype))


def table_grads(grads, token_ids, vocab_first, vocab_local, dense):
    local_ids = token_ids.reshape(-1) - vocab_first
    inside = (local_ids >= 0) & (local_ids < vocab_local)
    slots = jnp.where(inside, local_ids, vocab_local)
    length = -(-(vocab_local + 1) // 32) * 32
    summed = jax.ops.segment_sum(
        grads.reshape(-1, D).astype(jnp.float32), slots, num_segments=length
    )
    row = lax.broadcasted_iota(jnp.int32, (length, 1), 0)
    padded = jnp.pad(dense, ((0, length - vocab_local), (0, 0)))
    return jnp.where(row < vocab_local, summed + padded, 0.0)


REPLICAS = ("dp", "seq")
EVERYWHERE = ("fsdp", "dp", "seq")


def replica_rank():
    return lax.axis_index("dp") * lax.axis_size("seq") + lax.axis_index("seq")


def replica_count():
    return lax.axis_size("dp") * lax.axis_size("seq")


def gather_weights(master):
    amount = master.shape[0]
    parts = replica_count()
    if amount % (2 * parts):
        pairs = as_pairs(as_blocks(master.astype(jnp.bfloat16)))
        return lax.all_gather(pairs, "fsdp", axis=0, tiled=True)
    share = amount // parts
    own = lax.dynamic_slice_in_dim(master, replica_rank() * share, share, 0)
    pairs = as_pairs(as_blocks(own.astype(jnp.bfloat16)))
    return lax.all_gather(pairs, EVERYWHERE, axis=0, tiled=True)


def paired_mesh():
    return (
        lax.axis_size("dp") == 2 and lax.axis_size("seq") == 2 and lax.axis_size("fsdp") % 2 == 0
    )


def swap(values, axis):
    size = lax.axis_size(axis)
    return lax.ppermute(values, axis, [(place, place ^ 1) for place in range(size)])


def shift(values, step):
    size = lax.axis_size("fsdp")
    moves = [
        (place, place + 2 * step) for place in range(size) if 0 <= place + 2 * step < size
    ]
    return lax.ppermute(values, "fsdp", moves)


def choose(flag, if_set, if_clear):
    return jnp.where(flag == 1, if_set, if_clear)


def pick(values, place, axis):
    return lax.dynamic_index_in_dim(values, place, axis, False)


def narrow(values):
    return values.astype(jnp.bfloat16)


def wide(values):
    return values.astype(jnp.float32)


def agreed_scale(largest):
    for axis in ("seq", "dp"):
        largest = jnp.maximum(largest, swap(largest, axis))
    return 4096.0 / jnp.maximum(largest, 1e-30)


def placed(relative, first, second):
    def at(row, column):
        here = choose(second, relative[row][1 - column], relative[row][column])
        there = choose(second, relative[1 - row][1 - column], relative[1 - row][column])
        return choose(first, there, here)

    return [[at(0, 0), at(0, 1)], [at(1, 0), at(1, 1)]]


def reduce_blocks(pairs):
    if not paired_mesh():
        return lax.psum(
            lax.psum_scatter(pairs, "fsdp", scatter_dimension=0, tiled=True), REPLICAS
        )
    n_chips = lax.axis_size("fsdp") // 2
    core = lax.axis_index("fsdp") % 2
    chip = lax.axis_index("fsdp") // 2
    side, half = (lax.axis_index("dp"), lax.axis_index("seq"))
    amount = pairs.shape[0] // (2 * n_chips)
    quarter = amount // 4
    mid = BLOCK // 2
    pairs = pairs.reshape(n_chips, 2, amount, BLOCK, PAIR)
    chip_sum = wide(pick(pairs, core, 1)) + wide(swap(narrow(pick(pairs, 1 - core, 1)), "fsdp"))
    chip_sum = chip_sum.reshape(n_chips, 2, 2, quarter, BLOCK, PAIR)
    upper, lower = (chip_sum[..., :mid, :], chip_sum[..., mid:, :])
    upper = pick(upper, half, 2) + wide(swap(narrow(pick(upper, 1 - half, 2)), "seq"))
    lower = pick(lower, side, 1) + wide(swap(narrow(pick(lower, 1 - side, 1)), "dp"))
    upper = pick(upper, side, 1) + wide(swap(narrow(pick(upper, 1 - side, 1)), "dp"))
    lower = pick(lower, half, 1) + wide(swap(narrow(pick(lower, 1 - half, 1)), "seq"))
    line_sum = jnp.concatenate([upper, lower], axis=2)
    ahead = lax.dynamic_slice_in_dim(
        jnp.concatenate([line_sum, line_sum[:-1]], axis=0), chip, n_chips, 0
    )
    up = down = None
    for step in range(n_chips - 1, 0, -1):
        rising, falling = (ahead[step], ahead[n_chips - step])
        if up is not None:
            rising, falling = (rising + wide(up), falling + wide(down))
        up, down = (shift(narrow(rising), 1), shift(narrow(falling), -1))
    return ahead[0] + wide(up) + wide(down)


def share_blocks(own):
    side, half = (lax.axis_index("dp"), lax.axis_index("seq"))
    mid = BLOCK // 2
    scale = agreed_scale(jnp.max(jnp.abs(own)))
    own = lax.optimization_barrier((own * scale).astype(jnp.float16))
    upper, lower = (own[:, :mid], own[:, mid:])
    upper_side, lower_half = (swap(upper, "dp"), swap(lower, "seq"))
    upper_rest = swap(jnp.stack([upper, upper_side]), "seq")
    lower_rest = swap(jnp.stack([lower, lower_half]), "dp")
    relative = [
        [
            jnp.concatenate([upper, lower], axis=1),
            jnp.concatenate([upper_rest[0], lower_half], axis=1),
        ],
        [
            jnp.concatenate([upper_side, lower_rest[0]], axis=1),
            jnp.concatenate([upper_rest[1], lower_rest[1]], axis=1),
        ],
    ]
    whole = placed(relative, side, half)
    return wide(jnp.concatenate(whole[0] + whole[1], axis=0)) * (1.0 / scale)


def reduce_table(partial, bound):
    side, half = (lax.axis_index("dp"), lax.axis_index("seq"))
    scale = agreed_scale(bound)
    rows = partial.shape[0] // 4
    split = (partial * scale).reshape(2, 2, rows, D)

    def half_lanes(values, place):
        return lax.dynamic_slice_in_dim(values, place * (D // 2), D // 2, 1)

    def send(values, axis):
        return wide(swap(values.astype(jnp.float16), axis))

    top = pick(split[0], half, 0) + send(pick(split[0], 1 - half, 0), "seq")
    low = pick(split[1], side, 0) + send(pick(split[1], 1 - side, 0), "dp")
    top = half_lanes(top, side) + send(half_lanes(top, 1 - side), "dp")
    low = half_lanes(low, half) + send(half_lanes(low, 1 - half), "seq")
    return top, low, scale


def share_table(top, low, scale):
    side, half = (lax.axis_index("dp"), lax.axis_index("seq"))
    top = lax.optimization_barrier(top.astype(jnp.float16))
    low = lax.optimization_barrier(low.astype(jnp.float16))
    top_side, low_half = (swap(top, "dp"), swap(low, "seq"))
    top_rest = swap(jnp.stack([top, top_side]), "seq")
    low_rest = swap(jnp.stack([low, low_half]), "dp")
    top_all = placed([[top, top_side], [top_rest[0], top_rest[1]]], half, side)
    low_all = placed([[low, low_half], [low_rest[0], low_rest[1]]], side, half)
    rows = [jnp.concatenate(pieces, axis=1) for pieces in top_all + low_all]
    return wide(jnp.concatenate(rows, axis=0)) * (1.0 / scale)


def adam_update(weight, gradient, moment, second):
    moment = beta_first * moment + (1 - beta_first) * gradient
    second = beta_second * second + (1 - beta_second) * gradient * gradient
    corrected = moment / (1 - beta_first**STEP)
    scaled = second / (1 - beta_second**STEP)
    weight = weight - adam_rate * (
        corrected / (jnp.sqrt(scaled) + adam_eps) + weight_decay * weight
    )
    return (weight, moment, second)


def block_product(left, right, form):
    return jnp.einsum(form, left, right, precision=lax.Precision.HIGH)


def shampoo_ahead(moment, left_root, right_root):
    left_root, right_root = (as_blocks(left_root), as_blocks(right_root))
    shaped = block_product(left_root, as_blocks(moment), "nij,njk->nik")
    return (as_rows(block_product(shaped, right_root, "nij,njk->nik")), left_root, right_root)


def shampoo_products(gradient, left_root, right_root):
    shaped = block_product(left_root, gradient, "nij,njk->nik")
    return (
        as_rows(gradient),
        as_rows(block_product(shaped, right_root, "nij,njk->nik")),
        as_rows(block_product(gradient, gradient, "nij,nkj->nik")),
        as_rows(block_product(gradient, gradient, "nji,njk->nik")),
    )


def shampoo_update(weight, moment, left, right, ahead, products, factor):
    gradient, turned, left_square, right_square = products
    direction = beta_first * ahead + ((1 - beta_first) * factor) * turned
    square = (1 - stat_decay) * factor * factor
    return (
        weight - shampoo_rate * (direction + weight_decay * weight),
        beta_first * moment + ((1 - beta_first) * factor) * gradient,
        stat_decay * left + square * left_square,
        stat_decay * right + square * right_square,
    )


def on_device(
    enc_ids,
    span_mask,
    segments,
    targets,
    loss_weights,
    target_segments,
    embedding,
    emb_m,
    emb_v,
    gains,
    gain_m,
    gain_v,
    rel_bias,
    rel_m,
    rel_v,
    enc_w,
    enc_m,
    enc_left,
    enc_right,
    enc_lroot,
    enc_rroot,
    dec_w,
    dec_m,
    dec_left,
    dec_right,
    dec_lroot,
    dec_rroot,
):
    fsdp_rank = lax.axis_index("fsdp")
    seq_rank = lax.axis_index("seq")
    n_fsdp = lax.axis_size("fsdp")
    n_seq = lax.axis_size("seq")
    half_len = enc_ids.shape[1]
    rows, dec_len = targets.shape
    enc_len = half_len * n_seq
    enc_in = jnp.where(span_mask == 1, VOCAB - sentinel_offset, enc_ids)
    dec_in = jnp.concatenate([jnp.zeros((rows, 1), jnp.int32), targets[:, :-1]], axis=1)

    def by_rows(positions):
        return positions.reshape(n_seq, rows, half_len)

    message = jnp.concatenate(
        [by_rows(enc_in), by_rows(segments)], axis=2
    ).reshape(n_seq, -1)
    own = jnp.concatenate(
        [dec_in.reshape(-1), targets.reshape(-1), loss_weights.reshape(-1)]
    )
    message = jnp.concatenate([message.reshape(-1), own]).reshape(1, 1, -1)
    gathered = lax.all_gather(message, ("fsdp", "seq"), axis=0, tiled=True)
    gathered = gathered.reshape(n_fsdp, n_seq, -1)
    row_words = rows * 2 * half_len
    enc_words = lax.dynamic_slice_in_dim(gathered, seq_rank * row_words, row_words, 2)
    enc_words = enc_words.reshape(n_fsdp, n_seq, rows, 2, half_len).transpose(3, 0, 2, 1, 4)
    enc_words = enc_words.reshape(2, n_fsdp, rows * enc_len)
    all_enc = enc_words[0]
    row_segments = lax.dynamic_index_in_dim(enc_words[1], fsdp_rank, 0, False)
    row_segments = row_segments.reshape(rows, enc_len)
    dec_words = lax.dynamic_index_in_dim(gathered, seq_rank, 1, False)[:, n_seq * row_words :]
    dec_words = dec_words.reshape(n_fsdp, 3, rows * dec_len)
    all_dec, all_targets, all_weights = (dec_words[:, 0], dec_words[:, 1], dec_words[:, 2])
    all_tokens = jnp.concatenate([all_enc, all_dec], axis=1)

    table = embedding.astype(jnp.bfloat16)
    vocab_local = table.shape[0]
    vocab_first = fsdp_rank * vocab_local
    looked_up = lax.psum_scatter(
        table_rows(table, all_tokens, vocab_first), "fsdp", scatter_dimension=0, tiled=True
    ).reshape(-1, D)
    hidden0 = looked_up[: rows * enc_len].reshape(rows, enc_len, D).astype(jnp.float32)
    state0 = looked_up[rows * enc_len :].reshape(rows, dec_len, D).astype(jnp.float32)

    enc_mats = matrices_of(gather_weights(enc_w), layer_shapes(False))
    dec_mats = matrices_of(gather_weights(dec_w), layer_shapes(True))
    enc_onehot = tile_onehot(enc_len // TILE, False)
    dec_onehot = tile_onehot(dec_len // TILE, True)
    enc_bias = tile_bias(enc_onehot, rel_bias[0])
    dec_bias = tile_bias(dec_onehot, rel_bias[1])
    tile_at = D // LANES
    self_places = (0, tile_at, 2 * tile_at)
    cross_places = (0, 0, tile_at)

    normed0 = rms(hidden0, gains[0]).astype(jnp.bfloat16)
    enc_qkv = project(normed0, enc_mats[0]).astype(jnp.bfloat16)
    enc_attended = attend(
        enc_qkv, enc_qkv, self_places, enc_bias, row_segments, row_segments, False
    )
    hidden1 = hidden0 + project(enc_attended, enc_mats[1])
    hidden2, enc_cache = ff_forward(hidden1, gains[1], enc_mats[2], enc_mats[3])
    encoded = rms(hidden2, gains[2]).astype(jnp.bfloat16)
    pairs = project(encoded, dec_mats[3]).astype(jnp.bfloat16)

    normed3 = rms(state0, gains[3]).astype(jnp.bfloat16)
    self_qkv = project(normed3, dec_mats[0]).astype(jnp.bfloat16)
    self_attended = attend(
        self_qkv, self_qkv, self_places, dec_bias, target_segments, target_segments, True
    )
    state1 = state0 + project(self_attended, dec_mats[1])
    normed4 = rms(state1, gains[4]).astype(jnp.bfloat16)
    cross_query = project(normed4, dec_mats[2]).astype(jnp.bfloat16)
    cross_attended = attend(
        cross_query, pairs, cross_places, None, target_segments, row_segments, False
    )
    state2 = state1 + project(cross_attended, dec_mats[4])
    state3, dec_cache = ff_forward(state2, gains[5], dec_mats[5], dec_mats[6])
    out_scale = D ** (-0.5)
    final = (rms(state3, gains[6]) * out_scale).astype(jnp.bfloat16)

    all_final = lax.all_gather(final.reshape(rows * dec_len, D), "fsdp", axis=0, tiled=True)
    logits = jnp.einsum("nd,vd->nv", all_final, table, preferred_element_type=jnp.float32)
    local_ids = all_targets.reshape(-1) - vocab_first
    target_hot = local_ids[:, None] == jnp.arange(vocab_local, dtype=jnp.int32)[None, :]
    local_top = jnp.max(logits, axis=1)
    local_sum = jnp.sum(jnp.exp(logits - local_top[:, None]), axis=1)
    local_pick = jnp.sum(jnp.where(target_hot, logits, 0.0), axis=1)
    stats = lax.all_gather(
        jnp.stack([local_top, local_sum, local_pick])[None], "fsdp", axis=0, tiled=True
    )
    top_all = jnp.max(stats[:, 0], axis=0)
    sum_all = jnp.sum(stats[:, 1] * jnp.exp(stats[:, 0] - top_all), axis=0)
    pick_all = jnp.sum(stats[:, 2], axis=0)
    lse = top_all + jnp.log(sum_all)
    token_weights = all_weights.reshape(-1).astype(jnp.float32)
    group_loss = jnp.sum(token_weights * (lse - pick_all))
    group_count = jnp.sum(token_weights)
    grad_logits = (
        token_weights[:, None] * (jnp.exp(logits - lse[:, None]) - target_hot.astype(jnp.float32))
    ).astype(jnp.bfloat16)
    emb_grad = jnp.einsum("nv,nd->vd", grad_logits, all_final, preferred_element_type=jnp.float32)
    grad_final = lax.psum_scatter(
        jnp.dot(grad_logits, table, preferred_element_type=jnp.float32),
        "fsdp",
        scatter_dimension=0,
        tiled=True,
    ).reshape(rows, dec_len, D)

    grad_state3, gain_six = rms_back(state3, gains[6], grad_final * out_scale)
    grad_state2, gain_five, dec_in_grad, dec_down_grad = ff_back(
        state2, gains[5], dec_mats[5], dec_mats[6], dec_cache, grad_state3
    )
    branch_grad = grad_state2.astype(jnp.bfloat16)
    cross_out_grad = weight_grad(cross_attended, branch_grad)
    grad_cross = project_back(branch_grad, dec_mats[4]).astype(jnp.bfloat16)
    grad_cq, grad_ck, grad_cv = attend_back(
        cross_query, pairs, cross_places, None, target_segments, row_segments, False, grad_cross
    )
    grad_pairs = jnp.concatenate([grad_ck, grad_cv], axis=-1)
    cross_query_grad = weight_grad(normed4, grad_cq)
    grad_state1_part, gain_four = rms_back(state1, gains[4], project_back(grad_cq, dec_mats[2]))
    grad_state1 = grad_state2 + grad_state1_part
    cross_pair_grad = weight_grad(encoded, grad_pairs)
    grad_encoded = project_back(grad_pairs, dec_mats[3])
    branch_grad = grad_state1.astype(jnp.bfloat16)
    self_out_grad = weight_grad(self_attended, branch_grad)
    grad_self = project_back(branch_grad, dec_mats[1]).astype(jnp.bfloat16)
    grad_sq, grad_sk, grad_sv, dec_bias_grad = attend_back(
        self_qkv, self_qkv, self_places, dec_bias, target_segments, target_segments, True, grad_self
    )
    grad_sqkv = jnp.concatenate([grad_sq, grad_sk, grad_sv], axis=-1)
    self_qkv_grad = weight_grad(normed3, grad_sqkv)
    grad_state0_part, gain_three = rms_back(state0, gains[3], project_back(grad_sqkv, dec_mats[0]))
    grad_state0 = grad_state1 + grad_state0_part
    decoder_portion = jnp.concatenate(
        [
            pairs_of(matrix)
            for matrix in (
                self_qkv_grad,
                self_out_grad,
                cross_query_grad,
                cross_pair_grad,
                cross_out_grad,
                dec_in_grad,
                dec_down_grad,
            )
        ],
        axis=0,
    )
    dec_part = reduce_blocks(decoder_portion)

    grad_hidden2, gain_two = rms_back(hidden2, gains[2], grad_encoded)
    grad_hidden1, gain_one, encoder_input_gradient, encoder_down_gradient = ff_back(
        hidden1, gains[1], enc_mats[2], enc_mats[3], enc_cache, grad_hidden2
    )
    branch_grad = grad_hidden1.astype(jnp.bfloat16)
    encoder_output_gradient = weight_grad(enc_attended, branch_grad)
    grad_attn = project_back(branch_grad, enc_mats[1]).astype(jnp.bfloat16)
    grad_eq, grad_ek, grad_ev, enc_bias_grad = attend_back(
        enc_qkv, enc_qkv, self_places, enc_bias, row_segments, row_segments, False, grad_attn
    )
    grad_eqkv = jnp.concatenate([grad_eq, grad_ek, grad_ev], axis=-1)
    encoder_qkv_gradient = weight_grad(normed0, grad_eqkv)
    grad_hidden0_part, gain_zero = rms_back(hidden0, gains[0], project_back(grad_eqkv, enc_mats[0]))
    grad_hidden0 = grad_hidden1 + grad_hidden0_part
    encoder_portion = jnp.concatenate(
        [
            pairs_of(matrix)
            for matrix in (
                encoder_qkv_gradient,
                encoder_output_gradient,
                encoder_input_gradient,
                encoder_down_gradient,
            )
        ],
        axis=0,
    )
    enc_part = reduce_blocks(encoder_portion)

    back_rows = jnp.concatenate(
        [grad_hidden0.reshape(-1, D), grad_state0.reshape(-1, D)], axis=0
    ).astype(jnp.bfloat16)
    back_all = lax.all_gather(back_rows, "fsdp", axis=0, tiled=True)
    dense_bound = jnp.max(jnp.abs(emb_grad))
    bound = dense_bound + back_all.shape[0] * jnp.max(jnp.abs(back_all)).astype(jnp.float32)
    emb_grad = table_grads(back_all, all_tokens, vocab_first, vocab_local, emb_grad)
    gain_part = jnp.stack(
        [gain_zero, gain_one, gain_two, gain_three, gain_four, gain_five, gain_six]
    )
    rel_part = jnp.stack(
        [tile_bias_grad(enc_onehot, enc_bias_grad), tile_bias_grad(dec_onehot, dec_bias_grad)]
    )
    loss_part = jnp.where(fsdp_rank == 0, jnp.stack([group_loss, group_count]), 0.0)
    gain_total, rel_total, loss_total = lax.psum((gain_part, rel_part, loss_part), EVERYWHERE)
    loss_sum = loss_total[0]
    loss_count = jnp.maximum(loss_total[1], 1.0)
    share = 1.0 / loss_count
    gain_grad = gain_total * share
    rel_grad = rel_total * share

    if paired_mesh():
        dec_grad = from_pairs(share_blocks(dec_part) * share)
        enc_grad = from_pairs(share_blocks(enc_part) * share)
        top, low, scale = reduce_table(emb_grad, bound)
        squares = (
            jnp.sum(jnp.square(enc_part * share))
            + jnp.sum(jnp.square(dec_part * share))
            + jnp.sum(jnp.square(top * (share / scale)))
            + jnp.sum(jnp.square(low * (share / scale)))
        )
        squares_all = lax.psum(squares, EVERYWHERE)
        table_grad = share_table(top, low, scale)[:vocab_local] * share
    else:
        dec_whole, enc_whole = (dec_part * share, enc_part * share)
        dec_grad, enc_grad = (from_pairs(dec_whole), from_pairs(enc_whole))
        table_grad = lax.psum(emb_grad, REPLICAS)[:vocab_local] * share
        squares_all = lax.psum(
            jnp.sum(jnp.square(enc_whole))
            + jnp.sum(jnp.square(dec_whole))
            + jnp.sum(jnp.square(table_grad)),
            "fsdp",
        )

    enc_ahead, enc_lr, enc_rr = shampoo_ahead(enc_m, enc_lroot, enc_rroot)
    dec_ahead, dec_lr, dec_rr = shampoo_ahead(dec_m, dec_lroot, dec_rroot)
    dec_products = shampoo_products(dec_grad, dec_lr, dec_rr)
    enc_products = shampoo_products(enc_grad, enc_lr, enc_rr)
    grad_norm = jnp.sqrt(
        squares_all + jnp.sum(gain_grad * gain_grad) + jnp.sum(rel_grad * rel_grad)
    )
    factor = jnp.minimum(1.0, clip_limit / grad_norm)
    new_emb = adam_update(embedding, table_grad * factor, emb_m, emb_v)
    new_gain = adam_update(gains, gain_grad * factor, gain_m, gain_v)
    new_rel = adam_update(rel_bias, rel_grad * factor, rel_m, rel_v)
    new_enc = shampoo_update(enc_w, enc_m, enc_left, enc_right, enc_ahead, enc_products, factor)
    new_dec = shampoo_update(dec_w, dec_m, dec_left, dec_right, dec_ahead, dec_products, factor)
    return (
        loss_sum,
        loss_count,
        grad_norm,
        *new_emb,
        *new_gain,
        *new_rel,
        *new_enc,
        *new_dec,
    )


def solution(mesh):
    in_specs = (
        P(("dp", "fsdp"), "seq"),
        P(("dp", "fsdp"), "seq"),
        P(("dp", "fsdp"), "seq"),
        P(("dp", "fsdp", "seq"), None),
        P(("dp", "fsdp", "seq"), None),
        P(("dp", "fsdp", "seq"), None),
        P("fsdp", None),
        P("fsdp", None),
        P("fsdp", None),
        P(),
        P(),
        P(),
        P(),
        P(),
        P(),
        P("fsdp", None),
        P("fsdp", None),
        P("fsdp", None),
        P("fsdp", None),
        P("fsdp", None),
        P("fsdp", None),
        P("fsdp", None),
        P("fsdp", None),
        P("fsdp", None),
        P("fsdp", None),
        P("fsdp", None),
        P("fsdp", None),
    )
    out_specs = (
        P(),
        P(),
        P(),
        P("fsdp", None),
        P("fsdp", None),
        P("fsdp", None),
        P(),
        P(),
        P(),
        P(),
        P(),
        P(),
        P("fsdp", None),
        P("fsdp", None),
        P("fsdp", None),
        P("fsdp", None),
        P("fsdp", None),
        P("fsdp", None),
        P("fsdp", None),
        P("fsdp", None),
    )
    return jax.shard_map(
        on_device, mesh=mesh, in_specs=in_specs, out_specs=out_specs, check_vma=False
    )
```

time: 2660 us -> 1650 us (0.62)
  waiting for transfers between devices: 976 us -> 353 us
  local copies, waits for them, and re-layouts: 896 us -> 416 us
  matrix products: 359 us -> 242 us
  Pallas kernels: 0 us -> 72.4 us
  starting transfers between devices: 10.3 us -> 73.6 us
  other arithmetic: 242 us -> 303 us
    reduce_scatter x6 -> x1, waiting for transfers between devices: 531 us -> 89.5 us  [on_device(): lax.psum_scatter(table_rows(table, all_tokens, vocab_first), 'fsdp', scat...]
    reshape x56 -> x5, local copies, waits for them, and re-layouts: 390 us -> 0.16 us  [the longest x1 0.05 us: on_device(): gathered = gathered.reshape(n_fsdp, n_seq, -1)]
    psum x1 -> x0, waiting for transfers between devices: 257 us -> none  [on_device(): lax.psum((enc_shard, dec_shard, emb_grad, gain_part, rel_part, group_loss...]
    eq x1 -> x0, local copies, waits for them, and re-layouts: 186 us -> none  [bucket_onehot(): buckets[None] == jnp.arange(NBK, dtype=jnp.int32)[:, None, None]]
    ppermute x0 -> x44, waiting for transfers between devices: none -> 131 us  [the longest x32 124 us: swap(): lax.ppermute(values, axis, [(place, place ^ 1) for place in range(size)])]
    dot_general x30 -> x16, matrix products: 193 us -> 113 us  [the longest x12 100 us: block_product(): return jnp.einsum(form, left, right, precision=lax.Precision.HIGH)]
    ppermute x0 -> x44, starting transfers between devices: none -> 73.1 us  [the longest x32 40.5 us: swap(): lax.ppermute(values, axis, [(place, place ^ 1) for place in range(size)])]
    add x22 -> x20, other arithmetic: 19.5 us -> 92.6 us  [the longest x2 29.2 us: reduce_blocks(): wide(pick(pairs, core, 1))]
  transfers between devices with their start and end apart: 17 -> 50, of which waited for: 9 -> 22; matrix products, arithmetic and copies ran while one was open for 37% -> 39% of each run, Pallas kernels for 0% -> 1%
where the time goes in v1:
time: 1650 us; the launch traced here: 1640 us
  local copies, waits for them, and re-layouts  416 us (25%)
  waiting for transfers between devices  353 us (21%)
  other arithmetic  303 us (18%)
  matrix products  242 us (15%)
  blocking collectives  149 us (9%)
  starting transfers between devices  73.6 us (4%)
  Pallas kernels  72.4 us (4%)
  between operations  32.6 us (2%)
    ppermute x32, waiting for transfers between devices, swap(): lax.ppermute(values, axis, [(place, place ^ 1) for place in range(size)])  124 us
    all_gather x2, waiting for transfers between devices, gather_weights(): return lax.all_gather(pairs, EVERYWHERE, axis=0, tiled=True)  109 us
    dot_general x12, matrix products, block_product(): return jnp.einsum(form, left, right, precision=lax.Precision.HIGH)  100 us
    reduce_scatter x1, waiting for transfers between devices, on_device(): lax.psum_scatter(table_rows(table, all_tokens, vocab_first), 'fsdp', scat...  89.5 us
    unnamed x373, local copies, waits for them, and re-layouts  65.1 us
    psum x1, blocking collectives, on_device(): lax.psum((gain_part, rel_part, loss_part), EVERYWHERE)  60 us
    scatter-add x1, other arithmetic, table_grads(): jax.ops.segment_sum(grads.reshape(-1, D).astype(jnp.float32), slots, num_...  44 us
    pallas_call x3, Pallas kernels, attend_back(): pl.pallas_call(functools.partial(attend_back_kernel, biased=bias is not N...  43.5 us
  transfers between devices with their start and end apart: 50, of which 22 were waited for; matrix products, arithmetic and copies ran while one was open for 39% of the time, Pallas kernels for 1%

profile of v1, /device:TPU:0, one launch (start us, length us, event | category | flops | bytes accessed | tf_op | source)
XLA Modules:
  0.0 1641.8 jit_solution(3917757564291544840)
XLA Ops:
  16.1 34.3 %all-gather.2 = s32[16,1,1408]{2,1,0:T(1,128)S(1)} all-gather(s32[1,1,1408]{2,1,0:T(1,128)S(1)} %reshape.1416), channel_id=2, replica_groups=mesh['dp'=2,'fsdp'=8,'seq'=2] {'fsdp','seq'}, dimensions={0}, use_global_device_ids=true | all-gather | bytes 95744 | tf_op jit(solution)/shard_map/all_gather | solution.py:631
  51.5 27.1 %gather_fusion = bf16[5120,768]{1,0:T(8,128)(2,1)} fusion(bf16[4016,768]{1,0:T(8,128)(2,1)} %convert_element_type.938, s32[5120]{0:T(1024)S(1)} %broadcast_clamp_fusion), kind=kCustom, calls=%fused_computation | custom fusion | bytes 15749120 | tf_op jit(solution)/shard_map/jit(_take)/gather | solution.py:360
  102.6 89.5 %reduce-scatter.3.cloned.1.call-done = bf16[1,640,768]{2,1,0:T(8,128)(2,1)} async-done(((bf16[8,640,768]{2,1,0:T(8,128)(2,1)}), bf16[1,640,768]{2,1,0:T(8,128)(2,1)}) %reduce-scatter.3.cloned.1.call-update) | async-done | bytes 983056 | tf_op jit(solution)/shard_map/reduce_scatter | solution.py:648
  194.5 50.2 %all-gather.11.cloned.1.call-done = bf16[96,192,384]{2,1,0:T(8,128)(2,1)} async-done(((bf16[3,192,384]{2,1,0:T(8,128)(2,1)}), bf16[96,192,384]{2,1,0:T(8,128)(2,1)}) %all-gather.11.cloned.1.call-update) | async-done | bytes 14155792 | tf_op jit(solution)/shard_map/all_gather | solution.py:398
  284.6 18.1 %shard_map.411 = bf16[1,512,768]{2,1,0:T(8,128)(2,1)S(1)} custom-call(bf16[1,512,2304]{2,1,0:T(8,128)(2,1)S(1)} %fusion.34.q_ref.k_ref.v_ref, bf16[1,512,2304]{2,1,0:T(8,128)(2,1)S(1)} %fusion.34.q_ref.k_ref.v_ref, bf16[1,512,2304]{2,1,0:T(8,128)(2,1)S(1)} %fusion.34.q_ref.k_ref.v_ref, f32[12,5,128,128]{3,2,1,0:T(8,128)S(1)} %bitcast.763, ...), custom_call_target="tpu_custom_call" | custom-call | flops 1610612736 | bytes 3145728 | tf_op jit(solution)/shard_map/pallas_call | solution.py:229
  311.7 59.0 %all-gather.9.cloned.1.call-done = bf16[128,192,384]{2,1,0:T(8,128)(2,1)} async-done(((bf16[4,192,384]{2,1,0:T(8,128)(2,1)}), bf16[128,192,384]{2,1,0:T(8,128)(2,1)}) %all-gather.9.cloned.1.call-update) | async-done | bytes 18874384 | tf_op jit(solution)/shard_map/all_gather | solution.py:398
  433.1 23.3 %all-gather.13.cloned.1.call-done = bf16[1024,768]{1,0:T(8,128)(2,1)} async-done(((bf16[128,768]{1,0:T(8,128)(2,1)}), bf16[1024,768]{1,0:T(8,128)(2,1)}) %all-gather.13.cloned.1.call-update) | async-done | bytes 1572880 | tf_op jit(solution)/shard_map/all_gather | solution.py:690
  470.2 14.2 all-gather.3
  485.8 12.7 fusion.216
  538.5 10.6 fusion.245
  603.4 12.6 multiply_reduce_fusion.1
  630.9 29.7 %shard_map.414 = (bf16[1,512,768]{2,1,0:T(8,128)(2,1)S(1)}, bf16[1,512,768]{2,1,0:T(8,128)(2,1)S(1)}, bf16[1,512,768]{2,1,0:T(8,128)(2,1)S(1)}, f32[12,5,128,128]{3,2,1,0:T(8,128)S(1)}) custom-call(bf16[1,512,2304]{2,1,0:T(8,128)(2,1)S(1)} %copy-done.3, bf16[1,512,2304]{2,1,0:T(8,128)(2,1)S(1)} %copy-done.3, bf16[1,512,2304]{2,1,0:T(8,128)(2,1)S(1)} %copy-done.3, ...), custom_call_target="tpu_custom_call" | custom-call | flops 4026531840 | bytes 7864320 | tf_op jit(solution)/shard_map/pallas_call | solution.py:257
  685.5 19.2 %pad_maximum_fusion = f32[96,192,384]{2,1,0:T(8,128)} fusion(f32[32,192,384]{2,1,0:T(8,128)} %bitcast.852, f32[32,192,384]{2,1,0:T(8,128)} %bitcast.853, f32[8,192,384]{2,1,0:T(8,128)S(1)} %bitcast.844, f32[24,192,384]{2,1,0:T(8,128)} %bitcast.808), kind=kLoop, calls=%fused_computation.2 | loop fusion | flops 21233664 | bytes 56623104 | tf_op jit(solution)/shard_map/concatenate | solution.py:775
  782.9 11.3 fusion.5
  808.7 12.3 bitcast_add_fusion.1
  821.0 12.0 fusion.224
  851.0 26.4 %collective-permute-done.1 = bf16[4,2,3,96,384]{4,3,2,0,1:T(8,128)(2,1)} collective-permute-done((bf16[4,2,3,96,384]{4,3,2,0,1:T(8,128)(2,1)}, bf16[4,2,3,96,384]{4,3,2,0,1:T(8,128)(2,1)}, u32[]{:S(2)}, u32[]{:S(2)}) %collective-permute-start.1) | collective-permute-done | bytes 1769504 | tf_op jit(solution)/shard_map/ppermute | solution.py:409
  915.9 16.9 %bitcast_add_fusion = f32[4,16,192,384]{3,2,1,0:T(8,128)} fusion(bf16[4,16,192,384]{3,2,1,0:T(8,128)(2,1)} %collective-permute-done.11, f32[4,2,16,192,384]{4,3,2,1,0:T(8,128)} %bitcast.800, s32[]{:T(128)S(6)} %select_n.370), kind=kLoop, calls=%fused_computation.3 | loop fusion | flops 9437184 | bytes 47185924 | tf_op jit(solution)/shard_map/add | solution.py:464
  939.0 11.2 fusion.221
  969.8 16.2 abs_reduce_fusion
  986.0 60.0 %psum.28 = f32[2]{0:T(128)S(1)} all-reduce(f32[2]{0:T(128)S(1)} %broadcast_select_fusion.24), channel_id=1, replica_groups=mesh['dp'=2,'fsdp'=8,'seq'=2] {'fsdp','dp','seq'}, use_global_device_ids=true, to_apply=%region_16.17 | all-reduce | flops 2 | bytes 16 | tf_op jit(solution)/shard_map/psum | solution.py:803
  1106.6 21.1 %collective-permute-done.37 = f16[2,3,96,384]{3,2,1,0:T(8,128)(2,1)} collective-permute-done((f16[2,3,96,384]{3,2,1,0:T(8,128)(2,1)}, f16[2,3,96,384]{3,2,1,0:T(8,128)(2,1)}, u32[]{:S(2)}, u32[]{:S(2)}) %collective-permute-start.37) | collective-permute-done | bytes 442400 | tf_op jit(solution)/shard_map/ppermute | solution.py:409
  1165.0 44.0 %scatter_custom_fusion = f32[4032,768]{1,0:T(8,128)} fusion(f32[4032,768]{1,0:T(8,128)} %pad.4, s32[5120]{0:T(1024)S(1)} %bitcast.930, bf16[5120,768]{1,0:T(8,128)(2,1)} %all-gather.15.cloned.1.call-done), kind=kCustom, calls=%fused_computation.10 | custom fusion | flops 7864320 | bytes 20250624 | tf_op jit(solution)/shard_map/scatter-add | solution.py:369
  1214.0 11.5 select_multiply_fusion
  1253.3 20.9 %collective-permute-done.38 = f32[]{:T(128)} collective-permute-done((f32[]{:T(128)}, f32[]{:T(128)}, u32[]{:S(2)}, u32[]{:S(2)}) %collective-permute-start.38) | collective-permute-done | bytes 36 | tf_op jit(solution)/shard_map/ppermute | solution.py:409
  1329.1 40.6 %all-reduce.1 = (f32[]{:T(128)}, f32[7,768]{1,0:T(8,128)S(1)}, f32[2,32,12]{1,2,0:T(8,128)S(1)}) all-reduce(f32[]{:T(128)S(6)} %add.1078, f32[7,768]{1,0:T(8,128)S(1)} %stack.140, f32[2,32,12]{1,2,0:T(8,128)S(1)} %pad_maximum_fusion.22), channel_id=1, replica_groups=mesh['dp'=2,'fsdp'=8,'seq'=2] {'fsdp','dp','seq'}, use_global_device_ids=true, to_apply=%region_32.33 | all-reduce | flops 6145 | bytes 49160 | tf_op jit(solution)/shard_map/psum | solution.py:820
  1388.0 10.8 fusion.247
  1465.7 13.3 multiply_add_fusion.1
  1507.9 11.4 multiply_add_fusion.4
  1519.4 11.2 multiply_add_fusion.2
  1578.5 20.3 %collective-permute-done.31 = f16[2,1008,384]{2,1,0:T(8,128)(2,1)} collective-permute-done((f16[2,1008,384]{2,1,0:T(8,128)(2,1)}, f16[2,1008,384]{2,1,0:T(8,128)(2,1)}, u32[]{:S(2)}, u32[]{:S(2)}) %collective-permute-start.31) | collective-permute-done | bytes 1548320 | tf_op jit(solution)/shard_map/ppermute | solution.py:409
  1604.6 27.3 %multiply_subtract_fusion = (f32[4016,768]{1,0:T(8,128)}, f32[4016,768]{1,0:T(8,128)}, f32[4016,768]{1,0:T(8,128)}) fusion(f32[4016,768]{1,0:T(8,128)S(1)} %bitcast.790, f32[]{:T(128)S(6)} %min.19, f32[]{:T(128)S(6)} %div.145, f32[]{:T(128)S(6)} %div.151, f16[1008,384]{1,0:T(8,128)(2,1)S(1)} %get-tuple-element.242, ...), kind=kLoop, calls=%fused_computation.16 | loop fusion | flops 80191488 | bytes 80216080 | tf_op jit(solution)/shard_map/sub | solution.py:544
  (764 shorter events, 810.0 us)
Async XLA Ops:
  8.0 184.0 %reduce-scatter.3.cloned.1.call-start = ((), (), s32[]{:S(2)}) async-start(), calls=%async_computation.2 | async-start | bytes 8847360 | tf_op jit(solution)/shard_map/reduce_scatter | solution.py:648
  86.1 158.6 %all-gather.11.cloned.1.call-start = ((), (), s32[]{:S(2)}) async-start(), calls=%async_computation.4 | async-start | bytes 14598144 | tf_op jit(solution)/shard_map/all_gather | solution.py:398
  89.7 281.0 %all-gather.9.cloned.1.call-start = ((), (), s32[]{:S(2)}) async-start(), calls=%async_computation.3 | async-start | bytes 19464192 | tf_op jit(solution)/shard_map/all_gather | solution.py:398
  93.2 363.2 %all-gather.13.cloned.1.call-start = ((), (), s32[]{:S(2)}) async-start(), calls=%async_computation.5 | async-start | bytes 1769472 | tf_op jit(solution)/shard_map/all_gather | solution.py:690
  433.0 125.9 %reduce-scatter.5.cloned.1.call-start = ((), (), s32[]{:S(2)}) async-start(), calls=%async_computation.6 | async-start | bytes 3538944 | tf_op jit(solution)/shard_map/reduce_scatter | solution.py:711
  498.6 657.1 %all-gather.15.cloned.1.call-start = ((), (), s32[]{:S(2)}) async-start(), calls=%async_computation.7 | async-start | bytes 8847360 | tf_op jit(solution)/shard_map/all_gather | solution.py:792
  714.0 94.6 %collective-permute-start = (bf16[4,12,192,384]{3,2,1,0:T(8,128)(2,1)}, bf16[4,12,192,384]{3,2,1,0:T(8,128)(2,1)}, u32[]{:S(2)}, u32[]{:S(2)}) collective-permute-start(bf16[4,12,192,384]{3,2,1,0:T(8,128)(2,1)} %fusion.6), channel_id=1, source_target_pairs={{0,2},{2,0},{4,6},{6,4},{8,10},{10,8},{12,14},{14,12},{1,3},{3,1},... | collective-permute-start | bytes 21233672 | tf_op jit(solution)/shard_map/ppermute | solution.py:409
  794.2 121.6 %collective-permute-start.11 = (bf16[4,16,192,384]{3,2,1,0:T(8,128)(2,1)}, bf16[4,16,192,384]{3,2,1,0:T(8,128)(2,1)}, u32[]{:S(2)}, u32[]{:S(2)}) collective-permute-start(bf16[4,16,192,384]{3,2,1,0:T(8,128)(2,1)} %fusion.5), channel_id=1, source_target_pairs={{0,2},{2,0},{4,6},{6,4},{8,10},{10,8},{12,14},{14,12},{1,3},{3,1},... | collective-permute-start | bytes 28311560 | tf_op jit(solution)/shard_map/ppermute | solution.py:409
  836.4 41.0 %collective-permute-start.1 = (bf16[4,2,3,96,384]{4,3,2,0,1:T(8,128)(2,1)}, bf16[4,2,3,96,384]{4,3,2,0,1:T(8,128)(2,1)}, u32[]{:S(2)}, u32[]{:S(2)}) collective-permute-start(bf16[4,2,3,96,384]{4,3,2,0,1:T(8,128)(2,1)} %fusion.56), channel_id=1, source_target_pairs={{0,1},{1,0},{2,3},{3,2},{4,5},{5,4},{6,7},{7,6},{8,9},{9,8},{10,11... | collective-permute-start | bytes 5308424 | tf_op jit(solution)/shard_map/ppermute | solution.py:409
  846.4 41.8 %collective-permute-start.3 = (bf16[4,2,3,96,384]{4,3,2,1,0:T(8,128)(2,1)}, bf16[4,2,3,96,384]{4,3,2,1,0:T(8,128)(2,1)}, u32[]{:S(2)}, u32[]{:S(2)}) collective-permute-start(bf16[4,2,3,96,384]{4,3,2,1,0:T(8,128)(2,1)} %fusion.55), channel_id=1, source_target_pairs={{0,16},{16,0},{1,17},{17,1},{2,18},{18,2},{3,19},{19,3},{4,20},{20... | collective-permute-start | bytes 5308424 | tf_op jit(solution)/shard_map/ppermute | solution.py:409
  880.7 25.2 %collective-permute-start.2 = (bf16[4,3,96,384]{3,2,1,0:T(8,128)(2,1)S(1)}, bf16[4,3,96,384]{3,2,1,0:T(8,128)(2,1)S(1)}, u32[]{:S(2)}, u32[]{:S(2)}) collective-permute-start(bf16[4,3,96,384]{3,2,1,0:T(8,128)(2,1)S(1)} %fusion.105), channel_id=1, source_target_pairs={{0,16},{16,0},{1,17},{17,1},{2,18},{18,2},{3,19},{19,3},{4,20},{20... | collective-permute-start | bytes 2654216 | tf_op jit(solution)/shard_map/ppermute | solution.py:409
  933.1 29.2 %collective-permute-start.6 = (bf16[3,192,384]{2,1,0:T(8,128)(2,1)S(1)}, bf16[3,192,384]{2,1,0:T(8,128)(2,1)S(1)}, u32[]{:S(2)}, u32[]{:S(2)}) collective-permute-start(bf16[3,192,384]{2,1,0:T(8,128)(2,1)S(1)} %get-tuple-element.231), channel_id=1, source_target_pairs={{0,4},{2,6},{4,8},{6,10},{8,12},{10,14},{1,5},{3,7},{5,9},{7,11},{... | collective-permute-start | bytes 1327112 | tf_op jit(solution)/shard_map/ppermute | solution.py:417
  937.7 24.6 %collective-permute-start.9 = (bf16[3,192,384]{2,1,0:T(8,128)(2,1)S(1)}, bf16[3,192,384]{2,1,0:T(8,128)(2,1)S(1)}, u32[]{:S(2)}, u32[]{:S(2)}) collective-permute-start(bf16[3,192,384]{2,1,0:T(8,128)(2,1)S(1)} %get-tuple-element.232), channel_id=1, source_target_pairs={{4,0},{6,2},{8,4},{10,6},{12,8},{14,10},{5,1},{7,3},{9,5},{11,7},{... | collective-permute-start | bytes 1327112 | tf_op jit(solution)/shard_map/ppermute | solution.py:417
  957.7 133.3 %collective-permute-start.12 = (bf16[4,2,4,96,384]{4,3,2,0,1:T(8,128)(2,1)}, bf16[4,2,4,96,384]{4,3,2,0,1:T(8,128)(2,1)}, u32[]{:S(2)}, u32[]{:S(2)}) collective-permute-start(bf16[4,2,4,96,384]{4,3,2,0,1:T(8,128)(2,1)} %fusion.45), channel_id=1, source_target_pairs={{0,1},{1,0},{2,3},{3,2},{4,5},{5,4},{6,7},{7,6},{8,9},{9,8},{10,11... | collective-permute-start | bytes 7077896 | tf_op jit(solution)/shard_map/ppermute | solution.py:409
  960.8 134.1 %collective-permute-start.14 = (bf16[4,2,4,96,384]{4,3,2,1,0:T(8,128)(2,1)}, bf16[4,2,4,96,384]{4,3,2,1,0:T(8,128)(2,1)}, u32[]{:S(2)}, u32[]{:S(2)}) collective-permute-start(bf16[4,2,4,96,384]{4,3,2,1,0:T(8,128)(2,1)} %fusion.44), channel_id=1, source_target_pairs={{0,16},{16,0},{1,17},{17,1},{2,18},{18,2},{3,19},{19,3},{4,20},{20... | collective-permute-start | bytes 7077896 | tf_op jit(solution)/shard_map/ppermute | solution.py:409
  963.3 101.9 %collective-permute-start.10 = (bf16[3,192,384]{2,1,0:T(8,128)(2,1)}, bf16[3,192,384]{2,1,0:T(8,128)(2,1)S(1)}, u32[]{:S(2)}, u32[]{:S(2)}) collective-permute-start(bf16[3,192,384]{2,1,0:T(8,128)(2,1)} %get-tuple-element.230), channel_id=1, source_target_pairs={{4,0},{6,2},{8,4},{10,6},{12,8},{14,10},{5,1},{7,3},{9,5},{11,7},{... | collective-permute-start | bytes 1327112 | tf_op jit(solution)/shard_map/ppermute | solution.py:417
  964.6 100.6 %collective-permute-start.7 = (bf16[3,192,384]{2,1,0:T(8,128)(2,1)S(1)}, bf16[3,192,384]{2,1,0:T(8,128)(2,1)S(1)}, u32[]{:S(2)}, u32[]{:S(2)}) collective-permute-start(bf16[3,192,384]{2,1,0:T(8,128)(2,1)S(1)} %get-tuple-element.229), channel_id=1, source_target_pairs={{0,4},{2,6},{4,8},{6,10},{8,12},{10,14},{1,5},{3,7},{5,9},{7,11},{... | collective-permute-start | bytes 1327112 | tf_op jit(solution)/shard_map/ppermute | solution.py:417
  1094.7 34.1 %collective-permute-start.13 = (bf16[4,4,96,384]{3,2,1,0:T(8,128)(2,1)S(1)}, bf16[4,4,96,384]{3,2,1,0:T(8,128)(2,1)}, u32[]{:S(2)}, u32[]{:S(2)}) collective-permute-start(bf16[4,4,96,384]{3,2,1,0:T(8,128)(2,1)S(1)} %fusion.90), channel_id=1, source_target_pairs={{0,16},{16,0},{1,17},{17,1},{2,18},{18,2},{3,19},{19,3},{4,20},{20... | collective-permute-start | bytes 3538952 | tf_op jit(solution)/shard_map/ppermute | solution.py:409
  1101.3 29.9 %collective-permute-start.15 = (bf16[4,4,96,384]{3,2,1,0:T(8,128)(2,1)}, bf16[4,4,96,384]{3,2,1,0:T(8,128)(2,1)}, u32[]{:S(2)}, u32[]{:S(2)}) collective-permute-start(bf16[4,4,96,384]{3,2,1,0:T(8,128)(2,1)} %fusion.91), channel_id=1, source_target_pairs={{0,1},{1,0},{2,3},{3,2},{4,5},{5,4},{6,7},{7,6},{8,9},{9,8},{10,11... | collective-permute-start | bytes 3538952 | tf_op jit(solution)/shard_map/ppermute | solution.py:409
  1102.8 24.9 %collective-permute-start.37 = (f16[2,3,96,384]{3,2,1,0:T(8,128)(2,1)}, f16[2,3,96,384]{3,2,1,0:T(8,128)(2,1)}, u32[]{:S(2)}, u32[]{:S(2)}) collective-permute-start(f16[2,3,96,384]{3,2,1,0:T(8,128)(2,1)} %pad_maximum_fusion.18), channel_id=1, source_target_pairs={{0,16},{16,0},{1,17},{17,1},{2,18},{18,2},{3,19},{19,3},{4,20},{20... | collective-permute-start | bytes 1327112 | tf_op jit(solution)/shard_map/ppermute | solution.py:409
  1151.1 74.3 %collective-permute-start.17 = (bf16[4,192,384]{2,1,0:T(8,128)(2,1)}, bf16[4,192,384]{2,1,0:T(8,128)(2,1)S(1)}, u32[]{:S(2)}, u32[]{:S(2)}) collective-permute-start(bf16[4,192,384]{2,1,0:T(8,128)(2,1)} %get-tuple-element.219), channel_id=1, source_target_pairs={{0,4},{2,6},{4,8},{6,10},{8,12},{10,14},{1,5},{3,7},{5,9},{7,11},{... | collective-permute-start | bytes 1769480 | tf_op jit(solution)/shard_map/ppermute | solution.py:417
  1154.4 71.1 %collective-permute-start.20 = (bf16[4,192,384]{2,1,0:T(8,128)(2,1)S(1)}, bf16[4,192,384]{2,1,0:T(8,128)(2,1)S(1)}, u32[]{:S(2)}, u32[]{:S(2)}) collective-permute-start(bf16[4,192,384]{2,1,0:T(8,128)(2,1)S(1)} %get-tuple-element.220), channel_id=1, source_target_pairs={{4,0},{6,2},{8,4},{10,6},{12,8},{14,10},{5,1},{7,3},{9,5},{11,7},{... | collective-permute-start | bytes 1769480 | tf_op jit(solution)/shard_map/ppermute | solution.py:417
  1161.9 47.1 %collective-permute-start.22 = (f32[]{:T(128)}, f32[]{:T(128)}, u32[]{:S(2)}, u32[]{:S(2)}) collective-permute-start(f32[]{:T(128)} %add.1068), channel_id=1, source_target_pairs={{0,1},{1,0},{2,3},{3,2},{4,5},{5,4},{6,7},{7,6},{8,9},{9,8},{10,11... | collective-permute-start | bytes 20 | tf_op jit(solution)/shard_map/ppermute | solution.py:409
  1226.5 24.4 %collective-permute-start.21 = (bf16[4,192,384]{2,1,0:T(8,128)(2,1)}, bf16[4,192,384]{2,1,0:T(8,128)(2,1)S(1)}, u32[]{:S(2)}, u32[]{:S(2)}) collective-permute-start(bf16[4,192,384]{2,1,0:T(8,128)(2,1)} %get-tuple-element.218), channel_id=1, source_target_pairs={{4,0},{6,2},{8,4},{10,6},{12,8},{14,10},{5,1},{7,3},{9,5},{11,7},{... | collective-permute-start | bytes 1769480 | tf_op jit(solution)/shard_map/ppermute | solution.py:417
  1227.8 23.1 %collective-permute-start.18 = (bf16[4,192,384]{2,1,0:T(8,128)(2,1)S(1)}, bf16[4,192,384]{2,1,0:T(8,128)(2,1)S(1)}, u32[]{:S(2)}, u32[]{:S(2)}) collective-permute-start(bf16[4,192,384]{2,1,0:T(8,128)(2,1)S(1)} %get-tuple-element.217), channel_id=1, source_target_pairs={{0,4},{2,6},{4,8},{6,10},{8,12},{10,14},{1,5},{3,7},{5,9},{7,11},{... | collective-permute-start | bytes 1769480 | tf_op jit(solution)/shard_map/ppermute | solution.py:417
  1247.1 48.9 %collective-permute-start.24 = (f16[1008,768]{1,0:T(8,128)(2,1)}, f16[1008,768]{1,0:T(8,128)(2,1)}, u32[]{:S(2)}, u32[]{:S(2)}) collective-permute-start(f16[1008,768]{1,0:T(8,128)(2,1)} %fusion.86), channel_id=1, source_target_pairs={{0,1},{1,0},{2,3},{3,2},{4,5},{5,4},{6,7},{7,6},{8,9},{9,8},{10,11... | collective-permute-start | bytes 4644872 | tf_op jit(solution)/shard_map/ppermute | solution.py:409
  1250.3 50.5 %collective-permute-start.26 = (f16[1008,768]{1,0:T(8,128)(2,1)}, f16[1008,768]{1,0:T(8,128)(2,1)}, u32[]{:S(2)}, u32[]{:S(2)}) collective-permute-start(f16[1008,768]{1,0:T(8,128)(2,1)} %fusion.87), channel_id=1, source_target_pairs={{0,16},{16,0},{1,17},{17,1},{2,18},{18,2},{3,19},{19,3},{4,20},{20... | collective-permute-start | bytes 4644872 | tf_op jit(solution)/shard_map/ppermute | solution.py:409
  1251.8 22.4 %collective-permute-start.38 = (f32[]{:T(128)}, f32[]{:T(128)}, u32[]{:S(2)}, u32[]{:S(2)}) collective-permute-start(f32[]{:T(128)} %get-tuple-element.144), channel_id=1, source_target_pairs={{0,1},{1,0},{2,3},{3,2},{4,5},{5,4},{6,7},{7,6},{8,9},{9,8},{10,11... | collective-permute-start | bytes 20 | tf_op jit(solution)/shard_map/ppermute | solution.py:409
  1412.1 149.4 %collective-permute-start.30 = (f16[1008,384]{1,0:T(8,128)(2,1)S(1)}, f16[1008,384]{1,0:T(8,128)(2,1)}, u32[]{:S(2)}, u32[]{:S(2)}) collective-permute-start(f16[1008,384]{1,0:T(8,128)(2,1)S(1)} %copy-done.43), channel_id=1, source_target_pairs={{0,1},{1,0},{2,3},{3,2},{4,5},{5,4},{6,7},{7,6},{8,9},{9,8},{10,11... | collective-permute-start | bytes 2322440 | tf_op jit(solution)/shard_map/ppermute | solution.py:409
  1414.4 151.6 %collective-permute-start.28 = (f16[1008,384]{1,0:T(8,128)(2,1)S(1)}, f16[1008,384]{1,0:T(8,128)(2,1)S(1)}, u32[]{:S(2)}, u32[]{:S(2)}) collective-permute-start(f16[1008,384]{1,0:T(8,128)(2,1)S(1)} %copy-done.42), channel_id=1, source_target_pairs={{0,16},{16,0},{1,17},{17,1},{2,18},{18,2},{3,19},{19,3},{4,20},{20... | collective-permute-start | bytes 2322440 | tf_op jit(solution)/shard_map/ppermute | solution.py:409
  1564.4 34.4 %collective-permute-start.31 = (f16[2,1008,384]{2,1,0:T(8,128)(2,1)}, f16[2,1008,384]{2,1,0:T(8,128)(2,1)}, u32[]{:S(2)}, u32[]{:S(2)}) collective-permute-start(f16[2,1008,384]{2,1,0:T(8,128)(2,1)} %pad_maximum_fusion.8), channel_id=1, source_target_pairs={{0,16},{16,0},{1,17},{17,1},{2,18},{18,2},{3,19},{19,3},{4,20},{20... | collective-permute-start | bytes 4644872 | tf_op jit(solution)/shard_map/ppermute | solution.py:409
  1567.5 33.9 %collective-permute-start.29 = (f16[2,1008,384]{2,1,0:T(8,128)(2,1)}, f16[2,1008,384]{2,1,0:T(8,128)(2,1)}, u32[]{:S(2)}, u32[]{:S(2)}) collective-permute-start(f16[2,1008,384]{2,1,0:T(8,128)(2,1)} %pad_maximum_fusion.7), channel_id=1, source_target_pairs={{0,1},{1,0},{2,3},{3,2},{4,5},{5,4},{6,7},{7,6},{8,9},{9,8},{10,11... | collective-permute-start | bytes 4644872 | tf_op jit(solution)/shard_map/ppermute | solution.py:409
  (188 other events, 4925.4 us)
Sparse Core Ops, SparseCore 0:
  86.3 105.7 reduce-scatter.2
  433.2 23.2 all-gather.12
  498.7 39.9 reduce-scatter.4
  851.1 80.0 all-gather.14
Sparse Core Ops, SparseCore 1:
  90.1 154.6 all-gather.10
  248.1 122.5 all-gather.8

commit v2 on v1

--- a/solution.py
+++ b/solution.py
@@ -285,27 +285,171 @@
     return jnp.concatenate([split[:, 0], split[:, 1]], axis=-1)
 
 
-def from_pairs(pairs):
-    amount = pairs.shape[0]
-    split = jnp.stack([pairs[..., :BLOCK], pairs[..., BLOCK:]], axis=1)
-    return split.reshape(2 * amount, BLOCK, BLOCK)
+def unpack_kernel(pairs_ref, out_ref):
+    across = out_ref.shape[1] // PAIR
+    for row in range(out_ref.shape[0] // BLOCK):
+        for column in range(across):
+            out_ref[row * BLOCK : (row + 1) * BLOCK, column * PAIR : (column + 1) * PAIR] = (
+                pairs_ref[row * across + column]
+            )
 
 
 def matrices_of(pairs, shapes):
     matrix_list = []
-    offset = 0
+    place = 0
     for height, breadth in shapes:
-        tall, wide = (height // BLOCK, breadth // PAIR)
-        section = pairs[offset : offset + tall * wide].reshape(tall, wide, BLOCK, PAIR)
-        matrix_list.append(section.transpose(0, 2, 1, 3).reshape(height, breadth))
-        offset += tall * wide
+        group = 2 * breadth // PAIR
+        first = place // group
+        matrix_list.append(
+            pl.pallas_call(
+                unpack_kernel,
+                out_shape=jax.ShapeDtypeStruct((height, breadth), pairs.dtype),
+                grid=(height // PAIR,),
+                in_specs=[
+                    pl.BlockSpec(
+                        (group, BLOCK, PAIR), lambda step, first=first: (first + step, 0, 0)
+                    )
+                ],
+                out_specs=pl.BlockSpec((PAIR, breadth), lambda step: (step, 0)),
+                cost_estimate=pl.CostEstimate(
+                    flops=0, bytes_accessed=4 * height * breadth, transcendentals=0
+                ),
+                compiler_params=pltpu.CompilerParams(vmem_limit_bytes=32 << 20),
+            )(pairs)
+        )
+        place += group * (height // PAIR)
     return matrix_list
 
 
-def pairs_of(matrix):
-    height, breadth = matrix.shape
-    tiles = matrix.reshape(height // BLOCK, BLOCK, breadth // PAIR, PAIR)
-    return tiles.transpose(0, 2, 1, 3).reshape(-1, BLOCK, PAIR)
+def weight_grad_kernel(x_ref, g_ref, *rest):
+    out_ref = rest[-1]
+    across = out_ref.shape[0] // 2
+    for column in range(across):
+        product = lax.dot_general(
+            x_ref[...],
+            g_ref[:, column * PAIR : (column + 1) * PAIR],
+            (((0,), (0,)), ((), ())),
+            preferred_element_type=jnp.float32,
+        )
+        product = product.astype(jnp.bfloat16)
+        out_ref[column] = product[:BLOCK]
+        out_ref[across + column] = product[BLOCK:]
+
+
+def weight_grads(operands):
+    total = sum(x.shape[-1] * g.shape[-1] for x, g in operands) // (BLOCK * PAIR)
+    pairs = None
+    place = 0
+    for x, g in operands:
+        x = x.reshape(-1, x.shape[-1])
+        g = g.reshape(-1, g.shape[-1])
+        count, height = x.shape
+        breadth = g.shape[1]
+        group = 2 * breadth // PAIR
+        first = place // group
+        given = [] if pairs is None else [pairs]
+        pairs = pl.pallas_call(
+            weight_grad_kernel,
+            out_shape=jax.ShapeDtypeStruct((total, BLOCK, PAIR), jnp.bfloat16),
+            grid=(height // PAIR,),
+            in_specs=[
+                pl.BlockSpec((count, PAIR), lambda step: (0, step)),
+                pl.BlockSpec((count, breadth), lambda step: (0, 0)),
+            ]
+            + [pl.BlockSpec(memory_space=pl.ANY)] * len(given),
+            out_specs=pl.BlockSpec(
+                (group, BLOCK, PAIR), lambda step, first=first: (first + step, 0, 0)
+            ),
+            input_output_aliases={2: 0} if given else {},
+            cost_estimate=pl.CostEstimate(
+                flops=2 * count * height * breadth,
+                bytes_accessed=2 * (count * (height + breadth) + height * breadth),
+                transcendentals=0,
+            ),
+            compiler_params=pltpu.CompilerParams(vmem_limit_bytes=40 << 20),
+        )(x, g, *given)
+        place += group * (height // PAIR)
+    return pairs
+
+
+def split_float(values):
+    high = values.astype(jnp.bfloat16)
+    return high, (values - high.astype(jnp.float32)).astype(jnp.bfloat16)
+
+
+def full_product(left, right, contract):
+    def part(first, second):
+        return lax.dot_general(
+            first, second, (contract, ((), ())), preferred_element_type=jnp.float32
+        )
+
+    return (
+        part(left[0], right[1]) + part(left[1], right[0]) + part(left[0], right[0])
+    )
+
+
+ROW_COL = ((1,), (0,))
+ROW_ROW = ((1,), (1,))
+COL_COL = ((0,), (0,))
+
+
+def turned_product(left_root, middle, right_root):
+    shaped = full_product(split_float(left_root), middle, ROW_COL)
+    return full_product(split_float(shaped), split_float(right_root), ROW_COL)
+
+
+def ahead_kernel(m_ref, lr_ref, rr_ref, o_ref):
+    for place in range(m_ref.shape[0]):
+        o_ref[place] = turned_product(lr_ref[place], split_float(m_ref[place]), rr_ref[place])
+
+
+def products_kernel(g_ref, lr_ref, rr_ref, g_out, turned_out, left_out, right_out):
+    for place in range(2):
+        block = g_ref[0, :, place * BLOCK : (place + 1) * BLOCK]
+        g_out[place] = block
+        halves = split_float(block)
+        turned_out[place] = turned_product(lr_ref[place], halves, rr_ref[place])
+        left_out[place] = full_product(halves, halves, ROW_ROW)
+        right_out[place] = full_product(halves, halves, COL_COL)
+
+
+def block_cost(amount, products, arrays):
+    return pl.CostEstimate(
+        flops=6 * products * amount * BLOCK**3,
+        bytes_accessed=4 * arrays * amount * BLOCK * BLOCK,
+        transcendentals=0,
+    )
+
+
+def shampoo_ahead(moment, left_root, right_root):
+    blocks = [as_blocks(moment), as_blocks(left_root), as_blocks(right_root)]
+    amount = moment.shape[0]
+    spec = pl.BlockSpec((2, BLOCK, BLOCK), lambda pair: (pair, 0, 0))
+    ahead = pl.pallas_call(
+        ahead_kernel,
+        out_shape=jax.ShapeDtypeStruct((amount, BLOCK, BLOCK), jnp.float32),
+        grid=(amount // 2,),
+        in_specs=[spec] * 3,
+        out_specs=spec,
+        cost_estimate=block_cost(amount, 2, 4),
+        compiler_params=pltpu.CompilerParams(vmem_limit_bytes=32 << 20),
+    )(*blocks)
+    return as_rows(ahead), blocks[1], blocks[2]
+
+
+def shampoo_products(pairs, left_root, right_root):
+    amount = left_root.shape[0]
+    spec = pl.BlockSpec((2, BLOCK, BLOCK), lambda pair: (pair, 0, 0))
+    results = pl.pallas_call(
+        products_kernel,
+        out_shape=[jax.ShapeDtypeStruct((amount, BLOCK, BLOCK), jnp.float32)] * 4,
+        grid=(amount // 2,),
+        in_specs=[pl.BlockSpec((1, BLOCK, PAIR), lambda pair: (pair, 0, 0)), spec, spec],
+        out_specs=[spec] * 4,
+        cost_estimate=block_cost(amount, 4, 7),
+        compiler_params=pltpu.CompilerParams(vmem_limit_bytes=32 << 20),
+    )(pairs, left_root, right_root)
+    return [as_rows(result) for result in results]
 
 
 def project(left, right):
@@ -314,10 +458,6 @@
 
 def project_back(left, right):
     return jnp.einsum("btf,df->btd", left, right, preferred_element_type=jnp.float32)
-
-
-def weight_grad(inputs, grads):
-    return jnp.einsum("btd,btf->df", inputs, grads, preferred_element_type=jnp.float32)
 
 
 def rms(values, gain):
@@ -345,13 +485,11 @@
 def ff_back(hidden, gain, w_in, w_down, cache, grad_out):
     normed, inner, active = cache
     branch_grad = grad_out.astype(jnp.bfloat16)
-    down_grad = weight_grad(active, branch_grad)
     grad_active = project_back(branch_grad, w_down)
     unused, gelu_back = jax.vjp(jax.nn.gelu, inner)
     grad_inner = gelu_back(grad_active)[0].astype(jnp.bfloat16)
-    in_grad = weight_grad(normed, grad_inner)
     grad_part, grad_gain = rms_back(hidden, gain, project_back(grad_inner, w_in))
-    return (grad_out + grad_part, grad_gain, in_grad, down_grad)
+    return (grad_out + grad_part, grad_gain, (normed, grad_inner), (active, branch_grad))
 
 
 def table_rows(table, token_ids, vocab_first):
@@ -361,17 +499,12 @@
     return jnp.where(inside[..., None], picked, jnp.zeros((), table.dtype))
 
 
-def table_grads(grads, token_ids, vocab_first, vocab_local, dense):
+def table_grads(grads, token_ids, vocab_first, dense):
+    vocab_local = dense.shape[0]
     local_ids = token_ids.reshape(-1) - vocab_first
     inside = (local_ids >= 0) & (local_ids < vocab_local)
     slots = jnp.where(inside, local_ids, vocab_local)
-    length = -(-(vocab_local + 1) // 32) * 32
-    summed = jax.ops.segment_sum(
-        grads.reshape(-1, D).astype(jnp.float32), slots, num_segments=length
-    )
-    row = lax.broadcasted_iota(jnp.int32, (length, 1), 0)
-    padded = jnp.pad(dense, ((0, length - vocab_local), (0, 0)))
-    return jnp.where(row < vocab_local, summed + padded, 0.0)
+    return dense.at[slots].add(grads.astype(jnp.float32), mode="drop")
 
 
 REPLICAS = ("dp", "seq")
@@ -386,16 +519,16 @@
     return lax.axis_size("dp") * lax.axis_size("seq")
 
 
-def gather_weights(master):
-    amount = master.shape[0]
-    parts = replica_count()
-    if amount % (2 * parts):
-        pairs = as_pairs(as_blocks(master.astype(jnp.bfloat16)))
-        return lax.all_gather(pairs, "fsdp", axis=0, tiled=True)
-    share = amount // parts
-    own = lax.dynamic_slice_in_dim(master, replica_rank() * share, share, 0)
-    pairs = as_pairs(as_blocks(own.astype(jnp.bfloat16)))
-    return lax.all_gather(pairs, EVERYWHERE, axis=0, tiled=True)
+def own_weights(master):
+    share = master.shape[0] // replica_count()
+    if master.shape[0] % (2 * replica_count()) == 0:
+        master = lax.dynamic_slice_in_dim(master, replica_rank() * share, share, 0)
+    return as_pairs(as_blocks(master.astype(jnp.bfloat16)))
+
+
+def gather_weights(pairs, amount):
+    split = amount % (2 * replica_count()) == 0
+    return lax.all_gather(pairs, EVERYWHERE if split else "fsdp", axis=0, tiled=True)
 
 
 def paired_mesh():
@@ -448,10 +581,24 @@
     return [[at(0, 0), at(0, 1)], [at(1, 0), at(1, 1)]]
 
 
+def sum_small(values):
+    size = lax.axis_size("fsdp")
+    if not paired_mesh() or size & (size - 1):
+        return lax.psum(values, EVERYWHERE)
+    values = values + swap(values, "seq")
+    values = values + swap(values, "dp")
+    step = 1
+    while step < size:
+        moves = [(place, place ^ step) for place in range(size)]
+        values = values + lax.ppermute(values, "fsdp", moves)
+        step *= 2
+    return values
+
+
 def reduce_blocks(pairs):
     if not paired_mesh():
         return lax.psum(
-            lax.psum_scatter(pairs, "fsdp", scatter_dimension=0, tiled=True), REPLICAS
+            lax.psum_scatter(wide(pairs), "fsdp", scatter_dimension=0, tiled=True), REPLICAS
         )
     n_chips = lax.axis_size("fsdp") // 2
     core = lax.axis_index("fsdp") % 2
@@ -461,7 +608,7 @@
     quarter = amount // 4
     mid = BLOCK // 2
     pairs = pairs.reshape(n_chips, 2, amount, BLOCK, PAIR)
-    chip_sum = wide(pick(pairs, core, 1)) + wide(swap(narrow(pick(pairs, 1 - core, 1)), "fsdp"))
+    chip_sum = wide(pick(pairs, core, 1)) + wide(swap(pick(pairs, 1 - core, 1), "fsdp"))
     chip_sum = chip_sum.reshape(n_chips, 2, 2, quarter, BLOCK, PAIR)
     upper, lower = (chip_sum[..., :mid, :], chip_sum[..., mid:, :])
     upper = pick(upper, half, 2) + wide(swap(narrow(pick(upper, 1 - half, 2)), "seq"))
@@ -504,11 +651,19 @@
     return wide(jnp.concatenate(whole[0] + whole[1], axis=0)) * (1.0 / scale)
 
 
+def window_rows(half_rows):
+    return -(-half_rows // 16) * 8
+
+
 def reduce_table(partial, bound):
     side, half = (lax.axis_index("dp"), lax.axis_index("seq"))
     scale = agreed_scale(bound)
-    rows = partial.shape[0] // 4
-    split = (partial * scale).reshape(2, 2, rows, D)
+    half_rows = partial.shape[0] // 2
+    window = window_rows(half_rows)
+
+    def rows_of(first, place):
+        start = first + place * (half_rows - window)
+        return lax.dynamic_slice_in_dim(partial, start, window, 0) * scale
 
     def half_lanes(values, place):
         return lax.dynamic_slice_in_dim(values, place * (D // 2), D // 2, 1)
@@ -516,23 +671,36 @@
     def send(values, axis):
         return wide(swap(values.astype(jnp.float16), axis))
 
-    top = pick(split[0], half, 0) + send(pick(split[0], 1 - half, 0), "seq")
-    low = pick(split[1], side, 0) + send(pick(split[1], 1 - side, 0), "dp")
+    top = rows_of(0, half) + send(rows_of(0, 1 - half), "seq")
+    low = rows_of(half_rows, side) + send(rows_of(half_rows, 1 - side), "dp")
     top = half_lanes(top, side) + send(half_lanes(top, 1 - side), "dp")
     low = half_lanes(low, half) + send(half_lanes(low, 1 - half), "seq")
     return top, low, scale
 
 
-def share_table(top, low, scale):
+def table_squares(top, low, half_rows):
     side, half = (lax.axis_index("dp"), lax.axis_index("seq"))
+    again = 2 * window_rows(half_rows) - half_rows
+    row = lax.broadcasted_iota(jnp.int32, (top.shape[0], 1), 0)
+    return jnp.sum(jnp.where(row >= again * half, top * top, 0.0)) + jnp.sum(
+        jnp.where(row >= again * side, low * low, 0.0)
+    )
+
+
+def share_table(top, low, scale, half_rows):
+    side, half = (lax.axis_index("dp"), lax.axis_index("seq"))
+    again = 2 * window_rows(half_rows) - half_rows
     top = lax.optimization_barrier(top.astype(jnp.float16))
     low = lax.optimization_barrier(low.astype(jnp.float16))
     top_side, low_half = (swap(top, "dp"), swap(low, "seq"))
-    top_rest = swap(jnp.stack([top, top_side]), "seq")
-    low_rest = swap(jnp.stack([low, low_half]), "dp")
-    top_all = placed([[top, top_side], [top_rest[0], top_rest[1]]], half, side)
-    low_all = placed([[low, low_half], [low_rest[0], low_rest[1]]], side, half)
-    rows = [jnp.concatenate(pieces, axis=1) for pieces in top_all + low_all]
+    top_rest = (swap(top, "seq"), swap(top_side, "seq"))
+    low_rest = (swap(low, "dp"), swap(low_half, "dp"))
+    top_all = placed([[top, top_side], top_rest], half, side)
+    low_all = placed([[low, low_half], low_rest], side, half)
+    rows = []
+    for first, second in (top_all, low_all):
+        rows.append(jnp.concatenate(first, axis=1))
+        rows.append(jnp.concatenate(second, axis=1)[again:])
     return wide(jnp.concatenate(rows, axis=0)) * (1.0 / scale)
 
 
@@ -545,26 +713,6 @@
         corrected / (jnp.sqrt(scaled) + adam_eps) + weight_decay * weight
     )
     return (weight, moment, second)
-
-
-def block_product(left, right, form):
-    return jnp.einsum(form, left, right, precision=lax.Precision.HIGH)
-
-
-def shampoo_ahead(moment, left_root, right_root):
-    left_root, right_root = (as_blocks(left_root), as_blocks(right_root))
-    shaped = block_product(left_root, as_blocks(moment), "nij,njk->nik")
-    return (as_rows(block_product(shaped, right_root, "nij,njk->nik")), left_root, right_root)
-
-
-def shampoo_products(gradient, left_root, right_root):
-    shaped = block_product(left_root, gradient, "nij,njk->nik")
-    return (
-        as_rows(gradient),
-        as_rows(block_product(shaped, right_root, "nij,njk->nik")),
-        as_rows(block_product(gradient, gradient, "nij,nkj->nik")),
-        as_rows(block_product(gradient, gradient, "nji,njk->nik")),
-    )
 
 
 def shampoo_update(weight, moment, left, right, ahead, products, factor):
@@ -628,6 +776,11 @@
         [dec_in.reshape(-1), targets.reshape(-1), loss_weights.reshape(-1)]
     )
     message = jnp.concatenate([message.reshape(-1), own]).reshape(1, 1, -1)
+    enc_pairs, dec_pairs, message = lax.optimization_barrier(
+        (own_weights(enc_w), own_weights(dec_w), message)
+    )
+    enc_pairs = gather_weights(enc_pairs, enc_w.shape[0])
+    dec_pairs = gather_weights(dec_pairs, dec_w.shape[0])
     gathered = lax.all_gather(message, ("fsdp", "seq"), axis=0, tiled=True)
     gathered = gathered.reshape(n_fsdp, n_seq, -1)
     row_words = rows * 2 * half_len
@@ -651,8 +804,8 @@
     hidden0 = looked_up[: rows * enc_len].reshape(rows, enc_len, D).astype(jnp.float32)
     state0 = looked_up[rows * enc_len :].reshape(rows, dec_len, D).astype(jnp.float32)
 
-    enc_mats = matrices_of(gather_weights(enc_w), layer_shapes(False))
-    dec_mats = matrices_of(gather_weights(dec_w), layer_shapes(True))
+    enc_mats = matrices_of(enc_pairs, layer_shapes(False))
+    dec_mats = matrices_of(dec_pairs, layer_shapes(True))
     enc_onehot = tile_onehot(enc_len // TILE, False)
     dec_onehot = tile_onehot(dec_len // TILE, True)
     enc_bias = tile_bias(enc_onehot, rel_bias[0])
@@ -720,41 +873,37 @@
         state2, gains[5], dec_mats[5], dec_mats[6], dec_cache, grad_state3
     )
     branch_grad = grad_state2.astype(jnp.bfloat16)
-    cross_out_grad = weight_grad(cross_attended, branch_grad)
+    cross_out_grad = (cross_attended, branch_grad)
     grad_cross = project_back(branch_grad, dec_mats[4]).astype(jnp.bfloat16)
     grad_cq, grad_ck, grad_cv = attend_back(
         cross_query, pairs, cross_places, None, target_segments, row_segments, False, grad_cross
     )
     grad_pairs = jnp.concatenate([grad_ck, grad_cv], axis=-1)
-    cross_query_grad = weight_grad(normed4, grad_cq)
+    cross_query_grad = (normed4, grad_cq)
     grad_state1_part, gain_four = rms_back(state1, gains[4], project_back(grad_cq, dec_mats[2]))
     grad_state1 = grad_state2 + grad_state1_part
-    cross_pair_grad = weight_grad(encoded, grad_pairs)
+    cross_pair_grad = (encoded, grad_pairs)
     grad_encoded = project_back(grad_pairs, dec_mats[3])
     branch_grad = grad_state1.astype(jnp.bfloat16)
-    self_out_grad = weight_grad(self_attended, branch_grad)
+    self_out_grad = (self_attended, branch_grad)
     grad_self = project_back(branch_grad, dec_mats[1]).astype(jnp.bfloat16)
     grad_sq, grad_sk, grad_sv, dec_bias_grad = attend_back(
         self_qkv, self_qkv, self_places, dec_bias, target_segments, target_segments, True, grad_self
     )
     grad_sqkv = jnp.concatenate([grad_sq, grad_sk, grad_sv], axis=-1)
-    self_qkv_grad = weight_grad(normed3, grad_sqkv)
+    self_qkv_grad = (normed3, grad_sqkv)
     grad_state0_part, gain_three = rms_back(state0, gains[3], project_back(grad_sqkv, dec_mats[0]))
     grad_state0 = grad_state1 + grad_state0_part
-    decoder_portion = jnp.concatenate(
+    decoder_portion = weight_grads(
         [
-            pairs_of(matrix)
-            for matrix in (
-                self_qkv_grad,
-                self_out_grad,
-                cross_query_grad,
-                cross_pair_grad,
-                cross_out_grad,
-                dec_in_grad,
-                dec_down_grad,
-            )
-        ],
-        axis=0,
+            self_qkv_grad,
+            self_out_grad,
+            cross_query_grad,
+            cross_pair_grad,
+            cross_out_grad,
+            dec_in_grad,
+            dec_down_grad,
+        ]
     )
     dec_part = reduce_blocks(decoder_portion)
 
@@ -763,26 +912,22 @@
         hidden1, gains[1], enc_mats[2], enc_mats[3], enc_cache, grad_hidden2
     )
     branch_grad = grad_hidden1.astype(jnp.bfloat16)
-    encoder_output_gradient = weight_grad(enc_attended, branch_grad)
+    encoder_output_gradient = (enc_attended, branch_grad)
     grad_attn = project_back(branch_grad, enc_mats[1]).astype(jnp.bfloat16)
     grad_eq, grad_ek, grad_ev, enc_bias_grad = attend_back(
         enc_qkv, enc_qkv, self_places, enc_bias, row_segments, row_segments, False, grad_attn
     )
     grad_eqkv = jnp.concatenate([grad_eq, grad_ek, grad_ev], axis=-1)
-    encoder_qkv_gradient = weight_grad(normed0, grad_eqkv)
+    encoder_qkv_gradient = (normed0, grad_eqkv)
     grad_hidden0_part, gain_zero = rms_back(hidden0, gains[0], project_back(grad_eqkv, enc_mats[0]))
     grad_hidden0 = grad_hidden1 + grad_hidden0_part
-    encoder_portion = jnp.concatenate(
+    encoder_portion = weight_grads(
         [
-            pairs_of(matrix)
-            for matrix in (
-                encoder_qkv_gradient,
-                encoder_output_gradient,
-                encoder_input_gradient,
-                encoder_down_gradient,
-            )
-        ],
-        axis=0,
+            encoder_qkv_gradient,
+            encoder_output_gradient,
+            encoder_input_gradient,
+            encoder_down_gradient,
+        ]
     )
     enc_part = reduce_blocks(encoder_portion)
 
@@ -792,7 +937,7 @@
     back_all = lax.all_gather(back_rows, "fsdp", axis=0, tiled=True)
     dense_bound = jnp.max(jnp.abs(emb_grad))
     bound = dense_bound + back_all.shape[0] * jnp.max(jnp.abs(back_all)).astype(jnp.float32)
-    emb_grad = table_grads(back_all, all_tokens, vocab_first, vocab_local, emb_grad)
+    emb_grad = table_grads(back_all, all_tokens, vocab_first, emb_grad)
     gain_part = jnp.stack(
         [gain_zero, gain_one, gain_two, gain_three, gain_four, gain_five, gain_six]
     )
@@ -800,7 +945,13 @@
         [tile_bias_grad(enc_onehot, enc_bias_grad), tile_bias_grad(dec_onehot, dec_bias_grad)]
     )
     loss_part = jnp.where(fsdp_rank == 0, jnp.stack([group_loss, group_count]), 0.0)
-    gain_total, rel_total, loss_total = lax.psum((gain_part, rel_part, loss_part), EVERYWHERE)
+    small = jnp.concatenate(
+        [gain_part.reshape(-1), rel_part.reshape(-1), loss_part, jnp.zeros(126, jnp.float32)]
+    )
+    small = sum_small(small.reshape(-1, LANES)).reshape(-1)
+    gain_total = small[: 7 * D].reshape(7, D)
+    rel_total = small[7 * D : 7 * D + 2 * NBK * H].reshape(2, NBK, H)
+    loss_total = small[7 * D + 2 * NBK * H :]
     loss_sum = loss_total[0]
     loss_count = jnp.maximum(loss_total[1], 1.0)
     share = 1.0 / loss_count
@@ -808,24 +959,23 @@
     rel_grad = rel_total * share
 
     if paired_mesh():
-        dec_grad = from_pairs(share_blocks(dec_part) * share)
-        enc_grad = from_pairs(share_blocks(enc_part) * share)
+        dec_grad = share_blocks(dec_part) * share
+        enc_grad = share_blocks(enc_part) * share
+        half_rows = vocab_local // 2
         top, low, scale = reduce_table(emb_grad, bound)
         squares = (
             jnp.sum(jnp.square(enc_part * share))
             + jnp.sum(jnp.square(dec_part * share))
-            + jnp.sum(jnp.square(top * (share / scale)))
-            + jnp.sum(jnp.square(low * (share / scale)))
+            + table_squares(top * (share / scale), low * (share / scale), half_rows)
         )
-        squares_all = lax.psum(squares, EVERYWHERE)
-        table_grad = share_table(top, low, scale)[:vocab_local] * share
+        squares_all = sum_small(squares)
+        table_grad = share_table(top, low, scale, half_rows) * share
     else:
-        dec_whole, enc_whole = (dec_part * share, enc_part * share)
-        dec_grad, enc_grad = (from_pairs(dec_whole), from_pairs(enc_whole))
-        table_grad = lax.psum(emb_grad, REPLICAS)[:vocab_local] * share
+        dec_grad, enc_grad = (dec_part * share, enc_part * share)
+        table_grad = lax.psum(emb_grad, REPLICAS) * share
         squares_all = lax.psum(
-            jnp.sum(jnp.square(enc_whole))
-            + jnp.sum(jnp.square(dec_whole))
+            jnp.sum(jnp.square(enc_grad))
+            + jnp.sum(jnp.square(dec_grad))
             + jnp.sum(jnp.square(table_grad)),
             "fsdp",
         )

time: 1650 us -> 1470 us (0.89)
  matrix products: 242 us -> 104 us
  local copies, waits for them, and re-layouts: 416 us -> 281 us
  Pallas kernels: 72.4 us -> 176 us
  blocking collectives: 149 us -> 48.6 us
  waiting for transfers between devices: 353 us -> 394 us
  starting transfers between devices: 73.6 us -> 110 us
    dot_general x23 -> x0, matrix products: 133 us -> none  [the longest x12 100 us: block_product(): return jnp.einsum(form, left, right, precision=lax.Precision.HIGH)]
    pallas_call x0 -> x26, Pallas kernels: none -> 104 us  [the longest x11 37.2 us: weight_grads(): pl.pallas_call(weight_grad_kernel, out_shape=jax.ShapeDtypeStruct((total,...]
    psum x2 -> x0, blocking collectives: 101 us -> none  [the longest x1 60 us: on_device(): lax.psum((gain_part, rel_part, loss_part), EVERYWHERE)]
    reduce_scatter x1, waiting for transfers between devices: 0.01 us -> 39.3 us  [on_device(): lax.psum_scatter(jnp.dot(grad_logits, table, preferred_element_type=jnp.f...]
    transpose x11 -> x0, local copies, waits for them, and re-layouts: 36 us -> none  [matrices_of(): matrix_list.append(section.transpose(0, 2, 1, 3).reshape(height, breadth))]
    dot_general x20 -> x0, local copies, waits for them, and re-layouts: 34.4 us -> none  [weight_grad(): jnp.einsum('btd,btf->df', inputs, grads, preferred_element_type=jnp.float32)]
    slice x11 -> x1, local copies, waits for them, and re-layouts: 34.3 us -> 0.01 us  [on_device(): dec_bias = tile_bias(dec_onehot, rel_bias[1])]
    ppermute x32 -> x38, waiting for transfers between devices: 124 us -> 91.6 us  [swap(): lax.ppermute(values, axis, [(place, place ^ 1) for place in range(size)])]
  transfers between devices with their start and end apart: 50 -> 62, of which waited for: 22 -> 25; matrix products, arithmetic and copies ran while one was open for 39% -> 32% of each run, Pallas kernels for 1% -> 7%
where the time goes in v2:
time: 1470 us; the launch traced here: 1460 us
  waiting for transfers between devices  394 us (27%)
  other arithmetic  311 us (21%)
  local copies, waits for them, and re-layouts  281 us (19%)
  Pallas kernels  176 us (12%)
  starting transfers between devices  110 us (7%)
  matrix products  104 us (7%)
  blocking collectives  48.6 us (3%)
  between operations  34.5 us (2%)
    all_gather x2, waiting for transfers between devices, gather_weights(): lax.all_gather(pairs, EVERYWHERE if split else 'fsdp', axis=0, tiled=True)  129 us
    unnamed x400, local copies, waits for them, and re-layouts  97 us
    reduce_scatter x1, waiting for transfers between devices, on_device(): lax.psum_scatter(table_rows(table, all_tokens, vocab_first), 'fsdp', scat...  94.8 us
    ppermute x38, waiting for transfers between devices, swap(): lax.ppermute(values, axis, [(place, place ^ 1) for place in range(size)])  91.6 us
    ppermute x38, starting transfers between devices, swap(): lax.ppermute(values, axis, [(place, place ^ 1) for place in range(size)])  66.9 us
    scatter-add x1, other arithmetic, table_grads(): return dense.at[slots].add(grads.astype(jnp.float32), mode='drop')  43.9 us
    pallas_call x3, Pallas kernels, attend_back(): pl.pallas_call(functools.partial(attend_back_kernel, biased=bias is not N...  43.2 us
    reduce_scatter x1, waiting for transfers between devices, on_device(): lax.psum_scatter(jnp.dot(grad_logits, table, preferred_element_type=jnp.f...  39.3 us
  transfers between devices with their start and end apart: 62, of which 25 were waited for; matrix products, arithmetic and copies ran while one was open for 32% of the time, Pallas kernels for 7%

profile of v2, /device:TPU:0, one launch (start us, length us, event | category | flops | bytes accessed | tf_op | source)
XLA Modules:
  0.0 1458.8 jit_solution(8090995036632655435)
XLA Ops:
  22.8 34.2 %all_gather.18 = s32[16,1,1408]{2,1,0:T(1,128)S(1)} all-gather(s32[1,1,1408]{2,1,0:T(1,128)S(1)} %reshape.1270), channel_id=1, replica_groups=mesh['dp'=2,'fsdp'=8,'seq'=2] {'fsdp','seq'}, dimensions={0}, use_global_device_ids=true | all-gather | bytes 95744 | tf_op jit(solution)/shard_map/all_gather | solution.py:784
  58.3 27.1 %gather_fusion = bf16[5120,768]{1,0:T(8,128)(2,1)} fusion(bf16[4016,768]{1,0:T(8,128)(2,1)} %convert_element_type.919, s32[5120]{0:T(1024)S(1)} %broadcast_clamp_fusion), kind=kCustom, calls=%fused_computation | custom fusion | bytes 15749120 | tf_op jit(solution)/shard_map/jit(_take)/gather | solution.py:498
  105.1 94.8 %reduce-scatter.3.cloned.1.call-done = bf16[1,640,768]{2,1,0:T(8,128)(2,1)} async-done(((bf16[8,640,768]{2,1,0:T(8,128)(2,1)}), bf16[1,640,768]{2,1,0:T(8,128)(2,1)}) %reduce-scatter.3.cloned.1.call-update) | async-done | bytes 983056 | tf_op jit(solution)/shard_map/reduce_scatter | solution.py:801
  205.8 45.2 %all-gather.7.cloned.1.call-done.pairs_ref = bf16[96,192,384]{2,1,0:T(8,128)(2,1)} async-done(((bf16[3,192,384]{2,1,0:T(8,128)(2,1)}), bf16[96,192,384]{2,1,0:T(8,128)(2,1)}) %all-gather.7.cloned.1.call-update) | async-done | bytes 14155792 | tf_op jit(solution)/shard_map/all_gather | solution.py:531
  263.7 18.1 %shard_map.411 = bf16[1,512,768]{2,1,0:T(8,128)(2,1)S(1)} custom-call(bf16[1,512,2304]{2,1,0:T(8,128)(2,1)S(1)} %fusion.29.q_ref.k_ref.v_ref, bf16[1,512,2304]{2,1,0:T(8,128)(2,1)S(1)} %fusion.29.q_ref.k_ref.v_ref, bf16[1,512,2304]{2,1,0:T(8,128)(2,1)S(1)} %fusion.29.q_ref.k_ref.v_ref, f32[12,5,128,128]{3,2,1,0:T(8,128)S(1)} %bitcast.502, ...), custom_call_target="tpu_custom_call" | custom-call | flops 1610612736 | bytes 3145728 | tf_op jit(solution)/shard_map/pallas_call | solution.py:229
  293.6 83.4 %all-gather.9.cloned.1.call-done.pairs_ref = bf16[128,192,384]{2,1,0:T(8,128)(2,1)} async-done(((bf16[4,192,384]{2,1,0:T(8,128)(2,1)}), bf16[128,192,384]{2,1,0:T(8,128)(2,1)}) %all-gather.9.cloned.1.call-update) | async-done | bytes 18874384 | tf_op jit(solution)/shard_map/all_gather | solution.py:531
  436.9 23.3 %all-gather.11.cloned.1.call-done = bf16[1024,768]{1,0:T(8,128)(2,1)} async-done(((bf16[128,768]{1,0:T(8,128)(2,1)}), bf16[1024,768]{1,0:T(8,128)(2,1)}) %all-gather.11.cloned.1.call-update) | async-done | bytes 1572880 | tf_op jit(solution)/shard_map/all_gather | solution.py:843
  460.3 9.2 fusion.194
  473.9 14.4 all-gather.1
  490.3 12.4 fusion.180
  503.6 39.3 %reduce-scatter.5.cloned.1.call-done = f32[128,768]{1,0:T(8,128)} async-done(((f32[1024,768]{1,0:T(8,128)}), f32[128,768]{1,0:T(8,128)}) %reduce-scatter.5.cloned.1.call-update) | async-done | bytes 393232 | tf_op jit(solution)/shard_map/reduce_scatter | solution.py:864
  556.6 8.4 shard_map.424
  582.2 29.3 %shard_map.425 = (bf16[1,512,768]{2,1,0:T(8,128)(2,1)S(1)}, bf16[1,512,768]{2,1,0:T(8,128)(2,1)S(1)}, bf16[1,512,768]{2,1,0:T(8,128)(2,1)S(1)}, f32[12,5,128,128]{3,2,1,0:T(8,128)S(1)}) custom-call(bf16[1,512,2304]{2,1,0:T(8,128)(2,1)S(1)} %fusion.29.q_ref.k_ref.v_ref, bf16[1,512,2304]{2,1,0:T(8,128)(2,1)S(1)} %fusion.29.q_ref.k_ref.v_ref, ...), custom_call_target="tpu_custom_call" | custom-call | flops 4026531840 | bytes 7864320 | tf_op jit(solution)/shard_map/pallas_call | solution.py:257
  670.0 8.4 dynamic-slice_bitcast_fusion
  710.9 12.6 convert_add_fusion.1
  723.4 11.9 fusion.189
  766.9 13.1 collective-permute-done.6
  832.1 14.3 shard_map.440
  938.3 16.3 %collective-permute-done.44 = f32[]{:T(128)} collective-permute-done((f32[]{:T(128)}, f32[]{:T(128)}, u32[]{:S(2)}, u32[]{:S(2)}) %collective-permute-start.44) | collective-permute-done | bytes 36 | tf_op jit(solution)/shard_map/ppermute | solution.py:542
  974.9 16.3 %abs_reduce_fusion = (f32[]{:T(128)}, f32[4016,768]{1,0:T(8,128)}) fusion(bf16[1024,768]{1,0:T(8,128)(2,1)S(1)} %copy-done.177, f32[1024,4016]{0,1:T(8,128)} %copy-done.83, f32[1024]{0:T(1024)S(1)} %copy-done.167, s32[1024]{0:T(1024)S(1)} %copy-done.152, f32[1024]{0:T(1024)S(1)} %copy-done.162), kind=kOutput, calls=%fused_computation.20 | convolution fusion | flops 6347464704 | bytes 30371844 | tf_op jit(solution)/shard_map/nv,nd->vd/dot_general | solution.py:863
  1038.9 43.9 %scatter_custom_fusion = f32[4016,768]{1,0:T(8,128)} fusion(f32[4016,768]{1,0:T(8,128)} %get-tuple-element.276, s32[5120]{0:T(1024)} %bitcast.553, bf16[5120,768]{1,0:T(8,128)(2,1)} %all-gather.13.cloned.1.call-done), kind=kCustom, calls=%fused_computation.10 | custom fusion | flops 7864320 | bytes 20201472 | tf_op jit(solution)/shard_map/scatter-add | solution.py:507
  1100.8 13.7 collective-permute-start.51
  1138.8 14.2 shard_map.439
  1165.5 21.5 %collective-permute-done.32 = f16[1008,384]{1,0:T(8,128)(2,1)} collective-permute-done((f16[1008,384]{1,0:T(8,128)(2,1)}, f16[1008,384]{1,0:T(8,128)(2,1)}, u32[]{:S(2)}, u32[]{:S(2)}) %collective-permute-start.32) | collective-permute-done | bytes 774176 | tf_op jit(solution)/shard_map/ppermute | solution.py:542
  1204.0 20.0 %shard_map.441 = (f32[32,192,192]{2,1,0:T(8,128)S(1)}, f32[32,192,192]{2,1,0:T(8,128)S(1)}, f32[32,192,192]{2,1,0:T(8,128)}, f32[32,192,192]{2,1,0:T(8,128)}) custom-call(f32[16,192,384]{2,1,0:T(8,128)S(1)} %multiply_multiply_fusion.4.g_ref, f32[32,192,192]{2,1,0:T(8,128)} %reshape.1298.lr_ref, f32[32,192,192]{2,1,0:T(8,128)} %reshape.1299.rr_ref), custom_call_target="tpu_custom_call" | custom-call | flops 5435817984 | bytes 33030144 | tf_op jit(solution)/shard_map/pallas_call | solution.py:443
  1235.5 8.4 collective-permute-start.33
  1265.9 10.7 multiply_add_fusion.5
  1328.3 8.7 multiply_add_fusion.1
  1343.7 11.0 broadcast_multiply_fusion
  1373.3 11.4 multiply_add_fusion.4
  1404.5 11.6 collective-permute-done.39
  1418.9 30.3 %multiply_subtract_fusion = (f32[4016,768]{1,0:T(8,128)}, f32[4016,768]{1,0:T(8,128)}, f32[4016,768]{1,0:T(8,128)}) fusion(f32[4016,768]{1,0:T(8,128)} %param.33, f32[]{:T(128)S(6)} %min.19, f32[]{:T(128)S(6)} %div.146, f32[]{:T(128)S(6)} %div.151, f16[1008,384]{1,0:T(8,128)(2,1)S(1)} %copy-done.117, f16[1008,384]{1,0:T(8,128)(2,1)S(1)} %copy-done.116, ...), kind=kLoop, calls=%fused_computation.17 | loop fusion | flops 104865792 | bytes 80216080 | tf_op jit(solution)/shard_map/sub | solution.py:712
  (773 shorter events, 686.9 us)
Async XLA Ops:
  8.0 191.9 %reduce-scatter.3.cloned.1.call-start = ((), (), s32[]{:S(2)}) async-start(), calls=%async_computation.2 | async-start | bytes 8847360 | tf_op jit(solution)/shard_map/reduce_scatter | solution.py:801
  92.9 158.1 %all-gather.7.cloned.1.call-start = ((), (), s32[]{:S(2)}) async-start(), calls=%async_computation.3 | async-start | bytes 14598144 | tf_op jit(solution)/shard_map/all_gather | solution.py:531
  93.5 283.5 %all-gather.9.cloned.1.call-start = ((), (), s32[]{:S(2)}) async-start(), calls=%async_computation.4 | async-start | bytes 19464192 | tf_op jit(solution)/shard_map/all_gather | solution.py:531
  94.1 366.2 %all-gather.11.cloned.1.call-start = ((), (), s32[]{:S(2)}) async-start(), calls=%async_computation.5 | async-start | bytes 1769472 | tf_op jit(solution)/shard_map/all_gather | solution.py:843
  436.9 106.0 %reduce-scatter.5.cloned.1.call-start = ((), (), s32[]{:S(2)}) async-start(), calls=%async_computation.6 | async-start | bytes 3538944 | tf_op jit(solution)/shard_map/reduce_scatter | solution.py:864
  502.8 526.9 %all-gather.13.cloned.1.call-start = ((), (), s32[]{:S(2)}) async-start(), calls=%async_computation.7 | async-start | bytes 8847360 | tf_op jit(solution)/shard_map/all_gather | solution.py:937
  640.6 70.3 %collective-permute-start.5 = (bf16[4,12,192,384]{3,2,1,0:T(8,128)(2,1)}, bf16[4,12,192,384]{3,2,1,0:T(8,128)(2,1)}, u32[]{:S(2)}, u32[]{:S(2)}) collective-permute-start(bf16[4,12,192,384]{3,2,1,0:T(8,128)(2,1)} %dynamic-slice_bitcast_fusion.1), channel_id=1, source_target_pairs={{0,2},{2,0},{4,6},{6,4},{8,10},{10,8},{12,14},{14,12},{1,3},{3,1},... | collective-permute-start | bytes 21233672 | tf_op jit(solution)/shard_map/ppermute | solution.py:542
  678.4 118.8 %collective-permute-start.16 = (bf16[4,16,192,384]{3,2,1,0:T(8,128)(2,1)}, bf16[4,16,192,384]{3,2,1,0:T(8,128)(2,1)}, u32[]{:S(2)}, u32[]{:S(2)}) collective-permute-start(bf16[4,16,192,384]{3,2,1,0:T(8,128)(2,1)} %dynamic-slice_bitcast_fusion), channel_id=1, source_target_pairs={{0,2},{2,0},{4,6},{6,4},{8,10},{10,8},{12,14},{14,12},{1,3},{3,1},... | collective-permute-start | bytes 28311560 | tf_op jit(solution)/shard_map/ppermute | solution.py:542
  738.9 41.2 %collective-permute-start.6 = (bf16[4,2,3,96,384]{4,3,2,0,1:T(8,128)(2,1)}, bf16[4,2,3,96,384]{4,3,2,0,1:T(8,128)(2,1)}, u32[]{:S(2)}, u32[]{:S(2)}) collective-permute-start(bf16[4,2,3,96,384]{4,3,2,0,1:T(8,128)(2,1)} %fusion.46), channel_id=1, source_target_pairs={{0,1},{1,0},{2,3},{3,2},{4,5},{5,4},{6,7},{7,6},{8,9},{9,8},{10,11... | collective-permute-start | bytes 5308424 | tf_op jit(solution)/shard_map/ppermute | solution.py:542
  751.8 41.8 %collective-permute-start.8 = (bf16[4,2,3,96,384]{4,3,2,0,1:T(8,128)(2,1)}, bf16[4,2,3,96,384]{4,3,2,0,1:T(8,128)(2,1)}, u32[]{:S(2)}, u32[]{:S(2)}) collective-permute-start(bf16[4,2,3,96,384]{4,3,2,0,1:T(8,128)(2,1)} %fusion.47), channel_id=1, source_target_pairs={{0,16},{16,0},{1,17},{17,1},{2,18},{18,2},{3,19},{19,3},{4,20},{20... | collective-permute-start | bytes 5308424 | tf_op jit(solution)/shard_map/ppermute | solution.py:542
  766.3 100.7 %collective-permute-start = (f32[49,128]{1,0:T(8,128)}, f32[49,128]{1,0:T(8,128)}, u32[]{:S(2)}, u32[]{:S(2)}) collective-permute-start(f32[49,128]{1,0:T(8,128)} %bitcast.77), channel_id=1, source_target_pairs={{0,1},{1,0},{2,3},{3,2},{4,5},{5,4},{6,7},{7,6},{8,9},{9,8},{10,11... | collective-permute-start | bytes 75272 | tf_op jit(solution)/shard_map/ppermute | solution.py:542
  784.2 39.4 %collective-permute-start.7 = (bf16[4,3,96,384]{3,2,1,0:T(8,128)(2,1)}, bf16[4,3,96,384]{3,2,1,0:T(8,128)(2,1)}, u32[]{:S(2)}, u32[]{:S(2)}) collective-permute-start(bf16[4,3,96,384]{3,2,1,0:T(8,128)(2,1)} %fusion.80), channel_id=1, source_target_pairs={{0,16},{16,0},{1,17},{17,1},{2,18},{18,2},{3,19},{19,3},{4,20},{20... | collective-permute-start | bytes 2654216 | tf_op jit(solution)/shard_map/ppermute | solution.py:542
  816.4 98.6 %collective-permute-start.17 = (bf16[4,2,4,96,384]{4,3,2,0,1:T(8,128)(2,1)}, bf16[4,2,4,96,384]{4,3,2,0,1:T(8,128)(2,1)}, u32[]{:S(2)}, u32[]{:S(2)}) collective-permute-start(bf16[4,2,4,96,384]{4,3,2,0,1:T(8,128)(2,1)} %fusion.37), channel_id=1, source_target_pairs={{0,1},{1,0},{2,3},{3,2},{4,5},{5,4},{6,7},{7,6},{8,9},{9,8},{10,11... | collective-permute-start | bytes 7077896 | tf_op jit(solution)/shard_map/ppermute | solution.py:542
  822.2 99.2 %collective-permute-start.19 = (bf16[4,2,4,96,384]{4,3,2,0,1:T(8,128)(2,1)}, bf16[4,2,4,96,384]{4,3,2,0,1:T(8,128)(2,1)}, u32[]{:S(2)}, u32[]{:S(2)}) collective-permute-start(bf16[4,2,4,96,384]{4,3,2,0,1:T(8,128)(2,1)} %fusion.38), channel_id=1, source_target_pairs={{0,16},{16,0},{1,17},{17,1},{2,18},{18,2},{3,19},{19,3},{4,20},{20... | collective-permute-start | bytes 7077896 | tf_op jit(solution)/shard_map/ppermute | solution.py:542
  828.7 39.7 %collective-permute-start.10 = (bf16[3,192,384]{2,1,0:T(8,128)(2,1)}, bf16[3,192,384]{2,1,0:T(8,128)(2,1)}, u32[]{:S(2)}, u32[]{:S(2)}) collective-permute-start(bf16[3,192,384]{2,1,0:T(8,128)(2,1)} %get-tuple-element.191), channel_id=1, source_target_pairs={{0,4},{2,6},{4,8},{6,10},{8,12},{10,14},{1,5},{3,7},{5,9},{7,11},{... | collective-permute-start | bytes 1327112 | tf_op jit(solution)/shard_map/ppermute | solution.py:550
  830.8 37.6 %collective-permute-start.13 = (bf16[3,192,384]{2,1,0:T(8,128)(2,1)}, bf16[3,192,384]{2,1,0:T(8,128)(2,1)}, u32[]{:S(2)}, u32[]{:S(2)}) collective-permute-start(bf16[3,192,384]{2,1,0:T(8,128)(2,1)} %get-tuple-element.192), channel_id=1, source_target_pairs={{4,0},{6,2},{8,4},{10,6},{12,8},{14,10},{5,1},{7,3},{9,5},{11,7},{... | collective-permute-start | bytes 1327112 | tf_op jit(solution)/shard_map/ppermute | solution.py:550
  870.6 35.5 %collective-permute-start.11 = (bf16[3,192,384]{2,1,0:T(8,128)(2,1)}, bf16[3,192,384]{2,1,0:T(8,128)(2,1)}, u32[]{:S(2)}, u32[]{:S(2)}) collective-permute-start(bf16[3,192,384]{2,1,0:T(8,128)(2,1)} %get-tuple-element.189), channel_id=1, source_target_pairs={{0,4},{2,6},{4,8},{6,10},{8,12},{10,14},{1,5},{3,7},{5,9},{7,11},{... | collective-permute-start | bytes 1327112 | tf_op jit(solution)/shard_map/ppermute | solution.py:550
  919.9 43.4 %collective-permute-start.18 = (bf16[4,4,96,384]{3,2,1,0:T(8,128)(2,1)}, bf16[4,4,96,384]{3,2,1,0:T(8,128)(2,1)}, u32[]{:S(2)}, u32[]{:S(2)}) collective-permute-start(bf16[4,4,96,384]{3,2,1,0:T(8,128)(2,1)} %fusion.65), channel_id=1, source_target_pairs={{0,16},{16,0},{1,17},{17,1},{2,18},{18,2},{3,19},{19,3},{4,20},{20... | collective-permute-start | bytes 3538952 | tf_op jit(solution)/shard_map/ppermute | solution.py:542
  927.5 38.0 %collective-permute-start.20 = (bf16[4,4,96,384]{3,2,1,0:T(8,128)(2,1)}, bf16[4,4,96,384]{3,2,1,0:T(8,128)(2,1)}, u32[]{:S(2)}, u32[]{:S(2)}) collective-permute-start(bf16[4,4,96,384]{3,2,1,0:T(8,128)(2,1)} %fusion.66), channel_id=1, source_target_pairs={{0,1},{1,0},{2,3},{3,2},{4,5},{5,4},{6,7},{7,6},{8,9},{9,8},{10,11... | collective-permute-start | bytes 3538952 | tf_op jit(solution)/shard_map/ppermute | solution.py:542
  1023.8 69.7 %collective-permute-start.26 = (bf16[4,192,384]{2,1,0:T(8,128)(2,1)}, bf16[4,192,384]{2,1,0:T(8,128)(2,1)S(1)}, u32[]{:S(2)}, u32[]{:S(2)}) collective-permute-start(bf16[4,192,384]{2,1,0:T(8,128)(2,1)} %get-tuple-element.178), channel_id=1, source_target_pairs={{4,0},{6,2},{8,4},{10,6},{12,8},{14,10},{5,1},{7,3},{9,5},{11,7},{... | collective-permute-start | bytes 1769480 | tf_op jit(solution)/shard_map/ppermute | solution.py:550
  1025.1 68.4 %collective-permute-start.23 = (bf16[4,192,384]{2,1,0:T(8,128)(2,1)S(1)}, bf16[4,192,384]{2,1,0:T(8,128)(2,1)S(1)}, u32[]{:S(2)}, u32[]{:S(2)}) collective-permute-start(bf16[4,192,384]{2,1,0:T(8,128)(2,1)S(1)} %get-tuple-element.177), channel_id=1, source_target_pairs={{0,4},{2,6},{4,8},{6,10},{8,12},{10,14},{1,5},{3,7},{5,9},{7,11},{... | collective-permute-start | bytes 1769480 | tf_op jit(solution)/shard_map/ppermute | solution.py:550
  1035.9 46.9 %collective-permute-start.27 = (f32[]{:T(128)}, f32[]{:T(128)}, u32[]{:S(2)}, u32[]{:S(2)}) collective-permute-start(f32[]{:T(128)} %add.1100), channel_id=1, source_target_pairs={{0,1},{1,0},{2,3},{3,2},{4,5},{5,4},{6,7},{7,6},{8,9},{9,8},{10,11... | collective-permute-start | bytes 20 | tf_op jit(solution)/shard_map/ppermute | solution.py:542
  1091.2 41.2 %collective-permute-start.31 = (f16[1008,768]{1,0:T(8,128)(2,1)}, f16[1008,768]{1,0:T(8,128)(2,1)}, u32[]{:S(2)}, u32[]{:S(2)}) collective-permute-start(f16[1008,768]{1,0:T(8,128)(2,1)} %multiply_convert_fusion.2), channel_id=1, source_target_pairs={{0,16},{16,0},{1,17},{17,1},{2,18},{18,2},{3,19},{19,3},{4,20},{20... | collective-permute-start | bytes 4644872 | tf_op jit(solution)/shard_map/ppermute | solution.py:542
  1126.9 36.3 %collective-permute-start.53 = (f16[2,4,96,384]{3,2,1,0:T(8,128)(2,1)}, f16[2,4,96,384]{3,2,1,0:T(8,128)(2,1)}, u32[]{:S(2)}, u32[]{:S(2)}) collective-permute-start(f16[2,4,96,384]{3,2,1,0:T(8,128)(2,1)} %pad_maximum_fusion.2), channel_id=1, source_target_pairs={{0,1},{1,0},{2,3},{3,2},{4,5},{5,4},{6,7},{7,6},{8,9},{9,8},{10,11... | collective-permute-start | bytes 1769480 | tf_op jit(solution)/shard_map/ppermute | solution.py:542
  1131.2 33.2 %collective-permute-start.55 = (f16[2,4,96,384]{3,2,1,0:T(8,128)(2,1)}, f16[2,4,96,384]{3,2,1,0:T(8,128)(2,1)}, u32[]{:S(2)}, u32[]{:S(2)}) collective-permute-start(f16[2,4,96,384]{3,2,1,0:T(8,128)(2,1)} %pad_maximum_fusion.3), channel_id=1, source_target_pairs={{0,16},{16,0},{1,17},{17,1},{2,18},{18,2},{3,19},{19,3},{4,20},{20... | collective-permute-start | bytes 1769480 | tf_op jit(solution)/shard_map/ppermute | solution.py:542
  1135.5 56.9 %collective-permute-start.29 = (f16[1008,768]{1,0:T(8,128)(2,1)}, f16[1008,768]{1,0:T(8,128)(2,1)}, u32[]{:S(2)}, u32[]{:S(2)}) collective-permute-start(f16[1008,768]{1,0:T(8,128)(2,1)} %get-tuple-element.176), channel_id=1, source_target_pairs={{0,1},{1,0},{2,3},{3,2},{4,5},{5,4},{6,7},{7,6},{8,9},{9,8},{10,11... | collective-permute-start | bytes 4644872 | tf_op jit(solution)/shard_map/ppermute | solution.py:542
  1138.8 48.2 %collective-permute-start.32 = (f16[1008,384]{1,0:T(8,128)(2,1)}, f16[1008,384]{1,0:T(8,128)(2,1)}, u32[]{:S(2)}, u32[]{:S(2)}) collective-permute-start(f16[1008,384]{1,0:T(8,128)(2,1)} %dynamic-slice_convert_fusion.4), channel_id=1, source_target_pairs={{0,1},{1,0},{2,3},{3,2},{4,5},{5,4},{6,7},{7,6},{8,9},{9,8},{10,11... | collective-permute-start | bytes 2322440 | tf_op jit(solution)/shard_map/ppermute | solution.py:542
  1195.2 34.1 %collective-permute-start.30 = (f16[1008,384]{1,0:T(8,128)(2,1)S(1)}, f16[1008,384]{1,0:T(8,128)(2,1)S(1)}, u32[]{:S(2)}, u32[]{:S(2)}) collective-permute-start(f16[1008,384]{1,0:T(8,128)(2,1)S(1)} %dynamic-slice_convert_fusion.5), channel_id=1, source_target_pairs={{0,16},{16,0},{1,17},{17,1},{2,18},{18,2},{3,19},{19,3},{4,20},{20... | collective-permute-start | bytes 2322440 | tf_op jit(solution)/shard_map/ppermute | solution.py:542
  1196.9 47.0 %collective-permute-start.43 = (f16[1008,384]{1,0:T(8,128)(2,1)}, f16[1008,384]{1,0:T(8,128)(2,1)S(1)}, u32[]{:S(2)}, u32[]{:S(2)}) collective-permute-start(f16[1008,384]{1,0:T(8,128)(2,1)} %get-tuple-element.185), channel_id=1, source_target_pairs={{0,16},{16,0},{1,17},{17,1},{2,18},{18,2},{3,19},{19,3},{4,20},{20... | collective-permute-start | bytes 2322440 | tf_op jit(solution)/shard_map/ppermute | solution.py:542
  1202.1 41.8 %collective-permute-start.42 = (f16[1008,384]{1,0:T(8,128)(2,1)S(1)}, f16[1008,384]{1,0:T(8,128)(2,1)S(1)}, u32[]{:S(2)}, u32[]{:S(2)}) collective-permute-start(f16[1008,384]{1,0:T(8,128)(2,1)S(1)} %collective-permute-done.41), channel_id=1, source_target_pairs={{0,16},{16,0},{1,17},{17,1},{2,18},{18,2},{3,19},{19,3},{4,20},{20... | collective-permute-start | bytes 2322440 | tf_op jit(solution)/shard_map/ppermute | solution.py:542
  1231.4 167.5 %collective-permute-start.38 = (f16[1008,384]{1,0:T(8,128)(2,1)}, f16[1008,384]{1,0:T(8,128)(2,1)}, u32[]{:S(2)}, u32[]{:S(2)}) collective-permute-start(f16[1008,384]{1,0:T(8,128)(2,1)} %get-tuple-element.183), channel_id=1, source_target_pairs={{0,16},{16,0},{1,17},{17,1},{2,18},{18,2},{3,19},{19,3},{4,20},{20... | collective-permute-start | bytes 2322440 | tf_op jit(solution)/shard_map/ppermute | solution.py:542
  1232.5 172.0 %collective-permute-start.40 = (f16[1008,384]{1,0:T(8,128)(2,1)}, f16[1008,384]{1,0:T(8,128)(2,1)}, u32[]{:S(2)}, u32[]{:S(2)}) collective-permute-start(f16[1008,384]{1,0:T(8,128)(2,1)} %get-tuple-element.183), channel_id=1, source_target_pairs={{0,1},{1,0},{2,3},{3,2},{4,5},{5,4},{6,7},{7,6},{8,9},{9,8},{10,11... | collective-permute-start | bytes 2322440 | tf_op jit(solution)/shard_map/ppermute | solution.py:542
  (221 other events, 3612.1 us)
Sparse Core Ops, SparseCore 0:
  93.0 106.8 reduce-scatter.2
  437.0 23.2 all-gather.10
  502.9 39.9 reduce-scatter.4
  754.9 74.8 all-gather.12
Sparse Core Ops, SparseCore 1:
  96.8 154.1 all-gather.6
  254.3 122.6 all-gather.8

commit v3 on v2

--- a/solution.py
+++ b/solution.py
@@ -519,18 +519,6 @@
     return lax.axis_size("dp") * lax.axis_size("seq")
 
 
-def own_weights(master):
-    share = master.shape[0] // replica_count()
-    if master.shape[0] % (2 * replica_count()) == 0:
-        master = lax.dynamic_slice_in_dim(master, replica_rank() * share, share, 0)
-    return as_pairs(as_blocks(master.astype(jnp.bfloat16)))
-
-
-def gather_weights(pairs, amount):
-    split = amount % (2 * replica_count()) == 0
-    return lax.all_gather(pairs, EVERYWHERE if split else "fsdp", axis=0, tiled=True)
-
-
 def paired_mesh():
     return (
         lax.axis_size("dp") == 2 and lax.axis_size("seq") == 2 and lax.axis_size("fsdp") % 2 == 0
@@ -579,6 +567,202 @@
         return choose(first, there, here)
 
     return [[at(0, 0), at(0, 1)], [at(1, 0), at(1, 1)]]
+
+
+def own_weights(master):
+    share = master.shape[0] // replica_count()
+    if master.shape[0] % (2 * replica_count()) == 0:
+        master = lax.dynamic_slice_in_dim(master, replica_rank() * share, share, 0)
+    return as_pairs(as_blocks(master.astype(jnp.bfloat16)))
+
+
+def along_chips(own):
+    n_chips = lax.axis_size("fsdp") // 2
+    rising = falling = own
+    pieces = [own]
+    for _ in range(n_chips - 1):
+        rising, falling = (shift(rising, 1), shift(falling, -1))
+        pieces = [rising] + pieces + [falling]
+    first = n_chips - 1 - lax.axis_index("fsdp") // 2
+    return lax.dynamic_slice_in_dim(jnp.stack(pieces), first, n_chips, 0)
+
+
+def gather_weights(pairs, amount, shapes):
+    if not paired_mesh():
+        split = amount % (2 * replica_count()) == 0
+        everything = lax.all_gather(pairs, EVERYWHERE if split else "fsdp", axis=0, tiled=True)
+        return matrices_of(everything, shapes)
+    line = along_chips(pairs)
+    mid = BLOCK // 2
+    upper, lower = (line[:, :, :mid], line[:, :, mid:])
+    upper_side, lower_half = (swap(upper, "dp"), swap(lower, "seq"))
+    upper_half, lower_side = (swap(upper, "seq"), swap(lower, "dp"))
+    pieces = [
+        upper,
+        lower,
+        upper_half,
+        lower_half,
+        upper_side,
+        lower_side,
+        swap(upper_side, "seq"),
+        swap(lower_half, "dp"),
+    ]
+    pieces += [swap(piece, "fsdp") for piece in pieces]
+    return assembled(pieces, shapes)
+
+
+def assemble_kernel(place_ref, *refs, shapes):
+    pieces, outs = (refs[:16], refs[16 : 16 + len(shapes)])
+    buffer, in_sems, out_sems = refs[16 + len(shapes) :]
+    core, side, half = (place_ref[0], place_ref[1], place_ref[2])
+    n_chips, quarter, mid, _ = pieces[0].shape
+    copies = []
+    for index, piece in enumerate(pieces):
+        owner = ((side ^ (index // 4 % 2)) * 2 + (half ^ (index // 2 % 2))) * quarter
+        for chip in range(n_chips):
+            first = (2 * chip + (core ^ (index // 8))) * (4 * quarter) + owner
+            copies.append(
+                pltpu.make_async_copy(
+                    piece.at[chip],
+                    buffer.at[pl.ds(first, quarter), pl.ds((index % 2) * mid, mid), :],
+                    in_sems.at[index, chip],
+                )
+            )
+    for copy in copies:
+        copy.start()
+    for copy in copies:
+        copy.wait()
+    copies = []
+    for out_ref, (height, breadth) in zip(outs, shapes):
+        for row in range(height // BLOCK):
+            for column in range(breadth // PAIR):
+                copies.append(
+                    pltpu.make_async_copy(
+                        buffer.at[len(copies)],
+                        out_ref.at[pl.ds(row * BLOCK, BLOCK), pl.ds(column * PAIR, PAIR)],
+                        out_sems.at[len(copies)],
+                    )
+                )
+    for copy in copies:
+        copy.start()
+    for copy in copies:
+        copy.wait()
+
+
+def own_place():
+    return jnp.stack(
+        [lax.axis_index("fsdp") % 2, lax.axis_index("dp"), lax.axis_index("seq")]
+    ).astype(jnp.int32)
+
+
+def assembled(pieces, shapes):
+    n_chips, quarter, mid, _ = pieces[0].shape
+    total = 8 * n_chips * quarter
+    return pl.pallas_call(
+        functools.partial(assemble_kernel, shapes=shapes),
+        out_shape=[jax.ShapeDtypeStruct(shape, jnp.bfloat16) for shape in shapes],
+        in_specs=[pl.BlockSpec(memory_space=pltpu.SMEM)]
+        + [pl.BlockSpec(memory_space=pl.ANY)] * len(pieces),
+        out_specs=[pl.BlockSpec(memory_space=pl.ANY)] * len(shapes),
+        scratch_shapes=[
+            pltpu.VMEM((total, BLOCK, PAIR), jnp.bfloat16),
+            pltpu.SemaphoreType.DMA((len(pieces), n_chips)),
+            pltpu.SemaphoreType.DMA((total,)),
+        ],
+        cost_estimate=pl.CostEstimate(
+            flops=0, bytes_accessed=4 * total * BLOCK * PAIR, transcendentals=0
+        ),
+        compiler_params=pltpu.CompilerParams(vmem_limit_bytes=30 << 20),
+    )(own_place(), *pieces)
+
+
+def fold_kernel(place_ref, own_ref, got_ref, keep_up, send_up, keep_low, send_low):
+    total = wide(own_ref[0]) + wide(got_ref[0])
+    mid = BLOCK // 2
+    upper, lower = (total[:, :mid], total[:, mid:])
+    other_side, other_half = (pl.program_id(1), pl.program_id(2))
+
+    @pl.when(other_half == 0)
+    def _():
+        keep_up[0, 0] = upper
+
+    @pl.when(other_half == 1)
+    def _():
+        send_up[0, 0] = narrow(upper)
+
+    @pl.when(other_side == 0)
+    def _():
+        keep_low[0, 0] = lower
+
+    @pl.when(other_side == 1)
+    def _():
+        send_low[0, 0] = narrow(lower)
+
+
+def fold_cores(pairs, got, n_chips, quarter):
+    mid = BLOCK // 2
+
+    def quarter_of(place, other_side, other_half):
+        return (place[1] ^ other_side) * 2 + (place[2] ^ other_half)
+
+    whole = (1, quarter, BLOCK, PAIR)
+    part = (1, 1, quarter, mid, PAIR)
+    halves = (n_chips, 2, quarter, mid, PAIR)
+
+    def up_at(chip, other_side, other_half, place):
+        return (chip, place[1] ^ other_side, 0, 0, 0)
+
+    def keep_low_at(chip, other_side, other_half, place):
+        return (chip, jnp.where(other_side == 0, place[2] ^ other_half, place[2] ^ 1), 0, 0, 0)
+
+    def send_low_at(chip, other_side, other_half, place):
+        return (chip, jnp.where(other_side == 1, place[2] ^ other_half, place[2]), 0, 0, 0)
+
+    return pl.pallas_call(
+        fold_kernel,
+        out_shape=[
+            jax.ShapeDtypeStruct(halves, kind)
+            for kind in (jnp.float32, jnp.bfloat16, jnp.float32, jnp.bfloat16)
+        ],
+        grid_spec=pltpu.PrefetchScalarGridSpec(
+            num_scalar_prefetch=1,
+            grid=(n_chips, 2, 2),
+            in_specs=[
+                pl.BlockSpec(
+                    whole,
+                    lambda chip, side, half, place: (
+                        (2 * chip + place[0]) * 4 + quarter_of(place, side, half),
+                        0,
+                        0,
+                        0,
+                    ),
+                ),
+                pl.BlockSpec(
+                    whole,
+                    lambda chip, side, half, place: (
+                        chip * 4 + quarter_of(place, side, half),
+                        0,
+                        0,
+                        0,
+                    ),
+                ),
+            ],
+            out_specs=[
+                pl.BlockSpec(part, up_at),
+                pl.BlockSpec(part, up_at),
+                pl.BlockSpec(part, keep_low_at),
+                pl.BlockSpec(part, send_low_at),
+            ],
+        ),
+        cost_estimate=pl.CostEstimate(
+            flops=pairs.size // 2, bytes_accessed=5 * pairs.size, transcendentals=0
+        ),
+        compiler_params=pltpu.CompilerParams(vmem_limit_bytes=32 << 20),
+    )(
+        own_place(),
+        pairs.reshape(-1, quarter, BLOCK, PAIR),
+        got.reshape(-1, quarter, BLOCK, PAIR),
+    )
 
 
 def sum_small(values):
@@ -606,13 +790,11 @@
     side, half = (lax.axis_index("dp"), lax.axis_index("seq"))
     amount = pairs.shape[0] // (2 * n_chips)
     quarter = amount // 4
-    mid = BLOCK // 2
-    pairs = pairs.reshape(n_chips, 2, amount, BLOCK, PAIR)
-    chip_sum = wide(pick(pairs, core, 1)) + wide(swap(pick(pairs, 1 - core, 1), "fsdp"))
-    chip_sum = chip_sum.reshape(n_chips, 2, 2, quarter, BLOCK, PAIR)
-    upper, lower = (chip_sum[..., :mid, :], chip_sum[..., mid:, :])
-    upper = pick(upper, half, 2) + wide(swap(narrow(pick(upper, 1 - half, 2)), "seq"))
-    lower = pick(lower, side, 1) + wide(swap(narrow(pick(lower, 1 - side, 1)), "dp"))
+    split = pairs.reshape(n_chips, 2, amount, BLOCK, PAIR)
+    got = swap(pick(split, 1 - core, 1), "fsdp")
+    upper, upper_sent, lower, lower_sent = fold_cores(pairs, got, n_chips, quarter)
+    upper = upper + wide(swap(upper_sent, "seq"))
+    lower = lower + wide(swap(lower_sent, "dp"))
     upper = pick(upper, side, 1) + wide(swap(narrow(pick(upper, 1 - side, 1)), "dp"))
     lower = pick(lower, half, 1) + wide(swap(narrow(pick(lower, 1 - half, 1)), "seq"))
     line_sum = jnp.concatenate([upper, lower], axis=2)
@@ -766,33 +948,33 @@
     enc_in = jnp.where(span_mask == 1, VOCAB - sentinel_offset, enc_ids)
     dec_in = jnp.concatenate([jnp.zeros((rows, 1), jnp.int32), targets[:, :-1]], axis=1)
 
-    def by_rows(positions):
-        return positions.reshape(n_seq, rows, half_len)
-
+    halves = jnp.stack([enc_in, segments]).reshape(2, n_seq, rows, half_len)
+    if n_seq == 2:
+        kept = pick(halves, seq_rank, 1)
+        got = swap(pick(halves, 1 - seq_rank, 1), "seq")
+        parts = (choose(seq_rank, got, kept), choose(seq_rank, kept, got))
+        row_words = jnp.stack(parts, axis=2)
+    else:
+        row_words = lax.all_to_all(halves, "seq", 1, 1, tiled=True).transpose(0, 2, 1, 3)
+    row_words = row_words.reshape(2, rows, enc_len)
+    row_segments = row_words[1]
     message = jnp.concatenate(
-        [by_rows(enc_in), by_rows(segments)], axis=2
-    ).reshape(n_seq, -1)
-    own = jnp.concatenate(
-        [dec_in.reshape(-1), targets.reshape(-1), loss_weights.reshape(-1)]
-    )
-    message = jnp.concatenate([message.reshape(-1), own]).reshape(1, 1, -1)
+        [
+            row_words[0].reshape(-1),
+            dec_in.reshape(-1),
+            targets.reshape(-1),
+            loss_weights.reshape(-1),
+        ]
+    ).reshape(1, -1)
     enc_pairs, dec_pairs, message = lax.optimization_barrier(
         (own_weights(enc_w), own_weights(dec_w), message)
     )
-    enc_pairs = gather_weights(enc_pairs, enc_w.shape[0])
-    dec_pairs = gather_weights(dec_pairs, dec_w.shape[0])
-    gathered = lax.all_gather(message, ("fsdp", "seq"), axis=0, tiled=True)
-    gathered = gathered.reshape(n_fsdp, n_seq, -1)
-    row_words = rows * 2 * half_len
-    enc_words = lax.dynamic_slice_in_dim(gathered, seq_rank * row_words, row_words, 2)
-    enc_words = enc_words.reshape(n_fsdp, n_seq, rows, 2, half_len).transpose(3, 0, 2, 1, 4)
-    enc_words = enc_words.reshape(2, n_fsdp, rows * enc_len)
-    all_enc = enc_words[0]
-    row_segments = lax.dynamic_index_in_dim(enc_words[1], fsdp_rank, 0, False)
-    row_segments = row_segments.reshape(rows, enc_len)
-    dec_words = lax.dynamic_index_in_dim(gathered, seq_rank, 1, False)[:, n_seq * row_words :]
-    dec_words = dec_words.reshape(n_fsdp, 3, rows * dec_len)
-    all_dec, all_targets, all_weights = (dec_words[:, 0], dec_words[:, 1], dec_words[:, 2])
+    enc_mats = gather_weights(enc_pairs, enc_w.shape[0], layer_shapes(False))
+    dec_mats = gather_weights(dec_pairs, dec_w.shape[0], layer_shapes(True))
+    gathered = lax.all_gather(message, "fsdp", axis=0, tiled=True)
+    all_enc = gathered[:, : rows * enc_len]
+    rest = gathered[:, rows * enc_len :].reshape(n_fsdp, 3, rows * dec_len)
+    all_dec, all_targets, all_weights = (rest[:, 0], rest[:, 1], rest[:, 2])
     all_tokens = jnp.concatenate([all_enc, all_dec], axis=1)
 
     table = embedding.astype(jnp.bfloat16)
@@ -801,11 +983,14 @@
     looked_up = lax.psum_scatter(
         table_rows(table, all_tokens, vocab_first), "fsdp", scatter_dimension=0, tiled=True
     ).reshape(-1, D)
+    enc_ready = shampoo_ahead(enc_m, enc_lroot, enc_rroot)
+    dec_ready = shampoo_ahead(dec_m, dec_lroot, dec_rroot)
+    looked_up, enc_ready, dec_ready = lax.optimization_barrier((looked_up, enc_ready, dec_ready))
+    enc_ahead, enc_lr, enc_rr = enc_ready
+    dec_ahead, dec_lr, dec_rr = dec_ready
     hidden0 = looked_up[: rows * enc_len].reshape(rows, enc_len, D).astype(jnp.float32)
     state0 = looked_up[rows * enc_len :].reshape(rows, dec_len, D).astype(jnp.float32)
 
-    enc_mats = matrices_of(enc_pairs, layer_shapes(False))
-    dec_mats = matrices_of(dec_pairs, layer_shapes(True))
     enc_onehot = tile_onehot(enc_len // TILE, False)
     dec_onehot = tile_onehot(dec_len // TILE, True)
     enc_bias = tile_bias(enc_onehot, rel_bias[0])
@@ -980,10 +1165,9 @@
             "fsdp",
         )
 
-    enc_ahead, enc_lr, enc_rr = shampoo_ahead(enc_m, enc_lroot, enc_rroot)
-    dec_ahead, dec_lr, dec_rr = shampoo_ahead(dec_m, dec_lroot, dec_rroot)
     dec_products = shampoo_products(dec_grad, dec_lr, dec_rr)
     enc_products = shampoo_products(enc_grad, enc_lr, enc_rr)
+    dec_products, enc_products = lax.optimization_barrier((dec_products, enc_products))
     grad_norm = jnp.sqrt(
         squares_all + jnp.sum(gain_grad * gain_grad) + jnp.sum(rel_grad * rel_grad)
     )

time: 1470 us -> 1480 us (level)
  other arithmetic: 311 us -> 245 us
  starting transfers between devices: 110 us -> 159 us
  Pallas kernels: 176 us -> 216 us
  blocking collectives: 48.6 us -> 28.6 us
    all_gather x2 -> x0, waiting for transfers between devices: 129 us -> none  [gather_weights(): lax.all_gather(pairs, EVERYWHERE if split else 'fsdp', axis=0, tiled=True)]
    ppermute x38 -> x67, waiting for transfers between devices: 91.6 us -> 220 us  [swap(): lax.ppermute(values, axis, [(place, place ^ 1) for place in range(size)])]
    ppermute x12 -> x24, waiting for transfers between devices: 8.49 us -> 115 us  [shift(): return lax.ppermute(values, 'fsdp', moves)]
    reduce_scatter x1, waiting for transfers between devices: 94.8 us -> 0.01 us  [on_device(): lax.psum_scatter(table_rows(table, all_tokens, vocab_first), 'fsdp', scat...]
    reshape x5 -> x12, local copies, waits for them, and re-layouts: 0.11 us -> 63.6 us  [the longest x10 63.6 us: as_rows(): return blocks.reshape(blocks.shape[0], BLOCK * BLOCK)]
    add x10 -> x4, other arithmetic: 63.7 us -> 10.9 us  [the longest x2 5.63 us: reduce_blocks(): upper = upper + wide(swap(upper_sent, 'seq'))]
    pallas_call x11 -> x4, Pallas kernels: 10.6 us -> 50.3 us  [the longest x2 26.3 us: fold_cores(): pl.pallas_call(fold_kernel, out_shape=[jax.ShapeDtypeStruct(halves, kind)...]
    mul x6 -> x0, local copies, waits for them, and re-layouts: 36.2 us -> none  [the longest x2 12.8 us: shampoo_update(): (1 - beta_first) * factor * gradient]
  transfers between devices with their start and end apart: 62 -> 101, of which waited for: 25 -> 38; matrix products, arithmetic and copies ran while one was open for 32% -> 26% of each run, Pallas kernels for 7% -> 9%
where the time goes in v3:
time: 1480 us; the launch traced here: 1470 us
  waiting for transfers between devices  400 us (27%)
  local copies, waits for them, and re-layouts  280 us (19%)
  other arithmetic  245 us (17%)
  Pallas kernels  216 us (15%)
  starting transfers between devices  159 us (11%)
  matrix products  105 us (7%)
  between operations  34.2 us (2%)
  blocking collectives  28.6 us (2%)
    ppermute x67, waiting for transfers between devices, swap(): lax.ppermute(values, axis, [(place, place ^ 1) for place in range(size)])  220 us
    ppermute x24, waiting for transfers between devices, shift(): return lax.ppermute(values, 'fsdp', moves)  115 us
    unnamed x457, local copies, waits for them, and re-layouts  103 us
    ppermute x67, starting transfers between devices, swap(): lax.ppermute(values, axis, [(place, place ^ 1) for place in range(size)])  85.3 us
    reshape x10, local copies, waits for them, and re-layouts, as_rows(): return blocks.reshape(blocks.shape[0], BLOCK * BLOCK)  63.6 us
    ppermute x24, starting transfers between devices, shift(): return lax.ppermute(values, 'fsdp', moves)  61.8 us
    scatter-add x1, other arithmetic, table_grads(): return dense.at[slots].add(grads.astype(jnp.float32), mode='drop')  43.9 us
    pallas_call x3, Pallas kernels, attend_back(): pl.pallas_call(functools.partial(attend_back_kernel, biased=bias is not N...  43.6 us
  transfers between devices with their start and end apart: 101, of which 38 were waited for; matrix products, arithmetic and copies ran while one was open for 26% of the time, Pallas kernels for 9%

profile of v3, /device:TPU:0, one launch (start us, length us, event | category | flops | bytes accessed | tf_op | source)
XLA Modules:
  0.0 1467.1 jit_solution(9477180804012814120)
XLA Ops:
  24.7 14.2 all-gather.1
  39.6 27.1 %gather_fusion = bf16[5120,768]{1,0:T(8,128)(2,1)} fusion(bf16[4016,768]{1,0:T(8,128)(2,1)} %convert_element_type.861, s32[5120]{0:T(1024)S(1)} %broadcast_clamp_fusion), kind=kCustom, calls=%fused_computation | custom fusion | bytes 15749120 | tf_op jit(solution)/shard_map/jit(_take)/gather | solution.py:498
  82.3 13.9 collective-permute-done.1
  100.6 20.9 %collective-permute-done.21 = bf16[4,192,384]{2,1,0:T(8,128)(2,1)S(1)} collective-permute-done((bf16[4,192,384]{2,1,0:T(8,128)(2,1)S(1)}, bf16[4,192,384]{2,1,0:T(8,128)(2,1)S(1)}, u32[]{:S(2)}, u32[]{:S(2)}) %collective-permute-start.21) | collective-permute-done | bytes 589856 | tf_op jit(solution)/shard_map/ppermute | solution.py:538
  145.6 30.1 %collective-permute-done.5 = bf16[3,192,384]{2,1,0:T(8,128)(2,1)} collective-permute-done((bf16[3,192,384]{2,1,0:T(8,128)(2,1)S(1)}, bf16[3,192,384]{2,1,0:T(8,128)(2,1)}, u32[]{:S(2)}, u32[]{:S(2)}) %collective-permute-start.5) | collective-permute-done | bytes 442400 | tf_op jit(solution)/shard_map/ppermute | solution.py:538
  187.2 13.4 collective-permute-done.6
  225.4 17.1 %collective-permute-done.8.refs_3_ = bf16[4,3,96,384]{3,2,1,0:T(8,128)(2,1)S(1)} collective-permute-done((bf16[4,3,96,384]{3,2,1,0:T(8,128)(2,1)S(1)}, bf16[4,3,96,384]{3,2,1,0:T(8,128)(2,1)S(1)}, u32[]{:S(2)}, u32[]{:S(2)}) %collective-permute-start.8) | collective-permute-done | bytes 884768 | tf_op jit(solution)/shard_map/ppermute | solution.py:530
  248.1 19.8 %collective-permute-done.27.refs_2_ = bf16[4,4,96,384]{3,2,1,0:T(8,128)(2,1)} collective-permute-done((bf16[4,4,96,384]{3,2,1,0:T(8,128)(2,1)S(1)}, bf16[4,4,96,384]{3,2,1,0:T(8,128)(2,1)}, u32[]{:S(2)}, u32[]{:S(2)}) %collective-permute-start.27) | collective-permute-done | bytes 1179680 | tf_op jit(solution)/shard_map/ppermute | solution.py:530
  267.9 22.4 %collective-permute-done.28.refs_3_ = bf16[4,4,96,384]{3,2,1,0:T(8,128)(2,1)} collective-permute-done((bf16[4,4,96,384]{3,2,1,0:T(8,128)(2,1)S(1)}, bf16[4,4,96,384]{3,2,1,0:T(8,128)(2,1)}, u32[]{:S(2)}, u32[]{:S(2)}) %collective-permute-start.28) | collective-permute-done | bytes 1179680 | tf_op jit(solution)/shard_map/ppermute | solution.py:530
  390.4 14.3 shard_map.411
  442.8 12.1 shard_map.412
  460.0 11.9 shard_map.414
  484.8 18.2 %shard_map.413 = bf16[1,512,768]{2,1,0:T(8,128)(2,1)S(1)} custom-call(bf16[1,512,2304]{2,1,0:T(8,128)(2,1)S(1)} %fusion.27.q_ref.k_ref.v_ref, bf16[1,512,2304]{2,1,0:T(8,128)(2,1)S(1)} %fusion.27.q_ref.k_ref.v_ref, bf16[1,512,2304]{2,1,0:T(8,128)(2,1)S(1)} %fusion.27.q_ref.k_ref.v_ref, f32[12,5,128,128]{3,2,1,0:T(8,128)S(1)} %bitcast.435, ...), custom_call_target="tpu_custom_call" | custom-call | flops 1610612736 | bytes 3145728 | tf_op jit(solution)/shard_map/pallas_call | solution.py:229
  535.7 22.1 %all-gather.6.cloned.1.call-done = bf16[1024,768]{1,0:T(8,128)(2,1)} async-done(((bf16[128,768]{1,0:T(8,128)(2,1)}), bf16[1024,768]{1,0:T(8,128)(2,1)}) %all-gather.6.cloned.1.call-update) | async-done | bytes 1572880 | tf_op jit(solution)/shard_map/all_gather | solution.py:1028
  571.4 14.4 all-gather.2
  587.9 12.5 fusion.170
  601.2 39.3 %reduce-scatter.5.cloned.1.call-done = f32[128,768]{1,0:T(8,128)} async-done(((f32[1024,768]{1,0:T(8,128)}), f32[128,768]{1,0:T(8,128)}) %reduce-scatter.5.cloned.1.call-update) | async-done | bytes 393232 | tf_op jit(solution)/shard_map/reduce_scatter | solution.py:1049
  680.0 29.7 %shard_map.418 = (bf16[1,512,768]{2,1,0:T(8,128)(2,1)S(1)}, bf16[1,512,768]{2,1,0:T(8,128)(2,1)S(1)}, bf16[1,512,768]{2,1,0:T(8,128)(2,1)S(1)}, f32[12,5,128,128]{3,2,1,0:T(8,128)S(1)}) custom-call(bf16[1,512,2304]{2,1,0:T(8,128)(2,1)S(1)} %fusion.27.q_ref.k_ref.v_ref, bf16[1,512,2304]{2,1,0:T(8,128)(2,1)S(1)} %fusion.27.q_ref.k_ref.v_ref, ...), custom_call_target="tpu_custom_call" | custom-call | flops 4026531840 | bytes 7864320 | tf_op jit(solution)/shard_map/pallas_call | solution.py:257
  782.3 12.4 shard_map.424
  802.3 34.8 %collective-permute-done.49 = bf16[4,2,3,96,384]{4,3,2,0,1:T(8,128)(2,1)} collective-permute-done((bf16[4,2,3,96,384]{4,3,2,0,1:T(8,128)(2,1)}, bf16[4,2,3,96,384]{4,3,2,0,1:T(8,128)(2,1)}, u32[]{:S(2)}, u32[]{:S(2)}) %collective-permute-start.49) | collective-permute-done | bytes 1769504 | tf_op jit(solution)/shard_map/ppermute | solution.py:530
  863.6 13.8 shard_map.432
  898.0 34.2 %collective-permute-done.41 = f32[49,128]{1,0:T(8,128)} collective-permute-done((f32[49,128]{1,0:T(8,128)}, f32[49,128]{1,0:T(8,128)}, u32[]{:S(2)}, u32[]{:S(2)}) %collective-permute-start.41) | collective-permute-done | bytes 25120 | tf_op jit(solution)/shard_map/ppermute | solution.py:530
  980.9 20.5 %collective-permute-done.91 = f32[]{:T(128)} collective-permute-done((f32[]{:T(128)}, f32[]{:T(128)}, u32[]{:S(2)}, u32[]{:S(2)}) %collective-permute-start.91) | collective-permute-done | bytes 36 | tf_op jit(solution)/shard_map/ppermute | solution.py:530
  1021.8 16.4 %abs_reduce_fusion = (f32[]{:T(128)}, f32[4016,768]{1,0:T(8,128)}) fusion(bf16[1024,768]{1,0:T(8,128)(2,1)S(1)} %copy-done.200, f32[1024,4016]{0,1:T(8,128)} %copy-done.103, f32[1024]{0:T(1024)S(1)} %copy-done.193, s32[1024]{0:T(1024)S(1)} %copy-done.176, f32[1024]{0:T(1024)S(1)} %copy-done.187), kind=kOutput, calls=%fused_computation.18 | convolution fusion | flops 6347464704 | bytes 30371844 | tf_op jit(solution)/shard_map/nv,nd->vd/dot_general | solution.py:1048
  1085.6 43.9 %scatter_custom_fusion = f32[4016,768]{1,0:T(8,128)} fusion(f32[4016,768]{1,0:T(8,128)} %get-tuple-element.324, s32[5120]{0:T(1024)} %bitcast.497, bf16[5120,768]{1,0:T(8,128)(2,1)} %all-gather.8.cloned.1.call-done), kind=kCustom, calls=%fused_computation.9 | custom fusion | flops 7864320 | bytes 20201472 | tf_op jit(solution)/shard_map/scatter-add | solution.py:507
  1147.5 13.9 collective-permute-start.86
  1185.6 14.0 shard_map.434
  1244.2 22.1 %collective-permute-done.82 = f16[1008,384]{1,0:T(8,128)(2,1)} collective-permute-done((f16[1008,384]{1,0:T(8,128)(2,1)}, f16[1008,384]{1,0:T(8,128)(2,1)}, u32[]{:S(2)}, u32[]{:S(2)}) %collective-permute-start.82) | collective-permute-done | bytes 774176 | tf_op jit(solution)/shard_map/ppermute | solution.py:530
  1271.5 19.9 %shard_map.433 = (f32[32,192,192]{2,1,0:T(8,128)S(1)}, f32[32,192,192]{2,1,0:T(8,128)S(1)}, f32[32,192,192]{2,1,0:T(8,128)}, f32[32,192,192]{2,1,0:T(8,128)}) custom-call(f32[16,192,384]{2,1,0:T(8,128)S(1)} %multiply_multiply_fusion.4.g_ref, f32[32,192,192]{2,1,0:T(8,128)} %reshape.1225.lr_ref, f32[32,192,192]{2,1,0:T(8,128)} %reshape.1226.rr_ref), custom_call_target="tpu_custom_call" | custom-call | flops 5435817984 | bytes 33030144 | tf_op jit(solution)/shard_map/pallas_call | solution.py:443
  1389.2 11.2 multiply_add_fusion.1
  1411.7 13.1 collective-permute-done.80
  1427.6 30.5 %multiply_subtract_fusion = (f32[4016,768]{1,0:T(8,128)}, f32[4016,768]{1,0:T(8,128)}, f32[4016,768]{1,0:T(8,128)}) fusion(f32[4016,768]{1,0:T(8,128)} %param.33, f32[]{:T(128)S(6)} %min.19, f32[]{:T(128)S(6)} %div.148, f32[]{:T(128)S(6)} %div.153, f16[1008,384]{1,0:T(8,128)(2,1)S(1)} %copy-done.137, f16[1008,384]{1,0:T(8,128)(2,1)S(1)} %copy-done.136, ...), kind=kLoop, calls=%fused_computation.15 | loop fusion | flops 104865792 | bytes 80216080 | tf_op jit(solution)/shard_map/sub | solution.py:894
  (889 shorter events, 778.7 us)
Async XLA Ops:
  7.2 469.3 %reduce-scatter.3.cloned.1.call-start = ((), (), s32[]{:S(2)}) async-start(), calls=%async_computation.2 | async-start | bytes 8847360 | tf_op jit(solution)/shard_map/reduce_scatter | solution.py:983
  74.2 483.6 %all-gather.6.cloned.1.call-start = ((), (), s32[]{:S(2)}) async-start(), calls=%async_computation.3 | async-start | bytes 1769472 | tf_op jit(solution)/shard_map/all_gather | solution.py:1028
  79.7 47.0 %collective-permute-start.24 = (bf16[4,192,384]{2,1,0:T(8,128)(2,1)S(1)}, bf16[4,192,384]{2,1,0:T(8,128)(2,1)S(1)}, u32[]{:S(2)}, u32[]{:S(2)}) collective-permute-start(bf16[4,192,384]{2,1,0:T(8,128)(2,1)S(1)} %pad_maximum_fusion.1), channel_id=1, source_target_pairs={{4,0},{6,2},{8,4},{10,6},{12,8},{14,10},{5,1},{7,3},{9,5},{11,7},{... | collective-permute-start | bytes 1769480 | tf_op jit(solution)/shard_map/ppermute | solution.py:538
  81.0 49.2 %collective-permute-start.4 = (bf16[3,192,384]{2,1,0:T(8,128)(2,1)S(1)}, bf16[3,192,384]{2,1,0:T(8,128)(2,1)S(1)}, u32[]{:S(2)}, u32[]{:S(2)}) collective-permute-start(bf16[3,192,384]{2,1,0:T(8,128)(2,1)S(1)} %pad_maximum_fusion.7), channel_id=1, source_target_pairs={{4,0},{6,2},{8,4},{10,6},{12,8},{14,10},{5,1},{7,3},{9,5},{11,7},{... | collective-permute-start | bytes 1327112 | tf_op jit(solution)/shard_map/ppermute | solution.py:538
  121.5 55.5 %collective-permute-start.22 = (bf16[4,192,384]{2,1,0:T(8,128)(2,1)S(1)}, bf16[4,192,384]{2,1,0:T(8,128)(2,1)}, u32[]{:S(2)}, u32[]{:S(2)}) collective-permute-start(bf16[4,192,384]{2,1,0:T(8,128)(2,1)S(1)} %collective-permute-done.21), channel_id=1, source_target_pairs={{0,4},{2,6},{4,8},{6,10},{8,12},{10,14},{1,5},{3,7},{5,9},{7,11},{... | collective-permute-start | bytes 1769480 | tf_op jit(solution)/shard_map/ppermute | solution.py:538
  126.7 54.9 %collective-permute-start.25 = (bf16[4,192,384]{2,1,0:T(8,128)(2,1)S(1)}, bf16[4,192,384]{2,1,0:T(8,128)(2,1)}, u32[]{:S(2)}, u32[]{:S(2)}) collective-permute-start(bf16[4,192,384]{2,1,0:T(8,128)(2,1)S(1)} %collective-permute-done.24), channel_id=1, source_target_pairs={{4,0},{6,2},{8,4},{10,6},{12,8},{14,10},{5,1},{7,3},{9,5},{11,7},{... | collective-permute-start | bytes 1769480 | tf_op jit(solution)/shard_map/ppermute | solution.py:538
  130.2 45.5 %collective-permute-start.5 = (bf16[3,192,384]{2,1,0:T(8,128)(2,1)S(1)}, bf16[3,192,384]{2,1,0:T(8,128)(2,1)}, u32[]{:S(2)}, u32[]{:S(2)}) collective-permute-start(bf16[3,192,384]{2,1,0:T(8,128)(2,1)S(1)} %collective-permute-done.4), channel_id=1, source_target_pairs={{4,0},{6,2},{8,4},{10,6},{12,8},{14,10},{5,1},{7,3},{9,5},{11,7},{... | collective-permute-start | bytes 1327112 | tf_op jit(solution)/shard_map/ppermute | solution.py:538
  242.5 47.8 %collective-permute-start.28 = (bf16[4,4,96,384]{3,2,1,0:T(8,128)(2,1)S(1)}, bf16[4,4,96,384]{3,2,1,0:T(8,128)(2,1)}, u32[]{:S(2)}, u32[]{:S(2)}) collective-permute-start(bf16[4,4,96,384]{3,2,1,0:T(8,128)(2,1)S(1)} %get-tuple-element.229.refs_1_), channel_id=1, source_target_pairs={{0,1},{1,0},{2,3},{3,2},{4,5},{5,4},{6,7},{7,6},{8,9},{9,8},{10,11... | collective-permute-start | bytes 3538952 | tf_op jit(solution)/shard_map/ppermute | solution.py:530
  244.2 46.1 %collective-permute-start.29 = (bf16[4,4,96,384]{3,2,1,0:T(8,128)(2,1)S(1)}, bf16[4,4,96,384]{3,2,1,0:T(8,128)(2,1)}, u32[]{:S(2)}, u32[]{:S(2)}) collective-permute-start(bf16[4,4,96,384]{3,2,1,0:T(8,128)(2,1)S(1)} %get-tuple-element.230.refs_0_), channel_id=1, source_target_pairs={{0,16},{16,0},{1,17},{17,1},{2,18},{18,2},{3,19},{19,3},{4,20},{20... | collective-permute-start | bytes 3538952 | tf_op jit(solution)/shard_map/ppermute | solution.py:530
  246.2 52.1 %collective-permute-start.30 = (bf16[4,4,96,384]{3,2,1,0:T(8,128)(2,1)S(1)}, bf16[4,4,96,384]{3,2,1,0:T(8,128)(2,1)S(1)}, u32[]{:S(2)}, u32[]{:S(2)}) collective-permute-start(bf16[4,4,96,384]{3,2,1,0:T(8,128)(2,1)S(1)} %get-tuple-element.229.refs_1_), channel_id=1, source_target_pairs={{0,16},{16,0},{1,17},{17,1},{2,18},{18,2},{3,19},{19,3},{4,20},{20... | collective-permute-start | bytes 3538952 | tf_op jit(solution)/shard_map/ppermute | solution.py:530
  248.1 51.2 %collective-permute-start.33 = (bf16[4,4,96,384]{3,2,1,0:T(8,128)(2,1)S(1)}, bf16[4,4,96,384]{3,2,1,0:T(8,128)(2,1)S(1)}, u32[]{:S(2)}, u32[]{:S(2)}) collective-permute-start(bf16[4,4,96,384]{3,2,1,0:T(8,128)(2,1)S(1)} %get-tuple-element.230.refs_0_), channel_id=1, source_target_pairs={{0,2},{2,0},{4,6},{6,4},{8,10},{10,8},{12,14},{14,12},{1,3},{3,1},... | collective-permute-start | bytes 3538952 | tf_op jit(solution)/shard_map/ppermute | solution.py:530
  315.3 100.0 %collective-permute-start.31 = (bf16[4,4,96,384]{3,2,1,0:T(8,128)(2,1)}, bf16[4,4,96,384]{3,2,1,0:T(8,128)(2,1)}, u32[]{:S(2)}, u32[]{:S(2)}) collective-permute-start(bf16[4,4,96,384]{3,2,1,0:T(8,128)(2,1)} %collective-permute-done.29.refs_4_), channel_id=1, source_target_pairs={{0,1},{1,0},{2,3},{3,2},{4,5},{5,4},{6,7},{7,6},{8,9},{9,8},{10,11... | collective-permute-start | bytes 3538952 | tf_op jit(solution)/shard_map/ppermute | solution.py:530
  317.9 97.8 %collective-permute-start.32 = (bf16[4,4,96,384]{3,2,1,0:T(8,128)(2,1)}, bf16[4,4,96,384]{3,2,1,0:T(8,128)(2,1)}, u32[]{:S(2)}, u32[]{:S(2)}) collective-permute-start(bf16[4,4,96,384]{3,2,1,0:T(8,128)(2,1)} %collective-permute-done.28.refs_3_), channel_id=1, source_target_pairs={{0,16},{16,0},{1,17},{17,1},{2,18},{18,2},{3,19},{19,3},{4,20},{20... | collective-permute-start | bytes 3538952 | tf_op jit(solution)/shard_map/ppermute | solution.py:530
  320.2 95.6 %collective-permute-start.35 = (bf16[4,4,96,384]{3,2,1,0:T(8,128)(2,1)}, bf16[4,4,96,384]{3,2,1,0:T(8,128)(2,1)}, u32[]{:S(2)}, u32[]{:S(2)}) collective-permute-start(bf16[4,4,96,384]{3,2,1,0:T(8,128)(2,1)} %collective-permute-done.27.refs_2_), channel_id=1, source_target_pairs={{0,2},{2,0},{4,6},{6,4},{8,10},{10,8},{12,14},{14,12},{1,3},{3,1},... | collective-permute-start | bytes 3538952 | tf_op jit(solution)/shard_map/ppermute | solution.py:530
  321.2 93.5 %collective-permute-start.19 = (bf16[4,3,96,384]{3,2,1,0:T(8,128)(2,1)}, bf16[4,3,96,384]{3,2,1,0:T(8,128)(2,1)}, u32[]{:S(2)}, u32[]{:S(2)}) collective-permute-start(bf16[4,3,96,384]{3,2,1,0:T(8,128)(2,1)} %collective-permute-done.11.refs_6_), channel_id=1, source_target_pairs={{0,2},{2,0},{4,6},{6,4},{8,10},{10,8},{12,14},{14,12},{1,3},{3,1},... | collective-permute-start | bytes 2654216 | tf_op jit(solution)/shard_map/ppermute | solution.py:530
  322.6 92.6 %collective-permute-start.20 = (bf16[4,3,96,384]{3,2,1,0:T(8,128)(2,1)}, bf16[4,3,96,384]{3,2,1,0:T(8,128)(2,1)}, u32[]{:S(2)}, u32[]{:S(2)}) collective-permute-start(bf16[4,3,96,384]{3,2,1,0:T(8,128)(2,1)} %collective-permute-done.12.refs_7_), channel_id=1, source_target_pairs={{0,2},{2,0},{4,6},{6,4},{8,10},{10,8},{12,14},{14,12},{1,3},{3,1},... | collective-permute-start | bytes 2654216 | tf_op jit(solution)/shard_map/ppermute | solution.py:530
  535.6 104.8 %reduce-scatter.5.cloned.1.call-start = ((), (), s32[]{:S(2)}) async-start(), calls=%async_computation.4 | async-start | bytes 3538944 | tf_op jit(solution)/shard_map/reduce_scatter | solution.py:1049
  600.4 476.1 %all-gather.8.cloned.1.call-start = ((), (), s32[]{:S(2)}) async-start(), calls=%async_computation.5 | async-start | bytes 8847360 | tf_op jit(solution)/shard_map/all_gather | solution.py:1122
  772.8 90.9 %collective-permute-start.57 = (bf16[4,16,192,384]{3,2,1,0:T(8,128)(2,1)}, bf16[4,16,192,384]{3,2,1,0:T(8,128)(2,1)}, u32[]{:S(2)}, u32[]{:S(2)}) collective-permute-start(bf16[4,16,192,384]{3,2,1,0:T(8,128)(2,1)} %dynamic-slice_bitcast_fusion), channel_id=1, source_target_pairs={{0,2},{2,0},{4,6},{6,4},{8,10},{10,8},{12,14},{14,12},{1,3},{3,1},... | collective-permute-start | bytes 28311560 | tf_op jit(solution)/shard_map/ppermute | solution.py:530
  879.4 83.5 %collective-permute-start.58 = (bf16[4,2,4,96,384]{4,3,2,0,1:T(8,128)(2,1)}, bf16[4,2,4,96,384]{4,3,2,0,1:T(8,128)(2,1)}, u32[]{:S(2)}, u32[]{:S(2)}) collective-permute-start(bf16[4,2,4,96,384]{4,3,2,0,1:T(8,128)(2,1)} %copy.116), channel_id=1, source_target_pairs={{0,1},{1,0},{2,3},{3,2},{4,5},{5,4},{6,7},{7,6},{8,9},{9,8},{10,11... | collective-permute-start | bytes 7077896 | tf_op jit(solution)/shard_map/ppermute | solution.py:530
  883.3 86.1 %collective-permute-start.60 = (bf16[4,2,4,96,384]{4,3,2,0,1:T(8,128)(2,1)}, bf16[4,2,4,96,384]{4,3,2,0,1:T(8,128)(2,1)}, u32[]{:S(2)}, u32[]{:S(2)}) collective-permute-start(bf16[4,2,4,96,384]{4,3,2,0,1:T(8,128)(2,1)} %copy.118), channel_id=1, source_target_pairs={{0,16},{16,0},{1,17},{17,1},{2,18},{18,2},{3,19},{19,3},{4,20},{20... | collective-permute-start | bytes 7077896 | tf_op jit(solution)/shard_map/ppermute | solution.py:530
  1070.7 69.7 %collective-permute-start.67 = (bf16[4,192,384]{2,1,0:T(8,128)(2,1)}, bf16[4,192,384]{2,1,0:T(8,128)(2,1)S(1)}, u32[]{:S(2)}, u32[]{:S(2)}) collective-permute-start(bf16[4,192,384]{2,1,0:T(8,128)(2,1)} %get-tuple-element.224), channel_id=1, source_target_pairs={{4,0},{6,2},{8,4},{10,6},{12,8},{14,10},{5,1},{7,3},{9,5},{11,7},{... | collective-permute-start | bytes 1769480 | tf_op jit(solution)/shard_map/ppermute | solution.py:538
  1072.0 68.4 %collective-permute-start.64 = (bf16[4,192,384]{2,1,0:T(8,128)(2,1)S(1)}, bf16[4,192,384]{2,1,0:T(8,128)(2,1)S(1)}, u32[]{:S(2)}, u32[]{:S(2)}) collective-permute-start(bf16[4,192,384]{2,1,0:T(8,128)(2,1)S(1)} %get-tuple-element.223), channel_id=1, source_target_pairs={{0,4},{2,6},{4,8},{6,10},{8,12},{10,14},{1,5},{3,7},{5,9},{7,11},{... | collective-permute-start | bytes 1769480 | tf_op jit(solution)/shard_map/ppermute | solution.py:538
  1082.7 46.8 %collective-permute-start.68 = (f32[]{:T(128)}, f32[]{:T(128)}, u32[]{:S(2)}, u32[]{:S(2)}) collective-permute-start(f32[]{:T(128)} %add.1071), channel_id=1, source_target_pairs={{0,1},{1,0},{2,3},{3,2},{4,5},{5,4},{6,7},{7,6},{8,9},{9,8},{10,11... | collective-permute-start | bytes 20 | tf_op jit(solution)/shard_map/ppermute | solution.py:530
  1173.9 59.8 %collective-permute-start.88 = (f16[2,4,96,384]{3,2,1,0:T(8,128)(2,1)}, f16[2,4,96,384]{3,2,1,0:T(8,128)(2,1)}, u32[]{:S(2)}, u32[]{:S(2)}) collective-permute-start(f16[2,4,96,384]{3,2,1,0:T(8,128)(2,1)} %pad_maximum_fusion.2), channel_id=1, source_target_pairs={{0,1},{1,0},{2,3},{3,2},{4,5},{5,4},{6,7},{7,6},{8,9},{9,8},{10,11... | collective-permute-start | bytes 1769480 | tf_op jit(solution)/shard_map/ppermute | solution.py:530
  1178.1 56.8 %collective-permute-start.90 = (f16[2,4,96,384]{3,2,1,0:T(8,128)(2,1)}, f16[2,4,96,384]{3,2,1,0:T(8,128)(2,1)}, u32[]{:S(2)}, u32[]{:S(2)}) collective-permute-start(f16[2,4,96,384]{3,2,1,0:T(8,128)(2,1)} %pad_maximum_fusion.3), channel_id=1, source_target_pairs={{0,16},{16,0},{1,17},{17,1},{2,18},{18,2},{3,19},{19,3},{4,20},{20... | collective-permute-start | bytes 1769480 | tf_op jit(solution)/shard_map/ppermute | solution.py:530
  1183.4 52.7 %collective-permute-start.73 = (f16[1008,384]{1,0:T(8,128)(2,1)}, f16[1008,384]{1,0:T(8,128)(2,1)}, u32[]{:S(2)}, u32[]{:S(2)}) collective-permute-start(f16[1008,384]{1,0:T(8,128)(2,1)} %dynamic-slice_convert_fusion.4), channel_id=1, source_target_pairs={{0,1},{1,0},{2,3},{3,2},{4,5},{5,4},{6,7},{7,6},{8,9},{9,8},{10,11... | collective-permute-start | bytes 2322440 | tf_op jit(solution)/shard_map/ppermute | solution.py:530
  1243.3 80.2 %collective-permute-start.84 = (f16[1008,384]{1,0:T(8,128)(2,1)}, f16[1008,384]{1,0:T(8,128)(2,1)}, u32[]{:S(2)}, u32[]{:S(2)}) collective-permute-start(f16[1008,384]{1,0:T(8,128)(2,1)} %get-tuple-element.233), channel_id=1, source_target_pairs={{0,16},{16,0},{1,17},{17,1},{2,18},{18,2},{3,19},{19,3},{4,20},{20... | collective-permute-start | bytes 2322440 | tf_op jit(solution)/shard_map/ppermute | solution.py:530
  1266.3 57.2 %collective-permute-start.83 = (f16[1008,384]{1,0:T(8,128)(2,1)}, f16[1008,384]{1,0:T(8,128)(2,1)}, u32[]{:S(2)}, u32[]{:S(2)}) collective-permute-start(f16[1008,384]{1,0:T(8,128)(2,1)} %collective-permute-done.82), channel_id=1, source_target_pairs={{0,16},{16,0},{1,17},{17,1},{2,18},{18,2},{3,19},{19,3},{4,20},{20... | collective-permute-start | bytes 2322440 | tf_op jit(solution)/shard_map/ppermute | solution.py:530
  1270.6 58.0 %collective-permute-start.71 = (f16[1008,384]{1,0:T(8,128)(2,1)}, f16[1008,384]{1,0:T(8,128)(2,1)}, u32[]{:S(2)}, u32[]{:S(2)}) collective-permute-start(f16[1008,384]{1,0:T(8,128)(2,1)} %dynamic-slice_convert_fusion.5), channel_id=1, source_target_pairs={{0,16},{16,0},{1,17},{17,1},{2,18},{18,2},{3,19},{19,3},{4,20},{20... | collective-permute-start | bytes 2322440 | tf_op jit(solution)/shard_map/ppermute | solution.py:530
  1331.6 75.4 %collective-permute-start.79 = (f16[1008,384]{1,0:T(8,128)(2,1)}, f16[1008,384]{1,0:T(8,128)(2,1)}, u32[]{:S(2)}, u32[]{:S(2)}) collective-permute-start(f16[1008,384]{1,0:T(8,128)(2,1)} %get-tuple-element.231), channel_id=1, source_target_pairs={{0,16},{16,0},{1,17},{17,1},{2,18},{18,2},{3,19},{19,3},{4,20},{20... | collective-permute-start | bytes 2322440 | tf_op jit(solution)/shard_map/ppermute | solution.py:530
  1332.7 79.0 %collective-permute-start.81 = (f16[1008,384]{1,0:T(8,128)(2,1)}, f16[1008,384]{1,0:T(8,128)(2,1)}, u32[]{:S(2)}, u32[]{:S(2)}) collective-permute-start(f16[1008,384]{1,0:T(8,128)(2,1)} %get-tuple-element.231), channel_id=1, source_target_pairs={{0,1},{1,0},{2,3},{3,2},{4,5},{5,4},{6,7},{7,6},{8,9},{9,8},{10,11... | collective-permute-start | bytes 2322440 | tf_op jit(solution)/shard_map/ppermute | solution.py:530
  (284 other events, 3522.6 us)
Sparse Core Ops, SparseCore 0:
  74.3 150.4 reduce-scatter.2
  535.8 21.9 all-gather.5
  600.5 39.9 reduce-scatter.4
  802.4 75.1 all-gather.7

commit v4 on v3

--- a/solution.py
+++ b/solution.py
@@ -272,6 +272,8 @@
 
 
 def as_blocks(flat):
+    if flat.ndim == 3:
+        return flat
     return flat.reshape(flat.shape[0], BLOCK, BLOCK)
 
 
@@ -422,7 +424,7 @@
 
 
 def shampoo_ahead(moment, left_root, right_root):
-    blocks = [as_blocks(moment), as_blocks(left_root), as_blocks(right_root)]
+    blocks = [as_blocks(member) for member in (moment, left_root, right_root)]
     amount = moment.shape[0]
     spec = pl.BlockSpec((2, BLOCK, BLOCK), lambda pair: (pair, 0, 0))
     ahead = pl.pallas_call(
@@ -554,12 +556,6 @@
     return values.astype(jnp.float32)
 
 
-def agreed_scale(largest):
-    for axis in ("seq", "dp"):
-        largest = jnp.maximum(largest, swap(largest, axis))
-    return 4096.0 / jnp.maximum(largest, 1e-30)
-
-
 def placed(relative, first, second):
     def at(row, column):
         here = choose(second, relative[row][1 - column], relative[row][column])
@@ -576,104 +572,19 @@
     return as_pairs(as_blocks(master.astype(jnp.bfloat16)))
 
 
-def along_chips(own):
-    n_chips = lax.axis_size("fsdp") // 2
-    rising = falling = own
-    pieces = [own]
-    for _ in range(n_chips - 1):
-        rising, falling = (shift(rising, 1), shift(falling, -1))
-        pieces = [rising] + pieces + [falling]
-    first = n_chips - 1 - lax.axis_index("fsdp") // 2
-    return lax.dynamic_slice_in_dim(jnp.stack(pieces), first, n_chips, 0)
-
-
-def gather_weights(pairs, amount, shapes):
-    if not paired_mesh():
-        split = amount % (2 * replica_count()) == 0
-        everything = lax.all_gather(pairs, EVERYWHERE if split else "fsdp", axis=0, tiled=True)
-        return matrices_of(everything, shapes)
-    line = along_chips(pairs)
-    mid = BLOCK // 2
-    upper, lower = (line[:, :, :mid], line[:, :, mid:])
-    upper_side, lower_half = (swap(upper, "dp"), swap(lower, "seq"))
-    upper_half, lower_side = (swap(upper, "seq"), swap(lower, "dp"))
-    pieces = [
-        upper,
-        lower,
-        upper_half,
-        lower_half,
-        upper_side,
-        lower_side,
-        swap(upper_side, "seq"),
-        swap(lower_half, "dp"),
-    ]
-    pieces += [swap(piece, "fsdp") for piece in pieces]
-    return assembled(pieces, shapes)
-
-
-def assemble_kernel(place_ref, *refs, shapes):
-    pieces, outs = (refs[:16], refs[16 : 16 + len(shapes)])
-    buffer, in_sems, out_sems = refs[16 + len(shapes) :]
-    core, side, half = (place_ref[0], place_ref[1], place_ref[2])
-    n_chips, quarter, mid, _ = pieces[0].shape
-    copies = []
-    for index, piece in enumerate(pieces):
-        owner = ((side ^ (index // 4 % 2)) * 2 + (half ^ (index // 2 % 2))) * quarter
-        for chip in range(n_chips):
-            first = (2 * chip + (core ^ (index // 8))) * (4 * quarter) + owner
-            copies.append(
-                pltpu.make_async_copy(
-                    piece.at[chip],
-                    buffer.at[pl.ds(first, quarter), pl.ds((index % 2) * mid, mid), :],
-                    in_sems.at[index, chip],
-                )
-            )
-    for copy in copies:
-        copy.start()
-    for copy in copies:
-        copy.wait()
-    copies = []
-    for out_ref, (height, breadth) in zip(outs, shapes):
-        for row in range(height // BLOCK):
-            for column in range(breadth // PAIR):
-                copies.append(
-                    pltpu.make_async_copy(
-                        buffer.at[len(copies)],
-                        out_ref.at[pl.ds(row * BLOCK, BLOCK), pl.ds(column * PAIR, PAIR)],
-                        out_sems.at[len(copies)],
-                    )
-                )
-    for copy in copies:
-        copy.start()
-    for copy in copies:
-        copy.wait()
+def hold(values):
+    return lax.optimization_barrier(values)
+
+
+def gathered_weights(pairs, amount):
+    split = amount % (2 * replica_count()) == 0
+    return lax.all_gather(pairs, EVERYWHERE if split else "fsdp", axis=0, tiled=True)
 
 
 def own_place():
     return jnp.stack(
         [lax.axis_index("fsdp") % 2, lax.axis_index("dp"), lax.axis_index("seq")]
     ).astype(jnp.int32)
-
-
-def assembled(pieces, shapes):
-    n_chips, quarter, mid, _ = pieces[0].shape
-    total = 8 * n_chips * quarter
-    return pl.pallas_call(
-        functools.partial(assemble_kernel, shapes=shapes),
-        out_shape=[jax.ShapeDtypeStruct(shape, jnp.bfloat16) for shape in shapes],
-        in_specs=[pl.BlockSpec(memory_space=pltpu.SMEM)]
-        + [pl.BlockSpec(memory_space=pl.ANY)] * len(pieces),
-        out_specs=[pl.BlockSpec(memory_space=pl.ANY)] * len(shapes),
-        scratch_shapes=[
-            pltpu.VMEM((total, BLOCK, PAIR), jnp.bfloat16),
-            pltpu.SemaphoreType.DMA((len(pieces), n_chips)),
-            pltpu.SemaphoreType.DMA((total,)),
-        ],
-        cost_estimate=pl.CostEstimate(
-            flops=0, bytes_accessed=4 * total * BLOCK * PAIR, transcendentals=0
-        ),
-        compiler_params=pltpu.CompilerParams(vmem_limit_bytes=30 << 20),
-    )(own_place(), *pieces)
 
 
 def fold_kernel(place_ref, own_ref, got_ref, keep_up, send_up, keep_low, send_low):
@@ -765,12 +676,15 @@
     )
 
 
-def sum_small(values):
+def sum_replicas(values):
+    values = values + swap(values, "seq")
+    return values + swap(values, "dp")
+
+
+def sum_line(values):
     size = lax.axis_size("fsdp")
-    if not paired_mesh() or size & (size - 1):
-        return lax.psum(values, EVERYWHERE)
-    values = values + swap(values, "seq")
-    values = values + swap(values, "dp")
+    if size & (size - 1):
+        return lax.psum(values, "fsdp")
     step = 1
     while step < size:
         moves = [(place, place ^ step) for place in range(size)]
@@ -779,85 +693,122 @@
     return values
 
 
-def reduce_blocks(pairs):
-    if not paired_mesh():
-        return lax.psum(
-            lax.psum_scatter(wide(pairs), "fsdp", scatter_dimension=0, tiled=True), REPLICAS
-        )
+def summed_blocks(pairs):
+    shard = lax.psum_scatter(wide(pairs), "fsdp", scatter_dimension=0, tiled=True)
+    return lax.psum(shard, REPLICAS)
+
+
+def swap_halves(pairs):
     n_chips = lax.axis_size("fsdp") // 2
     core = lax.axis_index("fsdp") % 2
-    chip = lax.axis_index("fsdp") // 2
+    split = pairs.reshape(n_chips, 2, -1, BLOCK, PAIR)
+    return swap(pick(split, 1 - core, 1), "fsdp")
+
+
+def fold_blocks(pairs, got):
+    n_chips = lax.axis_size("fsdp") // 2
+    return fold_cores(pairs, got, n_chips, pairs.shape[0] // (8 * n_chips))
+
+
+def near_sums(folded):
+    return [folded[0], swap(folded[1], "seq"), folded[2], swap(folded[3], "dp")]
+
+
+def far_sums(near):
     side, half = (lax.axis_index("dp"), lax.axis_index("seq"))
-    amount = pairs.shape[0] // (2 * n_chips)
-    quarter = amount // 4
-    split = pairs.reshape(n_chips, 2, amount, BLOCK, PAIR)
-    got = swap(pick(split, 1 - core, 1), "fsdp")
-    upper, upper_sent, lower, lower_sent = fold_cores(pairs, got, n_chips, quarter)
-    upper = upper + wide(swap(upper_sent, "seq"))
-    lower = lower + wide(swap(lower_sent, "dp"))
-    upper = pick(upper, side, 1) + wide(swap(narrow(pick(upper, 1 - side, 1)), "dp"))
-    lower = pick(lower, half, 1) + wide(swap(narrow(pick(lower, 1 - half, 1)), "seq"))
-    line_sum = jnp.concatenate([upper, lower], axis=2)
-    ahead = lax.dynamic_slice_in_dim(
-        jnp.concatenate([line_sum, line_sum[:-1]], axis=0), chip, n_chips, 0
-    )
-    up = down = None
-    for step in range(n_chips - 1, 0, -1):
-        rising, falling = (ahead[step], ahead[n_chips - step])
-        if up is not None:
-            rising, falling = (rising + wide(up), falling + wide(down))
-        up, down = (shift(narrow(rising), 1), shift(narrow(falling), -1))
-    return ahead[0] + wide(up) + wide(down)
+    upper = near[0] + wide(near[1])
+    lower = near[2] + wide(near[3])
+    return [
+        pick(upper, side, 1),
+        swap(narrow(pick(upper, 1 - side, 1)), "dp"),
+        pick(lower, half, 1),
+        swap(narrow(pick(lower, 1 - half, 1)), "seq"),
+    ]
+
+
+def line_sums(far):
+    size = lax.axis_size("fsdp")
+    line = narrow(jnp.concatenate([far[0] + wide(far[1]), far[2] + wide(far[3])], axis=2))
+    cores = [list(range(core, size, 2)) for core in range(2)]
+    return lax.all_to_all(line, "fsdp", 0, 0, axis_index_groups=cores, tiled=True)
+
+
+def line_total(arrived):
+    return jnp.sum(wide(arrived), axis=0)
 
 
 def share_blocks(own):
-    side, half = (lax.axis_index("dp"), lax.axis_index("seq"))
-    mid = BLOCK // 2
-    scale = agreed_scale(jnp.max(jnp.abs(own)))
-    own = lax.optimization_barrier((own * scale).astype(jnp.float16))
-    upper, lower = (own[:, :mid], own[:, mid:])
-    upper_side, lower_half = (swap(upper, "dp"), swap(lower, "seq"))
-    upper_rest = swap(jnp.stack([upper, upper_side]), "seq")
-    lower_rest = swap(jnp.stack([lower, lower_half]), "dp")
-    relative = [
-        [
-            jnp.concatenate([upper, lower], axis=1),
-            jnp.concatenate([upper_rest[0], lower_half], axis=1),
-        ],
-        [
-            jnp.concatenate([upper_side, lower_rest[0]], axis=1),
-            jnp.concatenate([upper_rest[1], lower_rest[1]], axis=1),
-        ],
-    ]
-    whole = placed(relative, side, half)
-    return wide(jnp.concatenate(whole[0] + whole[1], axis=0)) * (1.0 / scale)
+    return wide(lax.all_gather(narrow(own), REPLICAS, axis=0, tiled=True))
 
 
 def window_rows(half_rows):
     return -(-half_rows // 16) * 8
 
 
-def reduce_table(partial, bound):
+def half_lanes(values, place):
+    return lax.dynamic_slice_in_dim(values, place * (D // 2), D // 2, 1)
+
+
+SCALE_ROWS = 8
+
+
+def scale_of(power):
+    return jnp.exp2(power.astype(jnp.float32))
+
+
+def scaled_swap(values, power, axis):
+    mark = jnp.full((SCALE_ROWS, values.shape[1]), power, jnp.float16)
+    message = jnp.concatenate([values.astype(jnp.float16), mark], axis=0)
+    got = swap(message, axis)
+    return got[:-SCALE_ROWS], got[-1, 0].astype(jnp.float32)
+
+
+def joined(values, power, got):
+    others, other_power = got
+    least = jnp.minimum(power, other_power)
+    return (
+        values * scale_of(least - power) + wide(others) * scale_of(least - other_power),
+        least,
+    )
+
+
+def near_table(partial, bound):
     side, half = (lax.axis_index("dp"), lax.axis_index("seq"))
-    scale = agreed_scale(bound)
     half_rows = partial.shape[0] // 2
     window = window_rows(half_rows)
+    power = jnp.clip(12.0 - jnp.ceil(jnp.log2(jnp.maximum(bound, 1e-37))), -120.0, 120.0)
 
     def rows_of(first, place):
         start = first + place * (half_rows - window)
-        return lax.dynamic_slice_in_dim(partial, start, window, 0) * scale
-
-    def half_lanes(values, place):
-        return lax.dynamic_slice_in_dim(values, place * (D // 2), D // 2, 1)
-
-    def send(values, axis):
-        return wide(swap(values.astype(jnp.float16), axis))
-
-    top = rows_of(0, half) + send(rows_of(0, 1 - half), "seq")
-    low = rows_of(half_rows, side) + send(rows_of(half_rows, 1 - side), "dp")
-    top = half_lanes(top, side) + send(half_lanes(top, 1 - side), "dp")
-    low = half_lanes(low, half) + send(half_lanes(low, 1 - half), "seq")
-    return top, low, scale
+        return lax.dynamic_slice_in_dim(partial, start, window, 0) * scale_of(power)
+
+    return [
+        rows_of(0, half),
+        scaled_swap(rows_of(0, 1 - half), power, "seq"),
+        rows_of(half_rows, side),
+        scaled_swap(rows_of(half_rows, 1 - side), power, "dp"),
+        power,
+    ]
+
+
+def far_table(near):
+    side, half = (lax.axis_index("dp"), lax.axis_index("seq"))
+    top, top_power = joined(near[0], near[4], near[1])
+    low, low_power = joined(near[2], near[4], near[3])
+    return [
+        half_lanes(top, side),
+        top_power,
+        scaled_swap(half_lanes(top, 1 - side), top_power, "dp"),
+        half_lanes(low, half),
+        low_power,
+        scaled_swap(half_lanes(low, 1 - half), low_power, "seq"),
+    ]
+
+
+def table_total(far):
+    top, power = joined(*far[:3])
+    low, _ = joined(*far[3:])
+    return top, low, scale_of(power)
 
 
 def table_squares(top, low, half_rows):
@@ -869,16 +820,21 @@
     )
 
 
-def share_table(top, low, scale, half_rows):
+def share_near(top, low):
+    top = hold(top.astype(jnp.float16))
+    low = hold(low.astype(jnp.float16))
+    return [jnp.stack([top, swap(top, "dp")]), jnp.stack([low, swap(low, "seq")])]
+
+
+def share_far(near):
+    return [swap(near[0], "seq"), swap(near[1], "dp")]
+
+
+def placed_table(near, far, scale, half_rows):
     side, half = (lax.axis_index("dp"), lax.axis_index("seq"))
     again = 2 * window_rows(half_rows) - half_rows
-    top = lax.optimization_barrier(top.astype(jnp.float16))
-    low = lax.optimization_barrier(low.astype(jnp.float16))
-    top_side, low_half = (swap(top, "dp"), swap(low, "seq"))
-    top_rest = (swap(top, "seq"), swap(top_side, "seq"))
-    low_rest = (swap(low, "dp"), swap(low_half, "dp"))
-    top_all = placed([[top, top_side], top_rest], half, side)
-    low_all = placed([[low, low_half], low_rest], side, half)
+    top_all = placed([near[0], far[0]], half, side)
+    low_all = placed([near[1], far[1]], side, half)
     rows = []
     for first, second in (top_all, low_all):
         rows.append(jnp.concatenate(first, axis=1))
@@ -948,10 +904,14 @@
     enc_in = jnp.where(span_mask == 1, VOCAB - sentinel_offset, enc_ids)
     dec_in = jnp.concatenate([jnp.zeros((rows, 1), jnp.int32), targets[:, :-1]], axis=1)
 
+    paired = paired_mesh()
+
     halves = jnp.stack([enc_in, segments]).reshape(2, n_seq, rows, half_len)
+    enc_own, dec_own, table = (own_weights(enc_w), own_weights(dec_w), narrow(embedding))
     if n_seq == 2:
         kept = pick(halves, seq_rank, 1)
         got = swap(pick(halves, 1 - seq_rank, 1), "seq")
+        got, enc_own, dec_own = hold((got, enc_own, dec_own))
         parts = (choose(seq_rank, got, kept), choose(seq_rank, kept, got))
         row_words = jnp.stack(parts, axis=2)
     else:
@@ -966,35 +926,27 @@
             loss_weights.reshape(-1),
         ]
     ).reshape(1, -1)
-    enc_pairs, dec_pairs, message = lax.optimization_barrier(
-        (own_weights(enc_w), own_weights(dec_w), message)
-    )
-    enc_mats = gather_weights(enc_pairs, enc_w.shape[0], layer_shapes(False))
-    dec_mats = gather_weights(dec_pairs, dec_w.shape[0], layer_shapes(True))
+    enc_pairs = gathered_weights(enc_own, enc_w.shape[0])
     gathered = lax.all_gather(message, "fsdp", axis=0, tiled=True)
     all_enc = gathered[:, : rows * enc_len]
     rest = gathered[:, rows * enc_len :].reshape(n_fsdp, 3, rows * dec_len)
     all_dec, all_targets, all_weights = (rest[:, 0], rest[:, 1], rest[:, 2])
     all_tokens = jnp.concatenate([all_enc, all_dec], axis=1)
-
-    table = embedding.astype(jnp.bfloat16)
     vocab_local = table.shape[0]
     vocab_first = fsdp_rank * vocab_local
-    looked_up = lax.psum_scatter(
-        table_rows(table, all_tokens, vocab_first), "fsdp", scatter_dimension=0, tiled=True
-    ).reshape(-1, D)
-    enc_ready = shampoo_ahead(enc_m, enc_lroot, enc_rroot)
-    dec_ready = shampoo_ahead(dec_m, dec_lroot, dec_rroot)
-    looked_up, enc_ready, dec_ready = lax.optimization_barrier((looked_up, enc_ready, dec_ready))
-    enc_ahead, enc_lr, enc_rr = enc_ready
-    dec_ahead, dec_lr, dec_rr = dec_ready
+    found = table_rows(table, all_tokens, vocab_first)
+    found, enc_pairs, dec_own = hold((found, enc_pairs, dec_own))
+    looked_up = lax.psum_scatter(found, "fsdp", scatter_dimension=0, tiled=True).reshape(-1, D)
+    dec_pairs = gathered_weights(dec_own, dec_w.shape[0])
+    enc_mats = matrices_of(enc_pairs, layer_shapes(False))
+    enc_onehot = tile_onehot(enc_len // TILE, False)
+    dec_onehot = tile_onehot(dec_len // TILE, True)
+    looked_up, enc_mats, enc_bias, dec_bias = hold(
+        (looked_up, enc_mats, tile_bias(enc_onehot, rel_bias[0]), tile_bias(dec_onehot, rel_bias[1]))
+    )
     hidden0 = looked_up[: rows * enc_len].reshape(rows, enc_len, D).astype(jnp.float32)
     state0 = looked_up[rows * enc_len :].reshape(rows, dec_len, D).astype(jnp.float32)
 
-    enc_onehot = tile_onehot(enc_len // TILE, False)
-    dec_onehot = tile_onehot(dec_len // TILE, True)
-    enc_bias = tile_bias(enc_onehot, rel_bias[0])
-    dec_bias = tile_bias(dec_onehot, rel_bias[1])
     tile_at = D // LANES
     self_places = (0, tile_at, 2 * tile_at)
     cross_places = (0, 0, tile_at)
@@ -1007,6 +959,15 @@
     hidden1 = hidden0 + project(enc_attended, enc_mats[1])
     hidden2, enc_cache = ff_forward(hidden1, gains[1], enc_mats[2], enc_mats[3])
     encoded = rms(hidden2, gains[2]).astype(jnp.bfloat16)
+    count = jnp.sum(all_weights).astype(jnp.float32)
+    if paired:
+        count = count + swap(count, "seq")
+        count = count + swap(count, "dp")
+    else:
+        count = lax.psum(count, REPLICAS)
+    encoded, count, dec_pairs = hold((encoded, count, dec_pairs))
+    share = 1.0 / jnp.maximum(count, 1.0)
+    dec_mats = matrices_of(dec_pairs, layer_shapes(True))
     pairs = project(encoded, dec_mats[3]).astype(jnp.bfloat16)
 
     normed3 = rms(state0, gains[3]).astype(jnp.bfloat16)
@@ -1041,17 +1002,19 @@
     lse = top_all + jnp.log(sum_all)
     token_weights = all_weights.reshape(-1).astype(jnp.float32)
     group_loss = jnp.sum(token_weights * (lse - pick_all))
-    group_count = jnp.sum(token_weights)
     grad_logits = (
         token_weights[:, None] * (jnp.exp(logits - lse[:, None]) - target_hot.astype(jnp.float32))
     ).astype(jnp.bfloat16)
-    emb_grad = jnp.einsum("nv,nd->vd", grad_logits, all_final, preferred_element_type=jnp.float32)
     grad_final = lax.psum_scatter(
         jnp.dot(grad_logits, table, preferred_element_type=jnp.float32),
         "fsdp",
         scatter_dimension=0,
         tiled=True,
     ).reshape(rows, dec_len, D)
+    dense_grad = jnp.einsum("nv,nd->vd", grad_logits, all_final, preferred_element_type=jnp.float32)
+    grad_final, dense_grad, dense_bound = hold(
+        (grad_final, dense_grad, jnp.max(jnp.abs(dense_grad)))
+    )
 
     grad_state3, gain_six = rms_back(state3, gains[6], grad_final * out_scale)
     grad_state2, gain_five, dec_in_grad, dec_down_grad = ff_back(
@@ -1090,7 +1053,8 @@
             dec_down_grad,
         ]
     )
-    dec_part = reduce_blocks(decoder_portion)
+    if paired:
+        dec_got = swap_halves(decoder_portion)
 
     grad_hidden2, gain_two = rms_back(hidden2, gains[2], grad_encoded)
     grad_hidden1, gain_one, encoder_input_gradient, encoder_down_gradient = ff_back(
@@ -1099,6 +1063,11 @@
     branch_grad = grad_hidden1.astype(jnp.bfloat16)
     encoder_output_gradient = (enc_attended, branch_grad)
     grad_attn = project_back(branch_grad, enc_mats[1]).astype(jnp.bfloat16)
+    if paired:
+        dec_got, decoder_portion, grad_attn = hold((dec_got, decoder_portion, grad_attn))
+        dec_folded = fold_blocks(decoder_portion, dec_got)
+        dec_folded, grad_attn = hold((dec_folded, grad_attn))
+        dec_close = near_sums(dec_folded)
     grad_eq, grad_ek, grad_ev, enc_bias_grad = attend_back(
         enc_qkv, enc_qkv, self_places, enc_bias, row_segments, row_segments, False, grad_attn
     )
@@ -1106,6 +1075,14 @@
     encoder_qkv_gradient = (normed0, grad_eqkv)
     grad_hidden0_part, gain_zero = rms_back(hidden0, gains[0], project_back(grad_eqkv, enc_mats[0]))
     grad_hidden0 = grad_hidden1 + grad_hidden0_part
+    back_rows = jnp.concatenate(
+        [grad_hidden0.reshape(-1, D), grad_state0.reshape(-1, D)], axis=0
+    ).astype(jnp.bfloat16)
+    if paired:
+        dec_close, back_rows, grad_eqkv = hold((dec_close, back_rows, grad_eqkv))
+        encoder_qkv_gradient = (normed0, grad_eqkv)
+        dec_far_sums = far_sums(dec_close)
+    back_all = lax.all_gather(back_rows, "fsdp", axis=0, tiled=True)
     encoder_portion = weight_grads(
         [
             encoder_qkv_gradient,
@@ -1114,60 +1091,93 @@
             encoder_down_gradient,
         ]
     )
-    enc_part = reduce_blocks(encoder_portion)
-
-    back_rows = jnp.concatenate(
-        [grad_hidden0.reshape(-1, D), grad_state0.reshape(-1, D)], axis=0
-    ).astype(jnp.bfloat16)
-    back_all = lax.all_gather(back_rows, "fsdp", axis=0, tiled=True)
-    dense_bound = jnp.max(jnp.abs(emb_grad))
-    bound = dense_bound + back_all.shape[0] * jnp.max(jnp.abs(back_all)).astype(jnp.float32)
-    emb_grad = table_grads(back_all, all_tokens, vocab_first, emb_grad)
+    if paired:
+        encoder_portion, dec_far_sums = hold((encoder_portion, dec_far_sums))
+        enc_got = swap_halves(encoder_portion)
+        enc_got, encoder_portion, enc_roots = hold(
+            (enc_got, encoder_portion, (enc_m, enc_lroot, enc_rroot))
+        )
+        enc_folded = hold(fold_blocks(encoder_portion, enc_got))
+        enc_close = near_sums(enc_folded)
+        enc_ready = shampoo_ahead(*enc_roots)
+        back_all, enc_close, enc_ready, dec_far_sums = hold(
+            (back_all, enc_close, enc_ready, dec_far_sums)
+        )
+        dec_arrived = line_sums(dec_far_sums)
+        enc_far_sums = far_sums(enc_close)
+        bound = dense_bound + back_all.shape[0] * jnp.max(jnp.abs(back_all)).astype(jnp.float32)
+    else:
+        enc_ready = shampoo_ahead(enc_m, enc_lroot, enc_rroot)
+        dec_ready = shampoo_ahead(dec_m, dec_lroot, dec_rroot)
+    emb_grad = table_grads(back_all, all_tokens, vocab_first, dense_grad)
     gain_part = jnp.stack(
         [gain_zero, gain_one, gain_two, gain_three, gain_four, gain_five, gain_six]
     )
     rel_part = jnp.stack(
         [tile_bias_grad(enc_onehot, enc_bias_grad), tile_bias_grad(dec_onehot, dec_bias_grad)]
     )
-    loss_part = jnp.where(fsdp_rank == 0, jnp.stack([group_loss, group_count]), 0.0)
-    small = jnp.concatenate(
-        [gain_part.reshape(-1), rel_part.reshape(-1), loss_part, jnp.zeros(126, jnp.float32)]
-    )
-    small = sum_small(small.reshape(-1, LANES)).reshape(-1)
-    gain_total = small[: 7 * D].reshape(7, D)
-    rel_total = small[7 * D : 7 * D + 2 * NBK * H].reshape(2, NBK, H)
-    loss_total = small[7 * D + 2 * NBK * H :]
-    loss_sum = loss_total[0]
-    loss_count = jnp.maximum(loss_total[1], 1.0)
-    share = 1.0 / loss_count
-    gain_grad = gain_total * share
-    rel_grad = rel_total * share
-
-    if paired_mesh():
-        dec_grad = share_blocks(dec_part) * share
-        enc_grad = share_blocks(enc_part) * share
+    small = [
+        gain_part.reshape(-1),
+        rel_part.reshape(-1),
+        jnp.where(fsdp_rank == 0, group_loss, 0.0).reshape(1),
+    ]
+    if paired:
         half_rows = vocab_local // 2
-        top, low, scale = reduce_table(emb_grad, bound)
+        dec_arrived, enc_far_sums, emb_grad, bound, dec_roots = hold(
+            (dec_arrived, enc_far_sums, emb_grad, bound, (dec_m, dec_lroot, dec_rroot))
+        )
+        table_close = near_table(emb_grad, bound)
+        enc_arrived = line_sums(enc_far_sums)
+        dec_own_sum = line_total(dec_arrived)
+        dec_grad = share_blocks(dec_own_sum) * share
+        dec_ready = shampoo_ahead(*dec_roots)
+        table_close, dec_ready, dec_grad, enc_arrived = hold(
+            (table_close, dec_ready, dec_grad, enc_arrived)
+        )
+        table_far = far_table(table_close)
+        dec_products = shampoo_products(dec_grad, *dec_ready[1:])
+        enc_own_sum = line_total(enc_arrived)
+        enc_grad = share_blocks(enc_own_sum) * share
+        table_far, dec_products = hold((table_far, dec_products))
+        top, low, scale = table_total(table_far)
         squares = (
-            jnp.sum(jnp.square(enc_part * share))
-            + jnp.sum(jnp.square(dec_part * share))
+            jnp.sum(jnp.square(enc_own_sum * share))
+            + jnp.sum(jnp.square(dec_own_sum * share))
             + table_squares(top * (share / scale), low * (share / scale), half_rows)
         )
-        squares_all = sum_small(squares)
-        table_grad = share_table(top, low, scale, half_rows) * share
     else:
-        dec_grad, enc_grad = (dec_part * share, enc_part * share)
+        dec_grad = summed_blocks(decoder_portion) * share
+        enc_grad = summed_blocks(encoder_portion) * share
+        dec_products = shampoo_products(dec_grad, *dec_ready[1:])
+        enc_products = shampoo_products(enc_grad, *enc_ready[1:])
         table_grad = lax.psum(emb_grad, REPLICAS) * share
-        squares_all = lax.psum(
+        squares = (
             jnp.sum(jnp.square(enc_grad))
             + jnp.sum(jnp.square(dec_grad))
-            + jnp.sum(jnp.square(table_grad)),
-            "fsdp",
-        )
-
-    dec_products = shampoo_products(dec_grad, dec_lr, dec_rr)
-    enc_products = shampoo_products(enc_grad, enc_lr, enc_rr)
-    dec_products, enc_products = lax.optimization_barrier((dec_products, enc_products))
+            + jnp.sum(jnp.square(table_grad))
+        ) / replica_count()
+    small = jnp.concatenate(small + [squares.reshape(1), jnp.zeros(126, jnp.float32)])
+    small = small.reshape(-1, LANES)
+    if paired:
+        small, top, low, enc_grad = hold((sum_replicas(small), top, low, enc_grad))
+        table_near = share_near(top, low)
+        small = sum_line(small)
+        enc_products = shampoo_products(enc_grad, *enc_ready[1:])
+        table_near, small, enc_products = hold((table_near, small, enc_products))
+        table_grad = placed_table(table_near, share_far(table_near), scale, half_rows) * share
+    else:
+        small = lax.psum(small, EVERYWHERE)
+    small = small.reshape(-1)
+    gain_grad = small[: 7 * D].reshape(7, D) * share
+    rel_grad = small[7 * D : 7 * D + 2 * NBK * H].reshape(2, NBK, H) * share
+    loss_sum = small[7 * D + 2 * NBK * H]
+    squares_all = small[7 * D + 2 * NBK * H + 1]
+    loss_count = jnp.maximum(count, 1.0)
+    if paired:
+        dec_ahead, enc_ahead = (dec_ready[0], enc_ready[0])
+    else:
+        dec_products, enc_products = hold((dec_products, enc_products))
+        dec_ahead, enc_ahead = (dec_ready[0], enc_ready[0])
     grad_norm = jnp.sqrt(
         squares_all + jnp.sum(gain_grad * gain_grad) + jnp.sum(rel_grad * rel_grad)
     )

time: 1480 us -> 1190 us (0.80)
  waiting for transfers between devices: 400 us -> 275 us
  starting transfers between devices: 159 us -> 41.8 us
  other arithmetic: 245 us -> 226 us
    ppermute x67 -> x23, waiting for transfers between devices: 220 us -> 40.7 us  [swap(): lax.ppermute(values, axis, [(place, place ^ 1) for place in range(size)])]
    all_gather x0 -> x4, waiting for transfers between devices: none -> 135 us  [the longest x2 135 us: gathered_weights(): lax.all_gather(pairs, EVERYWHERE if split else 'fsdp', axis=0, tiled=True)]
    ppermute x30 -> x3, waiting for transfers between devices: 119 us -> 1.2 us  [sum_line(): values = values + lax.ppermute(values, 'fsdp', moves)]
    ppermute x30 -> x3, starting transfers between devices: 73.8 us -> 4.15 us  [sum_line(): values = values + lax.ppermute(values, 'fsdp', moves)]
    ppermute x67 -> x23, starting transfers between devices: 85.3 us -> 27.4 us  [swap(): lax.ppermute(values, axis, [(place, place ^ 1) for place in range(size)])]
    reduce_scatter x1, waiting for transfers between devices: 0.01 us -> 51.5 us  [on_device(): lax.psum_scatter(found, 'fsdp', scatter_dimension=0, tiled=True)]
    reduce_scatter x1, waiting for transfers between devices: 39.3 us -> 22.5 us  [on_device(): lax.psum_scatter(jnp.dot(grad_logits, table, preferred_element_type=jnp.f...]
    unnamed x457 -> x428, local copies, waits for them, and re-layouts: 103 us -> 96.9 us
  transfers between devices with their start and end apart: 101 -> 36, of which waited for: 38 -> 15; matrix products, arithmetic and copies ran while one was open for 26% -> 33% of each run, Pallas kernels for 9% -> 11%
where the time goes in v4:
time: 1190 us; the launch traced here: 1180 us
  local copies, waits for them, and re-layouts  275 us (23%)
  waiting for transfers between devices  275 us (23%)
  other arithmetic  226 us (19%)
  Pallas kernels  207 us (17%)
  matrix products  100 us (8%)
  starting transfers between devices  41.8 us (4%)
  between operations  31.3 us (3%)
  blocking collectives  28.4 us (2%)
    all_gather x2, waiting for transfers between devices, gathered_weights(): lax.all_gather(pairs, EVERYWHERE if split else 'fsdp', axis=0, tiled=True)  135 us
    unnamed x428, local copies, waits for them, and re-layouts  96.9 us
    reshape x10, local copies, waits for them, and re-layouts, as_rows(): return blocks.reshape(blocks.shape[0], BLOCK * BLOCK)  62.9 us
    reduce_scatter x1, waiting for transfers between devices, on_device(): lax.psum_scatter(found, 'fsdp', scatter_dimension=0, tiled=True)  51.5 us
    scatter-add x1, other arithmetic, table_grads(): return dense.at[slots].add(grads.astype(jnp.float32), mode='drop')  44.5 us
    pallas_call x3, Pallas kernels, attend_back(): pl.pallas_call(functools.partial(attend_back_kernel, biased=bias is not N...  43.2 us
    ppermute x23, waiting for transfers between devices, swap(): lax.ppermute(values, axis, [(place, place ^ 1) for place in range(size)])  40.7 us
    reshape x6, local copies, waits for them, and re-layouts, as_blocks(): return flat.reshape(flat.shape[0], BLOCK, BLOCK)  38.1 us
  transfers between devices with their start and end apart: 36, of which 15 were waited for; matrix products, arithmetic and copies ran while one was open for 33% of the time, Pallas kernels for 11%

profile of v4, /device:TPU:0, one launch (start us, length us, event | category | flops | bytes accessed | tf_op | source)
XLA Modules:
  0.0 1184.8 jit_solution(8863100812647202040)
XLA Ops:
  18.4 7.8 convert_element_type.833
  26.4 14.2 %all-gather.2 = s32[8,1,896]{2,1,0:T(1,128)S(1)} all-gather(s32[1,1,896]{2,1,0:T(1,128)S(1)} %reshape.1383), channel_id=2, replica_groups=mesh['dp'=2,'fsdp'=8,'seq'=2] {'fsdp'}, dimensions={0}, use_global_device_ids=true | all-gather | bytes 32256 | tf_op jit(solution)/shard_map/all_gather | solution.py:930
  41.9 27.1 %gather_fusion = bf16[5120,768]{1,0:T(8,128)(2,1)} fusion(bf16[4016,768]{1,0:T(8,128)(2,1)} %convert_element_type.833, s32[5120]{0:T(1024)S(1)} %broadcast_clamp_fusion), kind=kCustom, calls=%fused_computation | custom fusion | bytes 15749120 | tf_op jit(solution)/shard_map/jit(_take)/gather | solution.py:500
  69.0 7.6 select_select_fusion
  76.6 45.5 %all-gather.11.cloned.1.call-done.pairs_ref = bf16[96,192,384]{2,1,0:T(8,128)(2,1)} async-done(((bf16[3,192,384]{2,1,0:T(8,128)(2,1)}), bf16[96,192,384]{2,1,0:T(8,128)(2,1)}) %all-gather.11.cloned.1.call-update) | async-done | bytes 14155792 | tf_op jit(solution)/shard_map/all_gather | solution.py:581
  156.4 51.5 %reduce-scatter.3.cloned.1.call-done = bf16[1,640,768]{2,1,0:T(8,128)(2,1)} async-done(((bf16[8,640,768]{2,1,0:T(8,128)(2,1)}), bf16[1,640,768]{2,1,0:T(8,128)(2,1)}) %reduce-scatter.3.cloned.1.call-update) | async-done | bytes 983056 | tf_op jit(solution)/shard_map/reduce_scatter | solution.py:939
  214.7 18.2 %shard_map.414 = bf16[1,512,768]{2,1,0:T(8,128)(2,1)S(1)} custom-call(bf16[1,512,2304]{2,1,0:T(8,128)(2,1)S(1)} %fusion.24.q_ref.k_ref.v_ref, bf16[1,512,2304]{2,1,0:T(8,128)(2,1)S(1)} %fusion.24.q_ref.k_ref.v_ref, bf16[1,512,2304]{2,1,0:T(8,128)(2,1)S(1)} %fusion.24.q_ref.k_ref.v_ref, f32[12,5,128,128]{3,2,1,0:T(8,128)S(1)} %bitcast.387, ...), custom_call_target="tpu_custom_call" | custom-call | flops 1610612736 | bytes 3145728 | tf_op jit(solution)/shard_map/pallas_call | solution.py:229
  244.8 89.5 %all-gather.13.cloned.1.call-done.pairs_ref = bf16[128,192,384]{2,1,0:T(8,128)(2,1)} async-done(((bf16[4,192,384]{2,1,0:T(8,128)(2,1)}), bf16[128,192,384]{2,1,0:T(8,128)(2,1)}) %all-gather.13.cloned.1.call-update) | async-done | bytes 18874384 | tf_op jit(solution)/shard_map/all_gather | solution.py:581
  374.1 23.3 %all-gather.15.cloned.1.call-done = bf16[1024,768]{1,0:T(8,128)(2,1)} async-done(((bf16[128,768]{1,0:T(8,128)(2,1)}), bf16[1024,768]{1,0:T(8,128)(2,1)}) %all-gather.15.cloned.1.call-update) | async-done | bytes 1572880 | tf_op jit(solution)/shard_map/all_gather | solution.py:989
  397.4 9.2 fusion.171
  411.1 14.1 %all-gather.3 = f32[8,3,1024]{2,1,0:T(4,128)S(1)} all-gather(f32[1,3,1024]{2,1,0:T(4,128)S(1)} %maximum_bitcast_fusion.2), channel_id=3, replica_groups=mesh['dp'=2,'fsdp'=8,'seq'=2] {'fsdp'}, dimensions={0}, use_global_device_ids=true | all-gather | bytes 110592 | tf_op jit(solution)/shard_map/all_gather | solution.py:996
  427.3 12.5 %fusion.160 = f32[1024,768]{1,0:T(8,128)} fusion(bf16[4016,768]{1,0:T(8,128)(2,1)} %convert_element_type.833, f32[1024,4016]{0,1:T(8,128)S(1)} %get-tuple-element.424, f32[1024]{0:T(1024)S(1)} %get-tuple-element.353, s32[1024]{0:T(1024)S(1)} %copy-done.158, f32[1024]{0:T(1024)S(1)} %copy-done.170), kind=kOutput, calls=%fused_computation.408 | convolution fusion | flops 6341296128 | bytes 25776128 | tf_op jit(solution)/shard_map/dot_general | solution.py:1009
  440.7 16.6 %abs_reduce_fusion = (f32[]{:T(128)}, f32[4016,768]{1,0:T(8,128)}) fusion(bf16[1024,768]{1,0:T(8,128)(2,1)} %all-gather.15.cloned.1.call-done, f32[1024,4016]{0,1:T(8,128)} %copy-done.84, f32[1024]{0:T(1024)} %copy-done.169, s32[1024]{0:T(1024)} %get-tuple-element.398, f32[1024]{0:T(1024)} %get-tuple-element.396), kind=kOutput, calls=%fused_computation.18 | convolution fusion | flops 6347464704 | bytes 30371844 | tf_op jit(solution)/shard_map/nv,nd->vd/dot_general | solution.py:1014
  457.3 22.5 %reduce-scatter.5.cloned.1.call-done = f32[128,768]{1,0:T(8,128)} async-done(((f32[1024,768]{1,0:T(8,128)}), f32[128,768]{1,0:T(8,128)}) %reduce-scatter.5.cloned.1.call-update) | async-done | bytes 393232 | tf_op jit(solution)/shard_map/reduce_scatter | solution.py:1008
  493.6 8.2 shard_map.424
  531.1 8.6 dynamic-slice_bitcast_fusion
  545.6 8.1 fusion.16.g_ref
  567.0 15.6 %shard_map.433 = (f32[4,2,4,96,384]{4,3,2,1,0:T(8,128)S(1)}, bf16[4,2,4,96,384]{4,3,2,1,0:T(8,128)(2,1)S(1)}, f32[4,2,4,96,384]{4,3,2,1,0:T(8,128)S(1)}, bf16[4,2,4,96,384]{4,3,2,1,0:T(8,128)(2,1)}) custom-call(s32[3]{0:T(128)S(1)} %pad_add_fusion.2.place_ref, bf16[32,4,192,384]{3,2,1,0:T(8,128)(2,1)} %bitcast.417, bf16[16,4,192,384]{3,2,1,0:T(8,128)(2,1)} %bitcast.453), custom_call_target="tpu_custom_call" | custom-call | flops 4718592 | bytes 47185920 | tf_op jit(solution)/shard_map/pallas_call | solution.py:632
  591.8 29.4 %shard_map.434 = (bf16[1,512,768]{2,1,0:T(8,128)(2,1)S(1)}, bf16[1,512,768]{2,1,0:T(8,128)(2,1)S(1)}, bf16[1,512,768]{2,1,0:T(8,128)(2,1)S(1)}, f32[12,5,128,128]{3,2,1,0:T(8,128)S(1)}) custom-call(bf16[1,512,2304]{2,1,0:T(8,128)(2,1)S(1)} %copy-done.6, bf16[1,512,2304]{2,1,0:T(8,128)(2,1)S(1)} %copy-done.6, bf16[1,512,2304]{2,1,0:T(8,128)(2,1)S(1)} %copy-done.6, ...), custom_call_target="tpu_custom_call" | custom-call | flops 4026531840 | bytes 7864320 | tf_op jit(solution)/shard_map/pallas_call | solution.py:257
  628.9 13.7 %collective-permute-done.4 = bf16[4,2,4,96,384]{4,3,2,0,1:T(8,128)(2,1)} collective-permute-done((bf16[4,2,4,96,384]{4,3,2,0,1:T(8,128)(2,1)}, bf16[4,2,4,96,384]{4,3,2,0,1:T(8,128)(2,1)}, u32[]{:S(2)}, u32[]{:S(2)}) %collective-permute-start.4) | collective-permute-done | bytes 2359328 | tf_op jit(solution)/shard_map/ppermute | solution.py:532
  673.4 6.8 shard_map.438
  686.7 11.8 collective-permute-done.8
  698.5 12.2 %shard_map.439 = (f32[4,2,3,96,384]{4,3,2,1,0:T(8,128)S(1)}, bf16[4,2,3,96,384]{4,3,2,1,0:T(8,128)(2,1)S(1)}, f32[4,2,3,96,384]{4,3,2,1,0:T(8,128)S(1)}, bf16[4,2,3,96,384]{4,3,2,1,0:T(8,128)(2,1)}) custom-call(s32[3]{0:T(128)S(1)} %pad_add_fusion.2.place_ref, bf16[32,3,192,384]{3,2,1,0:T(8,128)(2,1)} %bitcast.419, bf16[16,3,192,384]{3,2,1,0:T(8,128)(2,1)S(1)} %bitcast.389), custom_call_target="tpu_custom_call" | custom-call | flops 3538944 | bytes 35389440 | tf_op jit(solution)/shard_map/pallas_call | solution.py:632
  740.5 8.1 shard_map.440
  782.4 44.5 %scatter_custom_fusion = f32[4016,768]{1,0:T(8,128)} fusion(f32[4016,768]{1,0:T(8,128)} %get-tuple-element.214, s32[5120]{0:T(1024)} %bitcast.473, bf16[5120,768]{1,0:T(8,128)(2,1)} %all-gather.17.cloned.1.call-done), kind=kCustom, calls=%fused_computation.9 | custom fusion | flops 7864320 | bytes 20201472 | tf_op jit(solution)/shard_map/scatter-add | solution.py:509
  843.0 8.2 multiply_convert_fusion.2
  864.1 6.8 reshape.1286.lr_ref
  870.9 6.7 reshape.1287.rr_ref
  889.8 14.3 %shard_map.441 = f32[32,192,192]{2,1,0:T(8,128)S(1)} custom-call(f32[32,192,192]{2,1,0:T(8,128)S(1)} %copy-done.4, f32[32,192,192]{2,1,0:T(8,128)S(1)} %copy-done.2, f32[32,192,192]{2,1,0:T(8,128)} %reshape.1287.rr_ref), custom_call_target="tpu_custom_call" | custom-call | flops 2717908992 | bytes 18874368 | tf_op jit(solution)/shard_map/pallas_call | solution.py:430
  943.4 20.3 %shard_map.442 = (f32[32,192,192]{2,1,0:T(8,128)S(1)}, f32[32,192,192]{2,1,0:T(8,128)S(1)}, f32[32,192,192]{2,1,0:T(8,128)}, f32[32,192,192]{2,1,0:T(8,128)}) custom-call(f32[16,192,384]{2,1,0:T(8,128)S(1)} %copy-done.25, f32[32,192,192]{2,1,0:T(8,128)} %reshape.1286.lr_ref, f32[32,192,192]{2,1,0:T(8,128)} %reshape.1287.rr_ref), custom_call_target="tpu_custom_call" | custom-call | flops 5435817984 | bytes 33030144 | tf_op jit(solution)/shard_map/pallas_call | solution.py:445
  1036.9 13.8 %shard_map.443 = (f32[24,192,192]{2,1,0:T(8,128)S(1)}, f32[24,192,192]{2,1,0:T(8,128)S(1)}, f32[24,192,192]{2,1,0:T(8,128)S(1)}, f32[24,192,192]{2,1,0:T(8,128)S(1)}) custom-call(f32[12,192,384]{2,1,0:T(8,128)S(1)} %convert_multiply_fusion.1.g_ref, f32[24,192,192]{2,1,0:T(8,128)} %reshape.1282.lr_ref, f32[24,192,192]{2,1,0:T(8,128)} %reshape.1283.rr_ref), custom_call_target="tpu_custom_call" | custom-call | flops 4076863488 | bytes 24772608 | tf_op jit(solution)/shard_map/pallas_call | solution.py:445
  1144.9 30.3 %multiply_subtract_fusion = (f32[4016,768]{1,0:T(8,128)}, f32[4016,768]{1,0:T(8,128)}, f32[4016,768]{1,0:T(8,128)}) fusion(f32[4016,768]{1,0:T(8,128)} %param.33, f32[]{:T(128)S(6)} %min.40, f32[]{:T(128)S(6)} %div.121, f32[]{:T(128)S(6)} %div.123, f16[1008,384]{1,0:T(8,128)(2,1)S(1)} %get-tuple-element.373, f16[1008,384]{1,0:T(8,128)(2,1)S(1)} %get-tuple-element.372, ...), kind=kLoop, calls=%fused_computation.15 | loop fusion | flops 104865792 | bytes 80216080 | tf_op jit(solution)/shard_map/sub | solution.py:850
  (746 shorter events, 526.5 us)
Async XLA Ops:
  7.2 115.0 %all-gather.11.cloned.1.call-start = ((), (), s32[]{:S(2)}) async-start(), calls=%async_computation.4 | async-start | bytes 14598144 | tf_op jit(solution)/shard_map/all_gather | solution.py:581
  8.6 9.7 collective-permute-start
  18.4 189.5 %reduce-scatter.3.cloned.1.call-start = ((), (), s32[]{:S(2)}) async-start(), calls=%async_computation.5 | async-start | bytes 8847360 | tf_op jit(solution)/shard_map/reduce_scatter | solution.py:939
  122.2 212.2 %all-gather.13.cloned.1.call-start = ((), (), s32[]{:S(2)}) async-start(), calls=%async_computation.6 | async-start | bytes 19464192 | tf_op jit(solution)/shard_map/all_gather | solution.py:581
  122.9 274.5 %all-gather.15.cloned.1.call-start = ((), (), s32[]{:S(2)}) async-start(), calls=%async_computation.7 | async-start | bytes 1769472 | tf_op jit(solution)/shard_map/all_gather | solution.py:989
  374.1 105.7 %reduce-scatter.5.cloned.1.call-start = ((), (), s32[]{:S(2)}) async-start(), calls=%async_computation.8 | async-start | bytes 3538944 | tf_op jit(solution)/shard_map/reduce_scatter | solution.py:1008
  439.7 317.1 %all-gather.17.cloned.1.call-start = ((), (), s32[]{:S(2)}) async-start(), calls=%async_computation.9 | async-start | bytes 8847360 | tf_op jit(solution)/shard_map/all_gather | solution.py:1085
  539.7 23.6 %collective-permute-start.3 = (bf16[4,16,192,384]{3,2,1,0:T(8,128)(2,1)}, bf16[4,16,192,384]{3,2,1,0:T(8,128)(2,1)S(1)}, u32[]{:S(2)}, u32[]{:S(2)}) collective-permute-start(bf16[4,16,192,384]{3,2,1,0:T(8,128)(2,1)} %dynamic-slice_bitcast_fusion), channel_id=1, source_target_pairs={{0,2},{2,0},{4,6},{6,4},{8,10},{10,8},{12,14},{14,12},{1,3},{3,1},... | collective-permute-start | bytes 28311560 | tf_op jit(solution)/shard_map/ppermute | solution.py:532
  588.6 54.0 %collective-permute-start.4 = (bf16[4,2,4,96,384]{4,3,2,0,1:T(8,128)(2,1)}, bf16[4,2,4,96,384]{4,3,2,0,1:T(8,128)(2,1)}, u32[]{:S(2)}, u32[]{:S(2)}) collective-permute-start(bf16[4,2,4,96,384]{4,3,2,0,1:T(8,128)(2,1)} %copy.102), channel_id=1, source_target_pairs={{0,1},{1,0},{2,3},{3,2},{4,5},{5,4},{6,7},{7,6},{8,9},{9,8},{10,11... | collective-permute-start | bytes 7077896 | tf_op jit(solution)/shard_map/ppermute | solution.py:532
  590.1 53.7 %collective-permute-start.5 = (bf16[4,2,4,96,384]{4,3,2,1,0:T(8,128)(2,1)}, bf16[4,2,4,96,384]{4,3,2,1,0:T(8,128)(2,1)}, u32[]{:S(2)}, u32[]{:S(2)}) collective-permute-start(bf16[4,2,4,96,384]{4,3,2,1,0:T(8,128)(2,1)} %get-tuple-element.185), channel_id=1, source_target_pairs={{0,16},{16,0},{1,17},{17,1},{2,18},{18,2},{3,19},{19,3},{4,20},{20... | collective-permute-start | bytes 7077896 | tf_op jit(solution)/shard_map/ppermute | solution.py:532
  649.0 31.1 %collective-permute-start.6 = (bf16[4,4,96,384]{3,2,1,0:T(8,128)(2,1)}, bf16[4,4,96,384]{3,2,1,0:T(8,128)(2,1)}, u32[]{:S(2)}, u32[]{:S(2)}) collective-permute-start(bf16[4,4,96,384]{3,2,1,0:T(8,128)(2,1)} %fusion.51), channel_id=1, source_target_pairs={{0,16},{16,0},{1,17},{17,1},{2,18},{18,2},{3,19},{19,3},{4,20},{20... | collective-permute-start | bytes 3538952 | tf_op jit(solution)/shard_map/ppermute | solution.py:532
  655.8 27.0 %collective-permute-start.7 = (bf16[4,4,96,384]{3,2,1,0:T(8,128)(2,1)}, bf16[4,4,96,384]{3,2,1,0:T(8,128)(2,1)}, u32[]{:S(2)}, u32[]{:S(2)}) collective-permute-start(bf16[4,4,96,384]{3,2,1,0:T(8,128)(2,1)} %fusion.52), channel_id=1, source_target_pairs={{0,1},{1,0},{2,3},{3,2},{4,5},{5,4},{6,7},{7,6},{8,9},{9,8},{10,11... | collective-permute-start | bytes 3538952 | tf_op jit(solution)/shard_map/ppermute | solution.py:532
  686.6 11.9 %collective-permute-start.8 = (bf16[4,12,192,384]{3,2,1,0:T(8,128)(2,1)S(1)}, bf16[4,12,192,384]{3,2,1,0:T(8,128)(2,1)S(1)}, u32[]{:S(2)}, u32[]{:S(2)}) collective-permute-start(bf16[4,12,192,384]{3,2,1,0:T(8,128)(2,1)S(1)} %dynamic-slice_bitcast_fusion.1), channel_id=1, source_target_pairs={{0,2},{2,0},{4,6},{6,4},{8,10},{10,8},{12,14},{14,12},{1,3},{3,1},... | collective-permute-start | bytes 21233672 | tf_op jit(solution)/shard_map/ppermute | solution.py:532
  713.9 43.0 %collective-permute-start.9 = (bf16[4,2,3,96,384]{4,3,2,0,1:T(8,128)(2,1)}, bf16[4,2,3,96,384]{4,3,2,0,1:T(8,128)(2,1)}, u32[]{:S(2)}, u32[]{:S(2)}) collective-permute-start(bf16[4,2,3,96,384]{4,3,2,0,1:T(8,128)(2,1)} %copy.104), channel_id=1, source_target_pairs={{0,1},{1,0},{2,3},{3,2},{4,5},{5,4},{6,7},{7,6},{8,9},{9,8},{10,11... | collective-permute-start | bytes 5308424 | tf_op jit(solution)/shard_map/ppermute | solution.py:532
  714.3 42.5 %collective-permute-start.10 = (bf16[4,2,3,96,384]{4,3,2,1,0:T(8,128)(2,1)}, bf16[4,2,3,96,384]{4,3,2,1,0:T(8,128)(2,1)}, u32[]{:S(2)}, u32[]{:S(2)}) collective-permute-start(bf16[4,2,3,96,384]{4,3,2,1,0:T(8,128)(2,1)} %get-tuple-element.198), channel_id=1, source_target_pairs={{0,16},{16,0},{1,17},{17,1},{2,18},{18,2},{3,19},{19,3},{4,20},{20... | collective-permute-start | bytes 5308424 | tf_op jit(solution)/shard_map/ppermute | solution.py:532
  762.3 67.4 %all-to-all-start = ((bf16[4,4,192,384]{3,2,1,0:T(8,128)(2,1)}), bf16[4,4,192,384]{3,2,1,0:T(8,128)(2,1)}, u32[]{:S(2)}, u32[]{:S(2)}) async-start(bf16[4,4,192,384]{3,2,1,0:T(8,128)(2,1)} %pad_maximum_fusion), calls=%async_computation.2 | async-start | bytes 4718592 | tf_op jit(solution)/shard_map/all_to_all | solution.py:733
  766.8 152.6 %all-gather.19.cloned.1.call-start = ((), (), s32[]{:S(2)}) async-start(), calls=%async_computation.10 | async-start | bytes 2949120 | tf_op jit(solution)/shard_map/all_gather | solution.py:741
  772.6 57.1 %collective-permute-start.11 = (bf16[4,3,96,384]{3,2,1,0:T(8,128)(2,1)}, bf16[4,3,96,384]{3,2,1,0:T(8,128)(2,1)}, u32[]{:S(2)}, u32[]{:S(2)}) collective-permute-start(bf16[4,3,96,384]{3,2,1,0:T(8,128)(2,1)} %fusion.60), channel_id=1, source_target_pairs={{0,16},{16,0},{1,17},{17,1},{2,18},{18,2},{3,19},{19,3},{4,20},{20... | collective-permute-start | bytes 2654216 | tf_op jit(solution)/shard_map/ppermute | solution.py:532
  778.0 51.7 %collective-permute-start.12 = (bf16[4,3,96,384]{3,2,1,0:T(8,128)(2,1)}, bf16[4,3,96,384]{3,2,1,0:T(8,128)(2,1)}, u32[]{:S(2)}, u32[]{:S(2)}) collective-permute-start(bf16[4,3,96,384]{3,2,1,0:T(8,128)(2,1)} %fusion.61), channel_id=1, source_target_pairs={{0,1},{1,0},{2,3},{3,2},{4,5},{5,4},{6,7},{7,6},{8,9},{9,8},{10,11... | collective-permute-start | bytes 2654216 | tf_op jit(solution)/shard_map/ppermute | solution.py:532
  837.9 85.8 %all-to-all-start.1 = ((bf16[4,3,192,384]{3,2,1,0:T(8,128)(2,1)}), bf16[4,3,192,384]{3,2,1,0:T(8,128)(2,1)}, u32[]{:S(2)}, u32[]{:S(2)}) async-start(bf16[4,3,192,384]{3,2,1,0:T(8,128)(2,1)} %pad_maximum_fusion.1), calls=%async_computation.3 | async-start | bytes 3538944 | tf_op jit(solution)/shard_map/all_to_all | solution.py:733
  842.9 177.3 %all-gather.21.cloned.1.call-start = ((), (), s32[]{:S(2)}) async-start(), calls=%async_computation.11 | async-start | bytes 2211840 | tf_op jit(solution)/shard_map/all_gather | solution.py:741
  852.8 60.7 %collective-permute-start.13 = (f16[1016,768]{1,0:T(8,128)(2,1)}, f16[1016,768]{1,0:T(8,128)(2,1)}, u32[]{:S(2)}, u32[]{:S(2)}) collective-permute-start(f16[1016,768]{1,0:T(8,128)(2,1)} %concatenate.100), channel_id=1, source_target_pairs={{0,1},{1,0},{2,3},{3,2},{4,5},{5,4},{6,7},{7,6},{8,9},{9,8},{10,11... | collective-permute-start | bytes 4681736 | tf_op jit(solution)/shard_map/ppermute | solution.py:532
  854.8 60.6 %collective-permute-start.14 = (f16[1016,768]{1,0:T(8,128)(2,1)}, f16[1016,768]{1,0:T(8,128)(2,1)S(1)}, u32[]{:S(2)}, u32[]{:S(2)}) collective-permute-start(f16[1016,768]{1,0:T(8,128)(2,1)} %concatenate.101), channel_id=1, source_target_pairs={{0,16},{16,0},{1,17},{17,1},{2,18},{18,2},{3,19},{19,3},{4,20},{20... | collective-permute-start | bytes 4681736 | tf_op jit(solution)/shard_map/ppermute | solution.py:532
  930.6 66.1 %collective-permute-start.15 = (f16[1016,384]{1,0:T(8,128)(2,1)}, f16[1016,384]{1,0:T(8,128)(2,1)}, u32[]{:S(2)}, u32[]{:S(2)}) collective-permute-start(f16[1016,384]{1,0:T(8,128)(2,1)} %concatenate.103), channel_id=1, source_target_pairs={{0,16},{16,0},{1,17},{17,1},{2,18},{18,2},{3,19},{19,3},{4,20},{20... | collective-permute-start | bytes 2340872 | tf_op jit(solution)/shard_map/ppermute | solution.py:532
  933.8 64.8 %collective-permute-start.16 = (f16[1016,384]{1,0:T(8,128)(2,1)}, f16[1016,384]{1,0:T(8,128)(2,1)}, u32[]{:S(2)}, u32[]{:S(2)}) collective-permute-start(f16[1016,384]{1,0:T(8,128)(2,1)} %concatenate.104), channel_id=1, source_target_pairs={{0,1},{1,0},{2,3},{3,2},{4,5},{5,4},{6,7},{7,6},{8,9},{9,8},{10,11... | collective-permute-start | bytes 2340872 | tf_op jit(solution)/shard_map/ppermute | solution.py:532
  1011.9 3.9 collective-permute-start.17
  1023.2 61.0 %collective-permute-start.20 = (f16[1008,384]{1,0:T(8,128)(2,1)}, f16[1008,384]{1,0:T(8,128)(2,1)}, u32[]{:S(2)}, u32[]{:S(2)}) collective-permute-start(f16[1008,384]{1,0:T(8,128)(2,1)} %convert_element_type.977), channel_id=1, source_target_pairs={{0,1},{1,0},{2,3},{3,2},{4,5},{5,4},{6,7},{7,6},{8,9},{9,8},{10,11... | collective-permute-start | bytes 2322440 | tf_op jit(solution)/shard_map/ppermute | solution.py:532
  1024.8 61.3 %collective-permute-start.19 = (f16[1008,384]{1,0:T(8,128)(2,1)}, f16[1008,384]{1,0:T(8,128)(2,1)}, u32[]{:S(2)}, u32[]{:S(2)}) collective-permute-start(f16[1008,384]{1,0:T(8,128)(2,1)} %convert_element_type.976), channel_id=1, source_target_pairs={{0,16},{16,0},{1,17},{17,1},{2,18},{18,2},{3,19},{19,3},{4,20},{20... | collective-permute-start | bytes 2322440 | tf_op jit(solution)/shard_map/ppermute | solution.py:532
  1027.8 5.3 collective-permute-start.22
  1034.5 48.9 %collective-permute-start.23 = (f32[49,128]{1,0:T(8,128)}, f32[49,128]{1,0:T(8,128)}, u32[]{:S(2)}, u32[]{:S(2)}) collective-permute-start(f32[49,128]{1,0:T(8,128)} %add.1021), channel_id=1, source_target_pairs={{0,8},{2,10},{4,12},{6,14},{8,0},{10,2},{12,4},{14,6},{1,9},{3,11}... | collective-permute-start | bytes 75272 | tf_op jit(solution)/shard_map/ppermute | solution.py:691
  1104.1 35.7 %collective-permute-start.24 = (f16[2,1008,384]{2,1,0:T(8,128)(2,1)}, f16[2,1008,384]{2,1,0:T(8,128)(2,1)}, u32[]{:S(2)}, u32[]{:S(2)}) collective-permute-start(f16[2,1008,384]{2,1,0:T(8,128)(2,1)} %pad_maximum_fusion.2), channel_id=1, source_target_pairs={{0,1},{1,0},{2,3},{3,2},{4,5},{5,4},{6,7},{7,6},{8,9},{9,8},{10,11... | collective-permute-start | bytes 4644872 | tf_op jit(solution)/shard_map/ppermute | solution.py:532
  1105.6 37.0 %collective-permute-start.25 = (f16[2,1008,384]{2,1,0:T(8,128)(2,1)S(1)}, f16[2,1008,384]{2,1,0:T(8,128)(2,1)}, u32[]{:S(2)}, u32[]{:S(2)}) collective-permute-start(f16[2,1008,384]{2,1,0:T(8,128)(2,1)S(1)} %pad_maximum_fusion.3), channel_id=1, source_target_pairs={{0,16},{16,0},{1,17},{17,1},{2,18},{18,2},{3,19},{19,3},{4,20},{20... | collective-permute-start | bytes 4644872 | tf_op jit(solution)/shard_map/ppermute | solution.py:532
  (210 other events, 1613.3 us)
Sparse Core Ops, SparseCore 0:
  18.5 103.6 all-gather.10
  125.0 82.7 reduce-scatter.2
  211.3 123.0 all-gather.12
  374.2 23.2 all-gather.14
  439.9 39.9 reduce-scatter.4
  644.0 75.6 all-gather.16
  833.9 49.8 all-gather.18
  927.6 38.8 all-gather.20

commit v5 on v4

--- a/solution.py
+++ b/solution.py
@@ -434,9 +434,9 @@
         in_specs=[spec] * 3,
         out_specs=spec,
         cost_estimate=block_cost(amount, 2, 4),
-        compiler_params=pltpu.CompilerParams(vmem_limit_bytes=32 << 20),
+        compiler_params=pltpu.CompilerParams(vmem_limit_bytes=52 << 20),
     )(*blocks)
-    return as_rows(ahead), blocks[1], blocks[2]
+    return ahead, blocks[1], blocks[2]
 
 
 def shampoo_products(pairs, left_root, right_root):
@@ -449,7 +449,7 @@
         in_specs=[pl.BlockSpec((1, BLOCK, PAIR), lambda pair: (pair, 0, 0)), spec, spec],
         out_specs=[spec] * 4,
         cost_estimate=block_cost(amount, 4, 7),
-        compiler_params=pltpu.CompilerParams(vmem_limit_bytes=32 << 20),
+        compiler_params=pltpu.CompilerParams(vmem_limit_bytes=52 << 20),
     )(pairs, left_root, right_root)
     return [as_rows(result) for result in results]
 
@@ -574,6 +574,102 @@
 
 def hold(values):
     return lax.optimization_barrier(values)
+
+
+def chip_groups():
+    return [list(range(core, lax.axis_size("fsdp"), 2)) for core in range(2)]
+
+
+def along_line(own):
+    n_chips = lax.axis_size("fsdp") // 2
+    copies = jnp.broadcast_to(own[None], (n_chips,) + own.shape)
+    return lax.all_to_all(copies, "fsdp", 0, 0, axis_index_groups=chip_groups(), tiled=True)
+
+
+def exchange_near(line):
+    mid = BLOCK // 2
+    upper, lower = (line[:, :, :mid], line[:, :, mid:])
+    return [upper, lower, swap(upper, "seq"), swap(lower, "dp")]
+
+
+def exchange_far(near):
+    upper, lower, upper_half, lower_side = near
+    return [
+        swap(jnp.stack([lower, lower_side]), "seq"),
+        swap(jnp.stack([upper, upper_half]), "dp"),
+    ]
+
+
+def swap_cores(pieces):
+    return [swap(piece, "fsdp") for piece in pieces]
+
+
+def assemble_kernel(place_ref, *refs, shapes):
+    outs = refs[12 : 12 + len(shapes)]
+    buffer, in_sems, out_sems = refs[12 + len(shapes) :]
+    core, side, half = (place_ref[0], place_ref[1], place_ref[2])
+    n_chips, quarter, mid, _ = refs[0].shape
+    copies = []
+    for other in range(2):
+        upper, lower, upper_half, lower_side, by_half, by_side = refs[6 * other : 6 * other + 6]
+        pieces = [
+            (upper, lower),
+            (upper_half, by_half.at[0]),
+            (by_side.at[0], lower_side),
+            (by_side.at[1], by_half.at[1]),
+        ]
+        for place, both in enumerate(pieces):
+            owner = ((side ^ (place // 2)) * 2 + (half ^ (place % 2))) * quarter
+            for low, piece in enumerate(both):
+                for chip in range(n_chips):
+                    first = (2 * chip + (core ^ other)) * (4 * quarter) + owner
+                    copies.append(
+                        pltpu.make_async_copy(
+                            piece.at[chip],
+                            buffer.at[pl.ds(first, quarter), pl.ds(low * mid, mid), :],
+                            in_sems.at[len(copies)],
+                        )
+                    )
+    for copy in copies:
+        copy.start()
+    for copy in copies:
+        copy.wait()
+    copies = []
+    for out_ref, (height, breadth) in zip(outs, shapes):
+        for row in range(height // BLOCK):
+            for column in range(breadth // PAIR):
+                copies.append(
+                    pltpu.make_async_copy(
+                        buffer.at[len(copies)],
+                        out_ref.at[pl.ds(row * BLOCK, BLOCK), pl.ds(column * PAIR, PAIR)],
+                        out_sems.at[len(copies)],
+                    )
+                )
+    for copy in copies:
+        copy.start()
+    for copy in copies:
+        copy.wait()
+
+
+def assembled(pieces, shapes):
+    n_chips, quarter, mid, _ = pieces[0].shape
+    total = 8 * n_chips * quarter
+    return pl.pallas_call(
+        functools.partial(assemble_kernel, shapes=shapes),
+        out_shape=[jax.ShapeDtypeStruct(shape, jnp.bfloat16) for shape in shapes],
+        in_specs=[pl.BlockSpec(memory_space=pltpu.SMEM)]
+        + [pl.BlockSpec(memory_space=pl.ANY)] * len(pieces),
+        out_specs=[pl.BlockSpec(memory_space=pl.ANY)] * len(shapes),
+        scratch_shapes=[
+            pltpu.VMEM((total, BLOCK, PAIR), jnp.bfloat16),
+            pltpu.SemaphoreType.DMA((16 * n_chips,)),
+            pltpu.SemaphoreType.DMA((total,)),
+        ],
+        cost_estimate=pl.CostEstimate(
+            flops=0, bytes_accessed=4 * total * BLOCK * PAIR, transcendentals=0
+        ),
+        compiler_params=pltpu.CompilerParams(vmem_limit_bytes=30 << 20),
+    )(own_place(), *pieces)
 
 
 def gathered_weights(pairs, amount):
@@ -727,10 +823,8 @@
 
 
 def line_sums(far):
-    size = lax.axis_size("fsdp")
     line = narrow(jnp.concatenate([far[0] + wide(far[1]), far[2] + wide(far[3])], axis=2))
-    cores = [list(range(core, size, 2)) for core in range(2)]
-    return lax.all_to_all(line, "fsdp", 0, 0, axis_index_groups=cores, tiled=True)
+    return lax.all_to_all(line, "fsdp", 0, 0, axis_index_groups=chip_groups(), tiled=True)
 
 
 def line_total(arrived):
@@ -756,9 +850,12 @@
     return jnp.exp2(power.astype(jnp.float32))
 
 
-def scaled_swap(values, power, axis):
+def message_of(values, power):
     mark = jnp.full((SCALE_ROWS, values.shape[1]), power, jnp.float16)
-    message = jnp.concatenate([values.astype(jnp.float16), mark], axis=0)
+    return jnp.concatenate([values.astype(jnp.float16), mark], axis=0)
+
+
+def scaled_swap(message, axis):
     got = swap(message, axis)
     return got[:-SCALE_ROWS], got[-1, 0].astype(jnp.float32)
 
@@ -772,7 +869,7 @@
     )
 
 
-def near_table(partial, bound):
+def near_parts(partial, bound):
     side, half = (lax.axis_index("dp"), lax.axis_index("seq"))
     half_rows = partial.shape[0] // 2
     window = window_rows(half_rows)
@@ -784,11 +881,16 @@
 
     return [
         rows_of(0, half),
-        scaled_swap(rows_of(0, 1 - half), power, "seq"),
+        message_of(rows_of(0, 1 - half), power),
         rows_of(half_rows, side),
-        scaled_swap(rows_of(half_rows, 1 - side), power, "dp"),
+        message_of(rows_of(half_rows, 1 - side), power),
         power,
     ]
+
+
+def near_table(parts):
+    top, top_sent, low, low_sent, power = parts
+    return [top, scaled_swap(top_sent, "seq"), low, scaled_swap(low_sent, "dp"), power]
 
 
 def far_table(near):
@@ -798,10 +900,10 @@
     return [
         half_lanes(top, side),
         top_power,
-        scaled_swap(half_lanes(top, 1 - side), top_power, "dp"),
+        scaled_swap(message_of(half_lanes(top, 1 - side), top_power), "dp"),
         half_lanes(low, half),
         low_power,
-        scaled_swap(half_lanes(low, 1 - half), low_power, "seq"),
+        scaled_swap(message_of(half_lanes(low, 1 - half), low_power), "seq"),
     ]
 
 
@@ -928,6 +1030,9 @@
     ).reshape(1, -1)
     enc_pairs = gathered_weights(enc_own, enc_w.shape[0])
     gathered = lax.all_gather(message, "fsdp", axis=0, tiled=True)
+    gathered, dec_own = hold((gathered, dec_own))
+    if paired:
+        dec_line = along_line(dec_own)
     all_enc = gathered[:, : rows * enc_len]
     rest = gathered[:, rows * enc_len :].reshape(n_fsdp, 3, rows * dec_len)
     all_dec, all_targets, all_weights = (rest[:, 0], rest[:, 1], rest[:, 2])
@@ -935,15 +1040,37 @@
     vocab_local = table.shape[0]
     vocab_first = fsdp_rank * vocab_local
     found = table_rows(table, all_tokens, vocab_first)
-    found, enc_pairs, dec_own = hold((found, enc_pairs, dec_own))
-    looked_up = lax.psum_scatter(found, "fsdp", scatter_dimension=0, tiled=True).reshape(-1, D)
-    dec_pairs = gathered_weights(dec_own, dec_w.shape[0])
-    enc_mats = matrices_of(enc_pairs, layer_shapes(False))
+    enc_roots = (enc_m, enc_lroot, enc_rroot)
+    dec_roots = (dec_m, dec_lroot, dec_rroot)
+    found, enc_roots = hold((found, enc_roots))
+    enc_ready = shampoo_ahead(*enc_roots)
+    enc_ready, dec_roots = hold((enc_ready, dec_roots))
+    dec_ready = shampoo_ahead(*dec_roots)
     enc_onehot = tile_onehot(enc_len // TILE, False)
     dec_onehot = tile_onehot(dec_len // TILE, True)
-    looked_up, enc_mats, enc_bias, dec_bias = hold(
-        (looked_up, enc_mats, tile_bias(enc_onehot, rel_bias[0]), tile_bias(dec_onehot, rel_bias[1]))
-    )
+    if paired:
+        found, enc_pairs, enc_ready, dec_line, rel_tiles, dec_ready = hold(
+            (found, enc_pairs, enc_ready, dec_line, rel_bias, dec_ready)
+        )
+    else:
+        found, enc_pairs, rel_tiles = hold((found, enc_pairs, rel_bias))
+    looked_up = lax.psum_scatter(found, "fsdp", scatter_dimension=0, tiled=True).reshape(-1, D)
+    enc_mats = matrices_of(enc_pairs, layer_shapes(False))
+    enc_bias = tile_bias(enc_onehot, rel_tiles[0])
+    dec_bias = tile_bias(dec_onehot, rel_tiles[1])
+    if paired:
+        dec_near = exchange_near(dec_line)
+        enc_ahead, dec_ahead = (as_rows(enc_ready[0]), as_rows(dec_ready[0]))
+        dec_near, enc_mats, enc_bias, dec_bias, enc_ahead = hold(
+            (dec_near, enc_mats, enc_bias, dec_bias, enc_ahead)
+        )
+        dec_far = exchange_far(dec_near)
+        dec_cores = swap_cores(dec_near)
+        looked_up, dec_far, dec_cores, dec_ahead = hold((looked_up, dec_far, dec_cores, dec_ahead))
+        dec_cores = dec_cores + swap_cores(dec_far)
+    else:
+        dec_mats = matrices_of(gathered_weights(dec_own, dec_w.shape[0]), layer_shapes(True))
+        enc_ahead, dec_ahead = (as_rows(enc_ready[0]), as_rows(dec_ready[0]))
     hidden0 = looked_up[: rows * enc_len].reshape(rows, enc_len, D).astype(jnp.float32)
     state0 = looked_up[rows * enc_len :].reshape(rows, dec_len, D).astype(jnp.float32)
 
@@ -959,15 +1086,9 @@
     hidden1 = hidden0 + project(enc_attended, enc_mats[1])
     hidden2, enc_cache = ff_forward(hidden1, gains[1], enc_mats[2], enc_mats[3])
     encoded = rms(hidden2, gains[2]).astype(jnp.bfloat16)
-    count = jnp.sum(all_weights).astype(jnp.float32)
     if paired:
-        count = count + swap(count, "seq")
-        count = count + swap(count, "dp")
-    else:
-        count = lax.psum(count, REPLICAS)
-    encoded, count, dec_pairs = hold((encoded, count, dec_pairs))
-    share = 1.0 / jnp.maximum(count, 1.0)
-    dec_mats = matrices_of(dec_pairs, layer_shapes(True))
+        encoded, dec_cores = hold((encoded, dec_cores))
+        dec_mats = assembled(dec_near + dec_far + dec_cores, layer_shapes(True))
     pairs = project(encoded, dec_mats[3]).astype(jnp.bfloat16)
 
     normed3 = rms(state0, gains[3]).astype(jnp.bfloat16)
@@ -1011,9 +1132,17 @@
         scatter_dimension=0,
         tiled=True,
     ).reshape(rows, dec_len, D)
+    count = jnp.sum(all_weights).astype(jnp.float32)
+    if paired:
+        count, _ = hold((count, group_loss))
+        count = count + swap(count, "seq")
+        count = count + swap(count, "dp")
+    else:
+        count = lax.psum(count, REPLICAS)
+    share = 1.0 / jnp.maximum(count, 1.0)
     dense_grad = jnp.einsum("nv,nd->vd", grad_logits, all_final, preferred_element_type=jnp.float32)
-    grad_final, dense_grad, dense_bound = hold(
-        (grad_final, dense_grad, jnp.max(jnp.abs(dense_grad)))
+    grad_final, dense_grad, dense_bound, share = hold(
+        (grad_final, dense_grad, jnp.max(jnp.abs(dense_grad)), share)
     )
 
     grad_state3, gain_six = rms_back(state3, gains[6], grad_final * out_scale)
@@ -1094,21 +1223,12 @@
     if paired:
         encoder_portion, dec_far_sums = hold((encoder_portion, dec_far_sums))
         enc_got = swap_halves(encoder_portion)
-        enc_got, encoder_portion, enc_roots = hold(
-            (enc_got, encoder_portion, (enc_m, enc_lroot, enc_rroot))
-        )
+        enc_got, encoder_portion = hold((enc_got, encoder_portion))
         enc_folded = hold(fold_blocks(encoder_portion, enc_got))
         enc_close = near_sums(enc_folded)
-        enc_ready = shampoo_ahead(*enc_roots)
-        back_all, enc_close, enc_ready, dec_far_sums = hold(
-            (back_all, enc_close, enc_ready, dec_far_sums)
-        )
+        back_all, enc_folded, dec_far_sums = hold((back_all, enc_folded, dec_far_sums))
         dec_arrived = line_sums(dec_far_sums)
-        enc_far_sums = far_sums(enc_close)
         bound = dense_bound + back_all.shape[0] * jnp.max(jnp.abs(back_all)).astype(jnp.float32)
-    else:
-        enc_ready = shampoo_ahead(enc_m, enc_lroot, enc_rroot)
-        dec_ready = shampoo_ahead(dec_m, dec_lroot, dec_rroot)
     emb_grad = table_grads(back_all, all_tokens, vocab_first, dense_grad)
     gain_part = jnp.stack(
         [gain_zero, gain_one, gain_two, gain_three, gain_four, gain_five, gain_six]
@@ -1123,22 +1243,20 @@
     ]
     if paired:
         half_rows = vocab_local // 2
-        dec_arrived, enc_far_sums, emb_grad, bound, dec_roots = hold(
-            (dec_arrived, enc_far_sums, emb_grad, bound, (dec_m, dec_lroot, dec_rroot))
-        )
-        table_close = near_table(emb_grad, bound)
-        enc_arrived = line_sums(enc_far_sums)
+        dec_arrived, enc_close, emb_grad, bound = hold((dec_arrived, enc_close, emb_grad, bound))
+        enc_far_sums = far_sums(enc_close)
         dec_own_sum = line_total(dec_arrived)
         dec_grad = share_blocks(dec_own_sum) * share
-        dec_ready = shampoo_ahead(*dec_roots)
-        table_close, dec_ready, dec_grad, enc_arrived = hold(
-            (table_close, dec_ready, dec_grad, enc_arrived)
-        )
+        table_parts = near_parts(emb_grad, bound)
+        enc_far_sums, table_parts = hold((enc_far_sums, table_parts))
+        table_close = near_table(table_parts)
+        enc_arrived = line_sums(enc_far_sums)
+        table_close, dec_grad = hold((table_close, dec_grad))
         table_far = far_table(table_close)
         dec_products = shampoo_products(dec_grad, *dec_ready[1:])
+        table_far, dec_products, enc_arrived = hold((table_far, dec_products, enc_arrived))
         enc_own_sum = line_total(enc_arrived)
         enc_grad = share_blocks(enc_own_sum) * share
-        table_far, dec_products = hold((table_far, dec_products))
         top, low, scale = table_total(table_far)
         squares = (
             jnp.sum(jnp.square(enc_own_sum * share))
@@ -1173,11 +1291,8 @@
     loss_sum = small[7 * D + 2 * NBK * H]
     squares_all = small[7 * D + 2 * NBK * H + 1]
     loss_count = jnp.maximum(count, 1.0)
-    if paired:
-        dec_ahead, enc_ahead = (dec_ready[0], enc_ready[0])
-    else:
+    if not paired:
         dec_products, enc_products = hold((dec_products, enc_products))
-        dec_ahead, enc_ahead = (dec_ready[0], enc_ready[0])
     grad_norm = jnp.sqrt(
         squares_all + jnp.sum(gain_grad * gain_grad) + jnp.sum(rel_grad * rel_grad)
     )

time: 1190 us -> 1110 us (0.933)
  waiting for transfers between devices: 275 us -> 181 us
  local copies, waits for them, and re-layouts: 275 us -> 238 us
  Pallas kernels: 207 us -> 231 us
  matrix products: 100 us -> 112 us
    all_gather x2 -> x1, waiting for transfers between devices: 135 us -> 6.34 us  [gathered_weights(): lax.all_gather(pairs, EVERYWHERE if split else 'fsdp', axis=0, tiled=True)]
    ppermute x23 -> x33, waiting for transfers between devices: 40.7 us -> 129 us  [swap(): lax.ppermute(values, axis, [(place, place ^ 1) for place in range(size)])]
    reduce_scatter x1, waiting for transfers between devices: 51.5 us -> 0.01 us  [on_device(): lax.psum_scatter(found, 'fsdp', scatter_dimension=0, tiled=True)]
    unnamed x428 -> x382, local copies, waits for them, and re-layouts: 96.9 us -> 52.5 us
    ppermute x23 -> x33, starting transfers between devices: 27.4 us -> 32.5 us  [swap(): lax.ppermute(values, axis, [(place, place ^ 1) for place in range(size)])]
  transfers between devices with their start and end apart: 36 -> 46, of which waited for: 15 -> 19; matrix products, arithmetic and copies ran while one was open for 33% -> 36% of each run, Pallas kernels for 11% -> 12%
where the time goes in v5:
time: 1110 us; the launch traced here: 1100 us
  local copies, waits for them, and re-layouts  238 us (21%)
  Pallas kernels  231 us (21%)
  other arithmetic  228 us (21%)
  waiting for transfers between devices  181 us (16%)
  matrix products  112 us (10%)
  starting transfers between devices  50.7 us (5%)
  between operations  31.1 us (3%)
  blocking collectives  28.7 us (3%)
    ppermute x33, waiting for transfers between devices, swap(): lax.ppermute(values, axis, [(place, place ^ 1) for place in range(size)])  129 us
    reshape x10, local copies, waits for them, and re-layouts, as_rows(): return blocks.reshape(blocks.shape[0], BLOCK * BLOCK)  63.3 us
    unnamed x382, local copies, waits for them, and re-layouts  52.5 us
    scatter-add x1, other arithmetic, table_grads(): return dense.at[slots].add(grads.astype(jnp.float32), mode='drop')  43.9 us
    pallas_call x3, Pallas kernels, attend_back(): pl.pallas_call(functools.partial(attend_back_kernel, biased=bias is not N...  43.1 us
    pallas_call x2, Pallas kernels, shampoo_products(): pl.pallas_call(products_kernel, out_shape=[jax.ShapeDtypeStruct((amount,...  40.7 us
    pallas_call x3, Pallas kernels, attend(): pl.pallas_call(functools.partial(attend_kernel, biased=bias is not None,...  37.3 us
    pallas_call x11, Pallas kernels, weight_grads(): pl.pallas_call(weight_grad_kernel, out_shape=jax.ShapeDtypeStruct((total,...  37.2 us
  transfers between devices with their start and end apart: 46, of which 19 were waited for; matrix products, arithmetic and copies ran while one was open for 36% of the time, Pallas kernels for 12%

profile of v5, /device:TPU:0, one launch (start us, length us, event | category | flops | bytes accessed | tf_op | source)
XLA Modules:
  0.0 1101.1 jit_solution(8725859477681297445)
XLA Ops:
  17.7 14.3 %all-gather.2 = s32[8,1,896]{2,1,0:T(1,128)S(1)} all-gather(s32[1,1,896]{2,1,0:T(1,128)S(1)} %reshape.1431), channel_id=2, replica_groups=mesh['dp'=2,'fsdp'=8,'seq'=2] {'fsdp'}, dimensions={0}, use_global_device_ids=true | all-gather | bytes 32256 | tf_op jit(solution)/shard_map/all_gather | solution.py:1032
  38.3 7.7 convert_element_type.833
  47.3 27.1 %gather_fusion = bf16[5120,768]{1,0:T(8,128)(2,1)} fusion(bf16[4016,768]{1,0:T(8,128)(2,1)} %convert_element_type.833, s32[5120]{0:T(1024)S(1)} %broadcast_clamp_fusion), kind=kCustom, calls=%fused_computation | custom fusion | bytes 15749120 | tf_op jit(solution)/shard_map/jit(_take)/gather | solution.py:500
  74.5 7.7 select_select_fusion
  95.7 14.1 %shard_map.410 = f32[24,192,192]{2,1,0:T(8,128)} custom-call(f32[24,192,192]{2,1,0:T(8,128)} %reshape.1303.m_ref, f32[24,192,192]{2,1,0:T(8,128)} %reshape.1304.lr_ref, f32[24,192,192]{2,1,0:T(8,128)} %reshape.1305.rr_ref), custom_call_target="tpu_custom_call" | custom-call | flops 2038431744 | bytes 14155776 | tf_op jit(solution)/shard_map/pallas_call | solution.py:430
  109.8 7.1 reshape.1307.lr_ref
  130.4 18.6 %shard_map.411 = f32[32,192,192]{2,1,0:T(8,128)} custom-call(f32[32,192,192]{2,1,0:T(8,128)} %reshape.1306.m_ref, f32[32,192,192]{2,1,0:T(8,128)} %reshape.1307.lr_ref, f32[32,192,192]{2,1,0:T(8,128)} %reshape.1308.rr_ref), custom_call_target="tpu_custom_call" | custom-call | flops 2717908992 | bytes 18874368 | tf_op jit(solution)/shard_map/pallas_call | solution.py:430
  182.1 7.8 fusion.8
  213.5 33.4 %collective-permute-done.3.refs_4_ = bf16[2,4,4,96,384]{4,3,2,1,0:T(8,128)(2,1)} collective-permute-done((bf16[2,4,4,96,384]{4,3,2,1,0:T(8,128)(2,1)}, bf16[2,4,4,96,384]{4,3,2,1,0:T(8,128)(2,1)}, u32[]{:S(2)}, u32[]{:S(2)}) %collective-permute-start.3) | collective-permute-done | bytes 2359328 | tf_op jit(solution)/shard_map/ppermute | solution.py:532
  259.4 26.7 %shard_map.416 = bf16[1,512,768]{2,1,0:T(8,128)(2,1)S(1)} custom-call(bf16[1,512,2304]{2,1,0:T(8,128)(2,1)S(1)} %fusion.25.q_ref.k_ref.v_ref, bf16[1,512,2304]{2,1,0:T(8,128)(2,1)S(1)} %fusion.25.q_ref.k_ref.v_ref, bf16[1,512,2304]{2,1,0:T(8,128)(2,1)S(1)} %fusion.25.q_ref.k_ref.v_ref, f32[12,5,128,128]{3,2,1,0:T(8,128)S(1)} %copy-done.3, ...), custom_call_target="tpu_custom_call" | custom-call | flops 1610612736 | bytes 3145728 | tf_op jit(solution)/shard_map/pallas_call | solution.py:229
  298.3 11.1 %shard_map.417 = (bf16[768,2304]{1,0:T(8,128)(2,1)}, bf16[768,768]{1,0:T(8,128)(2,1)S(1)}, bf16[768,768]{1,0:T(8,128)(2,1)S(1)}, bf16[768,1536]{1,0:T(8,128)(2,1...) custom-call(s32[3]{0:T(128)S(1)} %pad_add_fusion.2.place_ref, ...), custom_call_target="tpu_custom_call" | custom-call | bytes 37748736 | tf_op jit(solution)/shard_map/pallas_call | solution.py:657
  333.9 23.3 %all-gather.12.cloned.1.call-done = bf16[1024,768]{1,0:T(8,128)(2,1)} async-done(((bf16[128,768]{1,0:T(8,128)(2,1)}), bf16[1024,768]{1,0:T(8,128)(2,1)}) %all-gather.12.cloned.1.call-update) | async-done | bytes 1572880 | tf_op jit(solution)/shard_map/all_gather | solution.py:1110
  357.2 9.2 fusion.174
  370.9 14.4 %all-gather.3 = f32[8,3,1024]{2,1,0:T(4,128)S(1)} all-gather(f32[1,3,1024]{2,1,0:T(4,128)S(1)} %maximum_bitcast_fusion.2), channel_id=3, replica_groups=mesh['dp'=2,'fsdp'=8,'seq'=2] {'fsdp'}, dimensions={0}, use_global_device_ids=true | all-gather | bytes 110592 | tf_op jit(solution)/shard_map/all_gather | solution.py:1117
  387.3 12.5 %fusion.163 = f32[1024,768]{1,0:T(8,128)} fusion(bf16[4016,768]{1,0:T(8,128)(2,1)} %convert_element_type.833, f32[1024,4016]{0,1:T(8,128)S(1)} %get-tuple-element.498, f32[1024]{0:T(1024)S(1)} %get-tuple-element.433, s32[1024]{0:T(1024)S(1)} %copy-done.138, f32[1024]{0:T(1024)S(1)} %copy-done.150), kind=kOutput, calls=%fused_computation.415 | convolution fusion | flops 6341296128 | bytes 25776128 | tf_op jit(solution)/shard_map/dot_general | solution.py:1130
  404.0 17.1 %abs_reduce_fusion = (f32[]{:T(128)}, f32[4016,768]{1,0:T(8,128)}) fusion(bf16[1024,768]{1,0:T(8,128)(2,1)} %all-gather.12.cloned.1.call-done, f32[1024,4016]{0,1:T(8,128)} %copy-done.63, f32[1024]{0:T(1024)} %copy-done.149, s32[1024]{0:T(1024)} %get-tuple-element.474, f32[1024]{0:T(1024)} %get-tuple-element.475), kind=kOutput, calls=%fused_computation.18 | convolution fusion | flops 6347464704 | bytes 30371844 | tf_op jit(solution)/shard_map/nv,nd->vd/dot_general | solution.py:1143
  425.9 13.9 %reduce-scatter.5.cloned.1.call-done = f32[128,768]{1,0:T(8,128)} async-done(((f32[1024,768]{1,0:T(8,128)}), f32[128,768]{1,0:T(8,128)}) %reduce-scatter.5.cloned.1.call-update) | async-done | bytes 393232 | tf_op jit(solution)/shard_map/reduce_scatter | solution.py:1129
  453.7 8.2 shard_map.420
  489.3 8.6 dynamic-slice_bitcast_fusion
  502.8 9.0 fusion.18.g_ref
  524.6 15.8 %shard_map.429 = (f32[4,2,4,96,384]{4,3,2,1,0:T(8,128)S(1)}, bf16[4,2,4,96,384]{4,3,2,1,0:T(8,128)(2,1)S(1)}, f32[4,2,4,96,384]{4,3,2,1,0:T(8,128)S(1)}, bf16[4,2,4,96,384]{4,3,2,1,0:T(8,128)(2,1)}) custom-call(s32[3]{0:T(128)S(1)} %copy-done.60, bf16[32,4,192,384]{3,2,1,0:T(8,128)(2,1)} %bitcast.433, bf16[16,4,192,384]{3,2,1,0:T(8,128)(2,1)} %bitcast.464), custom_call_target="tpu_custom_call" | custom-call | flops 4718592 | bytes 47185920 | tf_op jit(solution)/shard_map/pallas_call | solution.py:728
  549.6 29.3 %shard_map.430 = (bf16[1,512,768]{2,1,0:T(8,128)(2,1)S(1)}, bf16[1,512,768]{2,1,0:T(8,128)(2,1)S(1)}, bf16[1,512,768]{2,1,0:T(8,128)(2,1)S(1)}, f32[12,5,128,128]{3,2,1,0:T(8,128)S(1)}) custom-call(bf16[1,512,2304]{2,1,0:T(8,128)(2,1)S(1)} %copy-done.2, bf16[1,512,2304]{2,1,0:T(8,128)(2,1)S(1)} %copy-done.2, bf16[1,512,2304]{2,1,0:T(8,128)(2,1)S(1)} %copy-done.2, ...), custom_call_target="tpu_custom_call" | custom-call | flops 4026531840 | bytes 7864320 | tf_op jit(solution)/shard_map/pallas_call | solution.py:257
  586.5 13.8 %collective-permute-done.14 = bf16[4,2,4,96,384]{4,3,2,0,1:T(8,128)(2,1)} collective-permute-done((bf16[4,2,4,96,384]{4,3,2,0,1:T(8,128)(2,1)}, bf16[4,2,4,96,384]{4,3,2,0,1:T(8,128)(2,1)}, u32[]{:S(2)}, u32[]{:S(2)}) %collective-permute-start.14) | collective-permute-done | bytes 2359328 | tf_op jit(solution)/shard_map/ppermute | solution.py:532
  644.5 11.6 %collective-permute-done.18 = bf16[4,12,192,384]{3,2,1,0:T(8,128)(2,1)S(1)} collective-permute-done((bf16[4,12,192,384]{3,2,1,0:T(8,128)(2,1)S(1)}, bf16[4,12,192,384]{3,2,1,0:T(8,128)(2,1)S(1)}, u32[]{:S(2)}, u32[]{:S(2)}) %collective-permute-start.18) | collective-permute-done | bytes 7077920 | tf_op jit(solution)/shard_map/ppermute | solution.py:532
  656.2 12.2 %shard_map.435 = (f32[4,2,3,96,384]{4,3,2,1,0:T(8,128)S(1)}, bf16[4,2,3,96,384]{4,3,2,1,0:T(8,128)(2,1)S(1)}, f32[4,2,3,96,384]{4,3,2,1,0:T(8,128)S(1)}, bf16[4,2,3,96,384]{4,3,2,1,0:T(8,128)(2,1)}) custom-call(s32[3]{0:T(128)S(1)} %copy-done.60, bf16[32,3,192,384]{3,2,1,0:T(8,128)(2,1)} %bitcast.435, bf16[16,3,192,384]{3,2,1,0:T(8,128)(2,1)S(1)} %bitcast.403), custom_call_target="tpu_custom_call" | custom-call | flops 3538944 | bytes 35389440 | tf_op jit(solution)/shard_map/pallas_call | solution.py:728
  700.3 43.9 %scatter_custom_fusion = f32[4016,768]{1,0:T(8,128)} fusion(f32[4016,768]{1,0:T(8,128)} %get-tuple-element.282, s32[5120]{0:T(1024)} %bitcast.489, bf16[5120,768]{1,0:T(8,128)(2,1)} %all-gather.14.cloned.1.call-done), kind=kCustom, calls=%fused_computation.9 | custom fusion | flops 7864320 | bytes 20201472 | tf_op jit(solution)/shard_map/scatter-add | solution.py:509
  757.4 7.2 multiply_convert_fusion.2
  769.2 13.4 %collective-permute-done.21 = bf16[4,3,96,384]{3,2,1,0:T(8,128)(2,1)} collective-permute-done((bf16[4,3,96,384]{3,2,1,0:T(8,128)(2,1)}, bf16[4,3,96,384]{3,2,1,0:T(8,128)(2,1)}, u32[]{:S(2)}, u32[]{:S(2)}) %collective-permute-start.21) | collective-permute-done | bytes 884768 | tf_op jit(solution)/shard_map/ppermute | solution.py:532
  799.4 30.0 %collective-permute-done.23 = f16[1016,768]{1,0:T(8,128)(2,1)} collective-permute-done((f16[1016,768]{1,0:T(8,128)(2,1)}, f16[1016,768]{1,0:T(8,128)(2,1)}, u32[]{:S(2)}, u32[]{:S(2)}) %collective-permute-start.23) | collective-permute-done | bytes 1560608 | tf_op jit(solution)/shard_map/ppermute | solution.py:532
  852.3 23.1 %shard_map.436 = (f32[32,192,192]{2,1,0:T(8,128)}, f32[32,192,192]{2,1,0:T(8,128)}, f32[32,192,192]{2,1,0:T(8,128)}, f32[32,192,192]{2,1,0:T(8,128)}) custom-call(f32[16,192,384]{2,1,0:T(8,128)} %convert_multiply_fusion.g_ref, f32[32,192,192]{2,1,0:T(8,128)} %reshape.1307.lr_ref, f32[32,192,192]{2,1,0:T(8,128)} %reshape.1308.rr_ref), custom_call_target="tpu_custom_call" | custom-call | flops 5435817984 | bytes 33030144 | tf_op jit(solution)/shard_map/pallas_call | solution.py:445
  959.9 17.7 %shard_map.437 = (f32[24,192,192]{2,1,0:T(8,128)}, f32[24,192,192]{2,1,0:T(8,128)}, f32[24,192,192]{2,1,0:T(8,128)}, f32[24,192,192]{2,1,0:T(8,128)}) custom-call(f32[12,192,384]{2,1,0:T(8,128)} %convert_multiply_fusion.1.g_ref, f32[24,192,192]{2,1,0:T(8,128)} %reshape.1304.lr_ref, f32[24,192,192]{2,1,0:T(8,128)} %reshape.1305.rr_ref), custom_call_target="tpu_custom_call" | custom-call | flops 4076863488 | bytes 24772608 | tf_op jit(solution)/shard_map/pallas_call | solution.py:445
  1061.5 30.3 %multiply_subtract_fusion = (f32[4016,768]{1,0:T(8,128)}, f32[4016,768]{1,0:T(8,128)}, f32[4016,768]{1,0:T(8,128)}) fusion(f32[4016,768]{1,0:T(8,128)} %param.33, f32[]{:T(128)S(6)} %min.40, f32[]{:T(128)S(6)} %div.114, f32[]{:T(128)S(6)} %div.123, f16[1008,384]{1,0:T(8,128)(2,1)S(1)} %get-tuple-element.447, f16[1008,384]{1,0:T(8,128)(2,1)S(1)} %get-tuple-element.446, ...), kind=kLoop, calls=%fused_computation.15 | loop fusion | flops 104865792 | bytes 80216080 | tf_op jit(solution)/shard_map/sub | solution.py:952
  (718 shorter events, 530.2 us)
Async XLA Ops:
  7.2 148.1 %all-gather.10.cloned.1.call-start = ((), (), s32[]{:S(2)}) async-start(), calls=%async_computation.5 | async-start | bytes 14598144 | tf_op jit(solution)/shard_map/all_gather | solution.py:677
  33.7 115.2 %all-to-all-start = ((bf16[4,4,192,384]{3,2,1,0:T(8,128)(2,1)}), bf16[4,4,192,384]{3,2,1,0:T(8,128)(2,1)}, u32[]{:S(2)}, u32[]{:S(2)}) async-start(bf16[4,4,192,384]{3,2,1,0:T(8,128)(2,1)} %broadcast_in_dim.66), calls=%async_computation | async-start | bytes 4718592 | tf_op jit(solution)/shard_map/all_to_all | solution.py:586
  38.3 212.8 %reduce-scatter.3.cloned.1.call-start = ((), (), s32[]{:S(2)}) async-start(), calls=%async_computation.6 | async-start | bytes 8847360 | tf_op jit(solution)/shard_map/reduce_scatter | solution.py:1057
  155.3 201.9 %all-gather.12.cloned.1.call-start = ((), (), s32[]{:S(2)}) async-start(), calls=%async_computation.7 | async-start | bytes 1769472 | tf_op jit(solution)/shard_map/all_gather | solution.py:1110
  159.9 30.1 %collective-permute-start.2 = (bf16[4,4,96,384]{3,2,1,0:T(8,128)(2,1)}, bf16[4,4,96,384]{3,2,1,0:T(8,128)(2,1)S(1)}, u32[]{:S(2)}, u32[]{:S(2)}) collective-permute-start(bf16[4,4,96,384]{3,2,1,0:T(8,128)(2,1)} %get-tuple-element.204.refs_1_), channel_id=1, source_target_pairs={{0,16},{16,0},{1,17},{17,1},{2,18},{18,2},{3,19},{19,3},{4,20},{20... | collective-permute-start | bytes 3538952 | tf_op jit(solution)/shard_map/ppermute | solution.py:532
  161.4 28.6 %collective-permute-start.1 = (bf16[4,4,96,384]{3,2,1,0:T(8,128)(2,1)}, bf16[4,4,96,384]{3,2,1,0:T(8,128)(2,1)S(1)}, u32[]{:S(2)}, u32[]{:S(2)}) collective-permute-start(bf16[4,4,96,384]{3,2,1,0:T(8,128)(2,1)} %get-tuple-element.206.refs_0_), channel_id=1, source_target_pairs={{0,1},{1,0},{2,3},{3,2},{4,5},{5,4},{6,7},{7,6},{8,9},{9,8},{10,11... | collective-permute-start | bytes 3538952 | tf_op jit(solution)/shard_map/ppermute | solution.py:532
  192.9 54.0 %collective-permute-start.3 = (bf16[2,4,4,96,384]{4,3,2,1,0:T(8,128)(2,1)}, bf16[2,4,4,96,384]{4,3,2,1,0:T(8,128)(2,1)}, u32[]{:S(2)}, u32[]{:S(2)}) collective-permute-start(bf16[2,4,4,96,384]{4,3,2,1,0:T(8,128)(2,1)} %pad_maximum_fusion), channel_id=1, source_target_pairs={{0,1},{1,0},{2,3},{3,2},{4,5},{5,4},{6,7},{7,6},{8,9},{9,8},{10,11... | collective-permute-start | bytes 7077896 | tf_op jit(solution)/shard_map/ppermute | solution.py:532
  197.3 53.7 %collective-permute-start.4 = (bf16[2,4,4,96,384]{4,3,2,1,0:T(8,128)(2,1)}, bf16[2,4,4,96,384]{4,3,2,1,0:T(8,128)(2,1)}, u32[]{:S(2)}, u32[]{:S(2)}) collective-permute-start(bf16[2,4,4,96,384]{4,3,2,1,0:T(8,128)(2,1)} %pad_maximum_fusion.1), channel_id=1, source_target_pairs={{0,16},{16,0},{1,17},{17,1},{2,18},{18,2},{3,19},{19,3},{4,20},{20... | collective-permute-start | bytes 7077896 | tf_op jit(solution)/shard_map/ppermute | solution.py:532
  333.9 105.9 %reduce-scatter.5.cloned.1.call-start = ((), (), s32[]{:S(2)}) async-start(), calls=%async_computation.8 | async-start | bytes 3538944 | tf_op jit(solution)/shard_map/reduce_scatter | solution.py:1129
  399.8 277.7 %all-gather.14.cloned.1.call-start = ((), (), s32[]{:S(2)}) async-start(), calls=%async_computation.9 | async-start | bytes 8847360 | tf_op jit(solution)/shard_map/all_gather | solution.py:1214
  497.9 23.0 %collective-permute-start.13 = (bf16[4,16,192,384]{3,2,1,0:T(8,128)(2,1)}, bf16[4,16,192,384]{3,2,1,0:T(8,128)(2,1)S(1)}, u32[]{:S(2)}, u32[]{:S(2)}) collective-permute-start(bf16[4,16,192,384]{3,2,1,0:T(8,128)(2,1)} %dynamic-slice_bitcast_fusion), channel_id=1, source_target_pairs={{0,2},{2,0},{4,6},{6,4},{8,10},{10,8},{12,14},{14,12},{1,3},{3,1},... | collective-permute-start | bytes 28311560 | tf_op jit(solution)/shard_map/ppermute | solution.py:532
  546.4 54.0 %collective-permute-start.14 = (bf16[4,2,4,96,384]{4,3,2,0,1:T(8,128)(2,1)}, bf16[4,2,4,96,384]{4,3,2,0,1:T(8,128)(2,1)}, u32[]{:S(2)}, u32[]{:S(2)}) collective-permute-start(bf16[4,2,4,96,384]{4,3,2,0,1:T(8,128)(2,1)} %copy.120), channel_id=1, source_target_pairs={{0,1},{1,0},{2,3},{3,2},{4,5},{5,4},{6,7},{7,6},{8,9},{9,8},{10,11... | collective-permute-start | bytes 7077896 | tf_op jit(solution)/shard_map/ppermute | solution.py:532
  547.9 53.7 %collective-permute-start.15 = (bf16[4,2,4,96,384]{4,3,2,1,0:T(8,128)(2,1)}, bf16[4,2,4,96,384]{4,3,2,1,0:T(8,128)(2,1)}, u32[]{:S(2)}, u32[]{:S(2)}) collective-permute-start(bf16[4,2,4,96,384]{4,3,2,1,0:T(8,128)(2,1)} %get-tuple-element.260), channel_id=1, source_target_pairs={{0,16},{16,0},{1,17},{17,1},{2,18},{18,2},{3,19},{19,3},{4,20},{20... | collective-permute-start | bytes 7077896 | tf_op jit(solution)/shard_map/ppermute | solution.py:532
  606.8 31.1 %collective-permute-start.16 = (bf16[4,4,96,384]{3,2,1,0:T(8,128)(2,1)}, bf16[4,4,96,384]{3,2,1,0:T(8,128)(2,1)}, u32[]{:S(2)}, u32[]{:S(2)}) collective-permute-start(bf16[4,4,96,384]{3,2,1,0:T(8,128)(2,1)} %fusion.55), channel_id=1, source_target_pairs={{0,16},{16,0},{1,17},{17,1},{2,18},{18,2},{3,19},{19,3},{4,20},{20... | collective-permute-start | bytes 3538952 | tf_op jit(solution)/shard_map/ppermute | solution.py:532
  613.6 27.0 %collective-permute-start.17 = (bf16[4,4,96,384]{3,2,1,0:T(8,128)(2,1)}, bf16[4,4,96,384]{3,2,1,0:T(8,128)(2,1)}, u32[]{:S(2)}, u32[]{:S(2)}) collective-permute-start(bf16[4,4,96,384]{3,2,1,0:T(8,128)(2,1)} %fusion.56), channel_id=1, source_target_pairs={{0,1},{1,0},{2,3},{3,2},{4,5},{5,4},{6,7},{7,6},{8,9},{9,8},{10,11... | collective-permute-start | bytes 3538952 | tf_op jit(solution)/shard_map/ppermute | solution.py:532
  682.9 61.4 %all-to-all-start.1 = ((bf16[4,4,192,384]{3,2,1,0:T(8,128)(2,1)}), bf16[4,4,192,384]{3,2,1,0:T(8,128)(2,1)}, u32[]{:S(2)}, u32[]{:S(2)}) async-start(bf16[4,4,192,384]{3,2,1,0:T(8,128)(2,1)} %pad_maximum_fusion.2), calls=%async_computation.3 | async-start | bytes 4718592 | tf_op jit(solution)/shard_map/all_to_all | solution.py:827
  687.5 151.3 %all-gather.16.cloned.1.call-start = ((), (), s32[]{:S(2)}) async-start(), calls=%async_computation.10 | async-start | bytes 2949120 | tf_op jit(solution)/shard_map/all_gather | solution.py:835
  690.5 53.8 %collective-permute-start.20 = (bf16[4,2,3,96,384]{4,3,2,1,0:T(8,128)(2,1)}, bf16[4,2,3,96,384]{4,3,2,1,0:T(8,128)(2,1)}, u32[]{:S(2)}, u32[]{:S(2)}) collective-permute-start(bf16[4,2,3,96,384]{4,3,2,1,0:T(8,128)(2,1)} %get-tuple-element.273), channel_id=1, source_target_pairs={{0,16},{16,0},{1,17},{17,1},{2,18},{18,2},{3,19},{19,3},{4,20},{20... | collective-permute-start | bytes 5308424 | tf_op jit(solution)/shard_map/ppermute | solution.py:532
  692.0 52.2 %collective-permute-start.19 = (bf16[4,2,3,96,384]{4,3,2,0,1:T(8,128)(2,1)}, bf16[4,2,3,96,384]{4,3,2,0,1:T(8,128)(2,1)}, u32[]{:S(2)}, u32[]{:S(2)}) collective-permute-start(bf16[4,2,3,96,384]{4,3,2,0,1:T(8,128)(2,1)} %copy.122), channel_id=1, source_target_pairs={{0,1},{1,0},{2,3},{3,2},{4,5},{5,4},{6,7},{7,6},{8,9},{9,8},{10,11... | collective-permute-start | bytes 5308424 | tf_op jit(solution)/shard_map/ppermute | solution.py:532
  752.2 30.3 %collective-permute-start.21 = (bf16[4,3,96,384]{3,2,1,0:T(8,128)(2,1)}, bf16[4,3,96,384]{3,2,1,0:T(8,128)(2,1)}, u32[]{:S(2)}, u32[]{:S(2)}) collective-permute-start(bf16[4,3,96,384]{3,2,1,0:T(8,128)(2,1)} %fusion.63), channel_id=1, source_target_pairs={{0,16},{16,0},{1,17},{17,1},{2,18},{18,2},{3,19},{19,3},{4,20},{20... | collective-permute-start | bytes 2654216 | tf_op jit(solution)/shard_map/ppermute | solution.py:532
  756.8 31.6 %collective-permute-start.22 = (bf16[4,3,96,384]{3,2,1,0:T(8,128)(2,1)}, bf16[4,3,96,384]{3,2,1,0:T(8,128)(2,1)}, u32[]{:S(2)}, u32[]{:S(2)}) collective-permute-start(bf16[4,3,96,384]{3,2,1,0:T(8,128)(2,1)} %fusion.64), channel_id=1, source_target_pairs={{0,1},{1,0},{2,3},{3,2},{4,5},{5,4},{6,7},{7,6},{8,9},{9,8},{10,11... | collective-permute-start | bytes 2654216 | tf_op jit(solution)/shard_map/ppermute | solution.py:532
  788.4 41.1 %collective-permute-start.23 = (f16[1016,768]{1,0:T(8,128)(2,1)}, f16[1016,768]{1,0:T(8,128)(2,1)}, u32[]{:S(2)}, u32[]{:S(2)}) collective-permute-start(f16[1016,768]{1,0:T(8,128)(2,1)} %concatenate.100), channel_id=1, source_target_pairs={{0,1},{1,0},{2,3},{3,2},{4,5},{5,4},{6,7},{7,6},{8,9},{9,8},{10,11... | collective-permute-start | bytes 4681736 | tf_op jit(solution)/shard_map/ppermute | solution.py:532
  788.6 42.7 %collective-permute-start.24 = (f16[1016,768]{1,0:T(8,128)(2,1)}, f16[1016,768]{1,0:T(8,128)(2,1)}, u32[]{:S(2)}, u32[]{:S(2)}) collective-permute-start(f16[1016,768]{1,0:T(8,128)(2,1)} %concatenate.101), channel_id=1, source_target_pairs={{0,16},{16,0},{1,17},{17,1},{2,18},{18,2},{3,19},{19,3},{4,20},{20... | collective-permute-start | bytes 4681736 | tf_op jit(solution)/shard_map/ppermute | solution.py:532
  794.7 112.6 %all-to-all-start.2 = ((bf16[4,3,192,384]{3,2,1,0:T(8,128)(2,1)}), bf16[4,3,192,384]{3,2,1,0:T(8,128)(2,1)}, u32[]{:S(2)}, u32[]{:S(2)}) async-start(bf16[4,3,192,384]{3,2,1,0:T(8,128)(2,1)} %pad_maximum_fusion.3), calls=%async_computation.4 | async-start | bytes 3538944 | tf_op jit(solution)/shard_map/all_to_all | solution.py:827
  799.4 144.8 %all-gather.18.cloned.1.call-start = ((), (), s32[]{:S(2)}) async-start(), calls=%async_computation.11 | async-start | bytes 2211840 | tf_op jit(solution)/shard_map/all_gather | solution.py:835
  848.5 53.6 %collective-permute-start.25 = (f16[1016,384]{1,0:T(8,128)(2,1)}, f16[1016,384]{1,0:T(8,128)(2,1)}, u32[]{:S(2)}, u32[]{:S(2)}) collective-permute-start(f16[1016,384]{1,0:T(8,128)(2,1)} %concatenate.102), channel_id=1, source_target_pairs={{0,16},{16,0},{1,17},{17,1},{2,18},{18,2},{3,19},{19,3},{4,20},{20... | collective-permute-start | bytes 2340872 | tf_op jit(solution)/shard_map/ppermute | solution.py:532
  851.7 52.3 %collective-permute-start.26 = (f16[1016,384]{1,0:T(8,128)(2,1)}, f16[1016,384]{1,0:T(8,128)(2,1)S(1)}, u32[]{:S(2)}, u32[]{:S(2)}) collective-permute-start(f16[1016,384]{1,0:T(8,128)(2,1)} %concatenate.103), channel_id=1, source_target_pairs={{0,1},{1,0},{2,3},{3,2},{4,5},{5,4},{6,7},{7,6},{8,9},{9,8},{10,11... | collective-permute-start | bytes 2340872 | tf_op jit(solution)/shard_map/ppermute | solution.py:532
  948.9 52.5 %collective-permute-start.30 = (f16[1008,384]{1,0:T(8,128)(2,1)}, f16[1008,384]{1,0:T(8,128)(2,1)S(1)}, u32[]{:S(2)}, u32[]{:S(2)}) collective-permute-start(f16[1008,384]{1,0:T(8,128)(2,1)} %convert_element_type.977), channel_id=1, source_target_pairs={{0,1},{1,0},{2,3},{3,2},{4,5},{5,4},{6,7},{7,6},{8,9},{9,8},{10,11... | collective-permute-start | bytes 2322440 | tf_op jit(solution)/shard_map/ppermute | solution.py:532
  950.4 53.5 %collective-permute-start.29 = (f16[1008,384]{1,0:T(8,128)(2,1)S(1)}, f16[1008,384]{1,0:T(8,128)(2,1)S(1)}, u32[]{:S(2)}, u32[]{:S(2)}) collective-permute-start(f16[1008,384]{1,0:T(8,128)(2,1)S(1)} %convert_element_type.976), channel_id=1, source_target_pairs={{0,16},{16,0},{1,17},{17,1},{2,18},{18,2},{3,19},{19,3},{4,20},{20... | collective-permute-start | bytes 2322440 | tf_op jit(solution)/shard_map/ppermute | solution.py:532
  957.4 43.9 %collective-permute-start.33 = (f32[49,128]{1,0:T(8,128)S(1)}, f32[49,128]{1,0:T(8,128)S(1)}, u32[]{:S(2)}, u32[]{:S(2)}) collective-permute-start(f32[49,128]{1,0:T(8,128)S(1)} %add.1022), channel_id=1, source_target_pairs={{0,8},{2,10},{4,12},{6,14},{8,0},{10,2},{12,4},{14,6},{1,9},{3,11}... | collective-permute-start | bytes 75272 | tf_op jit(solution)/shard_map/ppermute | solution.py:787
  1020.7 35.7 %collective-permute-start.34 = (f16[2,1008,384]{2,1,0:T(8,128)(2,1)}, f16[2,1008,384]{2,1,0:T(8,128)(2,1)}, u32[]{:S(2)}, u32[]{:S(2)}) collective-permute-start(f16[2,1008,384]{2,1,0:T(8,128)(2,1)} %pad_maximum_fusion.4), channel_id=1, source_target_pairs={{0,1},{1,0},{2,3},{3,2},{4,5},{5,4},{6,7},{7,6},{8,9},{9,8},{10,11... | collective-permute-start | bytes 4644872 | tf_op jit(solution)/shard_map/ppermute | solution.py:532
  1022.1 37.0 %collective-permute-start.35 = (f16[2,1008,384]{2,1,0:T(8,128)(2,1)S(1)}, f16[2,1008,384]{2,1,0:T(8,128)(2,1)}, u32[]{:S(2)}, u32[]{:S(2)}) collective-permute-start(f16[2,1008,384]{2,1,0:T(8,128)(2,1)S(1)} %pad_maximum_fusion.5), channel_id=1, source_target_pairs={{0,16},{16,0},{1,17},{17,1},{2,18},{18,2},{3,19},{19,3},{4,20},{20... | collective-permute-start | bytes 4644872 | tf_op jit(solution)/shard_map/ppermute | solution.py:532
  (198 other events, 1971.3 us)
Sparse Core Ops, SparseCore 0:
  17.7 137.5 all-gather.9
  158.1 82.8 reduce-scatter.2
  334.0 23.1 all-gather.11
  399.9 39.9 reduce-scatter.4
  601.7 75.7 all-gather.13
  748.2 53.4 all-gather.15
  911.0 33.2 all-gather.17

commit v6 on v5

--- a/solution.py
+++ b/solution.py
@@ -85,23 +85,37 @@
     return (lane // DH) == half
 
 
-def block_scores(query, keys, bias_ref, half, row, row_segs, key_segs, causal):
-    scores = lax.dot_general(query, keys, (((1,), (1,)), ((), ())), preferred_element_type=jnp.float32)
+def both_heads(values):
+    return jnp.concatenate([jnp.where(head_lanes(half), values, 0) for half in range(2)], axis=0)
+
+
+def own_lanes(stacked):
+    return jnp.where(head_lanes(0), stacked[:TILE], stacked[TILE:])
+
+
+def block_probs(stacked, keys, bias_ref, row, row_segs, key_segs, causal):
+    scores = lax.dot_general(
+        stacked, keys, (((1,), (1,)), ((), ())), preferred_element_type=jnp.float32
+    )
     width = keys.shape[0]
-    if bias_ref is not None:
-        reach = tile_reach(width // TILE)
-        tiles = []
-        for column in range(width // TILE):
-            tiles.append(bias_ref[half, min(max(column - row, -reach), reach) + reach])
-        scores = scores + (jnp.concatenate(tiles, axis=1) if len(tiles) > 1 else tiles[0])
     mask = row_segs == key_segs
     if causal:
-        at_row = row * TILE + lax.broadcasted_iota(jnp.int32, scores.shape, 0)
-        at_key = lax.broadcasted_iota(jnp.int32, scores.shape, 1)
+        at_row = row * TILE + lax.broadcasted_iota(jnp.int32, (TILE, width), 0)
+        at_key = lax.broadcasted_iota(jnp.int32, (TILE, width), 1)
         mask = mask & (at_row >= at_key)
-    scores = jnp.where(mask, scores, neg_fill)
-    raised = jnp.exp(scores - jnp.max(scores, axis=-1, keepdims=True))
-    return raised * (1.0 / jnp.sum(raised, axis=-1, keepdims=True))
+    probs = []
+    for half in range(2):
+        own = scores[half * TILE : (half + 1) * TILE]
+        if bias_ref is not None:
+            reach = tile_reach(width // TILE)
+            tiles = []
+            for column in range(width // TILE):
+                tiles.append(bias_ref[half, min(max(column - row, -reach), reach) + reach])
+            own = own + (jnp.concatenate(tiles, axis=1) if len(tiles) > 1 else tiles[0])
+        own = jnp.where(mask, own, neg_fill)
+        raised = jnp.exp(own - jnp.max(own, axis=-1, keepdims=True))
+        probs.append(raised * (1.0 / jnp.sum(raised, axis=-1, keepdims=True)))
+    return jnp.concatenate(probs, axis=0)
 
 
 def attend_kernel(q_ref, k_ref, v_ref, *rest, biased, causal):
@@ -112,19 +126,11 @@
     key_segs = sk_ref[0]
     for row in range(q_ref.shape[1] // TILE):
         part = pl.ds(row * TILE, TILE)
-        query = q_ref[0, part, :]
-        row_segs = sq_ref[0, part, :]
-        result = None
-        for half in range(2):
-            lanes = head_lanes(half)
-            probs = block_scores(
-                jnp.where(lanes, query, 0), keys, bias_ref, half, row, row_segs, key_segs, causal
-            )
-            output = jnp.dot(
-                probs.astype(jnp.bfloat16), values, preferred_element_type=jnp.float32
-            )
-            result = output if result is None else jnp.where(lanes, output, result)
-        o_ref[0, part, :] = result.astype(jnp.bfloat16)
+        probs = block_probs(
+            both_heads(q_ref[0, part, :]), keys, bias_ref, row, sq_ref[0, part, :], key_segs, causal
+        )
+        output = jnp.dot(probs.astype(jnp.bfloat16), values, preferred_element_type=jnp.float32)
+        o_ref[0, part, :] = own_lanes(output).astype(jnp.bfloat16)
 
 
 def attend_back_kernel(q_ref, k_ref, v_ref, g_ref, *rest, biased, causal):
@@ -145,44 +151,36 @@
 
     grad_keys = None
     grad_values = None
+    down = (((0,), (0,)), ((), ()))
     for row in range(q_ref.shape[1] // TILE):
         part = pl.ds(row * TILE, TILE)
-        query = q_ref[0, part, :]
-        grad_out = g_ref[0, part, :]
-        row_segs = sq_ref[0, part, :]
-        grad_query = None
-        for half in range(2):
-            lanes = head_lanes(half)
-            own_query = jnp.where(lanes, query, 0)
-            own_grad = jnp.where(lanes, grad_out, 0)
-            probs = block_scores(
-                own_query, keys, bias_ref, half, row, row_segs, key_segs, causal
-            )
-            grad_probs = lax.dot_general(
-                own_grad, values, (((1,), (1,)), ((), ())), preferred_element_type=jnp.float32
-            )
-            drop = jnp.sum(probs * grad_probs, axis=-1, keepdims=True)
-            grad_scores = (probs * (grad_probs - drop)).astype(jnp.bfloat16)
-            down = (((0,), (0,)), ((), ()))
-            part_values = lax.dot_general(
-                probs.astype(jnp.bfloat16), own_grad, down, preferred_element_type=jnp.float32
-            )
-            part_keys = lax.dot_general(
-                grad_scores, own_query, down, preferred_element_type=jnp.float32
-            )
-            grad_values = part_values if grad_values is None else grad_values + part_values
-            grad_keys = part_keys if grad_keys is None else grad_keys + part_keys
-            own_grad_query = jnp.dot(grad_scores, keys, preferred_element_type=jnp.float32)
-            grad_query = (
-                own_grad_query if grad_query is None else jnp.where(lanes, own_grad_query, grad_query)
-            )
-            if biased:
-                wide = grad_scores.astype(jnp.float32)
-                reach = tile_reach(width // TILE)
+        query = both_heads(q_ref[0, part, :])
+        grad_out = both_heads(g_ref[0, part, :])
+        probs = block_probs(
+            query, keys, bias_ref, row, sq_ref[0, part, :], key_segs, causal
+        )
+        grad_probs = lax.dot_general(
+            grad_out, values, (((1,), (1,)), ((), ())), preferred_element_type=jnp.float32
+        )
+        drop = jnp.sum(probs * grad_probs, axis=-1, keepdims=True)
+        grad_scores = (probs * (grad_probs - drop)).astype(jnp.bfloat16)
+        part_values = lax.dot_general(
+            probs.astype(jnp.bfloat16), grad_out, down, preferred_element_type=jnp.float32
+        )
+        part_keys = lax.dot_general(grad_scores, query, down, preferred_element_type=jnp.float32)
+        grad_values = part_values if grad_values is None else grad_values + part_values
+        grad_keys = part_keys if grad_keys is None else grad_keys + part_keys
+        grad_query = jnp.dot(grad_scores, keys, preferred_element_type=jnp.float32)
+        dq_ref[0, part, :] = own_lanes(grad_query).astype(jnp.bfloat16)
+        if biased:
+            broad = grad_scores.astype(jnp.float32)
+            reach = tile_reach(width // TILE)
+            for half in range(2):
                 for column in range(width // TILE):
                     slot = min(max(column - row, -reach), reach) + reach
-                    db_ref[half, slot] += wide[:, column * TILE : (column + 1) * TILE]
-        dq_ref[0, part, :] = grad_query.astype(jnp.bfloat16)
+                    db_ref[half, slot] += broad[
+                        half * TILE : (half + 1) * TILE, column * TILE : (column + 1) * TILE
+                    ]
     dk_ref[0] = grad_keys.astype(jnp.bfloat16)
     dv_ref[0] = grad_values.astype(jnp.bfloat16)
 
@@ -451,6 +449,10 @@
         cost_estimate=block_cost(amount, 4, 7),
         compiler_params=pltpu.CompilerParams(vmem_limit_bytes=52 << 20),
     )(pairs, left_root, right_root)
+    return results
+
+
+def rows_of_all(results):
     return [as_rows(result) for result in results]
 
 
@@ -1107,7 +1109,16 @@
     out_scale = D ** (-0.5)
     final = (rms(state3, gains[6]) * out_scale).astype(jnp.bfloat16)
 
+    count = jnp.sum(all_weights).astype(jnp.float32)
+    final, count = hold((final, count))
     all_final = lax.all_gather(final.reshape(rows * dec_len, D), "fsdp", axis=0, tiled=True)
+    if paired:
+        count = count + swap(count, "seq")
+        count = count + swap(count, "dp")
+    else:
+        count = lax.psum(count, REPLICAS)
+    all_final, count = hold((all_final, count))
+    share = 1.0 / jnp.maximum(count, 1.0)
     logits = jnp.einsum("nd,vd->nv", all_final, table, preferred_element_type=jnp.float32)
     local_ids = all_targets.reshape(-1) - vocab_first
     target_hot = local_ids[:, None] == jnp.arange(vocab_local, dtype=jnp.int32)[None, :]
@@ -1132,17 +1143,9 @@
         scatter_dimension=0,
         tiled=True,
     ).reshape(rows, dec_len, D)
-    count = jnp.sum(all_weights).astype(jnp.float32)
-    if paired:
-        count, _ = hold((count, group_loss))
-        count = count + swap(count, "seq")
-        count = count + swap(count, "dp")
-    else:
-        count = lax.psum(count, REPLICAS)
-    share = 1.0 / jnp.maximum(count, 1.0)
     dense_grad = jnp.einsum("nv,nd->vd", grad_logits, all_final, preferred_element_type=jnp.float32)
-    grad_final, dense_grad, dense_bound, share = hold(
-        (grad_final, dense_grad, jnp.max(jnp.abs(dense_grad)), share)
+    grad_final, dense_grad, dense_bound = hold(
+        (grad_final, dense_grad, jnp.max(jnp.abs(dense_grad)))
     )
 
     grad_state3, gain_six = rms_back(state3, gains[6], grad_final * out_scale)
@@ -1236,11 +1239,13 @@
     rel_part = jnp.stack(
         [tile_bias_grad(enc_onehot, enc_bias_grad), tile_bias_grad(dec_onehot, dec_bias_grad)]
     )
-    small = [
-        gain_part.reshape(-1),
-        rel_part.reshape(-1),
-        jnp.where(fsdp_rank == 0, group_loss, 0.0).reshape(1),
-    ]
+    small = jnp.concatenate(
+        [
+            gain_part.reshape(-1),
+            rel_part.reshape(-1),
+            jnp.where(fsdp_rank == 0, group_loss, 0.0).reshape(1),
+        ]
+    )
     if paired:
         half_rows = vocab_local // 2
         dec_arrived, enc_close, emb_grad, bound = hold((dec_arrived, enc_close, emb_grad, bound))
@@ -1251,7 +1256,7 @@
         enc_far_sums, table_parts = hold((enc_far_sums, table_parts))
         table_close = near_table(table_parts)
         enc_arrived = line_sums(enc_far_sums)
-        table_close, dec_grad = hold((table_close, dec_grad))
+        table_close, dec_grad, small = hold((table_close, dec_grad, small))
         table_far = far_table(table_close)
         dec_products = shampoo_products(dec_grad, *dec_ready[1:])
         table_far, dec_products, enc_arrived = hold((table_far, dec_products, enc_arrived))
@@ -1266,22 +1271,24 @@
     else:
         dec_grad = summed_blocks(decoder_portion) * share
         enc_grad = summed_blocks(encoder_portion) * share
-        dec_products = shampoo_products(dec_grad, *dec_ready[1:])
-        enc_products = shampoo_products(enc_grad, *enc_ready[1:])
+        dec_products = rows_of_all(shampoo_products(dec_grad, *dec_ready[1:]))
+        enc_products = rows_of_all(shampoo_products(enc_grad, *enc_ready[1:]))
         table_grad = lax.psum(emb_grad, REPLICAS) * share
         squares = (
             jnp.sum(jnp.square(enc_grad))
             + jnp.sum(jnp.square(dec_grad))
             + jnp.sum(jnp.square(table_grad))
         ) / replica_count()
-    small = jnp.concatenate(small + [squares.reshape(1), jnp.zeros(126, jnp.float32)])
+    small = jnp.concatenate([small, squares.reshape(1), jnp.zeros(126, jnp.float32)])
     small = small.reshape(-1, LANES)
     if paired:
-        small, top, low, enc_grad = hold((sum_replicas(small), top, low, enc_grad))
+        small, top, low, dec_products = hold((sum_replicas(small), top, low, dec_products))
         table_near = share_near(top, low)
         small = sum_line(small)
+        dec_products, enc_grad = hold((rows_of_all(dec_products), enc_grad))
         enc_products = shampoo_products(enc_grad, *enc_ready[1:])
         table_near, small, enc_products = hold((table_near, small, enc_products))
+        enc_products = hold(rows_of_all(enc_products))
         table_grad = placed_table(table_near, share_far(table_near), scale, half_rows) * share
     else:
         small = lax.psum(small, EVERYWHERE)

time: 1110 us -> 1080 us (0.973)
  Pallas kernels: 231 us -> 200 us
  waiting for transfers between devices: 181 us -> 169 us
    pallas_call x3, Pallas kernels: 37.3 us -> 19.1 us  [attend(): pl.pallas_call(functools.partial(attend_kernel, biased=bias is not None,...]
    pallas_call x3, Pallas kernels: 43.1 us -> 30.5 us  [attend_back(): pl.pallas_call(functools.partial(attend_back_kernel, biased=bias is not N...]
    ppermute x33, waiting for transfers between devices: 129 us -> 116 us  [swap(): lax.ppermute(values, axis, [(place, place ^ 1) for place in range(size)])]
    unnamed x382 -> x380, local copies, waits for them, and re-layouts: 52.5 us -> 53.3 us
  transfers between devices with their start and end apart: 46 -> 46, of which waited for: 19 -> 19; matrix products, arithmetic and copies ran while one was open for 36% -> 39% of each run, Pallas kernels for 12% -> 10%
where the time goes in v6:
time: 1080 us; the launch traced here: 1070 us
  local copies, waits for them, and re-layouts  243 us (22%)
  other arithmetic  229 us (21%)
  Pallas kernels  200 us (19%)
  waiting for transfers between devices  169 us (16%)
  matrix products  114 us (11%)
  starting transfers between devices  50.4 us (5%)
  between operations  30.6 us (3%)
  blocking collectives  28.7 us (3%)
    ppermute x33, waiting for transfers between devices, swap(): lax.ppermute(values, axis, [(place, place ^ 1) for place in range(size)])  116 us
    reshape x10, local copies, waits for them, and re-layouts, as_rows(): return blocks.reshape(blocks.shape[0], BLOCK * BLOCK)  63 us
    unnamed x380, local copies, waits for them, and re-layouts  53.3 us
    scatter-add x1, other arithmetic, table_grads(): return dense.at[slots].add(grads.astype(jnp.float32), mode='drop')  43.9 us
    pallas_call x2, Pallas kernels, shampoo_products(): pl.pallas_call(products_kernel, out_shape=[jax.ShapeDtypeStruct((amount,...  40.7 us
    pallas_call x11, Pallas kernels, weight_grads(): pl.pallas_call(weight_grad_kernel, out_shape=jax.ShapeDtypeStruct((total,...  37.2 us
    reshape x6, local copies, waits for them, and re-layouts, as_blocks(): return flat.reshape(flat.shape[0], BLOCK, BLOCK)  34.1 us
    dot_general x11, matrix products, project_back(): jnp.einsum('btf,df->btd', left, right, preferred_element_type=jnp.float32)  34.1 us
  transfers between devices with their start and end apart: 46, of which 19 were waited for; matrix products, arithmetic and copies ran while one was open for 39% of the time, Pallas kernels for 10%

profile of v6, /device:TPU:0, one launch (start us, length us, event | category | flops | bytes accessed | tf_op | source)
XLA Modules:
  0.0 1065.4 jit_solution(12687738633166590827)
XLA Ops:
  17.7 14.3 %all-gather.3 = s32[8,1,896]{2,1,0:T(1,128)S(1)} all-gather(s32[1,1,896]{2,1,0:T(1,128)S(1)} %reshape.1434), channel_id=2, replica_groups=mesh['dp'=2,'fsdp'=8,'seq'=2] {'fsdp'}, dimensions={0}, use_global_device_ids=true | all-gather | bytes 32256 | tf_op jit(solution)/shard_map/all_gather | solution.py:1034
  38.3 7.7 convert_element_type.835
  47.4 27.1 %gather_fusion = bf16[5120,768]{1,0:T(8,128)(2,1)} fusion(bf16[4016,768]{1,0:T(8,128)(2,1)} %convert_element_type.835, s32[5120]{0:T(1024)S(1)} %broadcast_clamp_fusion), kind=kCustom, calls=%fused_computation | custom fusion | bytes 15749120 | tf_op jit(solution)/shard_map/jit(_take)/gather | solution.py:502
  74.5 7.7 select_select_fusion
  95.8 14.1 %shard_map.410 = f32[24,192,192]{2,1,0:T(8,128)} custom-call(f32[24,192,192]{2,1,0:T(8,128)} %reshape.1304.m_ref, f32[24,192,192]{2,1,0:T(8,128)} %reshape.1305.lr_ref, f32[24,192,192]{2,1,0:T(8,128)} %reshape.1306.rr_ref), custom_call_target="tpu_custom_call" | custom-call | flops 2038431744 | bytes 14155776 | tf_op jit(solution)/shard_map/pallas_call | solution.py:428
  130.4 18.6 %shard_map.411 = f32[32,192,192]{2,1,0:T(8,128)} custom-call(f32[32,192,192]{2,1,0:T(8,128)} %reshape.1307.m_ref, f32[32,192,192]{2,1,0:T(8,128)} %reshape.1308.lr_ref, f32[32,192,192]{2,1,0:T(8,128)} %reshape.1309.rr_ref), custom_call_target="tpu_custom_call" | custom-call | flops 2717908992 | bytes 18874368 | tf_op jit(solution)/shard_map/pallas_call | solution.py:428
  182.2 7.9 fusion.8
  214.2 32.8 %collective-permute-done.3.refs_4_ = bf16[2,4,4,96,384]{4,3,2,1,0:T(8,128)(2,1)} collective-permute-done((bf16[2,4,4,96,384]{4,3,2,1,0:T(8,128)(2,1)}, bf16[2,4,4,96,384]{4,3,2,1,0:T(8,128)(2,1)}, u32[]{:S(2)}, u32[]{:S(2)}) %collective-permute-start.3) | collective-permute-done | bytes 2359328 | tf_op jit(solution)/shard_map/ppermute | solution.py:534
  259.4 11.8 %shard_map.416 = bf16[1,512,768]{2,1,0:T(8,128)(2,1)S(1)} custom-call(bf16[1,512,2304]{2,1,0:T(8,128)(2,1)S(1)} %fusion.25.q_ref.k_ref.v_ref, bf16[1,512,2304]{2,1,0:T(8,128)(2,1)S(1)} %fusion.25.q_ref.k_ref.v_ref, bf16[1,512,2304]{2,1,0:T(8,128)(2,1)S(1)} %fusion.25.q_ref.k_ref.v_ref, f32[12,5,128,128]{3,2,1,0:T(8,128)S(1)} %copy-done.3, ...), custom_call_target="tpu_custom_call" | custom-call | flops 1610612736 | bytes 3145728 | tf_op jit(solution)/shard_map/pallas_call | solution.py:227
  283.6 11.1 %shard_map.417 = (bf16[768,2304]{1,0:T(8,128)(2,1)}, bf16[768,768]{1,0:T(8,128)(2,1)S(1)}, bf16[768,768]{1,0:T(8,128)(2,1)S(1)}, bf16[768,1536]{1,0:T(8,128)(2,1...) custom-call(s32[3]{0:T(128)S(1)} %pad_add_fusion.2.place_ref, ...), custom_call_target="tpu_custom_call" | custom-call | bytes 37748736 | tf_op jit(solution)/shard_map/pallas_call | solution.py:659
  324.1 14.8 %all-gather.19.cloned.1.call-done = bf16[1,1024,768]{2,1,0:T(8,128)(2,1)} async-done(((bf16[1,128,768]{2,1,0:T(8,128)(2,1)}), bf16[1,1024,768]{2,1,0:T(8,128)(2,1)}) %all-gather.19.cloned.1.call-update) | async-done | bytes 1572880 | tf_op jit(solution)/shard_map/all_gather | solution.py:1114
  339.0 9.2 fusion.175
  352.7 14.4 %all-gather.4 = f32[8,3,1024]{2,1,0:T(4,128)S(1)} all-gather(f32[1,3,1024]{2,1,0:T(4,128)S(1)} %maximum_bitcast_fusion.2), channel_id=4, replica_groups=mesh['dp'=2,'fsdp'=8,'seq'=2] {'fsdp'}, dimensions={0}, use_global_device_ids=true | all-gather | bytes 110592 | tf_op jit(solution)/shard_map/all_gather | solution.py:1128
  369.1 12.5 %fusion.164 = f32[1024,768]{1,0:T(8,128)} fusion(bf16[4016,768]{1,0:T(8,128)(2,1)} %convert_element_type.835, f32[1024,4016]{0,1:T(8,128)S(1)} %get-tuple-element.528, f32[1024]{0:T(1024)S(1)} %get-tuple-element.457, s32[1024]{0:T(1024)S(1)} %copy-done.141, f32[1024]{0:T(1024)S(1)} %copy-done.155), kind=kOutput, calls=%fused_computation.417 | convolution fusion | flops 6341296128 | bytes 25776128 | tf_op jit(solution)/shard_map/dot_general | solution.py:1141
  382.5 16.7 %abs_reduce_fusion = (f32[]{:T(128)}, f32[4016,768]{1,0:T(8,128)}) fusion(bf16[1024,768]{1,0:T(8,128)(2,1)} %bitcast.495, f32[1024,4016]{0,1:T(8,128)} %copy-done.64, f32[1024]{0:T(1024)} %copy-done.154, s32[1024]{0:T(1024)} %get-tuple-element.505, f32[1024]{0:T(1024)} %get-tuple-element.502), kind=kOutput, calls=%fused_computation.18 | convolution fusion | flops 6347464704 | bytes 30371844 | tf_op jit(solution)/shard_map/nv,nd->vd/dot_general | solution.py:1146
  399.2 22.4 %reduce-scatter.5.cloned.1.call-done = f32[128,768]{1,0:T(8,128)} async-done(((f32[1024,768]{1,0:T(8,128)}), f32[128,768]{1,0:T(8,128)}) %reduce-scatter.5.cloned.1.call-update) | async-done | bytes 393232 | tf_op jit(solution)/shard_map/reduce_scatter | solution.py:1140
  468.1 8.6 dynamic-slice_bitcast_fusion
  481.5 9.0 fusion.18.g_ref
  503.3 15.8 %shard_map.429 = (f32[4,2,4,96,384]{4,3,2,1,0:T(8,128)S(1)}, bf16[4,2,4,96,384]{4,3,2,1,0:T(8,128)(2,1)S(1)}, f32[4,2,4,96,384]{4,3,2,1,0:T(8,128)S(1)}, bf16[4,2,4,96,384]{4,3,2,1,0:T(8,128)(2,1)}) custom-call(s32[3]{0:T(128)S(1)} %copy-done.61, bf16[32,4,192,384]{3,2,1,0:T(8,128)(2,1)} %bitcast.436, bf16[16,4,192,384]{3,2,1,0:T(8,128)(2,1)} %bitcast.463), custom_call_target="tpu_custom_call" | custom-call | flops 4718592 | bytes 47185920 | tf_op jit(solution)/shard_map/pallas_call | solution.py:730
  528.4 19.7 %shard_map.430 = (bf16[1,512,768]{2,1,0:T(8,128)(2,1)S(1)}, bf16[1,512,768]{2,1,0:T(8,128)(2,1)S(1)}, bf16[1,512,768]{2,1,0:T(8,128)(2,1)S(1)}, f32[12,5,128,128]{3,2,1,0:T(8,128)S(1)}) custom-call(bf16[1,512,2304]{2,1,0:T(8,128)(2,1)S(1)} %copy-done.2, bf16[1,512,2304]{2,1,0:T(8,128)(2,1)S(1)} %copy-done.2, bf16[1,512,2304]{2,1,0:T(8,128)(2,1)S(1)} %copy-done.2, ...), custom_call_target="tpu_custom_call" | custom-call | flops 4026531840 | bytes 7864320 | tf_op jit(solution)/shard_map/pallas_call | solution.py:255
  555.7 23.4 %collective-permute-done.14 = bf16[4,2,4,96,384]{4,3,2,0,1:T(8,128)(2,1)} collective-permute-done((bf16[4,2,4,96,384]{4,3,2,0,1:T(8,128)(2,1)}, bf16[4,2,4,96,384]{4,3,2,0,1:T(8,128)(2,1)}, u32[]{:S(2)}, u32[]{:S(2)}) %collective-permute-start.14) | collective-permute-done | bytes 2359328 | tf_op jit(solution)/shard_map/ppermute | solution.py:534
  623.3 11.8 %collective-permute-done.18 = bf16[4,12,192,384]{3,2,1,0:T(8,128)(2,1)S(1)} collective-permute-done((bf16[4,12,192,384]{3,2,1,0:T(8,128)(2,1)S(1)}, bf16[4,12,192,384]{3,2,1,0:T(8,128)(2,1)S(1)}, u32[]{:S(2)}, u32[]{:S(2)}) %collective-permute-start.18) | collective-permute-done | bytes 7077920 | tf_op jit(solution)/shard_map/ppermute | solution.py:534
  635.1 12.2 %shard_map.435 = (f32[4,2,3,96,384]{4,3,2,1,0:T(8,128)S(1)}, bf16[4,2,3,96,384]{4,3,2,1,0:T(8,128)(2,1)S(1)}, f32[4,2,3,96,384]{4,3,2,1,0:T(8,128)S(1)}, bf16[4,2,3,96,384]{4,3,2,1,0:T(8,128)(2,1)}) custom-call(s32[3]{0:T(128)S(1)} %copy-done.61, bf16[32,3,192,384]{3,2,1,0:T(8,128)(2,1)} %bitcast.438, bf16[16,3,192,384]{3,2,1,0:T(8,128)(2,1)S(1)} %bitcast.406), custom_call_target="tpu_custom_call" | custom-call | flops 3538944 | bytes 35389440 | tf_op jit(solution)/shard_map/pallas_call | solution.py:730
  679.2 43.9 %scatter_custom_fusion = f32[4016,768]{1,0:T(8,128)} fusion(f32[4016,768]{1,0:T(8,128)} %get-tuple-element.297, s32[5120]{0:T(1024)} %bitcast.484, bf16[5120,768]{1,0:T(8,128)(2,1)} %all-gather.13.cloned.1.call-done), kind=kCustom, calls=%fused_computation.9 | custom fusion | flops 7864320 | bytes 20201472 | tf_op jit(solution)/shard_map/scatter-add | solution.py:511
  736.3 8.2 multiply_convert_fusion.2
  750.3 11.3 %collective-permute-done.21 = bf16[4,3,96,384]{3,2,1,0:T(8,128)(2,1)} collective-permute-done((bf16[4,3,96,384]{3,2,1,0:T(8,128)(2,1)}, bf16[4,3,96,384]{3,2,1,0:T(8,128)(2,1)}, u32[]{:S(2)}, u32[]{:S(2)}) %collective-permute-start.21) | collective-permute-done | bytes 884768 | tf_op jit(solution)/shard_map/ppermute | solution.py:534
  786.2 7.3 fusion.60
  793.8 14.4 %collective-permute-done.23 = f16[1016,768]{1,0:T(8,128)(2,1)} collective-permute-done((f16[1016,768]{1,0:T(8,128)(2,1)}, f16[1016,768]{1,0:T(8,128)(2,1)}, u32[]{:S(2)}, u32[]{:S(2)}) %collective-permute-start.23) | collective-permute-done | bytes 1560608 | tf_op jit(solution)/shard_map/ppermute | solution.py:534
  831.1 23.1 %shard_map.436 = (f32[32,192,192]{2,1,0:T(8,128)}, f32[32,192,192]{2,1,0:T(8,128)}, f32[32,192,192]{2,1,0:T(8,128)}, f32[32,192,192]{2,1,0:T(8,128)}) custom-call(f32[16,192,384]{2,1,0:T(8,128)} %convert_multiply_fusion.g_ref, f32[32,192,192]{2,1,0:T(8,128)} %reshape.1308.lr_ref, f32[32,192,192]{2,1,0:T(8,128)} %reshape.1309.rr_ref), custom_call_target="tpu_custom_call" | custom-call | flops 5435817984 | bytes 33030144 | tf_op jit(solution)/shard_map/pallas_call | solution.py:443
  930.0 17.7 %shard_map.437 = (f32[24,192,192]{2,1,0:T(8,128)}, f32[24,192,192]{2,1,0:T(8,128)}, f32[24,192,192]{2,1,0:T(8,128)}, f32[24,192,192]{2,1,0:T(8,128)}) custom-call(f32[12,192,384]{2,1,0:T(8,128)} %convert_multiply_fusion.1.g_ref, f32[24,192,192]{2,1,0:T(8,128)} %reshape.1305.lr_ref, f32[24,192,192]{2,1,0:T(8,128)} %reshape.1306.rr_ref), custom_call_target="tpu_custom_call" | custom-call | flops 4076863488 | bytes 24772608 | tf_op jit(solution)/shard_map/pallas_call | solution.py:443
  986.6 7.9 multiply_subtract_fusion.1
  1025.7 30.3 %multiply_subtract_fusion = (f32[4016,768]{1,0:T(8,128)}, f32[4016,768]{1,0:T(8,128)}, f32[4016,768]{1,0:T(8,128)}) fusion(f32[4016,768]{1,0:T(8,128)} %param.33, f32[]{:T(128)S(6)} %min.40, f32[]{:T(128)S(6)} %div.121, f32[]{:T(128)S(6)} %div.123, f16[1008,384]{1,0:T(8,128)(2,1)S(1)} %get-tuple-element.477, f16[1008,384]{1,0:T(8,128)(2,1)S(1)} %get-tuple-element.476, ...), kind=kLoop, calls=%fused_computation.15 | loop fusion | flops 104865792 | bytes 80216080 | tf_op jit(solution)/shard_map/sub | solution.py:954
  (713 shorter events, 527.2 us)
Async XLA Ops:
  7.2 148.1 %all-gather.11.cloned.1.call-start = ((), (), s32[]{:S(2)}) async-start(), calls=%async_computation.5 | async-start | bytes 14598144 | tf_op jit(solution)/shard_map/all_gather | solution.py:679
  33.7 115.2 %all-to-all-start = ((bf16[4,4,192,384]{3,2,1,0:T(8,128)(2,1)}), bf16[4,4,192,384]{3,2,1,0:T(8,128)(2,1)}, u32[]{:S(2)}, u32[]{:S(2)}) async-start(bf16[4,4,192,384]{3,2,1,0:T(8,128)(2,1)} %broadcast_in_dim.66), calls=%async_computation | async-start | bytes 4718592 | tf_op jit(solution)/shard_map/all_to_all | solution.py:588
  38.3 212.9 %reduce-scatter.3.cloned.1.call-start = ((), (), s32[]{:S(2)}) async-start(), calls=%async_computation.6 | async-start | bytes 8847360 | tf_op jit(solution)/shard_map/reduce_scatter | solution.py:1059
  155.3 183.7 %all-gather.19.cloned.1.call-start = ((), (), s32[]{:S(2)}) async-start(), calls=%async_computation.11 | async-start | bytes 1769472 | tf_op jit(solution)/shard_map/all_gather | solution.py:1114
  159.9 30.1 %collective-permute-start.2 = (bf16[4,4,96,384]{3,2,1,0:T(8,128)(2,1)}, bf16[4,4,96,384]{3,2,1,0:T(8,128)(2,1)S(1)}, u32[]{:S(2)}, u32[]{:S(2)}) collective-permute-start(bf16[4,4,96,384]{3,2,1,0:T(8,128)(2,1)} %get-tuple-element.219.refs_1_), channel_id=1, source_target_pairs={{0,16},{16,0},{1,17},{17,1},{2,18},{18,2},{3,19},{19,3},{4,20},{20... | collective-permute-start | bytes 3538952 | tf_op jit(solution)/shard_map/ppermute | solution.py:534
  161.4 28.6 %collective-permute-start.1 = (bf16[4,4,96,384]{3,2,1,0:T(8,128)(2,1)}, bf16[4,4,96,384]{3,2,1,0:T(8,128)(2,1)S(1)}, u32[]{:S(2)}, u32[]{:S(2)}) collective-permute-start(bf16[4,4,96,384]{3,2,1,0:T(8,128)(2,1)} %get-tuple-element.221.refs_0_), channel_id=1, source_target_pairs={{0,1},{1,0},{2,3},{3,2},{4,5},{5,4},{6,7},{7,6},{8,9},{9,8},{10,11... | collective-permute-start | bytes 3538952 | tf_op jit(solution)/shard_map/ppermute | solution.py:534
  193.0 53.9 %collective-permute-start.3 = (bf16[2,4,4,96,384]{4,3,2,1,0:T(8,128)(2,1)}, bf16[2,4,4,96,384]{4,3,2,1,0:T(8,128)(2,1)}, u32[]{:S(2)}, u32[]{:S(2)}) collective-permute-start(bf16[2,4,4,96,384]{4,3,2,1,0:T(8,128)(2,1)} %pad_maximum_fusion), channel_id=1, source_target_pairs={{0,1},{1,0},{2,3},{3,2},{4,5},{5,4},{6,7},{7,6},{8,9},{9,8},{10,11... | collective-permute-start | bytes 7077896 | tf_op jit(solution)/shard_map/ppermute | solution.py:534
  197.5 53.7 %collective-permute-start.4 = (bf16[2,4,4,96,384]{4,3,2,1,0:T(8,128)(2,1)}, bf16[2,4,4,96,384]{4,3,2,1,0:T(8,128)(2,1)}, u32[]{:S(2)}, u32[]{:S(2)}) collective-permute-start(bf16[2,4,4,96,384]{4,3,2,1,0:T(8,128)(2,1)} %pad_maximum_fusion.1), channel_id=1, source_target_pairs={{0,16},{16,0},{1,17},{17,1},{2,18},{18,2},{3,19},{19,3},{4,20},{20... | collective-permute-start | bytes 7077896 | tf_op jit(solution)/shard_map/ppermute | solution.py:534
  315.7 105.9 %reduce-scatter.5.cloned.1.call-start = ((), (), s32[]{:S(2)}) async-start(), calls=%async_computation.7 | async-start | bytes 3538944 | tf_op jit(solution)/shard_map/reduce_scatter | solution.py:1140
  381.5 274.7 %all-gather.13.cloned.1.call-start = ((), (), s32[]{:S(2)}) async-start(), calls=%async_computation.8 | async-start | bytes 8847360 | tf_op jit(solution)/shard_map/all_gather | solution.py:1217
  476.6 22.9 %collective-permute-start.13 = (bf16[4,16,192,384]{3,2,1,0:T(8,128)(2,1)}, bf16[4,16,192,384]{3,2,1,0:T(8,128)(2,1)S(1)}, u32[]{:S(2)}, u32[]{:S(2)}) collective-permute-start(bf16[4,16,192,384]{3,2,1,0:T(8,128)(2,1)} %dynamic-slice_bitcast_fusion), channel_id=1, source_target_pairs={{0,2},{2,0},{4,6},{6,4},{8,10},{10,8},{12,14},{14,12},{1,3},{3,1},... | collective-permute-start | bytes 28311560 | tf_op jit(solution)/shard_map/ppermute | solution.py:534
  525.2 54.0 %collective-permute-start.14 = (bf16[4,2,4,96,384]{4,3,2,0,1:T(8,128)(2,1)}, bf16[4,2,4,96,384]{4,3,2,0,1:T(8,128)(2,1)}, u32[]{:S(2)}, u32[]{:S(2)}) collective-permute-start(bf16[4,2,4,96,384]{4,3,2,0,1:T(8,128)(2,1)} %copy.117), channel_id=1, source_target_pairs={{0,1},{1,0},{2,3},{3,2},{4,5},{5,4},{6,7},{7,6},{8,9},{9,8},{10,11... | collective-permute-start | bytes 7077896 | tf_op jit(solution)/shard_map/ppermute | solution.py:534
  526.7 53.7 %collective-permute-start.15 = (bf16[4,2,4,96,384]{4,3,2,1,0:T(8,128)(2,1)}, bf16[4,2,4,96,384]{4,3,2,1,0:T(8,128)(2,1)}, u32[]{:S(2)}, u32[]{:S(2)}) collective-permute-start(bf16[4,2,4,96,384]{4,3,2,1,0:T(8,128)(2,1)} %get-tuple-element.271), channel_id=1, source_target_pairs={{0,16},{16,0},{1,17},{17,1},{2,18},{18,2},{3,19},{19,3},{4,20},{20... | collective-permute-start | bytes 7077896 | tf_op jit(solution)/shard_map/ppermute | solution.py:534
  585.5 31.1 %collective-permute-start.16 = (bf16[4,4,96,384]{3,2,1,0:T(8,128)(2,1)}, bf16[4,4,96,384]{3,2,1,0:T(8,128)(2,1)}, u32[]{:S(2)}, u32[]{:S(2)}) collective-permute-start(bf16[4,4,96,384]{3,2,1,0:T(8,128)(2,1)} %fusion.55), channel_id=1, source_target_pairs={{0,16},{16,0},{1,17},{17,1},{2,18},{18,2},{3,19},{19,3},{4,20},{20... | collective-permute-start | bytes 3538952 | tf_op jit(solution)/shard_map/ppermute | solution.py:534
  592.3 27.0 %collective-permute-start.17 = (bf16[4,4,96,384]{3,2,1,0:T(8,128)(2,1)}, bf16[4,4,96,384]{3,2,1,0:T(8,128)(2,1)}, u32[]{:S(2)}, u32[]{:S(2)}) collective-permute-start(bf16[4,4,96,384]{3,2,1,0:T(8,128)(2,1)} %fusion.56), channel_id=1, source_target_pairs={{0,1},{1,0},{2,3},{3,2},{4,5},{5,4},{6,7},{7,6},{8,9},{9,8},{10,11... | collective-permute-start | bytes 3538952 | tf_op jit(solution)/shard_map/ppermute | solution.py:534
  661.7 61.4 %all-to-all-start.1 = ((bf16[4,4,192,384]{3,2,1,0:T(8,128)(2,1)}), bf16[4,4,192,384]{3,2,1,0:T(8,128)(2,1)}, u32[]{:S(2)}, u32[]{:S(2)}) async-start(bf16[4,4,192,384]{3,2,1,0:T(8,128)(2,1)} %pad_maximum_fusion.2), calls=%async_computation.3 | async-start | bytes 4718592 | tf_op jit(solution)/shard_map/all_to_all | solution.py:829
  666.3 151.3 %all-gather.15.cloned.1.call-start = ((), (), s32[]{:S(2)}) async-start(), calls=%async_computation.9 | async-start | bytes 2949120 | tf_op jit(solution)/shard_map/all_gather | solution.py:837
  669.3 53.8 %collective-permute-start.20 = (bf16[4,2,3,96,384]{4,3,2,1,0:T(8,128)(2,1)}, bf16[4,2,3,96,384]{4,3,2,1,0:T(8,128)(2,1)}, u32[]{:S(2)}, u32[]{:S(2)}) collective-permute-start(bf16[4,2,3,96,384]{4,3,2,1,0:T(8,128)(2,1)} %get-tuple-element.288), channel_id=1, source_target_pairs={{0,16},{16,0},{1,17},{17,1},{2,18},{18,2},{3,19},{19,3},{4,20},{20... | collective-permute-start | bytes 5308424 | tf_op jit(solution)/shard_map/ppermute | solution.py:534
  670.8 52.3 %collective-permute-start.19 = (bf16[4,2,3,96,384]{4,3,2,0,1:T(8,128)(2,1)}, bf16[4,2,3,96,384]{4,3,2,0,1:T(8,128)(2,1)}, u32[]{:S(2)}, u32[]{:S(2)}) collective-permute-start(bf16[4,2,3,96,384]{4,3,2,0,1:T(8,128)(2,1)} %copy.121), channel_id=1, source_target_pairs={{0,1},{1,0},{2,3},{3,2},{4,5},{5,4},{6,7},{7,6},{8,9},{9,8},{10,11... | collective-permute-start | bytes 5308424 | tf_op jit(solution)/shard_map/ppermute | solution.py:534
  731.1 30.4 %collective-permute-start.21 = (bf16[4,3,96,384]{3,2,1,0:T(8,128)(2,1)}, bf16[4,3,96,384]{3,2,1,0:T(8,128)(2,1)}, u32[]{:S(2)}, u32[]{:S(2)}) collective-permute-start(bf16[4,3,96,384]{3,2,1,0:T(8,128)(2,1)} %fusion.63), channel_id=1, source_target_pairs={{0,16},{16,0},{1,17},{17,1},{2,18},{18,2},{3,19},{19,3},{4,20},{20... | collective-permute-start | bytes 2654216 | tf_op jit(solution)/shard_map/ppermute | solution.py:534
  735.7 31.4 %collective-permute-start.22 = (bf16[4,3,96,384]{3,2,1,0:T(8,128)(2,1)}, bf16[4,3,96,384]{3,2,1,0:T(8,128)(2,1)S(1)}, u32[]{:S(2)}, u32[]{:S(2)}) collective-permute-start(bf16[4,3,96,384]{3,2,1,0:T(8,128)(2,1)} %fusion.64), channel_id=1, source_target_pairs={{0,1},{1,0},{2,3},{3,2},{4,5},{5,4},{6,7},{7,6},{8,9},{9,8},{10,11... | collective-permute-start | bytes 2654216 | tf_op jit(solution)/shard_map/ppermute | solution.py:534
  767.1 41.2 %collective-permute-start.23 = (f16[1016,768]{1,0:T(8,128)(2,1)}, f16[1016,768]{1,0:T(8,128)(2,1)}, u32[]{:S(2)}, u32[]{:S(2)}) collective-permute-start(f16[1016,768]{1,0:T(8,128)(2,1)} %concatenate.103), channel_id=1, source_target_pairs={{0,1},{1,0},{2,3},{3,2},{4,5},{5,4},{6,7},{7,6},{8,9},{9,8},{10,11... | collective-permute-start | bytes 4681736 | tf_op jit(solution)/shard_map/ppermute | solution.py:534
  767.4 42.7 %collective-permute-start.24 = (f16[1016,768]{1,0:T(8,128)(2,1)}, f16[1016,768]{1,0:T(8,128)(2,1)}, u32[]{:S(2)}, u32[]{:S(2)}) collective-permute-start(f16[1016,768]{1,0:T(8,128)(2,1)} %concatenate.104), channel_id=1, source_target_pairs={{0,16},{16,0},{1,17},{17,1},{2,18},{18,2},{3,19},{19,3},{4,20},{20... | collective-permute-start | bytes 4681736 | tf_op jit(solution)/shard_map/ppermute | solution.py:534
  781.1 81.1 %all-to-all-start.2 = ((bf16[4,3,192,384]{3,2,1,0:T(8,128)(2,1)}), bf16[4,3,192,384]{3,2,1,0:T(8,128)(2,1)}, u32[]{:S(2)}, u32[]{:S(2)}) async-start(bf16[4,3,192,384]{3,2,1,0:T(8,128)(2,1)} %pad_maximum_fusion.3), calls=%async_computation.4 | async-start | bytes 3538944 | tf_op jit(solution)/shard_map/all_to_all | solution.py:829
  785.8 140.6 %all-gather.17.cloned.1.call-start = ((), (), s32[]{:S(2)}) async-start(), calls=%async_computation.10 | async-start | bytes 2211840 | tf_op jit(solution)/shard_map/all_gather | solution.py:837
  825.4 28.8 %collective-permute-start.25 = (f16[1016,384]{1,0:T(8,128)(2,1)}, f16[1016,384]{1,0:T(8,128)(2,1)}, u32[]{:S(2)}, u32[]{:S(2)}) collective-permute-start(f16[1016,384]{1,0:T(8,128)(2,1)} %concatenate.106), channel_id=1, source_target_pairs={{0,16},{16,0},{1,17},{17,1},{2,18},{18,2},{3,19},{19,3},{4,20},{20... | collective-permute-start | bytes 2340872 | tf_op jit(solution)/shard_map/ppermute | solution.py:534
  830.5 25.5 %collective-permute-start.26 = (f16[1016,384]{1,0:T(8,128)(2,1)}, f16[1016,384]{1,0:T(8,128)(2,1)}, u32[]{:S(2)}, u32[]{:S(2)}) collective-permute-start(f16[1016,384]{1,0:T(8,128)(2,1)} %concatenate.107), channel_id=1, source_target_pairs={{0,1},{1,0},{2,3},{3,2},{4,5},{5,4},{6,7},{7,6},{8,9},{9,8},{10,11... | collective-permute-start | bytes 2340872 | tf_op jit(solution)/shard_map/ppermute | solution.py:534
  883.7 38.2 %collective-permute-start.30 = (f16[1008,384]{1,0:T(8,128)(2,1)S(1)}, f16[1008,384]{1,0:T(8,128)(2,1)}, u32[]{:S(2)}, u32[]{:S(2)}) collective-permute-start(f16[1008,384]{1,0:T(8,128)(2,1)S(1)} %convert_element_type.978), channel_id=1, source_target_pairs={{0,1},{1,0},{2,3},{3,2},{4,5},{5,4},{6,7},{7,6},{8,9},{9,8},{10,11... | collective-permute-start | bytes 2322440 | tf_op jit(solution)/shard_map/ppermute | solution.py:534
  886.4 37.1 %collective-permute-start.29 = (f16[1008,384]{1,0:T(8,128)(2,1)}, f16[1008,384]{1,0:T(8,128)(2,1)}, u32[]{:S(2)}, u32[]{:S(2)}) collective-permute-start(f16[1008,384]{1,0:T(8,128)(2,1)} %convert_element_type.977), channel_id=1, source_target_pairs={{0,16},{16,0},{1,17},{17,1},{2,18},{18,2},{3,19},{19,3},{4,20},{20... | collective-permute-start | bytes 2322440 | tf_op jit(solution)/shard_map/ppermute | solution.py:534
  892.7 29.3 %collective-permute-start.33 = (f32[49,128]{1,0:T(8,128)S(1)}, f32[49,128]{1,0:T(8,128)S(1)}, u32[]{:S(2)}, u32[]{:S(2)}) collective-permute-start(f32[49,128]{1,0:T(8,128)S(1)} %add.1022), channel_id=1, source_target_pairs={{0,8},{2,10},{4,12},{6,14},{8,0},{10,2},{12,4},{14,6},{1,9},{3,11}... | collective-permute-start | bytes 75272 | tf_op jit(solution)/shard_map/ppermute | solution.py:789
  957.4 63.2 %collective-permute-start.34 = (f16[2,1008,384]{2,1,0:T(8,128)(2,1)}, f16[2,1008,384]{2,1,0:T(8,128)(2,1)}, u32[]{:S(2)}, u32[]{:S(2)}) collective-permute-start(f16[2,1008,384]{2,1,0:T(8,128)(2,1)} %pad_maximum_fusion.4), channel_id=1, source_target_pairs={{0,1},{1,0},{2,3},{3,2},{4,5},{5,4},{6,7},{7,6},{8,9},{9,8},{10,11... | collective-permute-start | bytes 4644872 | tf_op jit(solution)/shard_map/ppermute | solution.py:534
  957.8 65.6 %collective-permute-start.35 = (f16[2,1008,384]{2,1,0:T(8,128)(2,1)S(1)}, f16[2,1008,384]{2,1,0:T(8,128)(2,1)}, u32[]{:S(2)}, u32[]{:S(2)}) collective-permute-start(f16[2,1008,384]{2,1,0:T(8,128)(2,1)S(1)} %pad_maximum_fusion.5), channel_id=1, source_target_pairs={{0,16},{16,0},{1,17},{17,1},{2,18},{18,2},{3,19},{19,3},{4,20},{20... | collective-permute-start | bytes 4644872 | tf_op jit(solution)/shard_map/ppermute | solution.py:534
  (196 other events, 1930.4 us)
Sparse Core Ops, SparseCore 0:
  17.7 137.5 all-gather.10
  158.1 82.9 reduce-scatter.2
  315.8 23.1 all-gather.18
  381.7 39.9 reduce-scatter.4
  580.5 75.7 all-gather.12
  727.0 53.5 all-gather.14
  865.7 43.1 all-gather.16

commit v7 on v6

--- a/solution.py
+++ b/solution.py
@@ -403,14 +403,24 @@
         o_ref[place] = turned_product(lr_ref[place], split_float(m_ref[place]), rr_ref[place])
 
 
-def products_kernel(g_ref, lr_ref, rr_ref, g_out, turned_out, left_out, right_out):
+def products_kernel(rest_ref, g_ref, lr_ref, rr_ref, g_out, turned_out, left_out, right_out):
+    rest = rest_ref[0]
+
+    def single(first, second, contract):
+        return lax.dot_general(
+            first, second, (contract, ((), ())), preferred_element_type=jnp.float32
+        )
+
     for place in range(2):
         block = g_ref[0, :, place * BLOCK : (place + 1) * BLOCK]
-        g_out[place] = block
-        halves = split_float(block)
-        turned_out[place] = turned_product(lr_ref[place], halves, rr_ref[place])
-        left_out[place] = full_product(halves, halves, ROW_ROW)
-        right_out[place] = full_product(halves, halves, COL_COL)
+        g_out[place] = block.astype(jnp.float32) * rest
+        high, low = split_float(lr_ref[place])
+        shaped = single(low, block, ROW_COL) + single(high, block, ROW_COL)
+        turned_out[place] = rest * full_product(
+            split_float(shaped), split_float(rr_ref[place]), ROW_COL
+        )
+        left_out[place] = (rest * rest) * single(block, block, ROW_ROW)
+        right_out[place] = (rest * rest) * single(block, block, COL_COL)
 
 
 def block_cost(amount, products, arrays):
@@ -437,18 +447,25 @@
     return ahead, blocks[1], blocks[2]
 
 
-def shampoo_products(pairs, left_root, right_root):
+def shampoo_products(pairs, share, left_root, right_root):
     amount = left_root.shape[0]
+    power = jnp.exp2(jnp.floor(jnp.log2(share)))
+    pairs = narrow(wide(pairs) * power)
     spec = pl.BlockSpec((2, BLOCK, BLOCK), lambda pair: (pair, 0, 0))
     results = pl.pallas_call(
         products_kernel,
         out_shape=[jax.ShapeDtypeStruct((amount, BLOCK, BLOCK), jnp.float32)] * 4,
         grid=(amount // 2,),
-        in_specs=[pl.BlockSpec((1, BLOCK, PAIR), lambda pair: (pair, 0, 0)), spec, spec],
+        in_specs=[
+            pl.BlockSpec(memory_space=pltpu.SMEM),
+            pl.BlockSpec((1, BLOCK, PAIR), lambda pair: (pair, 0, 0)),
+            spec,
+            spec,
+        ],
         out_specs=[spec] * 4,
-        cost_estimate=block_cost(amount, 4, 7),
+        cost_estimate=block_cost(amount, 3, 7),
         compiler_params=pltpu.CompilerParams(vmem_limit_bytes=52 << 20),
-    )(pairs, left_root, right_root)
+    )((share / power).reshape(1), pairs, left_root, right_root)
     return results
 
 
@@ -834,7 +851,7 @@
 
 
 def share_blocks(own):
-    return wide(lax.all_gather(narrow(own), REPLICAS, axis=0, tiled=True))
+    return lax.all_gather(narrow(own), REPLICAS, axis=0, tiled=True)
 
 
 def window_rows(half_rows):
@@ -1251,17 +1268,17 @@
         dec_arrived, enc_close, emb_grad, bound = hold((dec_arrived, enc_close, emb_grad, bound))
         enc_far_sums = far_sums(enc_close)
         dec_own_sum = line_total(dec_arrived)
-        dec_grad = share_blocks(dec_own_sum) * share
+        dec_grad = share_blocks(dec_own_sum)
         table_parts = near_parts(emb_grad, bound)
         enc_far_sums, table_parts = hold((enc_far_sums, table_parts))
         table_close = near_table(table_parts)
         enc_arrived = line_sums(enc_far_sums)
         table_close, dec_grad, small = hold((table_close, dec_grad, small))
         table_far = far_table(table_close)
-        dec_products = shampoo_products(dec_grad, *dec_ready[1:])
+        dec_products = shampoo_products(dec_grad, share, *dec_ready[1:])
         table_far, dec_products, enc_arrived = hold((table_far, dec_products, enc_arrived))
         enc_own_sum = line_total(enc_arrived)
-        enc_grad = share_blocks(enc_own_sum) * share
+        enc_grad = share_blocks(enc_own_sum)
         top, low, scale = table_total(table_far)
         squares = (
             jnp.sum(jnp.square(enc_own_sum * share))
@@ -1269,14 +1286,14 @@
             + table_squares(top * (share / scale), low * (share / scale), half_rows)
         )
     else:
-        dec_grad = summed_blocks(decoder_portion) * share
-        enc_grad = summed_blocks(encoder_portion) * share
-        dec_products = rows_of_all(shampoo_products(dec_grad, *dec_ready[1:]))
-        enc_products = rows_of_all(shampoo_products(enc_grad, *enc_ready[1:]))
+        dec_sum = summed_blocks(decoder_portion)
+        enc_sum = summed_blocks(encoder_portion)
+        dec_products = rows_of_all(shampoo_products(narrow(dec_sum), share, *dec_ready[1:]))
+        enc_products = rows_of_all(shampoo_products(narrow(enc_sum), share, *enc_ready[1:]))
         table_grad = lax.psum(emb_grad, REPLICAS) * share
         squares = (
-            jnp.sum(jnp.square(enc_grad))
-            + jnp.sum(jnp.square(dec_grad))
+            jnp.sum(jnp.square(enc_sum * share))
+            + jnp.sum(jnp.square(dec_sum * share))
             + jnp.sum(jnp.square(table_grad))
         ) / replica_count()
     small = jnp.concatenate([small, squares.reshape(1), jnp.zeros(126, jnp.float32)])
@@ -1286,7 +1303,7 @@
         table_near = share_near(top, low)
         small = sum_line(small)
         dec_products, enc_grad = hold((rows_of_all(dec_products), enc_grad))
-        enc_products = shampoo_products(enc_grad, *enc_ready[1:])
+        enc_products = shampoo_products(enc_grad, share, *enc_ready[1:])
         table_near, small, enc_products = hold((table_near, small, enc_products))
         enc_products = hold(rows_of_all(enc_products))
         table_grad = placed_table(table_near, share_far(table_near), scale, half_rows) * share

time: 1080 us -> 1070 us (level)
  no operation moved by 1% of the time
where the time goes in v7:
time: 1070 us; the launch traced here: 1060 us
  local copies, waits for them, and re-layouts  244 us (23%)
  other arithmetic  226 us (21%)
  Pallas kernels  198 us (19%)
  waiting for transfers between devices  171 us (16%)
  matrix products  112 us (10%)
  starting transfers between devices  50.4 us (5%)
  between operations  30.9 us (3%)
  blocking collectives  28.4 us (3%)
    ppermute x33, waiting for transfers between devices, swap(): lax.ppermute(values, axis, [(place, place ^ 1) for place in range(size)])  118 us
    reshape x10, local copies, waits for them, and re-layouts, as_rows(): return blocks.reshape(blocks.shape[0], BLOCK * BLOCK)  63.1 us
    unnamed x380, local copies, waits for them, and re-layouts  53.7 us
    scatter-add x1, other arithmetic, table_grads(): return dense.at[slots].add(grads.astype(jnp.float32), mode='drop')  43.9 us
    pallas_call x2, Pallas kernels, shampoo_products(): pl.pallas_call(products_kernel, out_shape=[jax.ShapeDtypeStruct((amount,...  37.8 us
    pallas_call x11, Pallas kernels, weight_grads(): pl.pallas_call(weight_grad_kernel, out_shape=jax.ShapeDtypeStruct((total,...  37.4 us
    reshape x6, local copies, waits for them, and re-layouts, as_blocks(): return flat.reshape(flat.shape[0], BLOCK, BLOCK)  34.1 us
    dot_general x11, matrix products, project_back(): jnp.einsum('btf,df->btd', left, right, preferred_element_type=jnp.float32)  34.1 us
  transfers between devices with their start and end apart: 46, of which 19 were waited for; matrix products, arithmetic and copies ran while one was open for 39% of the time, Pallas kernels for 10%

profile of v7, /device:TPU:0, one launch (start us, length us, event | category | flops | bytes accessed | tf_op | source)
XLA Modules:
  0.0 1059.9 jit_solution(11867128039081441956)
XLA Ops:
  17.7 14.3 %all-gather.3 = s32[8,1,896]{2,1,0:T(1,128)S(1)} all-gather(s32[1,1,896]{2,1,0:T(1,128)S(1)} %reshape.1439), channel_id=2, replica_groups=mesh['dp'=2,'fsdp'=8,'seq'=2] {'fsdp'}, dimensions={0}, use_global_device_ids=true | all-gather | bytes 32256 | tf_op jit(solution)/shard_map/all_gather | solution.py:1051
  38.3 7.7 convert_element_type.841
  47.4 27.1 %gather_fusion = bf16[5120,768]{1,0:T(8,128)(2,1)} fusion(bf16[4016,768]{1,0:T(8,128)(2,1)} %convert_element_type.841, s32[5120]{0:T(1024)S(1)} %broadcast_clamp_fusion), kind=kCustom, calls=%fused_computation | custom fusion | bytes 15749120 | tf_op jit(solution)/shard_map/jit(_take)/gather | solution.py:519
  74.5 7.7 select_select_fusion
  95.8 14.1 %shard_map.410 = f32[24,192,192]{2,1,0:T(8,128)} custom-call(f32[24,192,192]{2,1,0:T(8,128)} %reshape.1308.m_ref, f32[24,192,192]{2,1,0:T(8,128)} %reshape.1309.lr_ref, f32[24,192,192]{2,1,0:T(8,128)} %reshape.1310.rr_ref), custom_call_target="tpu_custom_call" | custom-call | flops 2038431744 | bytes 14155776 | tf_op jit(solution)/shard_map/pallas_call | solution.py:438
  109.9 7.1 reshape.1312.lr_ref
  130.4 18.6 %shard_map.411 = f32[32,192,192]{2,1,0:T(8,128)} custom-call(f32[32,192,192]{2,1,0:T(8,128)} %reshape.1311.m_ref, f32[32,192,192]{2,1,0:T(8,128)} %reshape.1312.lr_ref, f32[32,192,192]{2,1,0:T(8,128)} %reshape.1313.rr_ref), custom_call_target="tpu_custom_call" | custom-call | flops 2717908992 | bytes 18874368 | tf_op jit(solution)/shard_map/pallas_call | solution.py:438
  182.0 7.8 fusion.8
  214.0 32.8 %collective-permute-done.3.refs_4_ = bf16[2,4,4,96,384]{4,3,2,1,0:T(8,128)(2,1)} collective-permute-done((bf16[2,4,4,96,384]{4,3,2,1,0:T(8,128)(2,1)}, bf16[2,4,4,96,384]{4,3,2,1,0:T(8,128)(2,1)}, u32[]{:S(2)}, u32[]{:S(2)}) %collective-permute-start.3) | collective-permute-done | bytes 2359328 | tf_op jit(solution)/shard_map/ppermute | solution.py:551
  259.3 11.9 %shard_map.416 = bf16[1,512,768]{2,1,0:T(8,128)(2,1)S(1)} custom-call(bf16[1,512,2304]{2,1,0:T(8,128)(2,1)S(1)} %fusion.25.q_ref.k_ref.v_ref, bf16[1,512,2304]{2,1,0:T(8,128)(2,1)S(1)} %fusion.25.q_ref.k_ref.v_ref, bf16[1,512,2304]{2,1,0:T(8,128)(2,1)S(1)} %fusion.25.q_ref.k_ref.v_ref, f32[12,5,128,128]{3,2,1,0:T(8,128)S(1)} %copy-done.3, ...), custom_call_target="tpu_custom_call" | custom-call | flops 1610612736 | bytes 3145728 | tf_op jit(solution)/shard_map/pallas_call | solution.py:227
  283.4 11.1 %shard_map.417 = (bf16[768,2304]{1,0:T(8,128)(2,1)}, bf16[768,768]{1,0:T(8,128)(2,1)S(1)}, bf16[768,768]{1,0:T(8,128)(2,1)S(1)}, bf16[768,1536]{1,0:T(8,128)(2,1...) custom-call(s32[3]{0:T(128)S(1)} %pad_add_fusion.2.place_ref, ...), custom_call_target="tpu_custom_call" | custom-call | bytes 37748736 | tf_op jit(solution)/shard_map/pallas_call | solution.py:676
  324.2 14.8 %all-gather.19.cloned.1.call-done = bf16[1,1024,768]{2,1,0:T(8,128)(2,1)} async-done(((bf16[1,128,768]{2,1,0:T(8,128)(2,1)}), bf16[1,1024,768]{2,1,0:T(8,128)(2,1)}) %all-gather.19.cloned.1.call-update) | async-done | bytes 1572880 | tf_op jit(solution)/shard_map/all_gather | solution.py:1131
  339.0 9.2 fusion.175
  352.7 14.1 %all-gather.4 = f32[8,3,1024]{2,1,0:T(4,128)S(1)} all-gather(f32[1,3,1024]{2,1,0:T(4,128)S(1)} %maximum_bitcast_fusion.2), channel_id=4, replica_groups=mesh['dp'=2,'fsdp'=8,'seq'=2] {'fsdp'}, dimensions={0}, use_global_device_ids=true | all-gather | bytes 110592 | tf_op jit(solution)/shard_map/all_gather | solution.py:1145
  368.9 12.5 %fusion.164 = f32[1024,768]{1,0:T(8,128)} fusion(bf16[4016,768]{1,0:T(8,128)(2,1)} %convert_element_type.841, f32[1024,4016]{0,1:T(8,128)S(1)} %get-tuple-element.528, f32[1024]{0:T(1024)S(1)} %get-tuple-element.457, s32[1024]{0:T(1024)S(1)} %copy-done.141, f32[1024]{0:T(1024)S(1)} %copy-done.155), kind=kOutput, calls=%fused_computation.417 | convolution fusion | flops 6341296128 | bytes 25776128 | tf_op jit(solution)/shard_map/dot_general | solution.py:1158
  382.3 16.7 %abs_reduce_fusion = (f32[]{:T(128)}, f32[4016,768]{1,0:T(8,128)}) fusion(bf16[1024,768]{1,0:T(8,128)(2,1)} %bitcast.496, f32[1024,4016]{0,1:T(8,128)} %copy-done.63, f32[1024]{0:T(1024)} %copy-done.154, s32[1024]{0:T(1024)} %get-tuple-element.505, f32[1024]{0:T(1024)} %get-tuple-element.502), kind=kOutput, calls=%fused_computation.18 | convolution fusion | flops 6347464704 | bytes 30371844 | tf_op jit(solution)/shard_map/nv,nd->vd/dot_general | solution.py:1163
  399.0 22.4 %reduce-scatter.5.cloned.1.call-done = f32[128,768]{1,0:T(8,128)} async-done(((f32[1024,768]{1,0:T(8,128)}), f32[128,768]{1,0:T(8,128)}) %reduce-scatter.5.cloned.1.call-update) | async-done | bytes 393232 | tf_op jit(solution)/shard_map/reduce_scatter | solution.py:1157
  468.1 8.6 dynamic-slice_bitcast_fusion
  481.6 9.0 fusion.18.g_ref
  503.4 15.5 %shard_map.429 = (f32[4,2,4,96,384]{4,3,2,1,0:T(8,128)S(1)}, bf16[4,2,4,96,384]{4,3,2,1,0:T(8,128)(2,1)S(1)}, f32[4,2,4,96,384]{4,3,2,1,0:T(8,128)S(1)}, bf16[4,2,4,96,384]{4,3,2,1,0:T(8,128)(2,1)}) custom-call(s32[3]{0:T(128)S(1)} %copy-done.60, bf16[32,4,192,384]{3,2,1,0:T(8,128)(2,1)} %bitcast.437, bf16[16,4,192,384]{3,2,1,0:T(8,128)(2,1)} %bitcast.464), custom_call_target="tpu_custom_call" | custom-call | flops 4718592 | bytes 47185920 | tf_op jit(solution)/shard_map/pallas_call | solution.py:747
  528.1 19.7 %shard_map.430 = (bf16[1,512,768]{2,1,0:T(8,128)(2,1)S(1)}, bf16[1,512,768]{2,1,0:T(8,128)(2,1)S(1)}, bf16[1,512,768]{2,1,0:T(8,128)(2,1)S(1)}, f32[12,5,128,128]{3,2,1,0:T(8,128)S(1)}) custom-call(bf16[1,512,2304]{2,1,0:T(8,128)(2,1)S(1)} %copy-done.2, bf16[1,512,2304]{2,1,0:T(8,128)(2,1)S(1)} %copy-done.2, bf16[1,512,2304]{2,1,0:T(8,128)(2,1)S(1)} %copy-done.2, ...), custom_call_target="tpu_custom_call" | custom-call | flops 4026531840 | bytes 7864320 | tf_op jit(solution)/shard_map/pallas_call | solution.py:255
  555.4 23.4 %collective-permute-done.14 = bf16[4,2,4,96,384]{4,3,2,0,1:T(8,128)(2,1)} collective-permute-done((bf16[4,2,4,96,384]{4,3,2,0,1:T(8,128)(2,1)}, bf16[4,2,4,96,384]{4,3,2,0,1:T(8,128)(2,1)}, u32[]{:S(2)}, u32[]{:S(2)}) %collective-permute-start.14) | collective-permute-done | bytes 2359328 | tf_op jit(solution)/shard_map/ppermute | solution.py:551
  623.0 11.8 %collective-permute-done.18 = bf16[4,12,192,384]{3,2,1,0:T(8,128)(2,1)S(1)} collective-permute-done((bf16[4,12,192,384]{3,2,1,0:T(8,128)(2,1)S(1)}, bf16[4,12,192,384]{3,2,1,0:T(8,128)(2,1)S(1)}, u32[]{:S(2)}, u32[]{:S(2)}) %collective-permute-start.18) | collective-permute-done | bytes 7077920 | tf_op jit(solution)/shard_map/ppermute | solution.py:551
  634.8 12.2 %shard_map.435 = (f32[4,2,3,96,384]{4,3,2,1,0:T(8,128)S(1)}, bf16[4,2,3,96,384]{4,3,2,1,0:T(8,128)(2,1)S(1)}, f32[4,2,3,96,384]{4,3,2,1,0:T(8,128)S(1)}, bf16[4,2,3,96,384]{4,3,2,1,0:T(8,128)(2,1)}) custom-call(s32[3]{0:T(128)S(1)} %copy-done.60, bf16[32,3,192,384]{3,2,1,0:T(8,128)(2,1)} %bitcast.439, bf16[16,3,192,384]{3,2,1,0:T(8,128)(2,1)S(1)} %bitcast.407), custom_call_target="tpu_custom_call" | custom-call | flops 3538944 | bytes 35389440 | tf_op jit(solution)/shard_map/pallas_call | solution.py:747
  678.9 43.9 %scatter_custom_fusion = f32[4016,768]{1,0:T(8,128)} fusion(f32[4016,768]{1,0:T(8,128)} %get-tuple-element.297, s32[5120]{0:T(1024)} %bitcast.485, bf16[5120,768]{1,0:T(8,128)(2,1)} %all-gather.13.cloned.1.call-done), kind=kCustom, calls=%fused_computation.9 | custom fusion | flops 7864320 | bytes 20201472 | tf_op jit(solution)/shard_map/scatter-add | solution.py:528
  736.0 8.2 multiply_convert_fusion.4
  750.0 11.3 %collective-permute-done.21 = bf16[4,3,96,384]{3,2,1,0:T(8,128)(2,1)} collective-permute-done((bf16[4,3,96,384]{3,2,1,0:T(8,128)(2,1)}, bf16[4,3,96,384]{3,2,1,0:T(8,128)(2,1)}, u32[]{:S(2)}, u32[]{:S(2)}) %collective-permute-start.21) | collective-permute-done | bytes 884768 | tf_op jit(solution)/shard_map/ppermute | solution.py:551
  792.3 15.7 %collective-permute-done.23 = f16[1016,768]{1,0:T(8,128)(2,1)} collective-permute-done((f16[1016,768]{1,0:T(8,128)(2,1)}, f16[1016,768]{1,0:T(8,128)(2,1)}, u32[]{:S(2)}, u32[]{:S(2)}) %collective-permute-start.23) | collective-permute-done | bytes 1560608 | tf_op jit(solution)/shard_map/ppermute | solution.py:551
  830.2 21.6 %shard_map.436 = (f32[32,192,192]{2,1,0:T(8,128)}, f32[32,192,192]{2,1,0:T(8,128)}, f32[32,192,192]{2,1,0:T(8,128)}, f32[32,192,192]{2,1,0:T(8,128)}) custom-call(f32[1]{0:T(128)} %bitcast.121.rest_ref, bf16[16,192,384]{2,1,0:T(8,128)(2,1)} %multiply_convert_fusion.2.g_ref, f32[32,192,192]{2,1,0:T(8,128)} %reshape.1312.lr_ref, f32[32,192,192]{2,1,0:T(8,128)} %reshape.1313.rr_ref), custom_call_target="tpu_custom_call" | custom-call | flops 4076863488 | bytes 33030144 | tf_op jit(solution)/shard_map/pallas_call | solution.py:455
  925.7 16.2 %shard_map.437 = (f32[24,192,192]{2,1,0:T(8,128)}, f32[24,192,192]{2,1,0:T(8,128)}, f32[24,192,192]{2,1,0:T(8,128)}, f32[24,192,192]{2,1,0:T(8,128)}) custom-call(f32[1]{0:T(128)} %bitcast.121.rest_ref, bf16[12,192,384]{2,1,0:T(8,128)(2,1)S(1)} %multiply_convert_fusion.3.g_ref, f32[24,192,192]{2,1,0:T(8,128)} %reshape.1309.lr_ref, ...), custom_call_target="tpu_custom_call" | custom-call | flops 3057647616 | bytes 24772608 | tf_op jit(solution)/shard_map/pallas_call | solution.py:455
  981.1 7.9 multiply_subtract_fusion.1
  1020.2 30.3 %multiply_subtract_fusion = (f32[4016,768]{1,0:T(8,128)}, f32[4016,768]{1,0:T(8,128)}, f32[4016,768]{1,0:T(8,128)}) fusion(f32[4016,768]{1,0:T(8,128)} %param.33, f32[]{:T(128)S(6)} %min.40, f32[]{:T(128)S(6)} %div.125, f32[]{:T(128)S(6)} %div.128, f16[1008,384]{1,0:T(8,128)(2,1)S(1)} %get-tuple-element.477, f16[1008,384]{1,0:T(8,128)(2,1)S(1)} %get-tuple-element.476, ...), kind=kLoop, calls=%fused_computation.15 | loop fusion | flops 104865792 | bytes 80216080 | tf_op jit(solution)/shard_map/sub | solution.py:971
  (713 shorter events, 523.9 us)
Async XLA Ops:
  7.2 148.1 %all-gather.11.cloned.1.call-start = ((), (), s32[]{:S(2)}) async-start(), calls=%async_computation.5 | async-start | bytes 14598144 | tf_op jit(solution)/shard_map/all_gather | solution.py:696
  33.7 115.2 %all-to-all-start = ((bf16[4,4,192,384]{3,2,1,0:T(8,128)(2,1)}), bf16[4,4,192,384]{3,2,1,0:T(8,128)(2,1)}, u32[]{:S(2)}, u32[]{:S(2)}) async-start(bf16[4,4,192,384]{3,2,1,0:T(8,128)(2,1)} %broadcast_in_dim.66), calls=%async_computation | async-start | bytes 4718592 | tf_op jit(solution)/shard_map/all_to_all | solution.py:605
  38.3 212.7 %reduce-scatter.3.cloned.1.call-start = ((), (), s32[]{:S(2)}) async-start(), calls=%async_computation.6 | async-start | bytes 8847360 | tf_op jit(solution)/shard_map/reduce_scatter | solution.py:1076
  155.3 183.8 %all-gather.19.cloned.1.call-start = ((), (), s32[]{:S(2)}) async-start(), calls=%async_computation.11 | async-start | bytes 1769472 | tf_op jit(solution)/shard_map/all_gather | solution.py:1131
  159.8 30.1 %collective-permute-start.2 = (bf16[4,4,96,384]{3,2,1,0:T(8,128)(2,1)}, bf16[4,4,96,384]{3,2,1,0:T(8,128)(2,1)S(1)}, u32[]{:S(2)}, u32[]{:S(2)}) collective-permute-start(bf16[4,4,96,384]{3,2,1,0:T(8,128)(2,1)} %get-tuple-element.219.refs_1_), channel_id=1, source_target_pairs={{0,16},{16,0},{1,17},{17,1},{2,18},{18,2},{3,19},{19,3},{4,20},{20... | collective-permute-start | bytes 3538952 | tf_op jit(solution)/shard_map/ppermute | solution.py:551
  161.3 28.6 %collective-permute-start.1 = (bf16[4,4,96,384]{3,2,1,0:T(8,128)(2,1)}, bf16[4,4,96,384]{3,2,1,0:T(8,128)(2,1)S(1)}, u32[]{:S(2)}, u32[]{:S(2)}) collective-permute-start(bf16[4,4,96,384]{3,2,1,0:T(8,128)(2,1)} %get-tuple-element.221.refs_0_), channel_id=1, source_target_pairs={{0,1},{1,0},{2,3},{3,2},{4,5},{5,4},{6,7},{7,6},{8,9},{9,8},{10,11... | collective-permute-start | bytes 3538952 | tf_op jit(solution)/shard_map/ppermute | solution.py:551
  192.8 53.9 %collective-permute-start.3 = (bf16[2,4,4,96,384]{4,3,2,1,0:T(8,128)(2,1)}, bf16[2,4,4,96,384]{4,3,2,1,0:T(8,128)(2,1)}, u32[]{:S(2)}, u32[]{:S(2)}) collective-permute-start(bf16[2,4,4,96,384]{4,3,2,1,0:T(8,128)(2,1)} %pad_maximum_fusion), channel_id=1, source_target_pairs={{0,1},{1,0},{2,3},{3,2},{4,5},{5,4},{6,7},{7,6},{8,9},{9,8},{10,11... | collective-permute-start | bytes 7077896 | tf_op jit(solution)/shard_map/ppermute | solution.py:551
  197.3 53.7 %collective-permute-start.4 = (bf16[2,4,4,96,384]{4,3,2,1,0:T(8,128)(2,1)}, bf16[2,4,4,96,384]{4,3,2,1,0:T(8,128)(2,1)}, u32[]{:S(2)}, u32[]{:S(2)}) collective-permute-start(bf16[2,4,4,96,384]{4,3,2,1,0:T(8,128)(2,1)} %pad_maximum_fusion.1), channel_id=1, source_target_pairs={{0,16},{16,0},{1,17},{17,1},{2,18},{18,2},{3,19},{19,3},{4,20},{20... | collective-permute-start | bytes 7077896 | tf_op jit(solution)/shard_map/ppermute | solution.py:551
  315.8 105.6 %reduce-scatter.5.cloned.1.call-start = ((), (), s32[]{:S(2)}) async-start(), calls=%async_computation.7 | async-start | bytes 3538944 | tf_op jit(solution)/shard_map/reduce_scatter | solution.py:1157
  381.4 274.6 %all-gather.13.cloned.1.call-start = ((), (), s32[]{:S(2)}) async-start(), calls=%async_computation.8 | async-start | bytes 8847360 | tf_op jit(solution)/shard_map/all_gather | solution.py:1234
  476.7 22.9 %collective-permute-start.13 = (bf16[4,16,192,384]{3,2,1,0:T(8,128)(2,1)}, bf16[4,16,192,384]{3,2,1,0:T(8,128)(2,1)S(1)}, u32[]{:S(2)}, u32[]{:S(2)}) collective-permute-start(bf16[4,16,192,384]{3,2,1,0:T(8,128)(2,1)} %dynamic-slice_bitcast_fusion), channel_id=1, source_target_pairs={{0,2},{2,0},{4,6},{6,4},{8,10},{10,8},{12,14},{14,12},{1,3},{3,1},... | collective-permute-start | bytes 28311560 | tf_op jit(solution)/shard_map/ppermute | solution.py:551
  524.9 54.0 %collective-permute-start.14 = (bf16[4,2,4,96,384]{4,3,2,0,1:T(8,128)(2,1)}, bf16[4,2,4,96,384]{4,3,2,0,1:T(8,128)(2,1)}, u32[]{:S(2)}, u32[]{:S(2)}) collective-permute-start(bf16[4,2,4,96,384]{4,3,2,0,1:T(8,128)(2,1)} %copy.117), channel_id=1, source_target_pairs={{0,1},{1,0},{2,3},{3,2},{4,5},{5,4},{6,7},{7,6},{8,9},{9,8},{10,11... | collective-permute-start | bytes 7077896 | tf_op jit(solution)/shard_map/ppermute | solution.py:551
  526.4 53.7 %collective-permute-start.15 = (bf16[4,2,4,96,384]{4,3,2,1,0:T(8,128)(2,1)}, bf16[4,2,4,96,384]{4,3,2,1,0:T(8,128)(2,1)}, u32[]{:S(2)}, u32[]{:S(2)}) collective-permute-start(bf16[4,2,4,96,384]{4,3,2,1,0:T(8,128)(2,1)} %get-tuple-element.271), channel_id=1, source_target_pairs={{0,16},{16,0},{1,17},{17,1},{2,18},{18,2},{3,19},{19,3},{4,20},{20... | collective-permute-start | bytes 7077896 | tf_op jit(solution)/shard_map/ppermute | solution.py:551
  585.2 31.1 %collective-permute-start.16 = (bf16[4,4,96,384]{3,2,1,0:T(8,128)(2,1)}, bf16[4,4,96,384]{3,2,1,0:T(8,128)(2,1)}, u32[]{:S(2)}, u32[]{:S(2)}) collective-permute-start(bf16[4,4,96,384]{3,2,1,0:T(8,128)(2,1)} %fusion.55), channel_id=1, source_target_pairs={{0,16},{16,0},{1,17},{17,1},{2,18},{18,2},{3,19},{19,3},{4,20},{20... | collective-permute-start | bytes 3538952 | tf_op jit(solution)/shard_map/ppermute | solution.py:551
  592.0 27.0 %collective-permute-start.17 = (bf16[4,4,96,384]{3,2,1,0:T(8,128)(2,1)}, bf16[4,4,96,384]{3,2,1,0:T(8,128)(2,1)}, u32[]{:S(2)}, u32[]{:S(2)}) collective-permute-start(bf16[4,4,96,384]{3,2,1,0:T(8,128)(2,1)} %fusion.56), channel_id=1, source_target_pairs={{0,1},{1,0},{2,3},{3,2},{4,5},{5,4},{6,7},{7,6},{8,9},{9,8},{10,11... | collective-permute-start | bytes 3538952 | tf_op jit(solution)/shard_map/ppermute | solution.py:551
  661.4 61.4 %all-to-all-start.1 = ((bf16[4,4,192,384]{3,2,1,0:T(8,128)(2,1)}), bf16[4,4,192,384]{3,2,1,0:T(8,128)(2,1)}, u32[]{:S(2)}, u32[]{:S(2)}) async-start(bf16[4,4,192,384]{3,2,1,0:T(8,128)(2,1)} %pad_maximum_fusion.2), calls=%async_computation.3 | async-start | bytes 4718592 | tf_op jit(solution)/shard_map/all_to_all | solution.py:846
  666.1 151.3 %all-gather.15.cloned.1.call-start = ((), (), s32[]{:S(2)}) async-start(), calls=%async_computation.9 | async-start | bytes 2949120 | tf_op jit(solution)/shard_map/all_gather | solution.py:854
  669.0 53.8 %collective-permute-start.20 = (bf16[4,2,3,96,384]{4,3,2,1,0:T(8,128)(2,1)}, bf16[4,2,3,96,384]{4,3,2,1,0:T(8,128)(2,1)}, u32[]{:S(2)}, u32[]{:S(2)}) collective-permute-start(bf16[4,2,3,96,384]{4,3,2,1,0:T(8,128)(2,1)} %get-tuple-element.288), channel_id=1, source_target_pairs={{0,16},{16,0},{1,17},{17,1},{2,18},{18,2},{3,19},{19,3},{4,20},{20... | collective-permute-start | bytes 5308424 | tf_op jit(solution)/shard_map/ppermute | solution.py:551
  670.5 52.3 %collective-permute-start.19 = (bf16[4,2,3,96,384]{4,3,2,0,1:T(8,128)(2,1)}, bf16[4,2,3,96,384]{4,3,2,0,1:T(8,128)(2,1)}, u32[]{:S(2)}, u32[]{:S(2)}) collective-permute-start(bf16[4,2,3,96,384]{4,3,2,0,1:T(8,128)(2,1)} %copy.121), channel_id=1, source_target_pairs={{0,1},{1,0},{2,3},{3,2},{4,5},{5,4},{6,7},{7,6},{8,9},{9,8},{10,11... | collective-permute-start | bytes 5308424 | tf_op jit(solution)/shard_map/ppermute | solution.py:551
  730.8 30.4 %collective-permute-start.21 = (bf16[4,3,96,384]{3,2,1,0:T(8,128)(2,1)}, bf16[4,3,96,384]{3,2,1,0:T(8,128)(2,1)}, u32[]{:S(2)}, u32[]{:S(2)}) collective-permute-start(bf16[4,3,96,384]{3,2,1,0:T(8,128)(2,1)} %fusion.63), channel_id=1, source_target_pairs={{0,16},{16,0},{1,17},{17,1},{2,18},{18,2},{3,19},{19,3},{4,20},{20... | collective-permute-start | bytes 2654216 | tf_op jit(solution)/shard_map/ppermute | solution.py:551
  735.4 31.4 %collective-permute-start.22 = (bf16[4,3,96,384]{3,2,1,0:T(8,128)(2,1)}, bf16[4,3,96,384]{3,2,1,0:T(8,128)(2,1)S(1)}, u32[]{:S(2)}, u32[]{:S(2)}) collective-permute-start(bf16[4,3,96,384]{3,2,1,0:T(8,128)(2,1)} %fusion.64), channel_id=1, source_target_pairs={{0,1},{1,0},{2,3},{3,2},{4,5},{5,4},{6,7},{7,6},{8,9},{9,8},{10,11... | collective-permute-start | bytes 2654216 | tf_op jit(solution)/shard_map/ppermute | solution.py:551
  766.8 41.2 %collective-permute-start.23 = (f16[1016,768]{1,0:T(8,128)(2,1)}, f16[1016,768]{1,0:T(8,128)(2,1)}, u32[]{:S(2)}, u32[]{:S(2)}) collective-permute-start(f16[1016,768]{1,0:T(8,128)(2,1)} %concatenate.103), channel_id=1, source_target_pairs={{0,1},{1,0},{2,3},{3,2},{4,5},{5,4},{6,7},{7,6},{8,9},{9,8},{10,11... | collective-permute-start | bytes 4681736 | tf_op jit(solution)/shard_map/ppermute | solution.py:551
  767.1 42.7 %collective-permute-start.24 = (f16[1016,768]{1,0:T(8,128)(2,1)}, f16[1016,768]{1,0:T(8,128)(2,1)}, u32[]{:S(2)}, u32[]{:S(2)}) collective-permute-start(f16[1016,768]{1,0:T(8,128)(2,1)} %concatenate.104), channel_id=1, source_target_pairs={{0,16},{16,0},{1,17},{17,1},{2,18},{18,2},{3,19},{19,3},{4,20},{20... | collective-permute-start | bytes 4681736 | tf_op jit(solution)/shard_map/ppermute | solution.py:551
  774.3 85.5 %all-to-all-start.2 = ((bf16[4,3,192,384]{3,2,1,0:T(8,128)(2,1)}), bf16[4,3,192,384]{3,2,1,0:T(8,128)(2,1)}, u32[]{:S(2)}, u32[]{:S(2)}) async-start(bf16[4,3,192,384]{3,2,1,0:T(8,128)(2,1)} %pad_maximum_fusion.3), calls=%async_computation.4 | async-start | bytes 3538944 | tf_op jit(solution)/shard_map/all_to_all | solution.py:846
  779.2 144.7 %all-gather.17.cloned.1.call-start = ((), (), s32[]{:S(2)}) async-start(), calls=%async_computation.10 | async-start | bytes 2211840 | tf_op jit(solution)/shard_map/all_gather | solution.py:854
  820.6 31.2 %collective-permute-start.25 = (f16[1016,384]{1,0:T(8,128)(2,1)}, f16[1016,384]{1,0:T(8,128)(2,1)}, u32[]{:S(2)}, u32[]{:S(2)}) collective-permute-start(f16[1016,384]{1,0:T(8,128)(2,1)} %concatenate.106), channel_id=1, source_target_pairs={{0,16},{16,0},{1,17},{17,1},{2,18},{18,2},{3,19},{19,3},{4,20},{20... | collective-permute-start | bytes 2340872 | tf_op jit(solution)/shard_map/ppermute | solution.py:551
  825.9 27.8 %collective-permute-start.26 = (f16[1016,384]{1,0:T(8,128)(2,1)}, f16[1016,384]{1,0:T(8,128)(2,1)}, u32[]{:S(2)}, u32[]{:S(2)}) collective-permute-start(f16[1016,384]{1,0:T(8,128)(2,1)} %concatenate.107), channel_id=1, source_target_pairs={{0,1},{1,0},{2,3},{3,2},{4,5},{5,4},{6,7},{7,6},{8,9},{9,8},{10,11... | collective-permute-start | bytes 2340872 | tf_op jit(solution)/shard_map/ppermute | solution.py:551
  881.4 38.1 %collective-permute-start.30 = (f16[1008,384]{1,0:T(8,128)(2,1)S(1)}, f16[1008,384]{1,0:T(8,128)(2,1)}, u32[]{:S(2)}, u32[]{:S(2)}) collective-permute-start(f16[1008,384]{1,0:T(8,128)(2,1)S(1)} %convert_element_type.985), channel_id=1, source_target_pairs={{0,1},{1,0},{2,3},{3,2},{4,5},{5,4},{6,7},{7,6},{8,9},{9,8},{10,11... | collective-permute-start | bytes 2322440 | tf_op jit(solution)/shard_map/ppermute | solution.py:551
  884.0 37.0 %collective-permute-start.29 = (f16[1008,384]{1,0:T(8,128)(2,1)}, f16[1008,384]{1,0:T(8,128)(2,1)}, u32[]{:S(2)}, u32[]{:S(2)}) collective-permute-start(f16[1008,384]{1,0:T(8,128)(2,1)} %convert_element_type.984), channel_id=1, source_target_pairs={{0,16},{16,0},{1,17},{17,1},{2,18},{18,2},{3,19},{19,3},{4,20},{20... | collective-permute-start | bytes 2322440 | tf_op jit(solution)/shard_map/ppermute | solution.py:551
  890.3 29.1 %collective-permute-start.33 = (f32[49,128]{1,0:T(8,128)S(1)}, f32[49,128]{1,0:T(8,128)S(1)}, u32[]{:S(2)}, u32[]{:S(2)}) collective-permute-start(f32[49,128]{1,0:T(8,128)S(1)} %add.1022), channel_id=1, source_target_pairs={{0,8},{2,10},{4,12},{6,14},{8,0},{10,2},{12,4},{14,6},{1,9},{3,11}... | collective-permute-start | bytes 75272 | tf_op jit(solution)/shard_map/ppermute | solution.py:806
  951.7 63.4 %collective-permute-start.34 = (f16[2,1008,384]{2,1,0:T(8,128)(2,1)}, f16[2,1008,384]{2,1,0:T(8,128)(2,1)}, u32[]{:S(2)}, u32[]{:S(2)}) collective-permute-start(f16[2,1008,384]{2,1,0:T(8,128)(2,1)} %pad_maximum_fusion.4), channel_id=1, source_target_pairs={{0,1},{1,0},{2,3},{3,2},{4,5},{5,4},{6,7},{7,6},{8,9},{9,8},{10,11... | collective-permute-start | bytes 4644872 | tf_op jit(solution)/shard_map/ppermute | solution.py:551
  952.1 65.8 %collective-permute-start.35 = (f16[2,1008,384]{2,1,0:T(8,128)(2,1)S(1)}, f16[2,1008,384]{2,1,0:T(8,128)(2,1)}, u32[]{:S(2)}, u32[]{:S(2)}) collective-permute-start(f16[2,1008,384]{2,1,0:T(8,128)(2,1)S(1)} %pad_maximum_fusion.5), channel_id=1, source_target_pairs={{0,16},{16,0},{1,17},{17,1},{2,18},{18,2},{3,19},{19,3},{4,20},{20... | collective-permute-start | bytes 4644872 | tf_op jit(solution)/shard_map/ppermute | solution.py:551
  (196 other events, 1940.0 us)
Sparse Core Ops, SparseCore 0:
  17.7 137.5 all-gather.10
  158.1 82.8 reduce-scatter.2
  315.9 23.0 all-gather.18
  381.5 39.9 reduce-scatter.4
  580.2 75.7 all-gather.12
  726.8 53.5 all-gather.14
  863.4 43.1 all-gather.16

commit v8 on v7

--- a/solution.py
+++ b/solution.py
@@ -411,8 +411,9 @@
             first, second, (contract, ((), ())), preferred_element_type=jnp.float32
         )
 
-    for place in range(2):
-        block = g_ref[0, :, place * BLOCK : (place + 1) * BLOCK]
+    for place in range(g_out.shape[0]):
+        first = place % 2 * BLOCK
+        block = g_ref[place // 2, :, first : first + BLOCK]
         g_out[place] = block.astype(jnp.float32) * rest
         high, low = split_float(lr_ref[place])
         shaped = single(low, block, ROW_COL) + single(high, block, ROW_COL)
@@ -451,14 +452,15 @@
     amount = left_root.shape[0]
     power = jnp.exp2(jnp.floor(jnp.log2(share)))
     pairs = narrow(wide(pairs) * power)
-    spec = pl.BlockSpec((2, BLOCK, BLOCK), lambda pair: (pair, 0, 0))
+    group = 4 if amount % 4 == 0 else 2
+    spec = pl.BlockSpec((group, BLOCK, BLOCK), lambda step: (step, 0, 0))
     results = pl.pallas_call(
         products_kernel,
         out_shape=[jax.ShapeDtypeStruct((amount, BLOCK, BLOCK), jnp.float32)] * 4,
-        grid=(amount // 2,),
+        grid=(amount // group,),
         in_specs=[
             pl.BlockSpec(memory_space=pltpu.SMEM),
-            pl.BlockSpec((1, BLOCK, PAIR), lambda pair: (pair, 0, 0)),
+            pl.BlockSpec((group // 2, BLOCK, PAIR), lambda step: (step, 0, 0)),
             spec,
             spec,
         ],

time: 1070 us -> 1070 us (level)
  no operation moved by 1% of the time
where the time goes in v8:
time: 1070 us; the launch traced here: 1060 us
  local copies, waits for them, and re-layouts  244 us (23%)
  other arithmetic  226 us (21%)
  Pallas kernels  193 us (18%)
  waiting for transfers between devices  171 us (16%)
  matrix products  112 us (10%)
  starting transfers between devices  50.4 us (5%)
  between operations  30.8 us (3%)
  blocking collectives  28.4 us (3%)
    ppermute x33, waiting for transfers between devices, swap(): lax.ppermute(values, axis, [(place, place ^ 1) for place in range(size)])  118 us
    reshape x10, local copies, waits for them, and re-layouts, as_rows(): return blocks.reshape(blocks.shape[0], BLOCK * BLOCK)  63 us
    unnamed x380, local copies, waits for them, and re-layouts  53.7 us
    scatter-add x1, other arithmetic, table_grads(): return dense.at[slots].add(grads.astype(jnp.float32), mode='drop')  43.9 us
    pallas_call x11, Pallas kernels, weight_grads(): pl.pallas_call(weight_grad_kernel, out_shape=jax.ShapeDtypeStruct((total,...  37.4 us
    reshape x6, local copies, waits for them, and re-layouts, as_blocks(): return flat.reshape(flat.shape[0], BLOCK, BLOCK)  34.1 us
    dot_general x11, matrix products, project_back(): jnp.einsum('btf,df->btd', left, right, preferred_element_type=jnp.float32)  34.1 us
    pallas_call x2, Pallas kernels, shampoo_products(): pl.pallas_call(products_kernel, out_shape=[jax.ShapeDtypeStruct((amount,...  33.1 us
  transfers between devices with their start and end apart: 46, of which 19 were waited for; matrix products, arithmetic and copies ran while one was open for 39% of the time, Pallas kernels for 10%

profile of v8, /device:TPU:0, one launch (start us, length us, event | category | flops | bytes accessed | tf_op | source)
XLA Modules:
  0.0 1055.0 jit_solution(10548901074961733341)
XLA Ops:
  17.7 14.3 %all-gather.3 = s32[8,1,896]{2,1,0:T(1,128)S(1)} all-gather(s32[1,1,896]{2,1,0:T(1,128)S(1)} %reshape.1439), channel_id=2, replica_groups=mesh['dp'=2,'fsdp'=8,'seq'=2] {'fsdp'}, dimensions={0}, use_global_device_ids=true | all-gather | bytes 32256 | tf_op jit(solution)/shard_map/all_gather | solution.py:1053
  38.3 7.7 convert_element_type.841
  47.4 27.1 %gather_fusion = bf16[5120,768]{1,0:T(8,128)(2,1)} fusion(bf16[4016,768]{1,0:T(8,128)(2,1)} %convert_element_type.841, s32[5120]{0:T(1024)S(1)} %broadcast_clamp_fusion), kind=kCustom, calls=%fused_computation | custom fusion | bytes 15749120 | tf_op jit(solution)/shard_map/jit(_take)/gather | solution.py:521
  74.5 7.7 select_select_fusion
  95.8 14.1 %shard_map.410 = f32[24,192,192]{2,1,0:T(8,128)} custom-call(f32[24,192,192]{2,1,0:T(8,128)} %reshape.1308.m_ref, f32[24,192,192]{2,1,0:T(8,128)} %reshape.1309.lr_ref, f32[24,192,192]{2,1,0:T(8,128)} %reshape.1310.rr_ref), custom_call_target="tpu_custom_call" | custom-call | flops 2038431744 | bytes 14155776 | tf_op jit(solution)/shard_map/pallas_call | solution.py:439
  109.9 7.1 reshape.1312.lr_ref
  130.4 18.6 %shard_map.411 = f32[32,192,192]{2,1,0:T(8,128)} custom-call(f32[32,192,192]{2,1,0:T(8,128)} %reshape.1311.m_ref, f32[32,192,192]{2,1,0:T(8,128)} %reshape.1312.lr_ref, f32[32,192,192]{2,1,0:T(8,128)} %reshape.1313.rr_ref), custom_call_target="tpu_custom_call" | custom-call | flops 2717908992 | bytes 18874368 | tf_op jit(solution)/shard_map/pallas_call | solution.py:439
  182.0 7.8 fusion.8
  214.0 32.8 %collective-permute-done.3.refs_4_ = bf16[2,4,4,96,384]{4,3,2,1,0:T(8,128)(2,1)} collective-permute-done((bf16[2,4,4,96,384]{4,3,2,1,0:T(8,128)(2,1)}, bf16[2,4,4,96,384]{4,3,2,1,0:T(8,128)(2,1)}, u32[]{:S(2)}, u32[]{:S(2)}) %collective-permute-start.3) | collective-permute-done | bytes 2359328 | tf_op jit(solution)/shard_map/ppermute | solution.py:553
  259.3 11.9 %shard_map.416 = bf16[1,512,768]{2,1,0:T(8,128)(2,1)S(1)} custom-call(bf16[1,512,2304]{2,1,0:T(8,128)(2,1)S(1)} %fusion.25.q_ref.k_ref.v_ref, bf16[1,512,2304]{2,1,0:T(8,128)(2,1)S(1)} %fusion.25.q_ref.k_ref.v_ref, bf16[1,512,2304]{2,1,0:T(8,128)(2,1)S(1)} %fusion.25.q_ref.k_ref.v_ref, f32[12,5,128,128]{3,2,1,0:T(8,128)S(1)} %copy-done.3, ...), custom_call_target="tpu_custom_call" | custom-call | flops 1610612736 | bytes 3145728 | tf_op jit(solution)/shard_map/pallas_call | solution.py:227
  283.4 11.1 %shard_map.417 = (bf16[768,2304]{1,0:T(8,128)(2,1)}, bf16[768,768]{1,0:T(8,128)(2,1)S(1)}, bf16[768,768]{1,0:T(8,128)(2,1)S(1)}, bf16[768,1536]{1,0:T(8,128)(2,1...) custom-call(s32[3]{0:T(128)S(1)} %pad_add_fusion.2.place_ref, ...), custom_call_target="tpu_custom_call" | custom-call | bytes 37748736 | tf_op jit(solution)/shard_map/pallas_call | solution.py:678
  324.2 14.8 %all-gather.19.cloned.1.call-done = bf16[1,1024,768]{2,1,0:T(8,128)(2,1)} async-done(((bf16[1,128,768]{2,1,0:T(8,128)(2,1)}), bf16[1,1024,768]{2,1,0:T(8,128)(2,1)}) %all-gather.19.cloned.1.call-update) | async-done | bytes 1572880 | tf_op jit(solution)/shard_map/all_gather | solution.py:1133
  339.0 9.2 fusion.175
  352.7 14.1 %all-gather.4 = f32[8,3,1024]{2,1,0:T(4,128)S(1)} all-gather(f32[1,3,1024]{2,1,0:T(4,128)S(1)} %maximum_bitcast_fusion.2), channel_id=4, replica_groups=mesh['dp'=2,'fsdp'=8,'seq'=2] {'fsdp'}, dimensions={0}, use_global_device_ids=true | all-gather | bytes 110592 | tf_op jit(solution)/shard_map/all_gather | solution.py:1147
  368.9 12.5 %fusion.164 = f32[1024,768]{1,0:T(8,128)} fusion(bf16[4016,768]{1,0:T(8,128)(2,1)} %convert_element_type.841, f32[1024,4016]{0,1:T(8,128)S(1)} %get-tuple-element.528, f32[1024]{0:T(1024)S(1)} %get-tuple-element.457, s32[1024]{0:T(1024)S(1)} %copy-done.141, f32[1024]{0:T(1024)S(1)} %copy-done.155), kind=kOutput, calls=%fused_computation.417 | convolution fusion | flops 6341296128 | bytes 25776128 | tf_op jit(solution)/shard_map/dot_general | solution.py:1160
  382.3 16.7 %abs_reduce_fusion = (f32[]{:T(128)}, f32[4016,768]{1,0:T(8,128)}) fusion(bf16[1024,768]{1,0:T(8,128)(2,1)} %bitcast.496, f32[1024,4016]{0,1:T(8,128)} %copy-done.63, f32[1024]{0:T(1024)} %copy-done.154, s32[1024]{0:T(1024)} %get-tuple-element.505, f32[1024]{0:T(1024)} %get-tuple-element.502), kind=kOutput, calls=%fused_computation.18 | convolution fusion | flops 6347464704 | bytes 30371844 | tf_op jit(solution)/shard_map/nv,nd->vd/dot_general | solution.py:1165
  399.0 22.4 %reduce-scatter.5.cloned.1.call-done = f32[128,768]{1,0:T(8,128)} async-done(((f32[1024,768]{1,0:T(8,128)}), f32[128,768]{1,0:T(8,128)}) %reduce-scatter.5.cloned.1.call-update) | async-done | bytes 393232 | tf_op jit(solution)/shard_map/reduce_scatter | solution.py:1159
  468.1 8.6 dynamic-slice_bitcast_fusion
  481.6 9.0 fusion.18.g_ref
  503.4 15.5 %shard_map.429 = (f32[4,2,4,96,384]{4,3,2,1,0:T(8,128)S(1)}, bf16[4,2,4,96,384]{4,3,2,1,0:T(8,128)(2,1)S(1)}, f32[4,2,4,96,384]{4,3,2,1,0:T(8,128)S(1)}, bf16[4,2,4,96,384]{4,3,2,1,0:T(8,128)(2,1)}) custom-call(s32[3]{0:T(128)S(1)} %copy-done.60, bf16[32,4,192,384]{3,2,1,0:T(8,128)(2,1)} %bitcast.437, bf16[16,4,192,384]{3,2,1,0:T(8,128)(2,1)} %bitcast.464), custom_call_target="tpu_custom_call" | custom-call | flops 4718592 | bytes 47185920 | tf_op jit(solution)/shard_map/pallas_call | solution.py:749
  528.1 19.7 %shard_map.430 = (bf16[1,512,768]{2,1,0:T(8,128)(2,1)S(1)}, bf16[1,512,768]{2,1,0:T(8,128)(2,1)S(1)}, bf16[1,512,768]{2,1,0:T(8,128)(2,1)S(1)}, f32[12,5,128,128]{3,2,1,0:T(8,128)S(1)}) custom-call(bf16[1,512,2304]{2,1,0:T(8,128)(2,1)S(1)} %copy-done.2, bf16[1,512,2304]{2,1,0:T(8,128)(2,1)S(1)} %copy-done.2, bf16[1,512,2304]{2,1,0:T(8,128)(2,1)S(1)} %copy-done.2, ...), custom_call_target="tpu_custom_call" | custom-call | flops 4026531840 | bytes 7864320 | tf_op jit(solution)/shard_map/pallas_call | solution.py:255
  555.4 23.4 %collective-permute-done.14 = bf16[4,2,4,96,384]{4,3,2,0,1:T(8,128)(2,1)} collective-permute-done((bf16[4,2,4,96,384]{4,3,2,0,1:T(8,128)(2,1)}, bf16[4,2,4,96,384]{4,3,2,0,1:T(8,128)(2,1)}, u32[]{:S(2)}, u32[]{:S(2)}) %collective-permute-start.14) | collective-permute-done | bytes 2359328 | tf_op jit(solution)/shard_map/ppermute | solution.py:553
  623.0 11.8 %collective-permute-done.18 = bf16[4,12,192,384]{3,2,1,0:T(8,128)(2,1)S(1)} collective-permute-done((bf16[4,12,192,384]{3,2,1,0:T(8,128)(2,1)S(1)}, bf16[4,12,192,384]{3,2,1,0:T(8,128)(2,1)S(1)}, u32[]{:S(2)}, u32[]{:S(2)}) %collective-permute-start.18) | collective-permute-done | bytes 7077920 | tf_op jit(solution)/shard_map/ppermute | solution.py:553
  634.8 12.2 %shard_map.435 = (f32[4,2,3,96,384]{4,3,2,1,0:T(8,128)S(1)}, bf16[4,2,3,96,384]{4,3,2,1,0:T(8,128)(2,1)S(1)}, f32[4,2,3,96,384]{4,3,2,1,0:T(8,128)S(1)}, bf16[4,2,3,96,384]{4,3,2,1,0:T(8,128)(2,1)}) custom-call(s32[3]{0:T(128)S(1)} %copy-done.60, bf16[32,3,192,384]{3,2,1,0:T(8,128)(2,1)} %bitcast.439, bf16[16,3,192,384]{3,2,1,0:T(8,128)(2,1)S(1)} %bitcast.407), custom_call_target="tpu_custom_call" | custom-call | flops 3538944 | bytes 35389440 | tf_op jit(solution)/shard_map/pallas_call | solution.py:749
  678.9 43.9 %scatter_custom_fusion = f32[4016,768]{1,0:T(8,128)} fusion(f32[4016,768]{1,0:T(8,128)} %get-tuple-element.297, s32[5120]{0:T(1024)} %bitcast.485, bf16[5120,768]{1,0:T(8,128)(2,1)} %all-gather.13.cloned.1.call-done), kind=kCustom, calls=%fused_computation.9 | custom fusion | flops 7864320 | bytes 20201472 | tf_op jit(solution)/shard_map/scatter-add | solution.py:530
  736.0 8.2 multiply_convert_fusion.4
  750.0 11.3 %collective-permute-done.21 = bf16[4,3,96,384]{3,2,1,0:T(8,128)(2,1)} collective-permute-done((bf16[4,3,96,384]{3,2,1,0:T(8,128)(2,1)}, bf16[4,3,96,384]{3,2,1,0:T(8,128)(2,1)}, u32[]{:S(2)}, u32[]{:S(2)}) %collective-permute-start.21) | collective-permute-done | bytes 884768 | tf_op jit(solution)/shard_map/ppermute | solution.py:553
  792.3 15.7 %collective-permute-done.23 = f16[1016,768]{1,0:T(8,128)(2,1)} collective-permute-done((f16[1016,768]{1,0:T(8,128)(2,1)}, f16[1016,768]{1,0:T(8,128)(2,1)}, u32[]{:S(2)}, u32[]{:S(2)}) %collective-permute-start.23) | collective-permute-done | bytes 1560608 | tf_op jit(solution)/shard_map/ppermute | solution.py:553
  830.2 19.0 %shard_map.436 = (f32[32,192,192]{2,1,0:T(8,128)}, f32[32,192,192]{2,1,0:T(8,128)}, f32[32,192,192]{2,1,0:T(8,128)}, f32[32,192,192]{2,1,0:T(8,128)}) custom-call(f32[1]{0:T(128)} %bitcast.121.rest_ref, bf16[16,192,384]{2,1,0:T(8,128)(2,1)} %multiply_convert_fusion.2.g_ref, f32[32,192,192]{2,1,0:T(8,128)} %reshape.1312.lr_ref, f32[32,192,192]{2,1,0:T(8,128)} %reshape.1313.rr_ref), custom_call_target="tpu_custom_call" | custom-call | flops 4076863488 | bytes 33030144 | tf_op jit(solution)/shard_map/pallas_call | solution.py:457
  923.1 14.0 %shard_map.437 = (f32[24,192,192]{2,1,0:T(8,128)}, f32[24,192,192]{2,1,0:T(8,128)}, f32[24,192,192]{2,1,0:T(8,128)}, f32[24,192,192]{2,1,0:T(8,128)}) custom-call(f32[1]{0:T(128)} %bitcast.121.rest_ref, bf16[12,192,384]{2,1,0:T(8,128)(2,1)S(1)} %multiply_convert_fusion.3.g_ref, f32[24,192,192]{2,1,0:T(8,128)} %reshape.1309.lr_ref, ...), custom_call_target="tpu_custom_call" | custom-call | flops 3057647616 | bytes 24772608 | tf_op jit(solution)/shard_map/pallas_call | solution.py:457
  976.3 7.9 multiply_subtract_fusion.1
  1015.4 30.3 %multiply_subtract_fusion = (f32[4016,768]{1,0:T(8,128)}, f32[4016,768]{1,0:T(8,128)}, f32[4016,768]{1,0:T(8,128)}) fusion(f32[4016,768]{1,0:T(8,128)} %param.33, f32[]{:T(128)S(6)} %min.40, f32[]{:T(128)S(6)} %div.125, f32[]{:T(128)S(6)} %div.128, f16[1008,384]{1,0:T(8,128)(2,1)S(1)} %get-tuple-element.477, f16[1008,384]{1,0:T(8,128)(2,1)S(1)} %get-tuple-element.476, ...), kind=kLoop, calls=%fused_computation.15 | loop fusion | flops 104865792 | bytes 80216080 | tf_op jit(solution)/shard_map/sub | solution.py:973
  (713 shorter events, 523.9 us)
Async XLA Ops:
  7.2 148.1 %all-gather.11.cloned.1.call-start = ((), (), s32[]{:S(2)}) async-start(), calls=%async_computation.5 | async-start | bytes 14598144 | tf_op jit(solution)/shard_map/all_gather | solution.py:698
  33.7 115.2 %all-to-all-start = ((bf16[4,4,192,384]{3,2,1,0:T(8,128)(2,1)}), bf16[4,4,192,384]{3,2,1,0:T(8,128)(2,1)}, u32[]{:S(2)}, u32[]{:S(2)}) async-start(bf16[4,4,192,384]{3,2,1,0:T(8,128)(2,1)} %broadcast_in_dim.66), calls=%async_computation | async-start | bytes 4718592 | tf_op jit(solution)/shard_map/all_to_all | solution.py:607
  38.3 212.7 %reduce-scatter.3.cloned.1.call-start = ((), (), s32[]{:S(2)}) async-start(), calls=%async_computation.6 | async-start | bytes 8847360 | tf_op jit(solution)/shard_map/reduce_scatter | solution.py:1078
  155.3 183.8 %all-gather.19.cloned.1.call-start = ((), (), s32[]{:S(2)}) async-start(), calls=%async_computation.11 | async-start | bytes 1769472 | tf_op jit(solution)/shard_map/all_gather | solution.py:1133
  159.8 30.1 %collective-permute-start.2 = (bf16[4,4,96,384]{3,2,1,0:T(8,128)(2,1)}, bf16[4,4,96,384]{3,2,1,0:T(8,128)(2,1)S(1)}, u32[]{:S(2)}, u32[]{:S(2)}) collective-permute-start(bf16[4,4,96,384]{3,2,1,0:T(8,128)(2,1)} %get-tuple-element.219.refs_1_), channel_id=1, source_target_pairs={{0,16},{16,0},{1,17},{17,1},{2,18},{18,2},{3,19},{19,3},{4,20},{20... | collective-permute-start | bytes 3538952 | tf_op jit(solution)/shard_map/ppermute | solution.py:553
  161.3 28.6 %collective-permute-start.1 = (bf16[4,4,96,384]{3,2,1,0:T(8,128)(2,1)}, bf16[4,4,96,384]{3,2,1,0:T(8,128)(2,1)S(1)}, u32[]{:S(2)}, u32[]{:S(2)}) collective-permute-start(bf16[4,4,96,384]{3,2,1,0:T(8,128)(2,1)} %get-tuple-element.221.refs_0_), channel_id=1, source_target_pairs={{0,1},{1,0},{2,3},{3,2},{4,5},{5,4},{6,7},{7,6},{8,9},{9,8},{10,11... | collective-permute-start | bytes 3538952 | tf_op jit(solution)/shard_map/ppermute | solution.py:553
  192.8 53.9 %collective-permute-start.3 = (bf16[2,4,4,96,384]{4,3,2,1,0:T(8,128)(2,1)}, bf16[2,4,4,96,384]{4,3,2,1,0:T(8,128)(2,1)}, u32[]{:S(2)}, u32[]{:S(2)}) collective-permute-start(bf16[2,4,4,96,384]{4,3,2,1,0:T(8,128)(2,1)} %pad_maximum_fusion), channel_id=1, source_target_pairs={{0,1},{1,0},{2,3},{3,2},{4,5},{5,4},{6,7},{7,6},{8,9},{9,8},{10,11... | collective-permute-start | bytes 7077896 | tf_op jit(solution)/shard_map/ppermute | solution.py:553
  197.3 53.7 %collective-permute-start.4 = (bf16[2,4,4,96,384]{4,3,2,1,0:T(8,128)(2,1)}, bf16[2,4,4,96,384]{4,3,2,1,0:T(8,128)(2,1)}, u32[]{:S(2)}, u32[]{:S(2)}) collective-permute-start(bf16[2,4,4,96,384]{4,3,2,1,0:T(8,128)(2,1)} %pad_maximum_fusion.1), channel_id=1, source_target_pairs={{0,16},{16,0},{1,17},{17,1},{2,18},{18,2},{3,19},{19,3},{4,20},{20... | collective-permute-start | bytes 7077896 | tf_op jit(solution)/shard_map/ppermute | solution.py:553
  315.8 105.6 %reduce-scatter.5.cloned.1.call-start = ((), (), s32[]{:S(2)}) async-start(), calls=%async_computation.7 | async-start | bytes 3538944 | tf_op jit(solution)/shard_map/reduce_scatter | solution.py:1159
  381.4 274.6 %all-gather.13.cloned.1.call-start = ((), (), s32[]{:S(2)}) async-start(), calls=%async_computation.8 | async-start | bytes 8847360 | tf_op jit(solution)/shard_map/all_gather | solution.py:1236
  476.7 22.9 %collective-permute-start.13 = (bf16[4,16,192,384]{3,2,1,0:T(8,128)(2,1)}, bf16[4,16,192,384]{3,2,1,0:T(8,128)(2,1)S(1)}, u32[]{:S(2)}, u32[]{:S(2)}) collective-permute-start(bf16[4,16,192,384]{3,2,1,0:T(8,128)(2,1)} %dynamic-slice_bitcast_fusion), channel_id=1, source_target_pairs={{0,2},{2,0},{4,6},{6,4},{8,10},{10,8},{12,14},{14,12},{1,3},{3,1},... | collective-permute-start | bytes 28311560 | tf_op jit(solution)/shard_map/ppermute | solution.py:553
  524.9 54.0 %collective-permute-start.14 = (bf16[4,2,4,96,384]{4,3,2,0,1:T(8,128)(2,1)}, bf16[4,2,4,96,384]{4,3,2,0,1:T(8,128)(2,1)}, u32[]{:S(2)}, u32[]{:S(2)}) collective-permute-start(bf16[4,2,4,96,384]{4,3,2,0,1:T(8,128)(2,1)} %copy.117), channel_id=1, source_target_pairs={{0,1},{1,0},{2,3},{3,2},{4,5},{5,4},{6,7},{7,6},{8,9},{9,8},{10,11... | collective-permute-start | bytes 7077896 | tf_op jit(solution)/shard_map/ppermute | solution.py:553
  526.4 53.7 %collective-permute-start.15 = (bf16[4,2,4,96,384]{4,3,2,1,0:T(8,128)(2,1)}, bf16[4,2,4,96,384]{4,3,2,1,0:T(8,128)(2,1)}, u32[]{:S(2)}, u32[]{:S(2)}) collective-permute-start(bf16[4,2,4,96,384]{4,3,2,1,0:T(8,128)(2,1)} %get-tuple-element.271), channel_id=1, source_target_pairs={{0,16},{16,0},{1,17},{17,1},{2,18},{18,2},{3,19},{19,3},{4,20},{20... | collective-permute-start | bytes 7077896 | tf_op jit(solution)/shard_map/ppermute | solution.py:553
  585.2 31.1 %collective-permute-start.16 = (bf16[4,4,96,384]{3,2,1,0:T(8,128)(2,1)}, bf16[4,4,96,384]{3,2,1,0:T(8,128)(2,1)}, u32[]{:S(2)}, u32[]{:S(2)}) collective-permute-start(bf16[4,4,96,384]{3,2,1,0:T(8,128)(2,1)} %fusion.55), channel_id=1, source_target_pairs={{0,16},{16,0},{1,17},{17,1},{2,18},{18,2},{3,19},{19,3},{4,20},{20... | collective-permute-start | bytes 3538952 | tf_op jit(solution)/shard_map/ppermute | solution.py:553
  592.0 27.0 %collective-permute-start.17 = (bf16[4,4,96,384]{3,2,1,0:T(8,128)(2,1)}, bf16[4,4,96,384]{3,2,1,0:T(8,128)(2,1)}, u32[]{:S(2)}, u32[]{:S(2)}) collective-permute-start(bf16[4,4,96,384]{3,2,1,0:T(8,128)(2,1)} %fusion.56), channel_id=1, source_target_pairs={{0,1},{1,0},{2,3},{3,2},{4,5},{5,4},{6,7},{7,6},{8,9},{9,8},{10,11... | collective-permute-start | bytes 3538952 | tf_op jit(solution)/shard_map/ppermute | solution.py:553
  661.4 61.4 %all-to-all-start.1 = ((bf16[4,4,192,384]{3,2,1,0:T(8,128)(2,1)}), bf16[4,4,192,384]{3,2,1,0:T(8,128)(2,1)}, u32[]{:S(2)}, u32[]{:S(2)}) async-start(bf16[4,4,192,384]{3,2,1,0:T(8,128)(2,1)} %pad_maximum_fusion.2), calls=%async_computation.3 | async-start | bytes 4718592 | tf_op jit(solution)/shard_map/all_to_all | solution.py:848
  666.1 151.3 %all-gather.15.cloned.1.call-start = ((), (), s32[]{:S(2)}) async-start(), calls=%async_computation.9 | async-start | bytes 2949120 | tf_op jit(solution)/shard_map/all_gather | solution.py:856
  669.0 53.8 %collective-permute-start.20 = (bf16[4,2,3,96,384]{4,3,2,1,0:T(8,128)(2,1)}, bf16[4,2,3,96,384]{4,3,2,1,0:T(8,128)(2,1)}, u32[]{:S(2)}, u32[]{:S(2)}) collective-permute-start(bf16[4,2,3,96,384]{4,3,2,1,0:T(8,128)(2,1)} %get-tuple-element.288), channel_id=1, source_target_pairs={{0,16},{16,0},{1,17},{17,1},{2,18},{18,2},{3,19},{19,3},{4,20},{20... | collective-permute-start | bytes 5308424 | tf_op jit(solution)/shard_map/ppermute | solution.py:553
  670.5 52.3 %collective-permute-start.19 = (bf16[4,2,3,96,384]{4,3,2,0,1:T(8,128)(2,1)}, bf16[4,2,3,96,384]{4,3,2,0,1:T(8,128)(2,1)}, u32[]{:S(2)}, u32[]{:S(2)}) collective-permute-start(bf16[4,2,3,96,384]{4,3,2,0,1:T(8,128)(2,1)} %copy.121), channel_id=1, source_target_pairs={{0,1},{1,0},{2,3},{3,2},{4,5},{5,4},{6,7},{7,6},{8,9},{9,8},{10,11... | collective-permute-start | bytes 5308424 | tf_op jit(solution)/shard_map/ppermute | solution.py:553
  730.8 30.4 %collective-permute-start.21 = (bf16[4,3,96,384]{3,2,1,0:T(8,128)(2,1)}, bf16[4,3,96,384]{3,2,1,0:T(8,128)(2,1)}, u32[]{:S(2)}, u32[]{:S(2)}) collective-permute-start(bf16[4,3,96,384]{3,2,1,0:T(8,128)(2,1)} %fusion.63), channel_id=1, source_target_pairs={{0,16},{16,0},{1,17},{17,1},{2,18},{18,2},{3,19},{19,3},{4,20},{20... | collective-permute-start | bytes 2654216 | tf_op jit(solution)/shard_map/ppermute | solution.py:553
  735.4 31.4 %collective-permute-start.22 = (bf16[4,3,96,384]{3,2,1,0:T(8,128)(2,1)}, bf16[4,3,96,384]{3,2,1,0:T(8,128)(2,1)S(1)}, u32[]{:S(2)}, u32[]{:S(2)}) collective-permute-start(bf16[4,3,96,384]{3,2,1,0:T(8,128)(2,1)} %fusion.64), channel_id=1, source_target_pairs={{0,1},{1,0},{2,3},{3,2},{4,5},{5,4},{6,7},{7,6},{8,9},{9,8},{10,11... | collective-permute-start | bytes 2654216 | tf_op jit(solution)/shard_map/ppermute | solution.py:553
  766.8 41.2 %collective-permute-start.23 = (f16[1016,768]{1,0:T(8,128)(2,1)}, f16[1016,768]{1,0:T(8,128)(2,1)}, u32[]{:S(2)}, u32[]{:S(2)}) collective-permute-start(f16[1016,768]{1,0:T(8,128)(2,1)} %concatenate.103), channel_id=1, source_target_pairs={{0,1},{1,0},{2,3},{3,2},{4,5},{5,4},{6,7},{7,6},{8,9},{9,8},{10,11... | collective-permute-start | bytes 4681736 | tf_op jit(solution)/shard_map/ppermute | solution.py:553
  767.1 42.7 %collective-permute-start.24 = (f16[1016,768]{1,0:T(8,128)(2,1)}, f16[1016,768]{1,0:T(8,128)(2,1)}, u32[]{:S(2)}, u32[]{:S(2)}) collective-permute-start(f16[1016,768]{1,0:T(8,128)(2,1)} %concatenate.104), channel_id=1, source_target_pairs={{0,16},{16,0},{1,17},{17,1},{2,18},{18,2},{3,19},{19,3},{4,20},{20... | collective-permute-start | bytes 4681736 | tf_op jit(solution)/shard_map/ppermute | solution.py:553
  774.3 82.9 %all-to-all-start.2 = ((bf16[4,3,192,384]{3,2,1,0:T(8,128)(2,1)}), bf16[4,3,192,384]{3,2,1,0:T(8,128)(2,1)}, u32[]{:S(2)}, u32[]{:S(2)}) async-start(bf16[4,3,192,384]{3,2,1,0:T(8,128)(2,1)} %pad_maximum_fusion.3), calls=%async_computation.4 | async-start | bytes 3538944 | tf_op jit(solution)/shard_map/all_to_all | solution.py:848
  779.2 142.1 %all-gather.17.cloned.1.call-start = ((), (), s32[]{:S(2)}) async-start(), calls=%async_computation.10 | async-start | bytes 2211840 | tf_op jit(solution)/shard_map/all_gather | solution.py:856
  820.6 28.6 %collective-permute-start.25 = (f16[1016,384]{1,0:T(8,128)(2,1)}, f16[1016,384]{1,0:T(8,128)(2,1)}, u32[]{:S(2)}, u32[]{:S(2)}) collective-permute-start(f16[1016,384]{1,0:T(8,128)(2,1)} %concatenate.106), channel_id=1, source_target_pairs={{0,16},{16,0},{1,17},{17,1},{2,18},{18,2},{3,19},{19,3},{4,20},{20... | collective-permute-start | bytes 2340872 | tf_op jit(solution)/shard_map/ppermute | solution.py:553
  825.9 25.2 %collective-permute-start.26 = (f16[1016,384]{1,0:T(8,128)(2,1)}, f16[1016,384]{1,0:T(8,128)(2,1)}, u32[]{:S(2)}, u32[]{:S(2)}) collective-permute-start(f16[1016,384]{1,0:T(8,128)(2,1)} %concatenate.107), channel_id=1, source_target_pairs={{0,1},{1,0},{2,3},{3,2},{4,5},{5,4},{6,7},{7,6},{8,9},{9,8},{10,11... | collective-permute-start | bytes 2340872 | tf_op jit(solution)/shard_map/ppermute | solution.py:553
  878.8 38.1 %collective-permute-start.30 = (f16[1008,384]{1,0:T(8,128)(2,1)S(1)}, f16[1008,384]{1,0:T(8,128)(2,1)}, u32[]{:S(2)}, u32[]{:S(2)}) collective-permute-start(f16[1008,384]{1,0:T(8,128)(2,1)S(1)} %convert_element_type.985), channel_id=1, source_target_pairs={{0,1},{1,0},{2,3},{3,2},{4,5},{5,4},{6,7},{7,6},{8,9},{9,8},{10,11... | collective-permute-start | bytes 2322440 | tf_op jit(solution)/shard_map/ppermute | solution.py:553
  881.4 37.0 %collective-permute-start.29 = (f16[1008,384]{1,0:T(8,128)(2,1)}, f16[1008,384]{1,0:T(8,128)(2,1)}, u32[]{:S(2)}, u32[]{:S(2)}) collective-permute-start(f16[1008,384]{1,0:T(8,128)(2,1)} %convert_element_type.984), channel_id=1, source_target_pairs={{0,16},{16,0},{1,17},{17,1},{2,18},{18,2},{3,19},{19,3},{4,20},{20... | collective-permute-start | bytes 2322440 | tf_op jit(solution)/shard_map/ppermute | solution.py:553
  887.7 29.1 %collective-permute-start.33 = (f32[49,128]{1,0:T(8,128)S(1)}, f32[49,128]{1,0:T(8,128)S(1)}, u32[]{:S(2)}, u32[]{:S(2)}) collective-permute-start(f32[49,128]{1,0:T(8,128)S(1)} %add.1022), channel_id=1, source_target_pairs={{0,8},{2,10},{4,12},{6,14},{8,0},{10,2},{12,4},{14,6},{1,9},{3,11}... | collective-permute-start | bytes 75272 | tf_op jit(solution)/shard_map/ppermute | solution.py:808
  946.9 63.4 %collective-permute-start.34 = (f16[2,1008,384]{2,1,0:T(8,128)(2,1)}, f16[2,1008,384]{2,1,0:T(8,128)(2,1)}, u32[]{:S(2)}, u32[]{:S(2)}) collective-permute-start(f16[2,1008,384]{2,1,0:T(8,128)(2,1)} %pad_maximum_fusion.4), channel_id=1, source_target_pairs={{0,1},{1,0},{2,3},{3,2},{4,5},{5,4},{6,7},{7,6},{8,9},{9,8},{10,11... | collective-permute-start | bytes 4644872 | tf_op jit(solution)/shard_map/ppermute | solution.py:553
  947.3 65.8 %collective-permute-start.35 = (f16[2,1008,384]{2,1,0:T(8,128)(2,1)S(1)}, f16[2,1008,384]{2,1,0:T(8,128)(2,1)}, u32[]{:S(2)}, u32[]{:S(2)}) collective-permute-start(f16[2,1008,384]{2,1,0:T(8,128)(2,1)S(1)} %pad_maximum_fusion.5), channel_id=1, source_target_pairs={{0,16},{16,0},{1,17},{17,1},{2,18},{18,2},{3,19},{19,3},{4,20},{20... | collective-permute-start | bytes 4644872 | tf_op jit(solution)/shard_map/ppermute | solution.py:553
  (196 other events, 1939.9 us)
Sparse Core Ops, SparseCore 0:
  17.7 137.5 all-gather.10
  158.1 82.8 reduce-scatter.2
  315.9 23.0 all-gather.18
  381.5 39.9 reduce-scatter.4
  580.2 75.7 all-gather.12
  726.8 53.5 all-gather.14
  860.8 43.1 all-gather.16
